TPU v7x, 128 devices: a whole 4x4x4 slice. The times are simulated.
128 devices in a mesh: row: 16 (over z, y), col: 8 (over x, core).
Axes of the slice: x: 4, y: 4, z: 4, core: 2. Of those that a mesh axis runs over, the one named last changes fastest.
Arguments:
- frame_one: bfloat16 [256, 256, 256], P('row', 'col'), may hold values from -6 to 6
- frame_two: bfloat16 [256, 256, 256], P('row', 'col'), may hold values from -6 to 6
- context: bfloat16 [256, 256, 256], P('row', 'col'), may hold values from -6 to 6
- cotangent: bfloat16 [256, 256, 128], P('row', 'col'), may hold values from -6 to 6
- corr_weight: bfloat16 [324, 256], replicated, may hold values from -0.3125 to 0.3125
- conv_weight: bfloat16 [3, 3, 256, 128], replicated, may hold values from -0.125 to 0.125
- partners: int32 [16, 8, 4], P('row', 'col'), may hold values from 0 to 14, as said below
- counts: int32 [16, 8], P('row', 'col'), may hold values from 1 to 4
- radius: int32 [16, 8], P('row', 'col'), may hold values from 1 to 4
Outputs:
- motion_features: bfloat16 [256, 256, 128], P('row', 'col')
- context_grad: bfloat16 [256, 256, 256], P('row', 'col')
- frame_one_grad: float32 [256, 256, 256], P('row', 'col')
- frame_two_grad: float32 [256, 256, 256], P('row', 'col')
- corr_weight_grad: float32 [324, 256], replicated
- conv_weight_grad: float32 [3, 3, 256, 128], replicated
Inputs may be any that keep to these rules, and one draw needn't show every extreme that they name: `partners`: each tile's 4 entries are different offsets. Offset 7 denotes the tile itself (dy = 0, dx = 0); it need not be among a tile's entries.
All inputs are finite; a program needn't handle non-finite values.
Results may differ from a plain program's by a relative error of at most 0.0075.
Values may be sent and summed in bfloat16 or wider, within the bound.
No kernel may reach another device: no remote copies, remote signals or barrier semaphores. Data moves between devices by JAX's collectives and lax.ppermute only.
A program may use at most 192 MiB of HBM per device.

v0:
```python
import math

import jax
import jax.numpy as jnp
from jax import lax
from jax.sharding import PartitionSpec as P

REACH = 4


def from_behind(array, axis, by):
    peers = lax.axis_size(axis)
    pairs = [(i, i + by) for i in range(peers) if 0 <= i + by < peers]
    return lax.ppermute(array, axis, pairs)


def with_halo(cells, sides, width):
    for axis, dim in sides:
        count = lax.axis_size(axis)
        ends = count - 1
        head = lax.slice_in_dim(cells, 0, width, axis=dim)
        tail = lax.slice_in_dim(cells, cells.shape[dim] - width, cells.shape[dim], axis=dim)
        cells = jnp.concatenate(
            [
                lax.ppermute(tail, axis, [(i, (i + 1) % count) for i in range(ends)]),
                cells,
                lax.ppermute(head, axis, [((i + 1) % count, i) for i in range(ends)]),
            ],
            axis=dim,
        )
    return cells


def take_band(scores):
    leading = scores.shape[:-2]
    across = scores.shape[-2]
    flat = scores.reshape(leading + (across * (across + 8),))
    flat = jnp.pad(flat, [(0, 0)] * len(leading) + [(0, across)])
    return flat.reshape(leading + (across, across + 9))[..., :9]


def spread_band(band):
    leading = band.shape[:-2]
    across = band.shape[-2]
    wide = jnp.pad(band, [(0, 0)] * len(leading) + [(0, 0), (0, across)])
    flat = wide.reshape(leading + (across * (across + 9),))[..., : across * (across + 8)]
    return flat.reshape(leading + (across, across + 8))


def part_gradient(grad_scores, source, scale):
    rows_tile, cols_tile, channels = source.shape
    span = grad_scores.shape[0]
    grad_windows = jnp.einsum(
        "uabe,abc->uaec", grad_scores, source, preferred_element_type=jnp.float32
    )
    summed = jnp.zeros((rows_tile + 2 * REACH, cols_tile + 2 * REACH, channels), jnp.float32)
    for tap_row in range(span):
        summed = summed.at[tap_row : tap_row + rows_tile].add(grad_windows[tap_row])
    return summed[REACH : REACH + rows_tile, REACH : REACH + cols_tile] * scale


def body(
    frame_one, frame_two, context, cotangent, corr_weight, conv_weight, partners, counts, radius
):
    rows_tile, cols_tile, channels = frame_one.shape
    slots = partners.shape[-1]
    span = 2 * REACH + 1
    width = slots * span * span
    cells = rows_tile * cols_tile
    hidden_width = context.shape[-1]
    out_width = conv_weight.shape[-1]
    scale = 1.0 / math.sqrt(channels)
    offsets = partners[0, 0]
    live = (jnp.arange(slots) < counts[0, 0]).astype(jnp.float32)
    inside = (jnp.abs(jnp.arange(span) - REACH) <= radius[0, 0]).astype(jnp.float32)
    mask = live[:, None, None] * inside[None, :, None] * inside[None, None, :]
    gathered = []
    for row_step in (-1, 0, 1):
        for col_step in (-2, -1, 0, 1, 2):
            moved = frame_two
            if row_step != 0:
                moved = from_behind(moved, "row", -row_step)
            if col_step != 0:
                moved = from_behind(moved, "col", -col_step)
            gathered.append(moved)
    candidates = jnp.stack(gathered)
    parts = jnp.take(candidates, offsets, axis=0)
    padded = jnp.pad(parts, ((0, 0), (REACH, REACH), (REACH, REACH), (0, 0)))
    windows = []
    bands = []
    for member in range(slots):
        stacked = jnp.stack(
            [padded[member, tap_row : tap_row + rows_tile] for tap_row in range(span)]
        )
        windows.append(stacked)
        scores = jnp.einsum(
            "abc,uaec->uabe", frame_one, stacked, preferred_element_type=jnp.float32
        )
        bands.append(take_band(scores))
    volume = jnp.stack(bands).transpose(2, 3, 0, 1, 4) * mask * scale
    corr_feat = volume.astype(jnp.bfloat16).reshape(cells, width)
    pre = jnp.dot(corr_feat, corr_weight, preferred_element_type=jnp.float32) + context.reshape(
        cells, hidden_width
    ).astype(jnp.float32)
    motion = jax.nn.silu(pre).astype(jnp.bfloat16).reshape(rows_tile, cols_tile, hidden_width)
    rimmed = with_halo(motion, (("row", 0), ("col", 1)), 1)
    grad_rim = with_halo(cotangent, (("row", 0), ("col", 1)), 1)
    flat_cot = cotangent.reshape(cells, out_width)
    output = jnp.zeros((cells, out_width), jnp.float32)
    grad_motion = jnp.zeros((cells, hidden_width), jnp.float32)
    conv_terms = []
    for tap_row in range(3):
        for tap_col in range(3):
            window = rimmed[tap_row : tap_row + rows_tile, tap_col : tap_col + cols_tile].reshape(
                cells, hidden_width
            )
            output = output + jnp.dot(
                window, conv_weight[tap_row, tap_col], preferred_element_type=jnp.float32
            )
            back = grad_rim[
                2 - tap_row : 2 - tap_row + rows_tile, 2 - tap_col : 2 - tap_col + cols_tile
            ].reshape(cells, out_width)
            grad_motion = grad_motion + jnp.dot(
                back, conv_weight[tap_row, tap_col].T, preferred_element_type=jnp.float32
            )
            conv_terms.append(
                lax.dot_general(
                    window, flat_cot, (((0,), (0,)), ((), ())), preferred_element_type=jnp.float32
                )
            )
    features = output.astype(jnp.bfloat16).reshape(rows_tile, cols_tile, out_width)
    conv_grad = jnp.stack(conv_terms).reshape(3, 3, hidden_width, out_width)
    sigma = jax.nn.sigmoid(pre)
    context_grad = (grad_motion * sigma * (1.0 + pre * (1.0 - sigma))).astype(jnp.bfloat16)
    corr_grad = lax.dot_general(
        corr_feat, context_grad, (((0,), (0,)), ((), ())), preferred_element_type=jnp.float32
    )
    corr_total, conv_total = lax.psum((corr_grad, conv_grad), ("row", "col"))
    grad_volume = jnp.dot(context_grad, corr_weight.T, preferred_element_type=jnp.float32).astype(
        jnp.bfloat16
    )
    grad_volume = grad_volume.reshape(rows_tile, cols_tile, slots, span, span) * mask.astype(
        jnp.bfloat16
    )
    grad_bands = grad_volume.transpose(2, 3, 0, 1, 4)
    first_grad = jnp.zeros((rows_tile, cols_tile, channels), jnp.float32)
    score_list = []
    for member in range(slots):
        grad_scores = spread_band(grad_bands[member])
        score_list.append(grad_scores)
        first_grad = first_grad + jnp.einsum(
            "uabe,uaec->abc", grad_scores, windows[member], preferred_element_type=jnp.float32
        )
    first_grad = first_grad * scale
    part_grads = [part_gradient(score_list[member], frame_one, scale) for member in range(slots)]
    slot_grads = (
        jnp.zeros((15,) + frame_two.shape, jnp.float32).at[offsets].add(jnp.stack(part_grads))
    )
    grid = slot_grads.reshape((3, 5) + frame_two.shape)
    middle = grid[1]
    for row_step, which_row in ((-1, 0), (1, 2)):
        middle = middle + from_behind(grid[which_row].astype(jnp.bfloat16), "row", row_step).astype(
            jnp.float32
        )
    second_grad = middle[2]
    for col_step in (-2, -1, 1, 2):
        second_grad = second_grad + from_behind(
            middle[col_step + 2].astype(jnp.bfloat16), "col", col_step
        ).astype(jnp.float32)
    return (
        features,
        context_grad.reshape(rows_tile, cols_tile, hidden_width),
        first_grad,
        second_grad,
        corr_total,
        conv_total,
    )


def solution(mesh):
    return jax.shard_map(
        body,
        mesh=mesh,
        in_specs=(
            P("row", "col", None),
            P("row", "col", None),
            P("row", "col", None),
            P("row", "col", None),
            P(),
            P(),
            P("row", "col", None),
            P("row", "col"),
            P("row", "col"),
        ),
        out_specs=(
            P("row", "col", None),
            P("row", "col", None),
            P("row", "col", None),
            P("row", "col", None),
            P(),
            P(),
        ),
        check_vma=False,
    )
```

profile of v0, /device:TPU:33, one launch (start us, length us, event | category | flops | bytes accessed | tf_op | source)
XLA Modules:
  0.0 452.0 jit_solution(13808255943673122853)
XLA Ops:
  7.2 3.3 collective-permute-start
  13.7 4.2 collective-permute-start.6
  18.7 4.2 collective-permute-start.19
  32.4 3.6 collective-permute-start.21
  39.1 4.3 collective-permute-start.9
  68.1 3.3 collective-permute-start.10
  72.1 3.5 collective-permute-start.11
  85.6 3.9 collective-permute-done.13
  103.3 3.2 reshape.1413
  113.3 3.4 copy.46
  116.7 3.7 convolution_bitcast_fusion.5
  120.4 3.5 reshape.1412
  130.6 3.4 copy.45
  134.0 3.7 convolution_bitcast_fusion.6
  147.6 3.4 copy.44
  151.0 3.7 convolution_bitcast_fusion.7
  154.7 3.7 reshape.1410
  165.1 3.5 copy.43
  174.7 5.1 %copy.47 = bf16[16,32,4,9,9]{4,1,0,3,2:T(8,128)(2,1)} copy(bf16[16,32,4,9,9]{1,0,4,3,2:T(8,128)(2,1)S(1)} %reshape.1338) | data formatting | bytes 663552 | tf_op jit(solution)/shard_map/reshape | solution.py:142
  192.2 3.8 fusion.12
  196.0 3.5 convolution_bitcast_fusion.3
  202.1 3.4 collective-permute-start.14
  213.0 4.9 %convolution_bitcast_fusion.2 = f32[9,16,40,256]{3,2,1,0:T(8,128)} fusion(bf16[9,16,32,40]{3,2,1,0:T(8,128)(2,1)} %reshape.1342, bf16[16,32,256]{2,1,0:T(8,128)(2,1)S(1)} %copy-done), kind=kOutput, calls=%fused_computation.54 | convolution fusion | flops 94371840 | bytes 6529024 | tf_op jit(solution)/shard_map/uabe,abc->uaec/dot_general | solution.py:53
  226.8 4.9 %convolution_bitcast_fusion.1 = f32[9,16,40,256]{3,2,1,0:T(8,128)} fusion(bf16[9,16,32,40]{3,2,1,0:T(8,128)(2,1)} %reshape.1344, bf16[16,32,256]{2,1,0:T(8,128)(2,1)S(1)} %copy-done), kind=kOutput, calls=%fused_computation.53 | convolution fusion | flops 94371840 | bytes 6529024 | tf_op jit(solution)/shard_map/uabe,abc->uaec/dot_general | solution.py:53
  253.3 4.1 broadcast_in_dim.21
  257.5 4.5 scatter_fusion
  262.0 3.8 convert.11
  270.7 5.4 %collective-permute-start.22 = (bf16[5,16,32,256]{3,2,1,0:T(8,128)(2,1)}, bf16[5,16,32,256]{3,2,1,0:T(8,128)(2,1)}, u32[]{:S(2)}, u32[]{:S(2)}) collective-permute-start(bf16[5,16,32,256]{3,2,1,0:T(8,128)(2,1)} %get-tuple-element.446), channel_id=1, source_target_pairs={{8,0},{16,8},{24,16},{32,24},{40,32},{48,40},{56,48},{64,56},{72,6... | collective-permute-start | bytes 3932168 | tf_op jit(solution)/shard_map/ppermute | solution.py:14
  276.9 5.3 %collective-permute-start.16 = (bf16[18,1,256]{2,1,0:T(2,128)(2,1)S(1)}, bf16[18,1,256]{2,1,0:T(2,128)(2,1)S(1)}, u32[]{:S(2)}, u32[]{:S(2)}) collective-permute-start(bf16[18,1,256]{2,1,0:T(2,128)(2,1)S(1)} %get-tuple-element.469), channel_id=1, source_target_pairs={{0,1},{1,2},{2,3},{3,4},{4,5},{5,6},{6,7},{8,9},{9,10},{10,11},{11... | collective-permute-start | bytes 27656 | tf_op jit(solution)/shard_map/ppermute | solution.py:25
  309.0 4.8 %collective-permute-start.26 = (bf16[16,32,256]{2,1,0:T(8,128)(2,1)S(1)}, bf16[16,32,256]{2,1,0:T(8,128)(2,1)S(1)}, u32[]{:S(2)}, u32[]{:S(2)}) collective-permute-start(bf16[16,32,256]{2,1,0:T(8,128)(2,1)S(1)} %get-tuple-element.450), channel_id=1, source_target_pairs={{0,1},{1,2},{2,3},{3,4},{4,5},{5,6},{6,7},{8,9},{9,10},{10,11},{11... | collective-permute-start | bytes 786440 | tf_op jit(solution)/shard_map/ppermute | solution.py:14
  319.2 4.7 %collective-permute-done.25 = bf16[16,32,256]{2,1,0:T(8,128)(2,1)S(1)} collective-permute-done((bf16[16,32,256]{2,1,0:T(8,128)(2,1)S(1)}, bf16[16,32,256]{2,1,0:T(8,128)(2,1)S(1)}, u32[]{:S(2)}, u32[]{:S(2)}) %collective-permute-start.25) | collective-permute-done | bytes 262176 | tf_op jit(solution)/shard_map/ppermute | solution.py:14
  327.6 112.9 %all-reduce.16.cloned.1.call-done = (f32[324,256]{1,0:T(8,128)}, f32[3,3,256,128]{3,2,1,0:T(8,128)}) async-done(((f32[324,256]{1,0:T(8,128)}, f32[3,3,256,128]{3,2,1,0:T(8,128)}), (f32[324,256]{1,0:T(8,128)}, f32[3,3,256,128]{3,2,1,0:T(8,128)})) %all-reduce.16.cloned.1.call-update) | async-done | bytes 1511440 | tf_op jit(solution)/shard_map/psum | solution.py:138
  (311 shorter events, 198.0 us)
Async XLA Ops:
  7.2 94.3 %copy-start = (bf16[16,32,256]{2,1,0:T(8,128)(2,1)S(1)}, bf16[16,32,256]{2,1,0:T(8,128)(2,1)}, u32[]{:S(2)}) copy-start(bf16[16,32,256]{2,1,0:T(8,128)(2,1)} %param.81) | copy-start | bytes 786436
  7.2 37.1 %copy-start.15 = (bf16[3,3,256,128]{3,2,1,0:T(8,128)(2,1)S(1)}, bf16[3,3,256,128]{3,2,1,0:T(8,128)(2,1)}, u32[]{:S(2)}) copy-start(bf16[3,3,256,128]{3,2,1,0:T(8,128)(2,1)} %param.86) | copy-start | bytes 1769476
  7.2 433.4 %all-reduce.16.cloned.1.call-start = ((), (), s32[]{:S(2)}) async-start(), calls=%async_computation | async-start | bytes 3031040 | tf_op jit(solution)/shard_map/psum | solution.py:138
  7.2 38.0 %collective-permute-start = (bf16[16,32,256]{2,1,0:T(8,128)(2,1)}, bf16[16,32,256]{2,1,0:T(8,128)(2,1)S(1)}, u32[]{:S(2)}, u32[]{:S(2)}) collective-permute-start(bf16[16,32,256]{2,1,0:T(8,128)(2,1)} %param.82), channel_id=1, source_target_pairs={{0,8},{8,16},{16,24},{24,32},{32,40},{40,48},{48,56},{56,64},{64,7... | collective-permute-start | bytes 786440 | tf_op jit(solution)/shard_map/ppermute | solution.py:14
  10.6 61.6 %collective-permute-start.5 = (bf16[16,32,256]{2,1,0:T(8,128)(2,1)}, bf16[16,32,256]{2,1,0:T(8,128)(2,1)S(1)}, u32[]{:S(2)}, u32[]{:S(2)}) collective-permute-start(bf16[16,32,256]{2,1,0:T(8,128)(2,1)} %param.82), channel_id=1, source_target_pairs={{0,2},{1,3},{2,4},{3,5},{4,6},{5,7},{8,10},{9,11},{10,12},{11,13},... | collective-permute-start | bytes 786440 | tf_op jit(solution)/shard_map/ppermute | solution.py:14
  13.7 62.6 %collective-permute-start.6 = (bf16[16,32,256]{2,1,0:T(8,128)(2,1)}, bf16[16,32,256]{2,1,0:T(8,128)(2,1)S(1)}, u32[]{:S(2)}, u32[]{:S(2)}) collective-permute-start(bf16[16,32,256]{2,1,0:T(8,128)(2,1)} %param.82), channel_id=1, source_target_pairs={{0,1},{1,2},{2,3},{3,4},{4,5},{5,6},{6,7},{8,9},{9,10},{10,11},{11... | collective-permute-start | bytes 786440 | tf_op jit(solution)/shard_map/ppermute | solution.py:14
  18.7 10.7 %collective-permute-start.19 = (bf16[1,32,128]{2,1,0:T(8,128)(2,1)S(1)}, bf16[1,32,128]{2,1,0:T(8,128)(2,1)S(1)}, u32[]{:S(2)}, u32[]{:S(2)}) collective-permute-start(bf16[1,32,128]{2,1,0:T(8,128)(2,1)S(1)} %get-tuple-element.489), channel_id=1, source_target_pairs={{8,0},{16,8},{24,16},{32,24},{40,32},{48,40},{56,48},{64,56},{72,6... | collective-permute-start | bytes 24584 | tf_op jit(solution)/shard_map/ppermute | solution.py:27
  22.9 6.5 %collective-permute-start.18 = (bf16[1,32,128]{2,1,0:T(8,128)(2,1)S(1)}, bf16[1,32,128]{2,1,0:T(8,128)(2,1)S(1)}, u32[]{:S(2)}, u32[]{:S(2)}) collective-permute-start(bf16[1,32,128]{2,1,0:T(8,128)(2,1)S(1)} %get-tuple-element.490), channel_id=1, source_target_pairs={{0,8},{8,16},{16,24},{24,32},{32,40},{40,48},{48,56},{56,64},{64,7... | collective-permute-start | bytes 24584 | tf_op jit(solution)/shard_map/ppermute | solution.py:25
  30.5 8.6 %collective-permute-start.20 = (bf16[18,1,128]{2,1,0:T(2,128)(2,1)S(1)}, bf16[18,1,128]{2,1,0:T(2,128)(2,1)S(1)}, u32[]{:S(2)}, u32[]{:S(2)}) collective-permute-start(bf16[18,1,128]{2,1,0:T(2,128)(2,1)S(1)} %get-tuple-element.484), channel_id=1, source_target_pairs={{1,0},{2,1},{3,2},{4,3},{5,4},{6,5},{7,6},{9,8},{10,9},{11,10},{12... | collective-permute-start | bytes 13832 | tf_op jit(solution)/shard_map/ppermute | solution.py:27
  32.4 11.0 %collective-permute-start.21 = (bf16[18,1,128]{2,1,0:T(2,128)(2,1)S(1)}, bf16[18,1,128]{2,1,0:T(2,128)(2,1)S(1)}, u32[]{:S(2)}, u32[]{:S(2)}) collective-permute-start(bf16[18,1,128]{2,1,0:T(2,128)(2,1)S(1)} %get-tuple-element.485), channel_id=1, source_target_pairs={{0,1},{1,2},{2,3},{3,4},{4,5},{5,6},{6,7},{8,9},{9,10},{10,11},{11... | collective-permute-start | bytes 13832 | tf_op jit(solution)/shard_map/ppermute | solution.py:25
  39.1 26.4 %collective-permute-start.9 = (bf16[16,32,256]{2,1,0:T(8,128)(2,1)}, bf16[16,32,256]{2,1,0:T(8,128)(2,1)S(1)}, u32[]{:S(2)}, u32[]{:S(2)}) collective-permute-start(bf16[16,32,256]{2,1,0:T(8,128)(2,1)} %param.82), channel_id=1, source_target_pairs={{8,0},{16,8},{24,16},{32,24},{40,32},{48,40},{56,48},{64,56},{72,6... | collective-permute-start | bytes 786440 | tf_op jit(solution)/shard_map/ppermute | solution.py:14
  45.2 8.9 %collective-permute-start.1 = (bf16[16,32,256]{2,1,0:T(8,128)(2,1)S(1)}, bf16[16,32,256]{2,1,0:T(8,128)(2,1)S(1)}, u32[]{:S(2)}, u32[]{:S(2)}) collective-permute-start(bf16[16,32,256]{2,1,0:T(8,128)(2,1)S(1)} %collective-permute-done), channel_id=1, source_target_pairs={{0,2},{1,3},{2,4},{3,5},{4,6},{5,7},{8,10},{9,11},{10,12},{11,13},... | collective-permute-start | bytes 786440 | tf_op jit(solution)/shard_map/ppermute | solution.py:14
  49.1 8.0 %collective-permute-start.2 = (bf16[16,32,256]{2,1,0:T(8,128)(2,1)S(1)}, bf16[16,32,256]{2,1,0:T(8,128)(2,1)S(1)}, u32[]{:S(2)}, u32[]{:S(2)}) collective-permute-start(bf16[16,32,256]{2,1,0:T(8,128)(2,1)S(1)} %collective-permute-done), channel_id=1, source_target_pairs={{0,1},{1,2},{2,3},{3,4},{4,5},{5,6},{6,7},{8,9},{9,10},{10,11},{11... | collective-permute-start | bytes 786440 | tf_op jit(solution)/shard_map/ppermute | solution.py:14
  54.2 8.6 %collective-permute-start.3 = (bf16[16,32,256]{2,1,0:T(8,128)(2,1)S(1)}, bf16[16,32,256]{2,1,0:T(8,128)(2,1)S(1)}, u32[]{:S(2)}, u32[]{:S(2)}) collective-permute-start(bf16[16,32,256]{2,1,0:T(8,128)(2,1)S(1)} %collective-permute-done), channel_id=1, source_target_pairs={{1,0},{2,1},{3,2},{4,3},{5,4},{6,5},{7,6},{9,8},{10,9},{11,10},{12... | collective-permute-start | bytes 786440 | tf_op jit(solution)/shard_map/ppermute | solution.py:14
  57.1 11.0 %collective-permute-start.4 = (bf16[16,32,256]{2,1,0:T(8,128)(2,1)S(1)}, bf16[16,32,256]{2,1,0:T(8,128)(2,1)S(1)}, u32[]{:S(2)}, u32[]{:S(2)}) collective-permute-start(bf16[16,32,256]{2,1,0:T(8,128)(2,1)S(1)} %collective-permute-done), channel_id=1, source_target_pairs={{2,0},{3,1},{4,2},{5,3},{6,4},{7,5},{10,8},{11,9},{12,10},{13,11},... | collective-permute-start | bytes 786440 | tf_op jit(solution)/shard_map/ppermute | solution.py:14
  62.8 17.0 %collective-permute-start.7 = (bf16[16,32,256]{2,1,0:T(8,128)(2,1)S(1)}, bf16[16,32,256]{2,1,0:T(8,128)(2,1)S(1)}, u32[]{:S(2)}, u32[]{:S(2)}) collective-permute-start(bf16[16,32,256]{2,1,0:T(8,128)(2,1)S(1)} %copy-done.26), channel_id=1, source_target_pairs={{1,0},{2,1},{3,2},{4,3},{5,4},{6,5},{7,6},{9,8},{10,9},{11,10},{12... | collective-permute-start | bytes 786440 | tf_op jit(solution)/shard_map/ppermute | solution.py:14
  65.4 16.6 %collective-permute-start.8 = (bf16[16,32,256]{2,1,0:T(8,128)(2,1)S(1)}, bf16[16,32,256]{2,1,0:T(8,128)(2,1)S(1)}, u32[]{:S(2)}, u32[]{:S(2)}) collective-permute-start(bf16[16,32,256]{2,1,0:T(8,128)(2,1)S(1)} %copy-done.26), channel_id=1, source_target_pairs={{2,0},{3,1},{4,2},{5,3},{6,4},{7,5},{10,8},{11,9},{12,10},{13,11},... | collective-permute-start | bytes 786440 | tf_op jit(solution)/shard_map/ppermute | solution.py:14
  68.1 14.6 %collective-permute-start.10 = (bf16[16,32,256]{2,1,0:T(8,128)(2,1)S(1)}, bf16[16,32,256]{2,1,0:T(8,128)(2,1)S(1)}, u32[]{:S(2)}, u32[]{:S(2)}) collective-permute-start(bf16[16,32,256]{2,1,0:T(8,128)(2,1)S(1)} %collective-permute-done.9), channel_id=1, source_target_pairs={{0,2},{1,3},{2,4},{3,5},{4,6},{5,7},{8,10},{9,11},{10,12},{11,13},... | collective-permute-start | bytes 786440 | tf_op jit(solution)/shard_map/ppermute | solution.py:14
  72.1 11.3 %collective-permute-start.11 = (bf16[16,32,256]{2,1,0:T(8,128)(2,1)S(1)}, bf16[16,32,256]{2,1,0:T(8,128)(2,1)S(1)}, u32[]{:S(2)}, u32[]{:S(2)}) collective-permute-start(bf16[16,32,256]{2,1,0:T(8,128)(2,1)S(1)} %collective-permute-done.9), channel_id=1, source_target_pairs={{0,1},{1,2},{2,3},{3,4},{4,5},{5,6},{6,7},{8,9},{9,10},{10,11},{11... | collective-permute-start | bytes 786440 | tf_op jit(solution)/shard_map/ppermute | solution.py:14
  76.4 8.5 %collective-permute-start.12 = (bf16[16,32,256]{2,1,0:T(8,128)(2,1)S(1)}, bf16[16,32,256]{2,1,0:T(8,128)(2,1)S(1)}, u32[]{:S(2)}, u32[]{:S(2)}) collective-permute-start(bf16[16,32,256]{2,1,0:T(8,128)(2,1)S(1)} %collective-permute-done.9), channel_id=1, source_target_pairs={{1,0},{2,1},{3,2},{4,3},{5,4},{6,5},{7,6},{9,8},{10,9},{11,10},{12... | collective-permute-start | bytes 786440 | tf_op jit(solution)/shard_map/ppermute | solution.py:14
  79.8 9.7 %collective-permute-start.13 = (bf16[16,32,256]{2,1,0:T(8,128)(2,1)S(1)}, bf16[16,32,256]{2,1,0:T(8,128)(2,1)S(1)}, u32[]{:S(2)}, u32[]{:S(2)}) collective-permute-start(bf16[16,32,256]{2,1,0:T(8,128)(2,1)S(1)} %collective-permute-done.9), channel_id=1, source_target_pairs={{2,0},{3,1},{4,2},{5,3},{6,4},{7,5},{10,8},{11,9},{12,10},{13,11},... | collective-permute-start | bytes 786440 | tf_op jit(solution)/shard_map/ppermute | solution.py:14
  200.1 76.0 %collective-permute-start.15 = (bf16[1,32,256]{2,1,0:T(8,128)(2,1)}, bf16[1,32,256]{2,1,0:T(8,128)(2,1)}, u32[]{:S(2)}, u32[]{:S(2)}) collective-permute-start(bf16[1,32,256]{2,1,0:T(8,128)(2,1)} %get-tuple-element.474), channel_id=1, source_target_pairs={{8,0},{16,8},{24,16},{32,24},{40,32},{48,40},{56,48},{64,56},{72,6... | collective-permute-start | bytes 49160 | tf_op jit(solution)/shard_map/ppermute | solution.py:27
  202.1 74.1 %collective-permute-start.14 = (bf16[1,32,256]{2,1,0:T(8,128)(2,1)}, bf16[1,32,256]{2,1,0:T(8,128)(2,1)}, u32[]{:S(2)}, u32[]{:S(2)}) collective-permute-start(bf16[1,32,256]{2,1,0:T(8,128)(2,1)} %get-tuple-element.473), channel_id=1, source_target_pairs={{0,8},{8,16},{16,24},{24,32},{32,40},{40,48},{48,56},{56,64},{64,7... | collective-permute-start | bytes 49160 | tf_op jit(solution)/shard_map/ppermute | solution.py:25
  267.8 20.9 %copy-start.18 = (bf16[16,32,128]{2,1,0:T(8,128)(2,1)S(1)}, bf16[16,32,128]{2,1,0:T(8,128)(2,1)}, u32[]{:S(2)}) copy-start(bf16[16,32,128]{2,1,0:T(8,128)(2,1)} %param.84) | copy-start | bytes 393220
  268.8 32.9 %collective-permute-start.23 = (bf16[5,16,32,256]{3,2,1,0:T(8,128)(2,1)}, bf16[5,16,32,256]{3,2,1,0:T(8,128)(2,1)S(1)}, u32[]{:S(2)}, u32[]{:S(2)}) collective-permute-start(bf16[5,16,32,256]{3,2,1,0:T(8,128)(2,1)} %get-tuple-element.447), channel_id=1, source_target_pairs={{0,8},{8,16},{16,24},{24,32},{32,40},{40,48},{48,56},{56,64},{64,7... | collective-permute-start | bytes 3932168 | tf_op jit(solution)/shard_map/ppermute | solution.py:14
  270.7 32.4 %collective-permute-start.22 = (bf16[5,16,32,256]{3,2,1,0:T(8,128)(2,1)}, bf16[5,16,32,256]{3,2,1,0:T(8,128)(2,1)}, u32[]{:S(2)}, u32[]{:S(2)}) collective-permute-start(bf16[5,16,32,256]{3,2,1,0:T(8,128)(2,1)} %get-tuple-element.446), channel_id=1, source_target_pairs={{8,0},{16,8},{24,16},{32,24},{40,32},{48,40},{56,48},{64,56},{72,6... | collective-permute-start | bytes 3932168 | tf_op jit(solution)/shard_map/ppermute | solution.py:14
  276.9 8.9 %collective-permute-start.16 = (bf16[18,1,256]{2,1,0:T(2,128)(2,1)S(1)}, bf16[18,1,256]{2,1,0:T(2,128)(2,1)S(1)}, u32[]{:S(2)}, u32[]{:S(2)}) collective-permute-start(bf16[18,1,256]{2,1,0:T(2,128)(2,1)S(1)} %get-tuple-element.469), channel_id=1, source_target_pairs={{0,1},{1,2},{2,3},{3,4},{4,5},{5,6},{6,7},{8,9},{9,10},{10,11},{11... | collective-permute-start | bytes 27656 | tf_op jit(solution)/shard_map/ppermute | solution.py:25
  282.2 5.5 %collective-permute-start.17 = (bf16[18,1,256]{2,1,0:T(2,128)(2,1)S(1)}, bf16[18,1,256]{2,1,0:T(2,128)(2,1)S(1)}, u32[]{:S(2)}, u32[]{:S(2)}) collective-permute-start(bf16[18,1,256]{2,1,0:T(2,128)(2,1)S(1)} %get-tuple-element.470), channel_id=1, source_target_pairs={{1,0},{2,1},{3,2},{4,3},{5,4},{6,5},{7,6},{9,8},{10,9},{11,10},{12... | collective-permute-start | bytes 27656 | tf_op jit(solution)/shard_map/ppermute | solution.py:27
  306.2 12.0 %collective-permute-start.27 = (bf16[16,32,256]{2,1,0:T(8,128)(2,1)S(1)}, bf16[16,32,256]{2,1,0:T(8,128)(2,1)S(1)}, u32[]{:S(2)}, u32[]{:S(2)}) collective-permute-start(bf16[16,32,256]{2,1,0:T(8,128)(2,1)S(1)} %get-tuple-element.449), channel_id=1, source_target_pairs={{0,2},{1,3},{2,4},{3,5},{4,6},{5,7},{8,10},{9,11},{10,12},{11,13},... | collective-permute-start | bytes 786440 | tf_op jit(solution)/shard_map/ppermute | solution.py:14
  309.0 10.3 %collective-permute-start.26 = (bf16[16,32,256]{2,1,0:T(8,128)(2,1)S(1)}, bf16[16,32,256]{2,1,0:T(8,128)(2,1)S(1)}, u32[]{:S(2)}, u32[]{:S(2)}) collective-permute-start(bf16[16,32,256]{2,1,0:T(8,128)(2,1)S(1)} %get-tuple-element.450), channel_id=1, source_target_pairs={{0,1},{1,2},{2,3},{3,4},{4,5},{5,6},{6,7},{8,9},{9,10},{10,11},{11... | collective-permute-start | bytes 786440 | tf_op jit(solution)/shard_map/ppermute | solution.py:14
  313.8 10.1 %collective-permute-start.25 = (bf16[16,32,256]{2,1,0:T(8,128)(2,1)S(1)}, bf16[16,32,256]{2,1,0:T(8,128)(2,1)S(1)}, u32[]{:S(2)}, u32[]{:S(2)}) collective-permute-start(bf16[16,32,256]{2,1,0:T(8,128)(2,1)S(1)} %get-tuple-element.451), channel_id=1, source_target_pairs={{1,0},{2,1},{3,2},{4,3},{5,4},{6,5},{7,6},{9,8},{10,9},{11,10},{12... | collective-permute-start | bytes 786440 | tf_op jit(solution)/shard_map/ppermute | solution.py:14
  315.7 11.0 %collective-permute-start.24 = (bf16[16,32,256]{2,1,0:T(8,128)(2,1)S(1)}, bf16[16,32,256]{2,1,0:T(8,128)(2,1)S(1)}, u32[]{:S(2)}, u32[]{:S(2)}) collective-permute-start(bf16[16,32,256]{2,1,0:T(8,128)(2,1)S(1)} %get-tuple-element.448), channel_id=1, source_target_pairs={{2,0},{3,1},{4,2},{5,3},{6,4},{7,5},{10,8},{11,9},{12,10},{13,11},... | collective-permute-start | bytes 786440 | tf_op jit(solution)/shard_map/ppermute | solution.py:14
  (35 other events, 147.2 us)
Sparse Core Ops, SparseCore 0:
  295.7 144.8 all-reduce.15
where the time goes:
time: 459 us; the launch traced here: 452 us
  waiting for transfers between devices  139 us (30%)
  local copies, waits for them, and re-layouts  134 us (29%)
  starting transfers between devices  79.6 us (17%)
  matrix products  52.9 us (12%)
  other arithmetic  29 us (6%)
  between operations  17.4 us (4%)
    psum x1, waiting for transfers between devices, body(): corr_total, conv_total = lax.psum((corr_grad, conv_grad), ('row', 'col'))  113 us
    ppermute x20, starting transfers between devices, from_behind(): return lax.ppermute(array, axis, pairs)  55.4 us
    unnamed x119, local copies, waits for them, and re-layouts  28.7 us
    ppermute x20, waiting for transfers between devices, from_behind(): return lax.ppermute(array, axis, pairs)  22.7 us
    another operation x8, local copies, waits for them, and re-layouts, body(): volume = jnp.stack(bands).transpose(2, 3, 0, 1, 4) * mask * scale  20.7 us
    reshape x8, local copies, waits for them, and re-layouts, take_band(): flat = scores.reshape(leading + (across * (across + 8),))  20.5 us
    dot_general x4, matrix products, part_gradient(): jnp.einsum('uabe,abc->uaec', grad_scores, source, preferred_element_type=...  14.3 us
    ppermute x4, starting transfers between devices, with_halo(): lax.ppermute(tail, axis, [(i, (i + 1) % count) for i in range(ends)])  14.2 us
  transfers between devices with their start and end apart: 29, of which 12 were waited for; matrix products, arithmetic and copies ran while one was open for 21% of the time, Pallas kernels for 0%

commit v1 on v0

v1 whole, which is shorter than its diff:
```python
import functools
import math

import jax
import jax.numpy as jnp
from jax import lax
from jax.experimental import pallas as pl
from jax.experimental.pallas import tpu as pltpu
from jax.sharding import PartitionSpec as P

REACH = 4
SPAN = 2 * REACH + 1
GROUP = 128
WINDOW = 384
LEAD, LEAD_BACK = 3, 4
F32 = jnp.float32
BF16 = jnp.bfloat16
VMEM_LIMIT = 56 * 1024 * 1024
VMEM = pl.BlockSpec(memory_space=pltpu.VMEM)
SMEM = pl.BlockSpec(memory_space=pltpu.SMEM)
ANY = pl.BlockSpec(memory_space=pl.ANY)


def from_behind(array, axis, by):
    peers = lax.axis_size(axis)
    pairs = [(i, i + by) for i in range(peers) if 0 <= i + by < peers]
    return lax.ppermute(array, axis, pairs)


def swap(array, axis, bits):
    return lax.ppermute(array, axis, [(i, i ^ bits) for i in range(lax.axis_size(axis))])


def with_halo(cells, sides, width):
    for axis, dim in sides:
        count = lax.axis_size(axis)
        ends = count - 1
        head = lax.slice_in_dim(cells, 0, width, axis=dim)
        tail = lax.slice_in_dim(cells, cells.shape[dim] - width, cells.shape[dim], axis=dim)
        cells = jnp.concatenate(
            [
                lax.ppermute(tail, axis, [(i, (i + 1) % count) for i in range(ends)]),
                cells,
                lax.ppermute(head, axis, [((i + 1) % count, i) for i in range(ends)]),
            ],
            axis=dim,
        )
    return cells


def tap_mask(radius, lead, backwards):
    cell = lax.broadcasted_iota(jnp.int32, (GROUP, WINDOW), 0)
    cell = GROUP - 1 - cell if backwards else cell
    tap = lax.broadcasted_iota(jnp.int32, (GROUP, WINDOW), 1)
    down = (tap >> 5) - REACH
    across = (tap & 31) - lead - REACH
    column = (cell & 31) + across
    return (
        (jnp.abs(down) <= radius)
        & (jnp.abs(across) <= radius)
        & (column >= 0)
        & (column < 32)
    )


def forward_kernel(
    info,
    first,
    context,
    cot_taps,
    corr_weight,
    back_weight,
    own,
    rows,
    sides,
    corners,
    near_own,
    near_rows,
    parts,
    motion,
    context_grad,
    weights_sent,
    weights_kept,
    taps,
    weight_grads,
    sems,
):
    cells = first.shape[0]
    slots = parts.shape[0]
    source = {}
    for o in range(15):
        dy, dx = o // 5 - 1, o % 5 - 2
        if dy == 0:
            source[o] = {
                0: own,
                -2: sides.at[0],
                2: sides.at[1],
                -1: near_own.at[0],
                1: near_own.at[1],
            }[dx]
        else:
            r = (dy + 1) // 2
            source[o] = {
                0: rows.at[r],
                -2: corners.at[r],
                2: corners.at[2 + r],
                -1: near_rows.at[r],
                1: near_rows.at[2 + r],
            }[dx]
    for k in range(slots):
        for o in range(15):
            @pl.when(info[k] == o)
            def _():
                pltpu.make_async_copy(
                    source[o], parts.at[k, pl.ds(GROUP, cells)], sems.at[k]
                ).start()
        parts[k, :GROUP] = jnp.zeros((GROUP, parts.shape[2]), BF16)
        parts[k, GROUP + cells :] = jnp.zeros((GROUP, parts.shape[2]), BF16)
    inside = tap_mask(info[slots + 1], LEAD, True)
    flip = (
        lax.broadcasted_iota(jnp.int32, (GROUP, GROUP), 0)
        + lax.broadcasted_iota(jnp.int32, (GROUP, GROUP), 1)
        == GROUP - 1
    ).astype(F32).astype(BF16)
    gains = []
    for k in range(slots):
        live = jnp.where(k < info[slots], 1.0 / math.sqrt(first.shape[1]), 0.0).astype(F32)
        gains.append(jnp.where(inside, live, 0.0))
    for k in range(slots):
        pltpu.make_async_copy(own, parts.at[k, pl.ds(GROUP, cells)], sems.at[k]).wait()
    for q in range(cells // GROUP):
        at = slice(q * GROUP, (q + 1) * GROUP)
        features = jnp.dot(flip, first[at], preferred_element_type=F32).astype(BF16)
        for k in range(slots):
            scores = lax.dot_general(
                features,
                parts[k, q * GROUP : q * GROUP + WINDOW],
                (((1,), (1,)), ((), ())),
                preferred_element_type=F32,
            )
            turn = WINDOW + REACH + LEAD - (GROUP - 1)
            band = pltpu.roll(scores, turn, 1, stride=1, stride_axis=0) * gains[k]
            packed = (
                band[:, :128]
                + pltpu.roll(band[:, 128:256], SPAN, 1)
                + pltpu.roll(band[:, 256:], 2 * SPAN, 1)
            )
            taps[at, k * 128 : (k + 1) * 128] = jnp.dot(
                flip, packed.astype(BF16), preferred_element_type=F32
            ).astype(BF16)
        pre = jnp.dot(taps[at], corr_weight[...], preferred_element_type=F32) + context[
            at
        ].astype(F32)
        grad_motion = jnp.zeros_like(pre)
        for a in range(3):
            start = (2 - a) * 32 + q * GROUP
            grad_motion += jnp.dot(
                cot_taps[start : start + GROUP], back_weight[a], preferred_element_type=F32
            )
        sigma = jax.nn.sigmoid(pre)
        motion[at] = (pre * sigma).astype(BF16)
        context_grad[at] = (grad_motion * sigma * (1.0 + pre * (1.0 - sigma))).astype(BF16)
    over_cells = (((0,), (0,)), ((), ()))
    for a in range(3):
        start = (2 - a) * 32
        term = lax.dot_general(
            motion[...], cot_taps[start : start + cells], over_cells, preferred_element_type=F32
        )
        for b in range(3):
            weight_grads[(3 * a + b) * 256 : (3 * a + b + 1) * 256] = term[
                :, b * 128 : (b + 1) * 128
            ]
    term = lax.dot_general(taps[...], context_grad[...], over_cells, preferred_element_type=F32)
    base = 9 * 256
    for h in range(2):
        weight_grads[base + h * 384 + 320 : base + (h + 1) * 384] = jnp.zeros((64, 128), F32)
        for k in range(slots):
            for u in range(SPAN):
                row = k * 128 + (u % 4) * 32 + (u // 4) * SPAN + LEAD
                to = base + h * 384 + (k * SPAN + u) * SPAN
                weight_grads[to : to + SPAN] = term[row : row + SPAN, h * 128 : (h + 1) * 128]
    half = weight_grads.shape[0] // 2
    core = info[slots + 2]
    weights_kept[...] = weight_grads[pl.ds(pl.multiple_of(core * half, half), half)]
    weights_sent[...] = weight_grads[pl.ds(pl.multiple_of((1 - core) * half, half), half)].astype(
        BF16
    )


def backward_kernel(
    info, first, context_grad, corr_weight, parts, first_grad, kept, lent, totals
):
    cells = first.shape[0]
    slots = parts.shape[0]
    scale = 1.0 / math.sqrt(first.shape[1])
    inside = tap_mask(info[slots + 1], LEAD_BACK, False)
    totals[...] = jnp.zeros_like(totals)
    kept[...] = jnp.zeros_like(kept)
    lent[...] = jnp.zeros_like(lent)
    for q in range(cells // GROUP):
        at = slice(q * GROUP, (q + 1) * GROUP)
        packed = (
            lax.dot_general(
                context_grad[at],
                corr_weight[...],
                (((1,), (1,)), ((), ())),
                preferred_element_type=F32,
            )
            .astype(BF16)
            .astype(F32)
        )
        first_here = jnp.zeros((GROUP, first.shape[1]), F32)
        for k in range(slots):
            mine = packed[:, k * 128 : (k + 1) * 128]
            band = jnp.concatenate(
                [mine, pltpu.roll(mine, 128 - SPAN, 1), pltpu.roll(mine, 128 - 2 * SPAN, 1)],
                axis=1,
            )
            band = jnp.where(inside & (k < info[slots]), band, 0.0)
            scores = pltpu.roll(band, WINDOW - REACH - LEAD_BACK, 1, stride=1, stride_axis=0).astype(BF16)
            window = slice(q * GROUP, q * GROUP + WINDOW)
            first_here += jnp.dot(scores, parts[k, window], preferred_element_type=F32)
            totals[k, window] += lax.dot_general(
                scores, first[at], (((0,), (0,)), ((), ())), preferred_element_type=F32
            )
        first_grad[at] = first_here * scale
    for k in range(slots):
        value = (totals[k, GROUP : GROUP + cells] * scale).astype(BF16)
        down, across = info[k] // 5, info[k] % 5
        even = across % 2 == 0

        @pl.when(even)
        def _():
            kept[down * 3 + across // 2] = value

        @pl.when(jnp.logical_not(even))
        def _():
            lent[down * 2 + across // 2] = value


def features_kernel(motion_taps, weight, out):
    cells = out.shape[0]
    total = jnp.zeros(out.shape, F32)
    for a in range(3):
        total += jnp.dot(
            motion_taps[a * 32 : a * 32 + cells], weight[a], preferred_element_type=F32
        )
    out[...] = total.astype(BF16)


def finish_kernel(info, s0, s1, s2, s3, far, conv, corr, whole):
    size = s0.shape[0]
    core, chip = info[6], info[7]
    half = whole.shape[0] // 2
    for s, ref in enumerate((s0, s1, s2, s3)):
        other = chip ^ s
        to = pl.multiple_of(core * half + other * size, size)
        whole[pl.ds(to, size)] = ref[...].astype(F32)
        to = pl.multiple_of((1 - core) * half + other * size, size)
        whole[pl.ds(to, size)] = far[s].astype(F32)
    conv[...] = whole[: conv.shape[0]]
    base = conv.shape[0]
    for h in range(2):
        corr[:, h * 128 : (h + 1) * 128] = whole[base + h * 384 : base + h * 384 + corr.shape[0]]


def call(kernel, out_shape, in_specs, scratch=(), flops=0):
    return pl.pallas_call(
        kernel,
        out_shape=out_shape,
        in_specs=in_specs,
        out_specs=jax.tree.map(lambda _: VMEM, out_shape),
        scratch_shapes=list(scratch),
        compiler_params=pltpu.CompilerParams(vmem_limit_bytes=VMEM_LIMIT),
        cost_estimate=pl.CostEstimate(flops=flops, bytes_accessed=flops // 300, transcendentals=0),
    )


def sum_weights(sent, kept):
    cur = kept + swap(sent, "col", 1).astype(F32)
    size = cur.shape[0] // 4
    chip = lax.axis_index("col") // 2
    pieces = [
        lax.dynamic_slice_in_dim(cur, (chip ^ s) * size, size, axis=0) for s in range(4)
    ]
    got = [swap(pieces[s].astype(BF16), "col", 2 * s).astype(F32) for s in (1, 2, 3)]
    cur = (pieces[0] + got[0]) + (got[1] + got[2])
    for unit in (1, 4):
        mine = cur.astype(BF16)
        got = [swap(mine, "row", unit * s).astype(F32) for s in (1, 2, 3)]
        cur = (mine.astype(F32) + got[0]) + (got[1] + got[2])
    mine = cur.astype(BF16)
    shards = [mine] + [swap(mine, "col", 2 * s) for s in (1, 2, 3)]
    far = swap(jnp.stack(shards), "col", 1)
    return shards, far


def body(
    frame_one, frame_two, context, cotangent, corr_weight, conv_weight, partners, counts, radius
):
    rows_tile, cols_tile, channels = frame_one.shape
    slots = partners.shape[-1]
    cells = rows_tile * cols_tile
    hidden = context.shape[-1]
    out_width = conv_weight.shape[-1]
    col = lax.axis_index("col")
    core = col % 2
    info = jnp.concatenate(
        [
            partners[0, 0],
            counts[0],
            radius[0],
            core[None].astype(jnp.int32),
            (col // 2)[None].astype(jnp.int32),
        ]
    )
    first = frame_one.reshape(cells, channels)
    own = frame_two.reshape(cells, channels)
    up, down = from_behind(own, "row", 1), from_behind(own, "row", -1)
    rows = jnp.stack([up, down])
    west, east = from_behind(own, "col", 2), from_behind(own, "col", -2)
    sides = jnp.stack([west, east])
    far_west, far_east = from_behind(rows, "col", 2), from_behind(rows, "col", -2)
    corners = jnp.concatenate([far_west, far_east])
    second_core = core == 1
    near_own = swap(
        jnp.stack([jnp.where(second_core, west, own), jnp.where(second_core, own, east)]),
        "col",
        1,
    )
    near_rows = swap(
        jnp.concatenate(
            [jnp.where(second_core, far_west, rows), jnp.where(second_core, rows, far_east)]
        ),
        "col",
        1,
    )
    grad_rim = with_halo(cotangent, (("row", 0), ("col", 1)), 1)
    cot_taps = jnp.concatenate(
        [grad_rim[:, 2 - b : 2 - b + cols_tile] for b in range(3)], axis=2
    ).reshape((rows_tile + 2) * cols_tile, 3 * out_width)
    spread = jnp.pad(
        corr_weight.reshape(slots, SPAN, SPAN, hidden), ((0, 0), (0, 3), (0, 0), (0, 0))
    )
    spread = spread.reshape(slots, 3, 4, SPAN, hidden).transpose(0, 2, 1, 3, 4)
    spread = spread.reshape(slots, 4, 3 * SPAN, hidden)
    spread, spread_back = (
        jnp.pad(spread, ((0, 0), (0, 0), (lead, 5 - lead), (0, 0))).reshape(slots * 128, hidden)
        for lead in (LEAD, LEAD_BACK)
    )
    back_weight = conv_weight.transpose(0, 1, 3, 2).reshape(3, 3 * out_width, hidden)
    shape = jax.ShapeDtypeStruct
    total_rows = 9 * hidden + 2 * 384
    parts, motion, context_grad, weights_sent, weights_kept = call(
        forward_kernel,
        (
            shape((slots, cells + 2 * GROUP, channels), BF16),
            shape((cells, hidden), BF16),
            shape((cells, hidden), BF16),
            shape((total_rows // 2, 128), BF16),
            shape((total_rows // 2, 128), F32),
        ),
        [SMEM] + [VMEM] * 5 + [ANY] * 6,
        [
            pltpu.VMEM((cells, slots * 128), BF16),
            pltpu.VMEM((total_rows, 128), F32),
            pltpu.SemaphoreType.DMA((slots,)),
        ],
        flops=3 * 10**9,
    )(
        info,
        first,
        context.reshape(cells, hidden),
        cot_taps,
        spread,
        back_weight,
        own,
        rows,
        sides,
        corners,
        near_own,
        near_rows,
    )
    shards, far = sum_weights(weights_sent, weights_kept)
    first_grad, kept, lent = call(
        backward_kernel,
        (
            shape((cells, channels), F32),
            shape((9, cells, channels), BF16),
            shape((6, cells, channels), BF16),
        ),
        [SMEM] + [VMEM] * 4,
        [pltpu.VMEM((slots, cells + 2 * GROUP, channels), F32)],
        flops=3 * 10**9,
    )(info, first, context_grad, spread_back, parts)
    kept = kept.reshape(3, 3, cells, channels).astype(F32)
    lent = swap(lent, "col", 1).reshape(3, 2, cells, channels).astype(F32)
    to_west = kept[:, 0] + jnp.where(second_core, lent[:, 0], 0.0)
    middle = kept[:, 1] + jnp.where(second_core, lent[:, 1], lent[:, 0])
    to_east = kept[:, 2] + jnp.where(second_core, 0.0, lent[:, 1])
    middle = middle + from_behind(to_west.astype(BF16), "col", -2).astype(F32)
    middle = middle + from_behind(to_east.astype(BF16), "col", 2).astype(F32)
    second_grad = middle[1]
    second_grad = second_grad + from_behind(middle[0].astype(BF16), "row", -1).astype(F32)
    second_grad = second_grad + from_behind(middle[2].astype(BF16), "row", 1).astype(F32)
    rimmed = with_halo(
        motion.reshape(rows_tile, cols_tile, hidden), (("row", 0), ("col", 1)), 1
    )
    motion_taps = jnp.concatenate(
        [rimmed[:, b : b + cols_tile] for b in range(3)], axis=2
    ).reshape((rows_tile + 2) * cols_tile, 3 * hidden)
    features = call(features_kernel, shape((cells, out_width), BF16), [VMEM] * 2, flops=10**9)(
        motion_taps, conv_weight.reshape(3, 3 * hidden, out_width)
    )
    conv_total, corr_total = call(
        finish_kernel,
        (shape((9 * hidden, out_width), F32), shape(corr_weight.shape, F32)),
        [SMEM] + [VMEM] * 5,
        [pltpu.VMEM((total_rows, 128), F32)],
    )(info, *shards, far)
    return (
        features.reshape(rows_tile, cols_tile, out_width),
        context_grad.reshape(rows_tile, cols_tile, hidden),
        first_grad.reshape(frame_one.shape),
        second_grad.reshape(frame_two.shape),
        corr_total,
        conv_total.reshape(conv_weight.shape),
    )


def solution(mesh):
    return jax.shard_map(
        body,
        mesh=mesh,
        in_specs=(
            P("row", "col", None),
            P("row", "col", None),
            P("row", "col", None),
            P("row", "col", None),
            P(),
            P(),
            P("row", "col", None),
            P("row", "col"),
            P("row", "col"),
        ),
        out_specs=(
            P("row", "col", None),
            P("row", "col", None),
            P("row", "col", None),
            P("row", "col", None),
            P(),
            P(),
        ),
        check_vma=False,
    )
```

time: 459 us -> 149 us (0.32); the launches traced: 452 us -> 147 us
  local copies, waits for them, and re-layouts: 134 us -> 6.17 us
  waiting for transfers between devices: 139 us -> 19.1 us
  matrix products: 52.9 us -> 0 us
  Pallas kernels: 0 us -> 24.7 us
  other arithmetic: 29 us -> 12.5 us
  between operations: 17.4 us -> 2.51 us
    psum x1 -> x0, waiting for transfers between devices: 113 us -> none  [body(): corr_total, conv_total = lax.psum((corr_grad, conv_grad), ('row', 'col'))]
    reshape x23 -> x2, local copies, waits for them, and re-layouts: 63.9 us -> 1.12 us  [the longest x1 0.99 us: body(): corr_weight.reshape(slots, SPAN, SPAN, hidden)]
    dot_general x42 -> x0, matrix products: 52.9 us -> none  [the longest x4 14.3 us: part_gradient(): jnp.einsum('uabe,abc->uaec', grad_scores, source, preferred_element_type=...]
    unnamed x119 -> x31, local copies, waits for them, and re-layouts: 28.7 us -> 0.86 us
    ppermute x20 -> x10, starting transfers between devices: 55.4 us -> 28.5 us  [from_behind(): return lax.ppermute(array, axis, pairs)]
    ppermute x0 -> x17, starting transfers between devices: none -> 25.2 us  [swap(): lax.ppermute(array, axis, [(i, i ^ bits) for i in range(lax.axis_size(axi...]
    pallas_call x0 -> x4, Pallas kernels: none -> 24.7 us  [the longest x1 11.1 us: body(): call(forward_kernel, (shape((slots, cells + 2 * GROUP, channels), BF16),...]
    another operation x13 -> x0, local copies, waits for them, and re-layouts: 22.4 us -> none  [the longest x8 20.7 us: body(): volume = jnp.stack(bands).transpose(2, 3, 0, 1, 4) * mask * scale]
  transfers between devices with their start and end apart: 29 -> 35, of which waited for: 12 -> 10; matrix products, arithmetic and copies ran while one was open for 21% -> 12% of each run, Pallas kernels for 0% -> 4%
where the time goes in v1:
time: 149 us; the launch traced here: 147 us
  starting transfers between devices  82.3 us (55%)
  Pallas kernels  24.7 us (17%)
  waiting for transfers between devices  19.1 us (13%)
  other arithmetic  12.5 us (8%)
  local copies, waits for them, and re-layouts  6.17 us (4%)
  between operations  2.51 us (2%)
    ppermute x10, starting transfers between devices, from_behind(): return lax.ppermute(array, axis, pairs)  28.5 us
    ppermute x17, starting transfers between devices, swap(): lax.ppermute(array, axis, [(i, i ^ bits) for i in range(lax.axis_size(axi...  25.2 us
    ppermute x4, starting transfers between devices, with_halo(): lax.ppermute(head, axis, [((i + 1) % count, i) for i in range(ends)])  19.7 us
    pallas_call x1, Pallas kernels, body(): call(forward_kernel, (shape((slots, cells + 2 * GROUP, channels), BF16),...  11.1 us
    ppermute x10, waiting for transfers between devices, from_behind(): return lax.ppermute(array, axis, pairs)  9.16 us
    ppermute x4, starting transfers between devices, with_halo(): lax.ppermute(tail, axis, [(i, (i + 1) % count) for i in range(ends)])  8.9 us
    ppermute x17, waiting for transfers between devices, swap(): lax.ppermute(array, axis, [(i, i ^ bits) for i in range(lax.axis_size(axi...  8.82 us
    pallas_call x1, Pallas kernels, body(): call(backward_kernel, (shape((cells, channels), F32), shape((9, cells, ch...  8.38 us
  transfers between devices with their start and end apart: 35, of which 10 were waited for; matrix products, arithmetic and copies ran while one was open for 12% of the time, Pallas kernels for 4%

profile of v1, /device:TPU:33, one launch (start us, length us, event | category | flops | bytes accessed | tf_op | source)
XLA Modules:
  0.0 147.2 jit_solution(4548984009222394027)
XLA Ops:
  0.6 4.3 %collective-permute-start.5 = (bf16[512,256]{1,0:T(8,128)(2,1)}, bf16[512,256]{1,0:T(8,128)(2,1)S(1)}, u32[]{:S(2)}, u32[]{:S(2)}) collective-permute-start(bf16[512,256]{1,0:T(8,128)(2,1)} %bitcast.134), channel_id=1, source_target_pairs={{8,0},{16,8},{24,16},{32,24},{40,32},{48,40},{56,48},{64,56},{72,6... | collective-permute-start | bytes 786440 | tf_op jit(solution)/shard_map/ppermute | solution.py:27
  5.0 1.9 %collective-permute-start.4 = (bf16[512,256]{1,0:T(8,128)(2,1)}, bf16[512,256]{1,0:T(8,128)(2,1)S(1)}, u32[]{:S(2)}, u32[]{:S(2)}) collective-permute-start(bf16[512,256]{1,0:T(8,128)(2,1)} %bitcast.135), channel_id=1, source_target_pairs={{0,8},{8,16},{16,24},{24,32},{32,40},{40,48},{48,56},{56,64},{64,7... | collective-permute-start | bytes 786440 | tf_op jit(solution)/shard_map/ppermute | solution.py:27
  6.9 3.3 %collective-permute-done.5 = bf16[512,256]{1,0:T(8,128)(2,1)S(1)} collective-permute-done((bf16[512,256]{1,0:T(8,128)(2,1)}, bf16[512,256]{1,0:T(8,128)(2,1)S(1)}, u32[]{:S(2)}, u32[]{:S(2)}) %collective-permute-start.5) | collective-permute-done | bytes 262176 | tf_op jit(solution)/shard_map/ppermute | solution.py:27
  10.2 5.8 %collective-permute-done.4 = bf16[512,256]{1,0:T(8,128)(2,1)S(1)} collective-permute-done((bf16[512,256]{1,0:T(8,128)(2,1)}, bf16[512,256]{1,0:T(8,128)(2,1)S(1)}, u32[]{:S(2)}, u32[]{:S(2)}) %collective-permute-start.4) | collective-permute-done | bytes 262176 | tf_op jit(solution)/shard_map/ppermute | solution.py:27
  17.4 4.0 %collective-permute-start.8 = (bf16[2,512,256]{2,1,0:T(8,128)(2,1)S(1)}, bf16[2,512,256]{2,1,0:T(8,128)(2,1)S(1)}, u32[]{:S(2)}, u32[]{:S(2)}) collective-permute-start(bf16[2,512,256]{2,1,0:T(8,128)(2,1)S(1)} %pad_maximum_fusion.8.rows), channel_id=1, source_target_pairs={{0,2},{1,3},{2,4},{3,5},{4,6},{5,7},{8,10},{9,11},{10,12},{11,13},... | collective-permute-start | bytes 1572872 | tf_op jit(solution)/shard_map/ppermute | solution.py:27
  22.2 1.9 %collective-permute-start = (bf16[1,32,128]{2,1,0:T(8,128)(2,1)S(1)}, bf16[1,32,128]{2,1,0:T(8,128)(2,1)S(1)}, u32[]{:S(2)}, u32[]{:S(2)}) collective-permute-start(bf16[1,32,128]{2,1,0:T(8,128)(2,1)S(1)} %get-tuple-element.46), channel_id=1, source_target_pairs={{0,8},{8,16},{16,24},{24,32},{32,40},{40,48},{48,56},{56,64},{64,7... | collective-permute-start | bytes 24584 | tf_op jit(solution)/shard_map/ppermute | solution.py:42
  25.4 4.0 %collective-permute-start.6 = (bf16[512,256]{1,0:T(8,128)(2,1)}, bf16[512,256]{1,0:T(8,128)(2,1)S(1)}, u32[]{:S(2)}, u32[]{:S(2)}) collective-permute-start(bf16[512,256]{1,0:T(8,128)(2,1)} %bitcast.137), channel_id=1, source_target_pairs={{0,2},{1,3},{2,4},{3,5},{4,6},{5,7},{8,10},{9,11},{10,12},{11,13},... | collective-permute-start | bytes 786440 | tf_op jit(solution)/shard_map/ppermute | solution.py:27
  30.6 5.5 %collective-permute-start.1 = (bf16[1,32,128]{2,1,0:T(8,128)(2,1)S(1)}, bf16[1,32,128]{2,1,0:T(8,128)(2,1)S(1)}, u32[]{:S(2)}, u32[]{:S(2)}) collective-permute-start(bf16[1,32,128]{2,1,0:T(8,128)(2,1)S(1)} %get-tuple-element.45), channel_id=1, source_target_pairs={{8,0},{16,8},{24,16},{32,24},{40,32},{48,40},{56,48},{64,56},{72,6... | collective-permute-start | bytes 24584 | tf_op jit(solution)/shard_map/ppermute | solution.py:44
  37.1 4.2 %collective-permute-start.11 = (bf16[4,512,256]{2,1,0:T(8,128)(2,1)S(1)}, bf16[4,512,256]{2,1,0:T(8,128)(2,1)}, u32[]{:S(2)}, u32[]{:S(2)}) collective-permute-start(bf16[4,512,256]{2,1,0:T(8,128)(2,1)S(1)} %pad_maximum_fusion.1), channel_id=1, source_target_pairs={{0,1},{1,0},{2,3},{3,2},{4,5},{5,4},{6,7},{7,6},{8,9},{9,8},{10,11... | collective-permute-start | bytes 3145736 | tf_op jit(solution)/shard_map/ppermute | solution.py:31
  42.9 3.0 %collective-permute-start.3 = (bf16[18,1,128]{2,1,0:T(2,128)(2,1)S(1)}, bf16[18,1,128]{2,1,0:T(2,128)(2,1)S(1)}, u32[]{:S(2)}, u32[]{:S(2)}) collective-permute-start(bf16[18,1,128]{2,1,0:T(2,128)(2,1)S(1)} %get-tuple-element.44), channel_id=1, source_target_pairs={{0,1},{1,2},{2,3},{3,4},{4,5},{5,6},{6,7},{8,9},{9,10},{10,11},{11... | collective-permute-start | bytes 13832 | tf_op jit(solution)/shard_map/ppermute | solution.py:42
  45.9 1.9 %collective-permute-start.2 = (bf16[18,1,128]{2,1,0:T(2,128)(2,1)S(1)}, bf16[18,1,128]{2,1,0:T(2,128)(2,1)S(1)}, u32[]{:S(2)}, u32[]{:S(2)}) collective-permute-start(bf16[18,1,128]{2,1,0:T(2,128)(2,1)S(1)} %get-tuple-element.43), channel_id=1, source_target_pairs={{1,0},{2,1},{3,2},{4,3},{5,4},{6,5},{7,6},{9,8},{10,9},{11,10},{12... | collective-permute-start | bytes 13832 | tf_op jit(solution)/shard_map/ppermute | solution.py:44
  51.9 2.0 %fusion.13 = bf16[18,32,384]{2,1,0:T(8,128)(2,1)} fusion(bf16[18,32,128]{2,1,0:T(8,128)(2,1)} %copy-done.10, bf16[18,1,128]{2,1,0:T(2,128)(2,1)S(1)} %collective-permute-done.3, bf16[18,1,128]{2,1,0:T(2,128)(2,1)S(1)} %collective-permute-done.2), kind=kLoop, calls=%fused_computation.35 | loop fusion | flops 2211840 | bytes 599040 | tf_op jit(solution)/shard_map/concatenate | solution.py:339
  55.8 11.1 %shard_map.136 = (bf16[4,768,256]{2,1,0:T(8,128)(2,1)}, bf16[512,256]{1,0:T(8,128)(2,1)}, bf16[512,256]{1,0:T(8,128)(2,1)}, bf16[1536,128]{1,0:T(8,128)(2,1)}, f32[1536,128]{1,0:T(8,128)}) custom-call(s32[8]{0:T(128)} %concatenate.35.info, bf16[512,256]{1,0:T(8,128)(2,1)} %bitcast.144, bf16[512,256]{1,0:T(8,128)(2,1)} %bitcast.143, ...), custom_call_target="tpu_custom_call" | custom-call | flops 3000000000 | bytes 10000000 | tf_op jit(solution)/shard_map/pallas_call | solution.py:354
  66.9 8.4 %shard_map.138 = (f32[512,256]{1,0:T(8,128)}, bf16[9,512,256]{2,1,0:T(8,128)(2,1)}, bf16[6,512,256]{2,1,0:T(8,128)(2,1)}) custom-call(s32[8]{0:T(128)} %concatenate.35.info, bf16[512,256]{1,0:T(8,128)(2,1)} %bitcast.145, bf16[512,256]{1,0:T(8,128)(2,1)} %get-tuple-element.17.context_grad, bf16[512,256]{1,0:T(8,128)(2,1)} %bitcast.139, ...), custom_call_target="tpu_custom_call" | custom-call | flops 3000000000 | bytes 10000000 | tf_op jit(solution)/shard_map/pallas_call | solution.py:385
  75.8 3.5 %collective-permute-done.21 = bf16[1536,128]{1,0:T(8,128)(2,1)S(1)} collective-permute-done((bf16[1536,128]{1,0:T(8,128)(2,1)S(1)}, bf16[1536,128]{1,0:T(8,128)(2,1)S(1)}, u32[]{:S(2)}, u32[]{:S(2)}) %collective-permute-start.21) | collective-permute-done | bytes 393248 | tf_op jit(solution)/shard_map/ppermute | solution.py:31
  81.1 2.0 %collective-permute-start.24 = (bf16[384,128]{1,0:T(8,128)(2,1)}, bf16[384,128]{1,0:T(8,128)(2,1)S(1)}, u32[]{:S(2)}, u32[]{:S(2)}) collective-permute-start(bf16[384,128]{1,0:T(8,128)(2,1)} %get-tuple-element.29), channel_id=1, source_target_pairs={{0,6},{1,7},{2,4},{3,5},{4,2},{5,3},{6,0},{7,1},{8,14},{9,15},{10,... | collective-permute-start | bytes 294920 | tf_op jit(solution)/shard_map/ppermute | solution.py:31
  84.8 2.0 %collective-permute-done.24 = bf16[384,128]{1,0:T(8,128)(2,1)S(1)} collective-permute-done((bf16[384,128]{1,0:T(8,128)(2,1)}, bf16[384,128]{1,0:T(8,128)(2,1)S(1)}, u32[]{:S(2)}, u32[]{:S(2)}) %collective-permute-start.24) | collective-permute-done | bytes 98336 | tf_op jit(solution)/shard_map/ppermute | solution.py:31
  90.2 4.6 %collective-permute-start.27 = (bf16[384,128]{1,0:T(8,128)(2,1)S(1)}, bf16[384,128]{1,0:T(8,128)(2,1)S(1)}, u32[]{:S(2)}, u32[]{:S(2)}) collective-permute-start(bf16[384,128]{1,0:T(8,128)(2,1)S(1)} %add_convert_fusion.2), channel_id=1, source_target_pairs={{0,24},{8,16},{16,8},{24,0},{32,56},{40,48},{48,40},{56,32},{64,88... | collective-permute-start | bytes 294920 | tf_op jit(solution)/shard_map/ppermute | solution.py:31
  97.7 3.0 %collective-permute-start.18 = (bf16[3,512,256]{2,1,0:T(8,128)(2,1)S(1)}, bf16[3,512,256]{2,1,0:T(8,128)(2,1)S(1)}, u32[]{:S(2)}, u32[]{:S(2)}) collective-permute-start(bf16[3,512,256]{2,1,0:T(8,128)(2,1)S(1)} %fusion.10), channel_id=1, source_target_pairs={{0,2},{1,3},{2,4},{3,5},{4,6},{5,7},{8,10},{9,11},{10,12},{11,13},... | collective-permute-start | bytes 2359304 | tf_op jit(solution)/shard_map/ppermute | solution.py:27
  102.1 1.7 %collective-permute-start.30 = (bf16[384,128]{1,0:T(8,128)(2,1)S(1)}, bf16[384,128]{1,0:T(8,128)(2,1)S(1)}, u32[]{:S(2)}, u32[]{:S(2)}) collective-permute-start(bf16[384,128]{1,0:T(8,128)(2,1)S(1)} %add_convert_fusion.1), channel_id=1, source_target_pairs={{0,96},{8,104},{16,112},{24,120},{32,64},{40,72},{48,80},{56,88},{... | collective-permute-start | bytes 294920 | tf_op jit(solution)/shard_map/ppermute | solution.py:31
  103.8 1.9 %collective-permute-start.28 = (bf16[384,128]{1,0:T(8,128)(2,1)S(1)}, bf16[384,128]{1,0:T(8,128)(2,1)S(1)}, u32[]{:S(2)}, u32[]{:S(2)}) collective-permute-start(bf16[384,128]{1,0:T(8,128)(2,1)S(1)} %add_convert_fusion.1), channel_id=1, source_target_pairs={{0,32},{8,40},{16,48},{24,56},{32,0},{40,8},{48,16},{56,24},{64,96... | collective-permute-start | bytes 294920 | tf_op jit(solution)/shard_map/ppermute | solution.py:31
  105.8 5.1 %collective-permute-start.13 = (bf16[1,32,256]{2,1,0:T(8,128)(2,1)S(1)}, bf16[1,32,256]{2,1,0:T(8,128)(2,1)S(1)}, u32[]{:S(2)}, u32[]{:S(2)}) collective-permute-start(bf16[1,32,256]{2,1,0:T(8,128)(2,1)S(1)} %get-tuple-element.40), channel_id=1, source_target_pairs={{8,0},{16,8},{24,16},{32,24},{40,32},{48,40},{56,48},{64,56},{72,6... | collective-permute-start | bytes 49160 | tf_op jit(solution)/shard_map/ppermute | solution.py:44
  110.9 1.9 %collective-permute-start.12 = (bf16[1,32,256]{2,1,0:T(8,128)(2,1)S(1)}, bf16[1,32,256]{2,1,0:T(8,128)(2,1)S(1)}, u32[]{:S(2)}, u32[]{:S(2)}) collective-permute-start(bf16[1,32,256]{2,1,0:T(8,128)(2,1)S(1)} %get-tuple-element.39), channel_id=1, source_target_pairs={{0,8},{8,16},{16,24},{24,32},{32,40},{40,48},{48,56},{56,64},{64,7... | collective-permute-start | bytes 49160 | tf_op jit(solution)/shard_map/ppermute | solution.py:42
  112.9 2.2 %collective-permute-start.31 = (bf16[384,128]{1,0:T(8,128)(2,1)S(1)}, bf16[384,128]{1,0:T(8,128)(2,1)S(1)}, u32[]{:S(2)}, u32[]{:S(2)}) collective-permute-start(bf16[384,128]{1,0:T(8,128)(2,1)S(1)} %add_convert_fusion.s0), channel_id=1, source_target_pairs={{0,2},{1,3},{2,0},{3,1},{4,6},{5,7},{6,4},{7,5},{8,10},{9,11},{10,... | collective-permute-start | bytes 294920 | tf_op jit(solution)/shard_map/ppermute | solution.py:31
  115.1 2.1 %collective-permute-start.32 = (bf16[384,128]{1,0:T(8,128)(2,1)S(1)}, bf16[384,128]{1,0:T(8,128)(2,1)S(1)}, u32[]{:S(2)}, u32[]{:S(2)}) collective-permute-start(bf16[384,128]{1,0:T(8,128)(2,1)S(1)} %add_convert_fusion.s0), channel_id=1, source_target_pairs={{0,4},{1,5},{2,6},{3,7},{4,0},{5,1},{6,2},{7,3},{8,12},{9,13},{10,... | collective-permute-start | bytes 294920 | tf_op jit(solution)/shard_map/ppermute | solution.py:31
  117.5 3.0 %collective-permute-start.33 = (bf16[384,128]{1,0:T(8,128)(2,1)S(1)}, bf16[384,128]{1,0:T(8,128)(2,1)S(1)}, u32[]{:S(2)}, u32[]{:S(2)}) collective-permute-start(bf16[384,128]{1,0:T(8,128)(2,1)S(1)} %add_convert_fusion.s0), channel_id=1, source_target_pairs={{0,6},{1,7},{2,4},{3,5},{4,2},{5,3},{6,0},{7,1},{8,14},{9,15},{10,... | collective-permute-start | bytes 294920 | tf_op jit(solution)/shard_map/ppermute | solution.py:31
  121.3 7.2 %collective-permute-start.15 = (bf16[18,1,256]{2,1,0:T(2,128)(2,1)S(1)}, bf16[18,1,256]{2,1,0:T(2,128)(2,1)S(1)}, u32[]{:S(2)}, u32[]{:S(2)}) collective-permute-start(bf16[18,1,256]{2,1,0:T(2,128)(2,1)S(1)} %get-tuple-element.36), channel_id=1, source_target_pairs={{1,0},{2,1},{3,2},{4,3},{5,4},{6,5},{7,6},{9,8},{10,9},{11,10},{12... | collective-permute-start | bytes 27656 | tf_op jit(solution)/shard_map/ppermute | solution.py:44
  128.6 2.1 %collective-permute-start.14 = (bf16[18,1,256]{2,1,0:T(2,128)(2,1)S(1)}, bf16[18,1,256]{2,1,0:T(2,128)(2,1)S(1)}, u32[]{:S(2)}, u32[]{:S(2)}) collective-permute-start(bf16[18,1,256]{2,1,0:T(2,128)(2,1)S(1)} %get-tuple-element.35), channel_id=1, source_target_pairs={{0,1},{1,2},{2,3},{3,4},{4,5},{5,6},{6,7},{8,9},{9,10},{10,11},{11... | collective-permute-start | bytes 27656 | tf_op jit(solution)/shard_map/ppermute | solution.py:42
  131.7 1.9 %collective-permute-start.20 = (bf16[512,256]{1,0:T(8,128)(2,1)S(1)}, bf16[512,256]{1,0:T(8,128)(2,1)S(1)}, u32[]{:S(2)}, u32[]{:S(2)}) collective-permute-start(bf16[512,256]{1,0:T(8,128)(2,1)S(1)} %get-tuple-element.32), channel_id=1, source_target_pairs={{0,8},{8,16},{16,24},{24,32},{32,40},{40,48},{48,56},{56,64},{64,7... | collective-permute-start | bytes 786440 | tf_op jit(solution)/shard_map/ppermute | solution.py:27
  133.6 5.5 %collective-permute-start.19 = (bf16[512,256]{1,0:T(8,128)(2,1)S(1)}, bf16[512,256]{1,0:T(8,128)(2,1)S(1)}, u32[]{:S(2)}, u32[]{:S(2)}) collective-permute-start(bf16[512,256]{1,0:T(8,128)(2,1)S(1)} %get-tuple-element.31), channel_id=1, source_target_pairs={{8,0},{16,8},{24,16},{32,24},{40,32},{48,40},{56,48},{64,56},{72,6... | collective-permute-start | bytes 786440 | tf_op jit(solution)/shard_map/ppermute | solution.py:27
  140.3 2.8 %shard_map.137 = bf16[512,128]{1,0:T(8,128)(2,1)} custom-call(bf16[576,768]{1,0:T(8,128)(2,1)} %bitcast.123, bf16[3,768,128]{2,1,0:T(8,128)(2,1)} %bitcast.126), custom_call_target="tpu_custom_call" | custom-call | flops 1000000000 | bytes 3333333 | tf_op jit(solution)/shard_map/pallas_call | solution.py:412
  143.9 2.5 %shard_map.139 = (f32[2304,128]{1,0:T(8,128)}, f32[324,256]{1,0:T(8,128)}) custom-call(s32[8]{0:T(128)} %concatenate.35.info, bf16[384,128]{1,0:T(8,128)(2,1)} %copy-done.2, bf16[384,128]{1,0:T(8,128)(2,1)} %copy-done.6, bf16[384,128]{1,0:T(8,128)(2,1)} %copy-done.7, bf16[384,128]{1,0:T(8,128)(2,1)} %copy-done.8, bf16[4,384,128]{2,1,0:T(8,128)(2,1)} %copy-done.5), custom_call_target="tpu_custom_call" | custom-call | tf_op jit(solution)/shard_map/pallas_call | solution.py:415
  (106 shorter events, 28.6 us)
Async XLA Ops:
  0.6 9.6 %collective-permute-start.5 = (bf16[512,256]{1,0:T(8,128)(2,1)}, bf16[512,256]{1,0:T(8,128)(2,1)S(1)}, u32[]{:S(2)}, u32[]{:S(2)}) collective-permute-start(bf16[512,256]{1,0:T(8,128)(2,1)} %bitcast.134), channel_id=1, source_target_pairs={{8,0},{16,8},{24,16},{32,24},{40,32},{48,40},{56,48},{64,56},{72,6... | collective-permute-start | bytes 786440 | tf_op jit(solution)/shard_map/ppermute | solution.py:27
  5.0 11.1 %collective-permute-start.4 = (bf16[512,256]{1,0:T(8,128)(2,1)}, bf16[512,256]{1,0:T(8,128)(2,1)S(1)}, u32[]{:S(2)}, u32[]{:S(2)}) collective-permute-start(bf16[512,256]{1,0:T(8,128)(2,1)} %bitcast.135), channel_id=1, source_target_pairs={{0,8},{8,16},{16,24},{24,32},{32,40},{40,48},{48,56},{56,64},{64,7... | collective-permute-start | bytes 786440 | tf_op jit(solution)/shard_map/ppermute | solution.py:27
  16.1 20.8 %collective-permute-start.9 = (bf16[2,512,256]{2,1,0:T(8,128)(2,1)S(1)}, bf16[2,512,256]{2,1,0:T(8,128)(2,1)S(1)}, u32[]{:S(2)}, u32[]{:S(2)}) collective-permute-start(bf16[2,512,256]{2,1,0:T(8,128)(2,1)S(1)} %pad_maximum_fusion.8.rows), channel_id=1, source_target_pairs={{2,0},{3,1},{4,2},{5,3},{6,4},{7,5},{10,8},{11,9},{12,10},{13,11},... | collective-permute-start | bytes 1572872 | tf_op jit(solution)/shard_map/ppermute | solution.py:27
  17.4 19.5 %collective-permute-start.8 = (bf16[2,512,256]{2,1,0:T(8,128)(2,1)S(1)}, bf16[2,512,256]{2,1,0:T(8,128)(2,1)S(1)}, u32[]{:S(2)}, u32[]{:S(2)}) collective-permute-start(bf16[2,512,256]{2,1,0:T(8,128)(2,1)S(1)} %pad_maximum_fusion.8.rows), channel_id=1, source_target_pairs={{0,2},{1,3},{2,4},{3,5},{4,6},{5,7},{8,10},{9,11},{10,12},{11,13},... | collective-permute-start | bytes 1572872 | tf_op jit(solution)/shard_map/ppermute | solution.py:27
  22.2 8.5 %collective-permute-start = (bf16[1,32,128]{2,1,0:T(8,128)(2,1)S(1)}, bf16[1,32,128]{2,1,0:T(8,128)(2,1)S(1)}, u32[]{:S(2)}, u32[]{:S(2)}) collective-permute-start(bf16[1,32,128]{2,1,0:T(8,128)(2,1)S(1)} %get-tuple-element.46), channel_id=1, source_target_pairs={{0,8},{8,16},{16,24},{24,32},{32,40},{40,48},{48,56},{56,64},{64,7... | collective-permute-start | bytes 24584 | tf_op jit(solution)/shard_map/ppermute | solution.py:42
  24.1 17.3 %collective-permute-start.7 = (bf16[512,256]{1,0:T(8,128)(2,1)}, bf16[512,256]{1,0:T(8,128)(2,1)S(1)}, u32[]{:S(2)}, u32[]{:S(2)}) collective-permute-start(bf16[512,256]{1,0:T(8,128)(2,1)} %bitcast.136), channel_id=1, source_target_pairs={{2,0},{3,1},{4,2},{5,3},{6,4},{7,5},{10,8},{11,9},{12,10},{13,11},... | collective-permute-start | bytes 786440 | tf_op jit(solution)/shard_map/ppermute | solution.py:27
  25.4 16.0 %collective-permute-start.6 = (bf16[512,256]{1,0:T(8,128)(2,1)}, bf16[512,256]{1,0:T(8,128)(2,1)S(1)}, u32[]{:S(2)}, u32[]{:S(2)}) collective-permute-start(bf16[512,256]{1,0:T(8,128)(2,1)} %bitcast.137), channel_id=1, source_target_pairs={{0,2},{1,3},{2,4},{3,5},{4,6},{5,7},{8,10},{9,11},{10,12},{11,13},... | collective-permute-start | bytes 786440 | tf_op jit(solution)/shard_map/ppermute | solution.py:27
  30.6 6.3 %collective-permute-start.1 = (bf16[1,32,128]{2,1,0:T(8,128)(2,1)S(1)}, bf16[1,32,128]{2,1,0:T(8,128)(2,1)S(1)}, u32[]{:S(2)}, u32[]{:S(2)}) collective-permute-start(bf16[1,32,128]{2,1,0:T(8,128)(2,1)S(1)} %get-tuple-element.45), channel_id=1, source_target_pairs={{8,0},{16,8},{24,16},{32,24},{40,32},{48,40},{56,48},{64,56},{72,6... | collective-permute-start | bytes 24584 | tf_op jit(solution)/shard_map/ppermute | solution.py:44
  37.1 18.6 %collective-permute-start.11 = (bf16[4,512,256]{2,1,0:T(8,128)(2,1)S(1)}, bf16[4,512,256]{2,1,0:T(8,128)(2,1)}, u32[]{:S(2)}, u32[]{:S(2)}) collective-permute-start(bf16[4,512,256]{2,1,0:T(8,128)(2,1)S(1)} %pad_maximum_fusion.1), channel_id=1, source_target_pairs={{0,1},{1,0},{2,3},{3,2},{4,5},{5,4},{6,7},{7,6},{8,9},{9,8},{10,11... | collective-permute-start | bytes 3145736 | tf_op jit(solution)/shard_map/ppermute | solution.py:31
  42.3 13.5 %collective-permute-start.10 = (bf16[2,512,256]{2,1,0:T(8,128)(2,1)}, bf16[2,512,256]{2,1,0:T(8,128)(2,1)}, u32[]{:S(2)}, u32[]{:S(2)}) collective-permute-start(bf16[2,512,256]{2,1,0:T(8,128)(2,1)} %pad_maximum_fusion.10), channel_id=1, source_target_pairs={{0,1},{1,0},{2,3},{3,2},{4,5},{5,4},{6,7},{7,6},{8,9},{9,8},{10,11... | collective-permute-start | bytes 1572872 | tf_op jit(solution)/shard_map/ppermute | solution.py:31
  42.9 8.9 %collective-permute-start.3 = (bf16[18,1,128]{2,1,0:T(2,128)(2,1)S(1)}, bf16[18,1,128]{2,1,0:T(2,128)(2,1)S(1)}, u32[]{:S(2)}, u32[]{:S(2)}) collective-permute-start(bf16[18,1,128]{2,1,0:T(2,128)(2,1)S(1)} %get-tuple-element.44), channel_id=1, source_target_pairs={{0,1},{1,2},{2,3},{3,4},{4,5},{5,6},{6,7},{8,9},{9,10},{10,11},{11... | collective-permute-start | bytes 13832 | tf_op jit(solution)/shard_map/ppermute | solution.py:42
  45.9 5.9 %collective-permute-start.2 = (bf16[18,1,128]{2,1,0:T(2,128)(2,1)S(1)}, bf16[18,1,128]{2,1,0:T(2,128)(2,1)S(1)}, u32[]{:S(2)}, u32[]{:S(2)}) collective-permute-start(bf16[18,1,128]{2,1,0:T(2,128)(2,1)S(1)} %get-tuple-element.43), channel_id=1, source_target_pairs={{1,0},{2,1},{3,2},{4,3},{5,4},{6,5},{7,6},{9,8},{10,9},{11,10},{12... | collective-permute-start | bytes 13832 | tf_op jit(solution)/shard_map/ppermute | solution.py:44
  75.3 20.3 %collective-permute-start.16 = (bf16[6,512,256]{2,1,0:T(8,128)(2,1)}, bf16[6,512,256]{2,1,0:T(8,128)(2,1)}, u32[]{:S(2)}, u32[]{:S(2)}) collective-permute-start(bf16[6,512,256]{2,1,0:T(8,128)(2,1)} %get-tuple-element.21), channel_id=1, source_target_pairs={{0,1},{1,0},{2,3},{3,2},{4,5},{5,4},{6,7},{7,6},{8,9},{9,8},{10,11... | collective-permute-start | bytes 4718600 | tf_op jit(solution)/shard_map/ppermute | solution.py:31
  81.1 5.7 %collective-permute-start.24 = (bf16[384,128]{1,0:T(8,128)(2,1)}, bf16[384,128]{1,0:T(8,128)(2,1)S(1)}, u32[]{:S(2)}, u32[]{:S(2)}) collective-permute-start(bf16[384,128]{1,0:T(8,128)(2,1)} %get-tuple-element.29), channel_id=1, source_target_pairs={{0,6},{1,7},{2,4},{3,5},{4,2},{5,3},{6,0},{7,1},{8,14},{9,15},{10,... | collective-permute-start | bytes 294920 | tf_op jit(solution)/shard_map/ppermute | solution.py:31
  83.1 5.0 %collective-permute-start.23 = (bf16[384,128]{1,0:T(8,128)(2,1)S(1)}, bf16[384,128]{1,0:T(8,128)(2,1)S(1)}, u32[]{:S(2)}, u32[]{:S(2)}) collective-permute-start(bf16[384,128]{1,0:T(8,128)(2,1)S(1)} %get-tuple-element.30), channel_id=1, source_target_pairs={{0,4},{1,5},{2,6},{3,7},{4,0},{5,1},{6,2},{7,3},{8,12},{9,13},{10,... | collective-permute-start | bytes 294920 | tf_op jit(solution)/shard_map/ppermute | solution.py:31
  90.2 11.8 %collective-permute-start.27 = (bf16[384,128]{1,0:T(8,128)(2,1)S(1)}, bf16[384,128]{1,0:T(8,128)(2,1)S(1)}, u32[]{:S(2)}, u32[]{:S(2)}) collective-permute-start(bf16[384,128]{1,0:T(8,128)(2,1)S(1)} %add_convert_fusion.2), channel_id=1, source_target_pairs={{0,24},{8,16},{16,8},{24,0},{32,56},{40,48},{48,40},{56,32},{64,88... | collective-permute-start | bytes 294920 | tf_op jit(solution)/shard_map/ppermute | solution.py:31
  94.8 7.2 %collective-permute-start.26 = (bf16[384,128]{1,0:T(8,128)(2,1)S(1)}, bf16[384,128]{1,0:T(8,128)(2,1)S(1)}, u32[]{:S(2)}, u32[]{:S(2)}) collective-permute-start(bf16[384,128]{1,0:T(8,128)(2,1)S(1)} %add_convert_fusion.2), channel_id=1, source_target_pairs={{0,16},{8,24},{16,0},{24,8},{32,48},{40,56},{48,32},{56,40},{64,80... | collective-permute-start | bytes 294920 | tf_op jit(solution)/shard_map/ppermute | solution.py:31
  94.8 7.2 %collective-permute-start.25 = (bf16[384,128]{1,0:T(8,128)(2,1)S(1)}, bf16[384,128]{1,0:T(8,128)(2,1)S(1)}, u32[]{:S(2)}, u32[]{:S(2)}) collective-permute-start(bf16[384,128]{1,0:T(8,128)(2,1)S(1)} %add_convert_fusion.2), channel_id=1, source_target_pairs={{0,8},{8,0},{16,24},{24,16},{32,40},{40,32},{48,56},{56,48},{64,72... | collective-permute-start | bytes 294920 | tf_op jit(solution)/shard_map/ppermute | solution.py:31
  97.7 33.4 %collective-permute-start.18 = (bf16[3,512,256]{2,1,0:T(8,128)(2,1)S(1)}, bf16[3,512,256]{2,1,0:T(8,128)(2,1)S(1)}, u32[]{:S(2)}, u32[]{:S(2)}) collective-permute-start(bf16[3,512,256]{2,1,0:T(8,128)(2,1)S(1)} %fusion.10), channel_id=1, source_target_pairs={{0,2},{1,3},{2,4},{3,5},{4,6},{5,7},{8,10},{9,11},{10,12},{11,13},... | collective-permute-start | bytes 2359304 | tf_op jit(solution)/shard_map/ppermute | solution.py:27
  100.7 30.5 %collective-permute-start.17 = (bf16[3,512,256]{2,1,0:T(8,128)(2,1)S(1)}, bf16[3,512,256]{2,1,0:T(8,128)(2,1)S(1)}, u32[]{:S(2)}, u32[]{:S(2)}) collective-permute-start(bf16[3,512,256]{2,1,0:T(8,128)(2,1)S(1)} %fusion.9), channel_id=1, source_target_pairs={{2,0},{3,1},{4,2},{5,3},{6,4},{7,5},{10,8},{11,9},{12,10},{13,11},... | collective-permute-start | bytes 2359304 | tf_op jit(solution)/shard_map/ppermute | solution.py:27
  103.8 7.1 %collective-permute-start.29 = (bf16[384,128]{1,0:T(8,128)(2,1)S(1)}, bf16[384,128]{1,0:T(8,128)(2,1)S(1)}, u32[]{:S(2)}, u32[]{:S(2)}) collective-permute-start(bf16[384,128]{1,0:T(8,128)(2,1)S(1)} %add_convert_fusion.1), channel_id=1, source_target_pairs={{0,64},{8,72},{16,80},{24,88},{32,96},{40,104},{48,112},{56,120},{... | collective-permute-start | bytes 294920 | tf_op jit(solution)/shard_map/ppermute | solution.py:31
  103.8 9.0 %collective-permute-start.28 = (bf16[384,128]{1,0:T(8,128)(2,1)S(1)}, bf16[384,128]{1,0:T(8,128)(2,1)S(1)}, u32[]{:S(2)}, u32[]{:S(2)}) collective-permute-start(bf16[384,128]{1,0:T(8,128)(2,1)S(1)} %add_convert_fusion.1), channel_id=1, source_target_pairs={{0,32},{8,40},{16,48},{24,56},{32,0},{40,8},{48,16},{56,24},{64,96... | collective-permute-start | bytes 294920 | tf_op jit(solution)/shard_map/ppermute | solution.py:31
  105.8 9.3 %collective-permute-start.13 = (bf16[1,32,256]{2,1,0:T(8,128)(2,1)S(1)}, bf16[1,32,256]{2,1,0:T(8,128)(2,1)S(1)}, u32[]{:S(2)}, u32[]{:S(2)}) collective-permute-start(bf16[1,32,256]{2,1,0:T(8,128)(2,1)S(1)} %get-tuple-element.40), channel_id=1, source_target_pairs={{8,0},{16,8},{24,16},{32,24},{40,32},{48,40},{56,48},{64,56},{72,6... | collective-permute-start | bytes 49160 | tf_op jit(solution)/shard_map/ppermute | solution.py:44
  110.9 6.6 %collective-permute-start.12 = (bf16[1,32,256]{2,1,0:T(8,128)(2,1)S(1)}, bf16[1,32,256]{2,1,0:T(8,128)(2,1)S(1)}, u32[]{:S(2)}, u32[]{:S(2)}) collective-permute-start(bf16[1,32,256]{2,1,0:T(8,128)(2,1)S(1)} %get-tuple-element.39), channel_id=1, source_target_pairs={{0,8},{8,16},{16,24},{24,32},{32,40},{40,48},{48,56},{56,64},{64,7... | collective-permute-start | bytes 49160 | tf_op jit(solution)/shard_map/ppermute | solution.py:42
  112.9 8.4 %collective-permute-start.31 = (bf16[384,128]{1,0:T(8,128)(2,1)S(1)}, bf16[384,128]{1,0:T(8,128)(2,1)S(1)}, u32[]{:S(2)}, u32[]{:S(2)}) collective-permute-start(bf16[384,128]{1,0:T(8,128)(2,1)S(1)} %add_convert_fusion.s0), channel_id=1, source_target_pairs={{0,2},{1,3},{2,0},{3,1},{4,6},{5,7},{6,4},{7,5},{8,10},{9,11},{10,... | collective-permute-start | bytes 294920 | tf_op jit(solution)/shard_map/ppermute | solution.py:31
  115.1 13.5 %collective-permute-start.32 = (bf16[384,128]{1,0:T(8,128)(2,1)S(1)}, bf16[384,128]{1,0:T(8,128)(2,1)S(1)}, u32[]{:S(2)}, u32[]{:S(2)}) collective-permute-start(bf16[384,128]{1,0:T(8,128)(2,1)S(1)} %add_convert_fusion.s0), channel_id=1, source_target_pairs={{0,4},{1,5},{2,6},{3,7},{4,0},{5,1},{6,2},{7,3},{8,12},{9,13},{10,... | collective-permute-start | bytes 294920 | tf_op jit(solution)/shard_map/ppermute | solution.py:31
  117.5 13.2 %collective-permute-start.33 = (bf16[384,128]{1,0:T(8,128)(2,1)S(1)}, bf16[384,128]{1,0:T(8,128)(2,1)S(1)}, u32[]{:S(2)}, u32[]{:S(2)}) collective-permute-start(bf16[384,128]{1,0:T(8,128)(2,1)S(1)} %add_convert_fusion.s0), channel_id=1, source_target_pairs={{0,6},{1,7},{2,4},{3,5},{4,2},{5,3},{6,0},{7,1},{8,14},{9,15},{10,... | collective-permute-start | bytes 294920 | tf_op jit(solution)/shard_map/ppermute | solution.py:31
  121.3 17.8 %collective-permute-start.15 = (bf16[18,1,256]{2,1,0:T(2,128)(2,1)S(1)}, bf16[18,1,256]{2,1,0:T(2,128)(2,1)S(1)}, u32[]{:S(2)}, u32[]{:S(2)}) collective-permute-start(bf16[18,1,256]{2,1,0:T(2,128)(2,1)S(1)} %get-tuple-element.36), channel_id=1, source_target_pairs={{1,0},{2,1},{3,2},{4,3},{5,4},{6,5},{7,6},{9,8},{10,9},{11,10},{12... | collective-permute-start | bytes 27656 | tf_op jit(solution)/shard_map/ppermute | solution.py:44
  128.6 10.5 %collective-permute-start.14 = (bf16[18,1,256]{2,1,0:T(2,128)(2,1)S(1)}, bf16[18,1,256]{2,1,0:T(2,128)(2,1)S(1)}, u32[]{:S(2)}, u32[]{:S(2)}) collective-permute-start(bf16[18,1,256]{2,1,0:T(2,128)(2,1)S(1)} %get-tuple-element.35), channel_id=1, source_target_pairs={{0,1},{1,2},{2,3},{3,4},{4,5},{5,6},{6,7},{8,9},{9,10},{10,11},{11... | collective-permute-start | bytes 27656 | tf_op jit(solution)/shard_map/ppermute | solution.py:42
  130.8 12.3 %collective-permute-start.34 = (bf16[4,384,128]{2,1,0:T(8,128)(2,1)S(1)}, bf16[4,384,128]{2,1,0:T(8,128)(2,1)S(1)}, u32[]{:S(2)}, u32[]{:S(2)}) collective-permute-start(bf16[4,384,128]{2,1,0:T(8,128)(2,1)S(1)} %pad_maximum_fusion.13), channel_id=1, source_target_pairs={{0,1},{1,0},{2,3},{3,2},{4,5},{5,4},{6,7},{7,6},{8,9},{9,8},{10,11... | collective-permute-start | bytes 1179656 | tf_op jit(solution)/shard_map/ppermute | solution.py:31
  131.7 14.7 %collective-permute-start.20 = (bf16[512,256]{1,0:T(8,128)(2,1)S(1)}, bf16[512,256]{1,0:T(8,128)(2,1)S(1)}, u32[]{:S(2)}, u32[]{:S(2)}) collective-permute-start(bf16[512,256]{1,0:T(8,128)(2,1)S(1)} %get-tuple-element.32), channel_id=1, source_target_pairs={{0,8},{8,16},{16,24},{24,32},{32,40},{40,48},{48,56},{56,64},{64,7... | collective-permute-start | bytes 786440 | tf_op jit(solution)/shard_map/ppermute | solution.py:27
  133.6 12.7 %collective-permute-start.19 = (bf16[512,256]{1,0:T(8,128)(2,1)S(1)}, bf16[512,256]{1,0:T(8,128)(2,1)S(1)}, u32[]{:S(2)}, u32[]{:S(2)}) collective-permute-start(bf16[512,256]{1,0:T(8,128)(2,1)S(1)} %get-tuple-element.31), channel_id=1, source_target_pairs={{8,0},{16,8},{24,16},{32,24},{40,32},{48,40},{56,48},{64,56},{72,6... | collective-permute-start | bytes 786440 | tf_op jit(solution)/shard_map/ppermute | solution.py:27
  (17 other events, 161.7 us)

commit v2 on v1

v2 whole, which is shorter than its diff:
```python
import functools
import math

import jax
import jax.numpy as jnp
from jax import lax
from jax.experimental import pallas as pl
from jax.experimental.pallas import tpu as pltpu
from jax.sharding import PartitionSpec as P

REACH = 4
SPAN = 2 * REACH + 1
GROUP = 128
WINDOW = 384
LEAD, LEAD_BACK = 3, 4
F32 = jnp.float32
BF16 = jnp.bfloat16
VMEM_LIMIT = 56 * 1024 * 1024
VMEM = pl.BlockSpec(memory_space=pltpu.VMEM)
SMEM = pl.BlockSpec(memory_space=pltpu.SMEM)
ANY = pl.BlockSpec(memory_space=pl.ANY)


def swap(array, axis, bits):
    return lax.ppermute(array, axis, [(i, i ^ bits) for i in range(lax.axis_size(axis))])


def swap_pairs(array, axis, odd, unit=1):
    count = lax.axis_size(axis) // unit
    pairs = []
    for i in range(odd, count - 1, 2):
        for low in range(unit):
            here, there = i * unit + low, (i + 1) * unit + low
            pairs += [(here, there), (there, here)]
    return lax.ppermute(array, axis, pairs)


def rim(cells, row_even, col_even):
    top, bottom = cells[0], cells[-1]
    even = swap_pairs(jnp.where(row_even, bottom, top), "row", 0)
    odd = swap_pairs(jnp.where(row_even, top, bottom), "row", 1)
    north, south = jnp.where(row_even, odd, even), jnp.where(row_even, even, odd)
    left = jnp.concatenate([north[:1], cells[:, 0], south[:1]])
    right = jnp.concatenate([north[-1:], cells[:, -1], south[-1:]])
    even = swap_pairs(jnp.where(col_even, right, left), "col", 0)
    odd = swap_pairs(jnp.where(col_even, left, right), "col", 1)
    west, east = jnp.where(col_even, odd, even), jnp.where(col_even, even, odd)
    return north, south, west, east


def write_taps(taps, own, north, south, west, east, backwards):
    width = own.shape[1]
    line = north.shape[0]
    taps[:line, width : 2 * width] = north[...]
    taps[line:-line, width : 2 * width] = own[...]
    taps[-line:, width : 2 * width] = south[...]
    middle = taps[:, width : 2 * width].astype(F32)
    place = lax.broadcasted_iota(jnp.int32, middle.shape, 0) % line

    def stretched(ends):
        shape = (ends.shape[0], line, width)
        return jnp.broadcast_to(ends[...].astype(F32)[:, None], shape).reshape(middle.shape)

    left = jnp.where(place == 0, stretched(west), pltpu.roll(middle, 1, 0)).astype(BF16)
    right = jnp.where(
        place == line - 1, stretched(east), pltpu.roll(middle, middle.shape[0] - 1, 0)
    ).astype(BF16)
    taps[:, :width] = right if backwards else left
    taps[:, 2 * width :] = left if backwards else right


def tap_mask(radius, lead, backwards):
    cell = lax.broadcasted_iota(jnp.int32, (GROUP, WINDOW), 0)
    cell = GROUP - 1 - cell if backwards else cell
    tap = lax.broadcasted_iota(jnp.int32, (GROUP, WINDOW), 1)
    down = (tap >> 5) - REACH
    across = (tap & 31) - lead - REACH
    column = (cell & 31) + across
    return (
        (jnp.abs(down) <= radius)
        & (jnp.abs(across) <= radius)
        & (column >= 0)
        & (column < 32)
    )


def flip_matrix():
    return (
        (
            lax.broadcasted_iota(jnp.int32, (GROUP, GROUP), 0)
            + lax.broadcasted_iota(jnp.int32, (GROUP, GROUP), 1)
            == GROUP - 1
        )
        .astype(F32)
        .astype(BF16)
    )


def early_kernel(
    first, cotangent, north, south, west, east, back_weight, cot_taps, grad_motion, flipped
):
    cells = first.shape[0]
    write_taps(cot_taps, cotangent, north, south, west, east, True)
    total = jnp.zeros(grad_motion.shape, F32)
    for a in range(3):
        start = (2 - a) * 32
        total += jnp.dot(
            cot_taps[start : start + cells], back_weight[a], preferred_element_type=F32
        )
    grad_motion[...] = total
    flip = flip_matrix()
    for q in range(cells // GROUP):
        at = slice(q * GROUP, (q + 1) * GROUP)
        flipped[at] = jnp.dot(flip, first[at], preferred_element_type=F32).astype(BF16)


def forward_kernel(info, flipped, context, cot_taps, grad_motion, corr_weight, *refs):
    tiles, refs = refs[:18], refs[18:]
    parts, motion, context_grad, weights_sent, weights_kept, taps, weight_grads, sems = refs
    cells = flipped.shape[0]
    slots = parts.shape[0]
    for k in range(slots):
        for t in range(18):
            @pl.when(info[k] == t)
            def _():
                pltpu.make_async_copy(
                    tiles[t], parts.at[k, pl.ds(GROUP, cells)], sems.at[k]
                ).start()
        parts[k, :GROUP] = jnp.zeros((GROUP, parts.shape[2]), BF16)
        parts[k, GROUP + cells :] = jnp.zeros((GROUP, parts.shape[2]), BF16)
    inside = tap_mask(info[slots + 1], LEAD, True)
    flip = flip_matrix()
    gains = []
    for k in range(slots):
        live = jnp.where(k < info[slots], 1.0 / math.sqrt(flipped.shape[1]), 0.0).astype(F32)
        gains.append(jnp.where(inside, live, 0.0))
    for k in range(slots):
        pltpu.make_async_copy(tiles[0], parts.at[k, pl.ds(GROUP, cells)], sems.at[k]).wait()
    for q in range(cells // GROUP):
        at = slice(q * GROUP, (q + 1) * GROUP)
        features = flipped[at]
        for k in range(slots):
            scores = lax.dot_general(
                features,
                parts[k, q * GROUP : q * GROUP + WINDOW],
                (((1,), (1,)), ((), ())),
                preferred_element_type=F32,
            )
            turn = WINDOW + REACH + LEAD - (GROUP - 1)
            band = pltpu.roll(scores, turn, 1, stride=1, stride_axis=0) * gains[k]
            packed = (
                band[:, :128]
                + pltpu.roll(band[:, 128:256], SPAN, 1)
                + pltpu.roll(band[:, 256:], 2 * SPAN, 1)
            )
            taps[at, k * 128 : (k + 1) * 128] = jnp.dot(
                flip, packed.astype(BF16), preferred_element_type=F32
            ).astype(BF16)
    pre = jnp.dot(taps[...], corr_weight[...], preferred_element_type=F32) + context[...].astype(
        F32
    )
    sigma = jax.nn.sigmoid(pre)
    motion[...] = (pre * sigma).astype(BF16)
    context_grad[...] = (grad_motion[...] * sigma * (1.0 + pre * (1.0 - sigma))).astype(BF16)
    over_cells = (((0,), (0,)), ((), ()))
    for a in range(3):
        start = (2 - a) * 32
        term = lax.dot_general(
            motion[...], cot_taps[start : start + cells], over_cells, preferred_element_type=F32
        )
        for b in range(3):
            weight_grads[(3 * a + b) * 256 : (3 * a + b + 1) * 256] = term[
                :, b * 128 : (b + 1) * 128
            ]
    term = lax.dot_general(taps[...], context_grad[...], over_cells, preferred_element_type=F32)
    base = 9 * 256
    for h in range(2):
        weight_grads[base + h * 384 + 320 : base + (h + 1) * 384] = jnp.zeros((64, 128), F32)
        for k in range(slots):
            for u in range(SPAN):
                row = k * 128 + (u % 4) * 32 + (u // 4) * SPAN + LEAD
                to = base + h * 384 + (k * SPAN + u) * SPAN
                weight_grads[to : to + SPAN] = term[row : row + SPAN, h * 128 : (h + 1) * 128]
    half = weight_grads.shape[0] // 2
    core = info[slots + 2]
    weights_kept[...] = weight_grads[pl.ds(pl.multiple_of(core * half, half), half)]
    weights_sent[...] = weight_grads[pl.ds(pl.multiple_of((1 - core) * half, half), half)].astype(
        BF16
    )


def backward_kernel(
    info, first, context_grad, corr_weight, parts, first_grad, kept, lent, totals
):
    cells = first.shape[0]
    slots = parts.shape[0]
    scale = 1.0 / math.sqrt(first.shape[1])
    inside = tap_mask(info[slots + 1], LEAD_BACK, False)
    totals[...] = jnp.zeros_like(totals)
    kept[...] = jnp.zeros_like(kept)
    lent[...] = jnp.zeros_like(lent)
    for q in range(cells // GROUP):
        at = slice(q * GROUP, (q + 1) * GROUP)
        packed = (
            lax.dot_general(
                context_grad[at],
                corr_weight[...],
                (((1,), (1,)), ((), ())),
                preferred_element_type=F32,
            )
            .astype(BF16)
            .astype(F32)
        )
        first_here = jnp.zeros((GROUP, first.shape[1]), F32)
        for k in range(slots):
            mine = packed[:, k * 128 : (k + 1) * 128]
            band = jnp.concatenate(
                [mine, pltpu.roll(mine, 128 - SPAN, 1), pltpu.roll(mine, 128 - 2 * SPAN, 1)],
                axis=1,
            )
            band = jnp.where(inside & (k < info[slots]), band, 0.0)
            scores = pltpu.roll(band, WINDOW - REACH - LEAD_BACK, 1, stride=1, stride_axis=0).astype(BF16)
            window = slice(q * GROUP, q * GROUP + WINDOW)
            first_here += jnp.dot(scores, parts[k, window], preferred_element_type=F32)
            totals[k, window] += lax.dot_general(
                scores, first[at], (((0,), (0,)), ((), ())), preferred_element_type=F32
            )
        first_grad[at] = first_here * scale
    for k in range(slots):
        value = (totals[k, GROUP : GROUP + cells] * scale).astype(BF16)
        place = info[k]
        same = place % 2 == 0

        @pl.when(same)
        def _():
            kept[place // 2] = value

        @pl.when(jnp.logical_not(same))
        def _():
            lent[place // 6 * 2 + (place % 6 > 1).astype(jnp.int32)] = value


def features_kernel(motion, north, south, west, east, weight, out, taps):
    cells = out.shape[0]
    write_taps(taps, motion, north, south, west, east, False)
    total = jnp.zeros(out.shape, F32)
    for a in range(3):
        total += jnp.dot(taps[a * 32 : a * 32 + cells], weight[a], preferred_element_type=F32)
    out[...] = total.astype(BF16)


def finish_kernel(info, *refs):
    shards, (conv, corr, whole) = refs[:8], refs[8:]
    size = shards[0].shape[0]
    core, chip = info[6], info[7]
    half = whole.shape[0] // 2
    for s in range(4):
        other = chip ^ s
        to = pl.multiple_of(core * half + other * size, size)
        whole[pl.ds(to, size)] = shards[s][...].astype(F32)
        to = pl.multiple_of((1 - core) * half + other * size, size)
        whole[pl.ds(to, size)] = shards[4 + s][...].astype(F32)
    conv[...] = whole[: conv.shape[0]]
    base = conv.shape[0]
    for h in range(2):
        corr[:, h * 128 : (h + 1) * 128] = whole[base + h * 384 : base + h * 384 + corr.shape[0]]


def call(kernel, out_shape, in_specs, scratch=(), flops=0):
    return pl.pallas_call(
        kernel,
        out_shape=out_shape,
        in_specs=in_specs,
        out_specs=jax.tree.map(lambda _: VMEM, out_shape),
        scratch_shapes=list(scratch),
        compiler_params=pltpu.CompilerParams(vmem_limit_bytes=VMEM_LIMIT),
        cost_estimate=pl.CostEstimate(flops=flops, bytes_accessed=flops // 300, transcendentals=0),
    )


def sum_weights(sent, kept):
    cur = kept + swap(sent, "col", 1).astype(F32)
    size = cur.shape[0] // 4
    chip = lax.axis_index("col") // 2
    pieces = [
        lax.dynamic_slice_in_dim(cur, (chip ^ s) * size, size, axis=0) for s in range(4)
    ]
    got = [swap(pieces[s].astype(BF16), "col", 2 * s).astype(F32) for s in (1, 2, 3)]
    cur = (pieces[0] + got[0]) + (got[1] + got[2])
    for unit in (1, 4):
        mine = cur.astype(BF16)
        got = [swap(mine, "row", unit * s).astype(F32) for s in (1, 2, 3)]
        cur = (mine.astype(F32) + got[0]) + (got[1] + got[2])
    mine = cur.astype(BF16)
    shards = [mine] + [swap(mine, "col", 2 * s) for s in (1, 2, 3)]
    return shards + [swap(shard, "col", 1) for shard in shards]


def body(
    frame_one, frame_two, context, cotangent, corr_weight, conv_weight, partners, counts, radius
):
    rows_tile, cols_tile, channels = frame_one.shape
    slots = partners.shape[-1]
    cells = rows_tile * cols_tile
    hidden = context.shape[-1]
    out_width = conv_weight.shape[-1]
    row, col = lax.axis_index("row"), lax.axis_index("col")
    core, chip = col % 2, col // 2
    row_even, chip_even, col_even = row % 2 == 0, chip % 2 == 0, core == 0

    def role(step, even):
        return jnp.where(step == 0, 0, jnp.where((step > 0) == even, 1, 2))

    down, across = partners[0, 0] // 5 - 1, partners[0, 0] % 5 - 2
    chip_step = (core + across) >> 1
    place = role(down, row_even) * 6 + role(chip_step, chip_even) * 2 + (across & 1)
    info = jnp.concatenate(
        [place, counts[0], radius[0], core[None], chip[None]]
    ).astype(jnp.int32)
    first = frame_one.reshape(cells, channels)
    own = frame_two.reshape(cells, channels)
    tiles = {(0, 0): own}
    for r in (1, 2):
        tiles[r, 0] = swap_pairs(own, "row", r - 1)
        tiles[0, r] = swap_pairs(own, "col", r - 1, 2)
    for r in (1, 2):
        tiles[r, r] = swap_pairs(tiles[r, 0], "col", r - 1, 2)
        tiles[r, 3 - r] = swap_pairs(tiles[0, 3 - r], "row", r - 1)
    around = []
    for r in range(3):
        for x in range(3):
            around += [tiles[r, x], swap(tiles[r, x], "col", 1)]
    spread = jnp.pad(
        corr_weight.reshape(slots, SPAN, SPAN, hidden), ((0, 0), (0, 3), (0, 0), (0, 0))
    )
    spread = spread.reshape(slots, 3, 4, SPAN, hidden).transpose(0, 2, 1, 3, 4)
    spread = spread.reshape(slots, 4, 3 * SPAN, hidden)
    spread, spread_back = (
        jnp.pad(spread, ((0, 0), (0, 0), (lead, 5 - lead), (0, 0))).reshape(slots * 128, hidden)
        for lead in (LEAD, LEAD_BACK)
    )
    back_weight = conv_weight.transpose(0, 1, 3, 2).reshape(3, 3 * out_width, hidden)
    shape = jax.ShapeDtypeStruct
    total_rows = 9 * hidden + 2 * 384
    cot_taps, grad_motion, flipped = call(
        early_kernel,
        (
            shape(((rows_tile + 2) * cols_tile, 3 * out_width), BF16),
            shape((cells, hidden), F32),
            shape((cells, channels), BF16),
        ),
        [VMEM] * 7,
        flops=10**9,
    )(
        first,
        cotangent.reshape(cells, out_width),
        *rim(cotangent, row_even, col_even),
        back_weight,
    )
    parts, motion, context_grad, weights_sent, weights_kept = call(
        forward_kernel,
        (
            shape((slots, cells + 2 * GROUP, channels), BF16),
            shape((cells, hidden), BF16),
            shape((cells, hidden), BF16),
            shape((total_rows // 2, 128), BF16),
            shape((total_rows // 2, 128), F32),
        ),
        [SMEM] + [VMEM] * 5 + [ANY] * 18,
        [
            pltpu.VMEM((cells, slots * 128), BF16),
            pltpu.VMEM((total_rows, 128), F32),
            pltpu.SemaphoreType.DMA((slots,)),
        ],
        flops=3 * 10**9,
    )(info, flipped, context.reshape(cells, hidden), cot_taps, grad_motion, spread, *around)
    shards = sum_weights(weights_sent, weights_kept)
    first_grad, kept, lent = call(
        backward_kernel,
        (
            shape((cells, channels), F32),
            shape((9, cells, channels), BF16),
            shape((6, cells, channels), BF16),
        ),
        [SMEM] + [VMEM] * 4,
        [pltpu.VMEM((slots, cells + 2 * GROUP, channels), F32)],
        flops=3 * 10**9,
    )(info, first, context_grad, spread_back, parts)
    lent = swap(lent, "col", 1).reshape(3, 2, cells, channels).astype(F32)
    kept = kept.reshape(3, 3, cells, channels).astype(F32)
    side = jnp.where((core == 0) == chip_even, 1, 2)
    sums = {}
    for r in range(3):
        sums[r, 0] = kept[r, 0] + lent[r, 0]
        for x in (1, 2):
            sums[r, x] = kept[r, x] + jnp.where(side == x, lent[r, 1], 0.0)
    for r in (1, 2):
        sums[r, 0] += swap_pairs(sums[r, r].astype(BF16), "col", r - 1, 2).astype(F32)
        sums[0, 3 - r] += swap_pairs(sums[r, 3 - r].astype(BF16), "row", r - 1).astype(F32)
    second_grad = sums[0, 0]
    for r in (1, 2):
        second_grad += swap_pairs(sums[r, 0].astype(BF16), "row", r - 1).astype(F32)
        second_grad += swap_pairs(sums[0, r].astype(BF16), "col", r - 1, 2).astype(F32)
    features = call(
        features_kernel,
        shape((cells, out_width), BF16),
        [VMEM] * 6,
        [pltpu.VMEM(((rows_tile + 2) * cols_tile, 3 * hidden), BF16)],
        flops=10**9,
    )(
        motion,
        *rim(motion.reshape(rows_tile, cols_tile, hidden), row_even, col_even),
        conv_weight.reshape(3, 3 * hidden, out_width),
    )
    conv_total, corr_total = call(
        finish_kernel,
        (shape((9 * hidden, out_width), F32), shape(corr_weight.shape, F32)),
        [SMEM] + [VMEM] * 8,
        [pltpu.VMEM((total_rows, 128), F32)],
    )(info, *shards)
    return (
        features.reshape(rows_tile, cols_tile, out_width),
        context_grad.reshape(rows_tile, cols_tile, hidden),
        first_grad.reshape(frame_one.shape),
        second_grad.reshape(frame_two.shape),
        corr_total,
        conv_total.reshape(conv_weight.shape),
    )


def solution(mesh):
    return jax.shard_map(
        body,
        mesh=mesh,
        in_specs=(
            P("row", "col", None),
            P("row", "col", None),
            P("row", "col", None),
            P("row", "col", None),
            P(),
            P(),
            P("row", "col", None),
            P("row", "col"),
            P("row", "col"),
        ),
        out_specs=(
            P("row", "col", None),
            P("row", "col", None),
            P("row", "col", None),
            P("row", "col", None),
            P(),
            P(),
        ),
        check_vma=False,
    )
```

time: 149 us -> 151 us (1.013)
  waiting for transfers between devices: 19.1 us -> 24.8 us
  starting transfers between devices: 82.3 us -> 78.4 us
  other arithmetic: 12.5 us -> 9.15 us
  Pallas kernels: 24.7 us -> 26.4 us
    ppermute x17 -> x27, waiting for transfers between devices: 8.82 us -> 14.7 us  [swap(): lax.ppermute(array, axis, [(i, i ^ bits) for i in range(lax.axis_size(axi...]
    ppermute x18 -> x24, starting transfers between devices: 57.1 us -> 52.7 us  [swap_pairs(): return lax.ppermute(array, axis, pairs)]
    concatenate x4 -> x0, other arithmetic: 4.37 us -> none  [the longest x1 2 us: body(): jnp.concatenate([grad_rim[:, 2 - b:2 - b + cols_tile] for b in range(3)],...]
    pallas_call x1 -> x2, Pallas kernels: 2.76 us -> 5.47 us  [the longest x1 2.81 us: body(): call(early_kernel, (shape(((rows_tile + 2) * cols_tile, 3 * out_width), B...]
    select_n x1 -> x8, other arithmetic: 0.09 us -> 2.74 us  [the longest x2 1.47 us: rim(): even = swap_pairs(jnp.where(row_even, bottom, top), 'row', 0)]
    another operation x6 -> x0, other arithmetic: 2.27 us -> none  [the longest x2 0.9 us: body(): jnp.stack([jnp.where(second_core, west, own), jnp.where(second_core, own,...]
    convert_element_type x1, other arithmetic: 0.44 us -> 2.2 us  [body(): kept = kept.reshape(3, 3, cells, channels).astype(F32)]
    ppermute x17 -> x27, starting transfers between devices: 25.2 us -> 25.7 us  [swap(): lax.ppermute(array, axis, [(i, i ^ bits) for i in range(lax.axis_size(axi...]
  transfers between devices with their start and end apart: 35 -> 51, of which waited for: 10 -> 16; matrix products, arithmetic and copies ran while one was open for 12% -> 9% of each run, Pallas kernels for 4% -> 11%
where the time goes in v2:
time: 151 us; the launch traced here: 149 us
  starting transfers between devices  78.4 us (52%)
  Pallas kernels  26.4 us (17%)
  waiting for transfers between devices  24.8 us (16%)
  other arithmetic  9.15 us (6%)
  local copies, waits for them, and re-layouts  7.61 us (5%)
  between operations  2.67 us (2%)
    ppermute x24, starting transfers between devices, swap_pairs(): return lax.ppermute(array, axis, pairs)  52.7 us
    ppermute x27, starting transfers between devices, swap(): lax.ppermute(array, axis, [(i, i ^ bits) for i in range(lax.axis_size(axi...  25.7 us
    ppermute x27, waiting for transfers between devices, swap(): lax.ppermute(array, axis, [(i, i ^ bits) for i in range(lax.axis_size(axi...  14.7 us
    ppermute x24, waiting for transfers between devices, swap_pairs(): return lax.ppermute(array, axis, pairs)  10.1 us
    pallas_call x1, Pallas kernels, body(): call(forward_kernel, (shape((slots, cells + 2 * GROUP, channels), BF16),...  10.1 us
    pallas_call x1, Pallas kernels, body(): call(backward_kernel, (shape((cells, channels), F32), shape((9, cells, ch...  8.29 us
  transfers between devices with their start and end apart: 51, of which 16 were waited for; matrix products, arithmetic and copies ran while one was open for 9% of the time, Pallas kernels for 11%

profile of v2, /device:TPU:33, one launch (start us, length us, event | category | flops | bytes accessed | tf_op | source)
XLA Modules:
  0.0 149.0 jit_solution(16253861130076200871)
XLA Ops:
  4.6 3.3 %collective-permute-start = (bf16[32,128]{1,0:T(8,128)(2,1)S(1)}, bf16[32,128]{1,0:T(8,128)(2,1)S(1)}, u32[]{:S(2)}, u32[]{:S(2)}) collective-permute-start(bf16[32,128]{1,0:T(8,128)(2,1)S(1)} %get-tuple-element.52), channel_id=1, source_target_pairs={{8,16},{16,8},{24,32},{32,24},{40,48},{48,40},{56,64},{64,56},{72,... | collective-permute-start | bytes 24584 | tf_op jit(solution)/shard_map/ppermute | solution.py:35
  8.8 2.3 %collective-permute-done = bf16[32,128]{1,0:T(8,128)(2,1)S(1)} collective-permute-done((bf16[32,128]{1,0:T(8,128)(2,1)S(1)}, bf16[32,128]{1,0:T(8,128)(2,1)S(1)}, u32[]{:S(2)}, u32[]{:S(2)}) %collective-permute-start) | collective-permute-done | bytes 8224 | tf_op jit(solution)/shard_map/ppermute | solution.py:35
  11.2 2.5 %collective-permute-start.3 = (bf16[18,128]{1,0:T(8,128)(2,1)S(1)}, bf16[18,128]{1,0:T(8,128)(2,1)S(1)}, u32[]{:S(2)}, u32[]{:S(2)}) collective-permute-start(bf16[18,128]{1,0:T(8,128)(2,1)S(1)} %get-tuple-element.67), channel_id=1, source_target_pairs={{0,1},{1,0},{2,3},{3,2},{4,5},{5,4},{6,7},{7,6},{8,9},{9,8},{10,11... | collective-permute-start | bytes 13832 | tf_op jit(solution)/shard_map/ppermute | solution.py:35
  13.6 5.4 %collective-permute-start.2 = (bf16[18,128]{1,0:T(8,128)(2,1)S(1)}, bf16[18,128]{1,0:T(8,128)(2,1)S(1)}, u32[]{:S(2)}, u32[]{:S(2)}) collective-permute-start(bf16[18,128]{1,0:T(8,128)(2,1)S(1)} %get-tuple-element.68), channel_id=1, source_target_pairs={{1,2},{2,1},{3,4},{4,3},{5,6},{6,5},{9,10},{10,9},{11,12},{12,11},... | collective-permute-start | bytes 13832 | tf_op jit(solution)/shard_map/ppermute | solution.py:35
  20.6 3.3 %collective-permute-start.15 = (bf16[512,256]{1,0:T(8,128)(2,1)}, bf16[512,256]{1,0:T(8,128)(2,1)S(1)}, u32[]{:S(2)}, u32[]{:S(2)}) collective-permute-start(bf16[512,256]{1,0:T(8,128)(2,1)} %bitcast.122), channel_id=1, source_target_pairs={{8,16},{16,8},{24,32},{32,24},{40,48},{48,40},{56,64},{64,56},{72,... | collective-permute-start | bytes 786440 | tf_op jit(solution)/shard_map/ppermute | solution.py:35
  25.9 2.1 %copy.21 = bf16[3,3,128,256]{3,2,1,0:T(8,128)(2,1)} copy(bf16[3,3,128,256]{2,3,1,0:T(8,128)(2,1)} %bitcast.106) | data formatting | bytes 1179648 | tf_op jit(solution)/shard_map/transpose | solution.py:342
  29.4 1.8 %collective-permute-start.11 = (bf16[512,256]{1,0:T(8,128)(2,1)S(1)}, bf16[512,256]{1,0:T(8,128)(2,1)S(1)}, u32[]{:S(2)}, u32[]{:S(2)}) collective-permute-start(bf16[512,256]{1,0:T(8,128)(2,1)S(1)} %collective-permute-done.9.refs_6_), channel_id=1, source_target_pairs={{0,2},{2,0},{1,3},{3,1},{4,6},{6,4},{5,7},{7,5},{8,10},{10,8},{9,1... | collective-permute-start | bytes 786440 | tf_op jit(solution)/shard_map/ppermute | solution.py:35
  32.5 3.4 %collective-permute-start.17 = (bf16[512,256]{1,0:T(8,128)(2,1)S(1)}, bf16[512,256]{1,0:T(8,128)(2,1)S(1)}, u32[]{:S(2)}, u32[]{:S(2)}) collective-permute-start(bf16[512,256]{1,0:T(8,128)(2,1)S(1)} %collective-permute-done.5.refs_2_), channel_id=1, source_target_pairs={{8,16},{16,8},{24,32},{32,24},{40,48},{48,40},{56,64},{64,56},{72,... | collective-permute-start | bytes 786440 | tf_op jit(solution)/shard_map/ppermute | solution.py:35
  41.2 2.8 %collective-permute-done.17.refs_14_ = bf16[512,256]{1,0:T(8,128)(2,1)S(1)} collective-permute-done((bf16[512,256]{1,0:T(8,128)(2,1)S(1)}, bf16[512,256]{1,0:T(8,128)(2,1)S(1)}, u32[]{:S(2)}, u32[]{:S(2)}) %collective-permute-start.17) | collective-permute-done | bytes 262176 | tf_op jit(solution)/shard_map/ppermute | solution.py:35
  46.0 2.8 %shard_map.136 = (bf16[576,384]{1,0:T(8,128)(2,1)}, f32[512,256]{1,0:T(8,128)}, bf16[512,256]{1,0:T(8,128)(2,1)}) custom-call(bf16[512,256]{1,0:T(8,128)(2,1)} %bitcast.124, bf16[512,128]{1,0:T(8,128)(2,1)} %bitcast.115, bf16[32,128]{1,0:T(8,128)(2,1)} %copy-done.10, bf16[32,128]{1,0:T(8,128)(2,1)} %copy-done.9, bf16[18,128]{1,0:T(8,128)(2,1)} %get-tuple-element.66.west, ...), custom_call_target="tpu_custom_call" | custom-call | flops 1000000000 | bytes 3333333 | tf_op jit(solution)/shard_map/pallas_call | solution.py:345
  49.9 10.1 %shard_map.137 = (bf16[4,768,256]{2,1,0:T(8,128)(2,1)}, bf16[512,256]{1,0:T(8,128)(2,1)}, bf16[512,256]{1,0:T(8,128)(2,1)}, bf16[1536,128]{1,0:T(8,128)(2,1)}, f32[1536,128]{1,0:T(8,128)}) custom-call(s32[8]{0:T(128)} %concatenate.15.info, bf16[512,256]{1,0:T(8,128)(2,1)} %get-tuple-element.19.flipped, bf16[512,256]{1,0:T(8,128)(2,1)} %bitcast.117, ...), custom_call_target="tpu_custom_call" | custom-call | flops 3000000000 | bytes 10000000 | tf_op jit(solution)/shard_map/pallas_call | solution.py:360
  60.7 3.5 %collective-permute-start.21 = (bf16[32,256]{1,0:T(8,128)(2,1)S(1)}, bf16[32,256]{1,0:T(8,128)(2,1)S(1)}, u32[]{:S(2)}, u32[]{:S(2)}) collective-permute-start(bf16[32,256]{1,0:T(8,128)(2,1)S(1)} %get-tuple-element.48), channel_id=1, source_target_pairs={{8,16},{16,8},{24,32},{32,24},{40,48},{48,40},{56,64},{64,56},{72,... | collective-permute-start | bytes 49160 | tf_op jit(solution)/shard_map/ppermute | solution.py:35
  64.2 8.3 %shard_map.139 = (f32[512,256]{1,0:T(8,128)}, bf16[9,512,256]{2,1,0:T(8,128)(2,1)}, bf16[6,512,256]{2,1,0:T(8,128)(2,1)}) custom-call(s32[8]{0:T(128)} %concatenate.15.info, bf16[512,256]{1,0:T(8,128)(2,1)} %bitcast.125, bf16[512,256]{1,0:T(8,128)(2,1)} %get-tuple-element.23.context_grad, bf16[512,256]{1,0:T(8,128)(2,1)} %bitcast.110, ...), custom_call_target="tpu_custom_call" | custom-call | flops 3000000000 | bytes 10000000 | tf_op jit(solution)/shard_map/pallas_call | solution.py:378
  74.2 2.2 %convert.2 = f32[3,3,512,256]{3,2,1,0:T(8,128)S(1)} convert(bf16[3,3,512,256]{3,2,1,0:T(8,128)(2,1)} %bitcast.102) | non-fusion elementwise | flops 1179648 | bytes 7077888 | tf_op jit(solution)/shard_map/convert_element_type | solution.py:390
  78.7 4.9 %collective-permute-start.36 = (bf16[384,128]{1,0:T(8,128)(2,1)S(1)}, bf16[384,128]{1,0:T(8,128)(2,1)S(1)}, u32[]{:S(2)}, u32[]{:S(2)}) collective-permute-start(bf16[384,128]{1,0:T(8,128)(2,1)S(1)} %get-tuple-element.42), channel_id=1, source_target_pairs={{0,4},{1,5},{2,6},{3,7},{4,0},{5,1},{6,2},{7,3},{8,12},{9,13},{10,... | collective-permute-start | bytes 294920 | tf_op jit(solution)/shard_map/ppermute | solution.py:25
  84.0 2.4 %collective-permute-done.36 = bf16[384,128]{1,0:T(8,128)(2,1)S(1)} collective-permute-done((bf16[384,128]{1,0:T(8,128)(2,1)S(1)}, bf16[384,128]{1,0:T(8,128)(2,1)S(1)}, u32[]{:S(2)}, u32[]{:S(2)}) %collective-permute-start.36) | collective-permute-done | bytes 98336 | tf_op jit(solution)/shard_map/ppermute | solution.py:25
  87.5 3.6 %collective-permute-start.40 = (bf16[384,128]{1,0:T(8,128)(2,1)S(1)}, bf16[384,128]{1,0:T(8,128)(2,1)S(1)}, u32[]{:S(2)}, u32[]{:S(2)}) collective-permute-start(bf16[384,128]{1,0:T(8,128)(2,1)S(1)} %add_convert_fusion.2), channel_id=1, source_target_pairs={{0,24},{8,16},{16,8},{24,0},{32,56},{40,48},{48,40},{56,32},{64,88... | collective-permute-start | bytes 294920 | tf_op jit(solution)/shard_map/ppermute | solution.py:25
  91.7 2.1 %collective-permute-start.24 = (bf16[18,256]{1,0:T(8,128)(2,1)S(1)}, bf16[18,256]{1,0:T(8,128)(2,1)S(1)}, u32[]{:S(2)}, u32[]{:S(2)}) collective-permute-start(bf16[18,256]{1,0:T(8,128)(2,1)S(1)} %get-tuple-element.57), channel_id=1, source_target_pairs={{0,1},{1,0},{2,3},{3,2},{4,5},{5,4},{6,7},{7,6},{8,9},{9,8},{10,11... | collective-permute-start | bytes 27656 | tf_op jit(solution)/shard_map/ppermute | solution.py:35
  93.9 2.2 %collective-permute-done.39 = bf16[384,128]{1,0:T(8,128)(2,1)S(1)} collective-permute-done((bf16[384,128]{1,0:T(8,128)(2,1)S(1)}, bf16[384,128]{1,0:T(8,128)(2,1)S(1)}, u32[]{:S(2)}, u32[]{:S(2)}) %collective-permute-start.39) | collective-permute-done | bytes 98336 | tf_op jit(solution)/shard_map/ppermute | solution.py:25
  100.0 2.3 %collective-permute-start.26 = (bf16[512,256]{1,0:T(8,128)(2,1)S(1)}, bf16[512,256]{1,0:T(8,128)(2,1)S(1)}, u32[]{:S(2)}, u32[]{:S(2)}) collective-permute-start(bf16[512,256]{1,0:T(8,128)(2,1)S(1)} %get-tuple-element.36), channel_id=1, source_target_pairs={{0,2},{2,0},{1,3},{3,1},{4,6},{6,4},{5,7},{7,5},{8,10},{10,8},{9,1... | collective-permute-start | bytes 786440 | tf_op jit(solution)/shard_map/ppermute | solution.py:35
  103.0 3.8 %collective-permute-start.28 = (bf16[512,256]{1,0:T(8,128)(2,1)S(1)}, bf16[512,256]{1,0:T(8,128)(2,1)S(1)}, u32[]{:S(2)}, u32[]{:S(2)}) collective-permute-start(bf16[512,256]{1,0:T(8,128)(2,1)S(1)} %get-tuple-element.39), channel_id=1, source_target_pairs={{8,16},{16,8},{24,32},{32,24},{40,48},{48,40},{56,64},{64,56},{72,... | collective-permute-start | bytes 786440 | tf_op jit(solution)/shard_map/ppermute | solution.py:35
  106.9 3.7 %collective-permute-start.44 = (bf16[384,128]{1,0:T(8,128)(2,1)S(1)}, bf16[384,128]{1,0:T(8,128)(2,1)S(1)}, u32[]{:S(2)}, u32[]{:S(2)}) collective-permute-start(bf16[384,128]{1,0:T(8,128)(2,1)S(1)} %add_convert_fusion.refs_0_), channel_id=1, source_target_pairs={{0,2},{1,3},{2,0},{3,1},{4,6},{5,7},{6,4},{7,5},{8,10},{9,11},{10,... | collective-permute-start | bytes 294920 | tf_op jit(solution)/shard_map/ppermute | solution.py:25
  110.6 2.0 %collective-permute-done.44.refs_1_ = bf16[384,128]{1,0:T(8,128)(2,1)S(1)} collective-permute-done((bf16[384,128]{1,0:T(8,128)(2,1)S(1)}, bf16[384,128]{1,0:T(8,128)(2,1)S(1)}, u32[]{:S(2)}, u32[]{:S(2)}) %collective-permute-start.44) | collective-permute-done | bytes 98336 | tf_op jit(solution)/shard_map/ppermute | solution.py:25
  112.6 3.4 %collective-permute-start.45 = (bf16[384,128]{1,0:T(8,128)(2,1)S(1)}, bf16[384,128]{1,0:T(8,128)(2,1)S(1)}, u32[]{:S(2)}, u32[]{:S(2)}) collective-permute-start(bf16[384,128]{1,0:T(8,128)(2,1)S(1)} %add_convert_fusion.refs_0_), channel_id=1, source_target_pairs={{0,4},{1,5},{2,6},{3,7},{4,0},{5,1},{6,2},{7,3},{8,12},{9,13},{10,... | collective-permute-start | bytes 294920 | tf_op jit(solution)/shard_map/ppermute | solution.py:25
  116.0 2.4 %collective-permute-done.45.refs_2_ = bf16[384,128]{1,0:T(8,128)(2,1)S(1)} collective-permute-done((bf16[384,128]{1,0:T(8,128)(2,1)S(1)}, bf16[384,128]{1,0:T(8,128)(2,1)S(1)}, u32[]{:S(2)}, u32[]{:S(2)}) %collective-permute-start.45) | collective-permute-done | bytes 98336 | tf_op jit(solution)/shard_map/ppermute | solution.py:25
  118.4 9.6 %collective-permute-start.23 = (bf16[18,256]{1,0:T(8,128)(2,1)S(1)}, bf16[18,256]{1,0:T(8,128)(2,1)S(1)}, u32[]{:S(2)}, u32[]{:S(2)}) collective-permute-start(bf16[18,256]{1,0:T(8,128)(2,1)S(1)} %get-tuple-element.58), channel_id=1, source_target_pairs={{1,2},{2,1},{3,4},{4,3},{5,6},{6,5},{9,10},{10,9},{11,12},{12,11},... | collective-permute-start | bytes 27656 | tf_op jit(solution)/shard_map/ppermute | solution.py:35
  130.2 2.7 %collective-permute-done.46.refs_3_ = bf16[384,128]{1,0:T(8,128)(2,1)} collective-permute-done((bf16[384,128]{1,0:T(8,128)(2,1)S(1)}, bf16[384,128]{1,0:T(8,128)(2,1)}, u32[]{:S(2)}, u32[]{:S(2)}) %collective-permute-start.46) | collective-permute-done | bytes 98336 | tf_op jit(solution)/shard_map/ppermute | solution.py:25
  134.2 3.2 %collective-permute-start.31 = (bf16[512,256]{1,0:T(8,128)(2,1)}, bf16[512,256]{1,0:T(8,128)(2,1)}, u32[]{:S(2)}, u32[]{:S(2)}) collective-permute-start(bf16[512,256]{1,0:T(8,128)(2,1)} %get-tuple-element.34), channel_id=1, source_target_pairs={{8,16},{16,8},{24,32},{32,24},{40,48},{48,40},{56,64},{64,56},{72,... | collective-permute-start | bytes 786440 | tf_op jit(solution)/shard_map/ppermute | solution.py:35
  137.4 2.4 %collective-permute-start.29 = (bf16[512,256]{1,0:T(8,128)(2,1)}, bf16[512,256]{1,0:T(8,128)(2,1)}, u32[]{:S(2)}, u32[]{:S(2)}) collective-permute-start(bf16[512,256]{1,0:T(8,128)(2,1)} %get-tuple-element.35), channel_id=1, source_target_pairs={{0,2},{2,0},{1,3},{3,1},{4,6},{6,4},{5,7},{7,5},{8,10},{10,8},{9,1... | collective-permute-start | bytes 786440 | tf_op jit(solution)/shard_map/ppermute | solution.py:35
  140.4 2.7 %shard_map.138 = bf16[512,128]{1,0:T(8,128)(2,1)} custom-call(bf16[512,256]{1,0:T(8,128)(2,1)} %get-tuple-element.22.motion, bf16[32,256]{1,0:T(8,128)(2,1)} %copy-done.8, bf16[32,256]{1,0:T(8,128)(2,1)} %copy-done.7, bf16[18,256]{1,0:T(8,128)(2,1)} %get-tuple-element.56.west, bf16[18,256]{1,0:T(8,128)(2,1)} %get-tuple-element.55.east, ...), custom_call_target="tpu_custom_call" | custom-call | flops 1000000000 | bytes 3333333 | tf_op jit(solution)/shard_map/pallas_call | solution.py:404
  143.1 2.5 %shard_map.140 = (f32[2304,128]{1,0:T(8,128)}, f32[324,256]{1,0:T(8,128)}) custom-call(s32[8]{0:T(128)} %concatenate.15.info, bf16[384,128]{1,0:T(8,128)(2,1)} %copy-done.1, bf16[384,128]{1,0:T(8,128)(2,1)} %copy-done.2, bf16[384,128]{1,0:T(8,128)(2,1)} %copy-done.3, bf16[384,128]{1,0:T(8,128)(2,1)} %collective-permute-done.46.refs_3_, ...), custom_call_target="tpu_custom_call" | custom-call | tf_op jit(solution)/shard_map/pallas_call | solution.py:415
  146.9 2.1 %fusion.20 = f32[512,256]{1,0:T(8,128)} fusion(f32[3,2,512,256]{3,2,1,0:T(8,128)S(1)} %convert.3, f32[3,3,512,256]{3,2,1,0:T(8,128)S(1)} %convert.2, bf16[512,256]{1,0:T(8,128)(2,1)} %collective-permute-done.33, bf16[512,256]{1,0:T(8,128)(2,1)} %collective-permute-done.31, bf16[512,256]{1,0:T(8,128)(2,1)} %collective-permute-done.29, ...), kind=kLoop, calls=%fused_computation.30 | loop fusion | flops 1179648 | bytes 2621440 | tf_op jit(solution)/shard_map/add | solution.py:403
  (169 shorter events, 34.5 us)
Async XLA Ops:
  0.6 23.3 %collective-permute-start.5 = (bf16[512,256]{1,0:T(8,128)(2,1)}, bf16[512,256]{1,0:T(8,128)(2,1)S(1)}, u32[]{:S(2)}, u32[]{:S(2)}) collective-permute-start(bf16[512,256]{1,0:T(8,128)(2,1)} %bitcast.118), channel_id=1, source_target_pairs={{0,2},{2,0},{1,3},{3,1},{4,6},{6,4},{5,7},{7,5},{8,10},{10,8},{9,1... | collective-permute-start | bytes 786440 | tf_op jit(solution)/shard_map/ppermute | solution.py:35
  1.9 22.1 %collective-permute-start.7 = (bf16[512,256]{1,0:T(8,128)(2,1)}, bf16[512,256]{1,0:T(8,128)(2,1)S(1)}, u32[]{:S(2)}, u32[]{:S(2)}) collective-permute-start(bf16[512,256]{1,0:T(8,128)(2,1)} %bitcast.119), channel_id=1, source_target_pairs={{2,4},{4,2},{3,5},{5,3},{10,12},{12,10},{11,13},{13,11},{18,20},{2... | collective-permute-start | bytes 786440 | tf_op jit(solution)/shard_map/ppermute | solution.py:35
  11.2 8.0 %collective-permute-start.3 = (bf16[18,128]{1,0:T(8,128)(2,1)S(1)}, bf16[18,128]{1,0:T(8,128)(2,1)S(1)}, u32[]{:S(2)}, u32[]{:S(2)}) collective-permute-start(bf16[18,128]{1,0:T(8,128)(2,1)S(1)} %get-tuple-element.67), channel_id=1, source_target_pairs={{0,1},{1,0},{2,3},{3,2},{4,5},{5,4},{6,7},{7,6},{8,9},{9,8},{10,11... | collective-permute-start | bytes 13832 | tf_op jit(solution)/shard_map/ppermute | solution.py:35
  19.1 10.1 %collective-permute-start.9 = (bf16[512,256]{1,0:T(8,128)(2,1)}, bf16[512,256]{1,0:T(8,128)(2,1)S(1)}, u32[]{:S(2)}, u32[]{:S(2)}) collective-permute-start(bf16[512,256]{1,0:T(8,128)(2,1)} %bitcast.120), channel_id=1, source_target_pairs={{0,8},{8,0},{16,24},{24,16},{32,40},{40,32},{48,56},{56,48},{64,72... | collective-permute-start | bytes 786440 | tf_op jit(solution)/shard_map/ppermute | solution.py:35
  19.2 10.2 %collective-permute-start.4 = (bf16[512,256]{1,0:T(8,128)(2,1)}, bf16[512,256]{1,0:T(8,128)(2,1)S(1)}, u32[]{:S(2)}, u32[]{:S(2)}) collective-permute-start(bf16[512,256]{1,0:T(8,128)(2,1)} %bitcast.121), channel_id=1, source_target_pairs={{0,1},{1,0},{2,3},{3,2},{4,5},{5,4},{6,7},{7,6},{8,9},{9,8},{10,11... | collective-permute-start | bytes 786440 | tf_op jit(solution)/shard_map/ppermute | solution.py:25
  20.6 11.9 %collective-permute-start.15 = (bf16[512,256]{1,0:T(8,128)(2,1)}, bf16[512,256]{1,0:T(8,128)(2,1)S(1)}, u32[]{:S(2)}, u32[]{:S(2)}) collective-permute-start(bf16[512,256]{1,0:T(8,128)(2,1)} %bitcast.122), channel_id=1, source_target_pairs={{8,16},{16,8},{24,32},{32,24},{40,48},{48,40},{56,64},{64,56},{72,... | collective-permute-start | bytes 786440 | tf_op jit(solution)/shard_map/ppermute | solution.py:35
  24.0 8.5 %collective-permute-start.6 = (bf16[512,256]{1,0:T(8,128)(2,1)S(1)}, bf16[512,256]{1,0:T(8,128)(2,1)S(1)}, u32[]{:S(2)}, u32[]{:S(2)}) collective-permute-start(bf16[512,256]{1,0:T(8,128)(2,1)S(1)} %collective-permute-done.5.refs_2_), channel_id=1, source_target_pairs={{0,1},{1,0},{2,3},{3,2},{4,5},{5,4},{6,7},{7,6},{8,9},{9,8},{10,11... | collective-permute-start | bytes 786440 | tf_op jit(solution)/shard_map/ppermute | solution.py:25
  24.1 11.8 %collective-permute-start.8 = (bf16[512,256]{1,0:T(8,128)(2,1)S(1)}, bf16[512,256]{1,0:T(8,128)(2,1)S(1)}, u32[]{:S(2)}, u32[]{:S(2)}) collective-permute-start(bf16[512,256]{1,0:T(8,128)(2,1)S(1)} %collective-permute-done.7.refs_4_), channel_id=1, source_target_pairs={{0,1},{1,0},{2,3},{3,2},{4,5},{5,4},{6,7},{7,6},{8,9},{9,8},{10,11... | collective-permute-start | bytes 786440 | tf_op jit(solution)/shard_map/ppermute | solution.py:25
  29.2 8.9 %collective-permute-start.10 = (bf16[512,256]{1,0:T(8,128)(2,1)S(1)}, bf16[512,256]{1,0:T(8,128)(2,1)S(1)}, u32[]{:S(2)}, u32[]{:S(2)}) collective-permute-start(bf16[512,256]{1,0:T(8,128)(2,1)S(1)} %collective-permute-done.9.refs_6_), channel_id=1, source_target_pairs={{0,1},{1,0},{2,3},{3,2},{4,5},{5,4},{6,7},{7,6},{8,9},{9,8},{10,11... | collective-permute-start | bytes 786440 | tf_op jit(solution)/shard_map/ppermute | solution.py:25
  29.4 9.4 %collective-permute-start.11 = (bf16[512,256]{1,0:T(8,128)(2,1)S(1)}, bf16[512,256]{1,0:T(8,128)(2,1)S(1)}, u32[]{:S(2)}, u32[]{:S(2)}) collective-permute-start(bf16[512,256]{1,0:T(8,128)(2,1)S(1)} %collective-permute-done.9.refs_6_), channel_id=1, source_target_pairs={{0,2},{2,0},{1,3},{3,1},{4,6},{6,4},{5,7},{7,5},{8,10},{10,8},{9,1... | collective-permute-start | bytes 786440 | tf_op jit(solution)/shard_map/ppermute | solution.py:35
  32.5 7.5 %collective-permute-start.13 = (bf16[512,256]{1,0:T(8,128)(2,1)S(1)}, bf16[512,256]{1,0:T(8,128)(2,1)S(1)}, u32[]{:S(2)}, u32[]{:S(2)}) collective-permute-start(bf16[512,256]{1,0:T(8,128)(2,1)S(1)} %collective-permute-done.7.refs_4_), channel_id=1, source_target_pairs={{0,8},{8,0},{16,24},{24,16},{32,40},{40,32},{48,56},{56,48},{64,72... | collective-permute-start | bytes 786440 | tf_op jit(solution)/shard_map/ppermute | solution.py:35
  32.5 11.5 %collective-permute-start.17 = (bf16[512,256]{1,0:T(8,128)(2,1)S(1)}, bf16[512,256]{1,0:T(8,128)(2,1)S(1)}, u32[]{:S(2)}, u32[]{:S(2)}) collective-permute-start(bf16[512,256]{1,0:T(8,128)(2,1)S(1)} %collective-permute-done.5.refs_2_), channel_id=1, source_target_pairs={{8,16},{16,8},{24,32},{32,24},{40,48},{48,40},{56,64},{64,56},{72,... | collective-permute-start | bytes 786440 | tf_op jit(solution)/shard_map/ppermute | solution.py:35
  35.9 9.3 %collective-permute-start.19 = (bf16[512,256]{1,0:T(8,128)(2,1)S(1)}, bf16[512,256]{1,0:T(8,128)(2,1)S(1)}, u32[]{:S(2)}, u32[]{:S(2)}) collective-permute-start(bf16[512,256]{1,0:T(8,128)(2,1)S(1)} %collective-permute-done.15.refs_12_), channel_id=1, source_target_pairs={{2,4},{4,2},{3,5},{5,3},{10,12},{12,10},{11,13},{13,11},{18,20},{2... | collective-permute-start | bytes 786440 | tf_op jit(solution)/shard_map/ppermute | solution.py:35
  38.2 10.6 %collective-permute-start.16 = (bf16[512,256]{1,0:T(8,128)(2,1)S(1)}, bf16[512,256]{1,0:T(8,128)(2,1)S(1)}, u32[]{:S(2)}, u32[]{:S(2)}) collective-permute-start(bf16[512,256]{1,0:T(8,128)(2,1)S(1)} %collective-permute-done.15.refs_12_), channel_id=1, source_target_pairs={{0,1},{1,0},{2,3},{3,2},{4,5},{5,4},{6,7},{7,6},{8,9},{9,8},{10,11... | collective-permute-start | bytes 786440 | tf_op jit(solution)/shard_map/ppermute | solution.py:25
  38.8 10.0 %collective-permute-start.12 = (bf16[512,256]{1,0:T(8,128)(2,1)S(1)}, bf16[512,256]{1,0:T(8,128)(2,1)S(1)}, u32[]{:S(2)}, u32[]{:S(2)}) collective-permute-start(bf16[512,256]{1,0:T(8,128)(2,1)S(1)} %collective-permute-done.11.refs_8_), channel_id=1, source_target_pairs={{0,1},{1,0},{2,3},{3,2},{4,5},{5,4},{6,7},{7,6},{8,9},{9,8},{10,11... | collective-permute-start | bytes 786440 | tf_op jit(solution)/shard_map/ppermute | solution.py:25
  40.0 8.8 %collective-permute-start.14 = (bf16[512,256]{1,0:T(8,128)(2,1)S(1)}, bf16[512,256]{1,0:T(8,128)(2,1)S(1)}, u32[]{:S(2)}, u32[]{:S(2)}) collective-permute-start(bf16[512,256]{1,0:T(8,128)(2,1)S(1)} %collective-permute-done.13.refs_10_), channel_id=1, source_target_pairs={{0,1},{1,0},{2,3},{3,2},{4,5},{5,4},{6,7},{7,6},{8,9},{9,8},{10,11... | collective-permute-start | bytes 786440 | tf_op jit(solution)/shard_map/ppermute | solution.py:25
  60.7 15.8 %collective-permute-start.22 = (bf16[32,256]{1,0:T(8,128)(2,1)S(1)}, bf16[32,256]{1,0:T(8,128)(2,1)S(1)}, u32[]{:S(2)}, u32[]{:S(2)}) collective-permute-start(bf16[32,256]{1,0:T(8,128)(2,1)S(1)} %get-tuple-element.47), channel_id=1, source_target_pairs={{0,8},{8,0},{16,24},{24,16},{32,40},{40,32},{48,56},{56,48},{64,72... | collective-permute-start | bytes 49160 | tf_op jit(solution)/shard_map/ppermute | solution.py:35
  60.7 15.8 %collective-permute-start.21 = (bf16[32,256]{1,0:T(8,128)(2,1)S(1)}, bf16[32,256]{1,0:T(8,128)(2,1)S(1)}, u32[]{:S(2)}, u32[]{:S(2)}) collective-permute-start(bf16[32,256]{1,0:T(8,128)(2,1)S(1)} %get-tuple-element.48), channel_id=1, source_target_pairs={{8,16},{16,8},{24,32},{32,24},{40,48},{48,40},{56,64},{64,56},{72,... | collective-permute-start | bytes 49160 | tf_op jit(solution)/shard_map/ppermute | solution.py:35
  73.5 25.9 %collective-permute-start.25 = (bf16[6,512,256]{2,1,0:T(8,128)(2,1)}, bf16[6,512,256]{2,1,0:T(8,128)(2,1)S(1)}, u32[]{:S(2)}, u32[]{:S(2)}) collective-permute-start(bf16[6,512,256]{2,1,0:T(8,128)(2,1)} %get-tuple-element.27), channel_id=1, source_target_pairs={{0,1},{1,0},{2,3},{3,2},{4,5},{5,4},{6,7},{7,6},{8,9},{9,8},{10,11... | collective-permute-start | bytes 4718600 | tf_op jit(solution)/shard_map/ppermute | solution.py:25
  78.7 7.7 %collective-permute-start.36 = (bf16[384,128]{1,0:T(8,128)(2,1)S(1)}, bf16[384,128]{1,0:T(8,128)(2,1)S(1)}, u32[]{:S(2)}, u32[]{:S(2)}) collective-permute-start(bf16[384,128]{1,0:T(8,128)(2,1)S(1)} %get-tuple-element.42), channel_id=1, source_target_pairs={{0,4},{1,5},{2,6},{3,7},{4,0},{5,1},{6,2},{7,3},{8,12},{9,13},{10,... | collective-permute-start | bytes 294920 | tf_op jit(solution)/shard_map/ppermute | solution.py:25
  91.7 15.1 %collective-permute-start.24 = (bf16[18,256]{1,0:T(8,128)(2,1)S(1)}, bf16[18,256]{1,0:T(8,128)(2,1)S(1)}, u32[]{:S(2)}, u32[]{:S(2)}) collective-permute-start(bf16[18,256]{1,0:T(8,128)(2,1)S(1)} %get-tuple-element.57), channel_id=1, source_target_pairs={{0,1},{1,0},{2,3},{3,2},{4,5},{5,4},{6,7},{7,6},{8,9},{9,8},{10,11... | collective-permute-start | bytes 27656 | tf_op jit(solution)/shard_map/ppermute | solution.py:35
  100.0 28.0 %collective-permute-start.26 = (bf16[512,256]{1,0:T(8,128)(2,1)S(1)}, bf16[512,256]{1,0:T(8,128)(2,1)S(1)}, u32[]{:S(2)}, u32[]{:S(2)}) collective-permute-start(bf16[512,256]{1,0:T(8,128)(2,1)S(1)} %get-tuple-element.36), channel_id=1, source_target_pairs={{0,2},{2,0},{1,3},{3,1},{4,6},{6,4},{5,7},{7,5},{8,10},{10,8},{9,1... | collective-permute-start | bytes 786440 | tf_op jit(solution)/shard_map/ppermute | solution.py:35
  102.3 25.8 %collective-permute-start.32 = (bf16[512,256]{1,0:T(8,128)(2,1)S(1)}, bf16[512,256]{1,0:T(8,128)(2,1)S(1)}, u32[]{:S(2)}, u32[]{:S(2)}) collective-permute-start(bf16[512,256]{1,0:T(8,128)(2,1)S(1)} %get-tuple-element.37), channel_id=1, source_target_pairs={{0,8},{8,0},{16,24},{24,16},{32,40},{40,32},{48,56},{56,48},{64,72... | collective-permute-start | bytes 786440 | tf_op jit(solution)/shard_map/ppermute | solution.py:35
  102.3 26.2 %collective-permute-start.30 = (bf16[512,256]{1,0:T(8,128)(2,1)S(1)}, bf16[512,256]{1,0:T(8,128)(2,1)S(1)}, u32[]{:S(2)}, u32[]{:S(2)}) collective-permute-start(bf16[512,256]{1,0:T(8,128)(2,1)S(1)} %get-tuple-element.38), channel_id=1, source_target_pairs={{2,4},{4,2},{3,5},{5,3},{10,12},{12,10},{11,13},{13,11},{18,20},{2... | collective-permute-start | bytes 786440 | tf_op jit(solution)/shard_map/ppermute | solution.py:35
  103.0 25.7 %collective-permute-start.28 = (bf16[512,256]{1,0:T(8,128)(2,1)S(1)}, bf16[512,256]{1,0:T(8,128)(2,1)S(1)}, u32[]{:S(2)}, u32[]{:S(2)}) collective-permute-start(bf16[512,256]{1,0:T(8,128)(2,1)S(1)} %get-tuple-element.39), channel_id=1, source_target_pairs={{8,16},{16,8},{24,32},{32,24},{40,48},{48,40},{56,64},{64,56},{72,... | collective-permute-start | bytes 786440 | tf_op jit(solution)/shard_map/ppermute | solution.py:35
  118.4 14.5 %collective-permute-start.23 = (bf16[18,256]{1,0:T(8,128)(2,1)S(1)}, bf16[18,256]{1,0:T(8,128)(2,1)S(1)}, u32[]{:S(2)}, u32[]{:S(2)}) collective-permute-start(bf16[18,256]{1,0:T(8,128)(2,1)S(1)} %get-tuple-element.58), channel_id=1, source_target_pairs={{1,2},{2,1},{3,4},{4,3},{5,6},{6,5},{9,10},{10,9},{11,12},{12,11},... | collective-permute-start | bytes 27656 | tf_op jit(solution)/shard_map/ppermute | solution.py:35
  128.4 9.0 %collective-permute-start.48 = (bf16[384,128]{1,0:T(8,128)(2,1)S(1)}, bf16[384,128]{1,0:T(8,128)(2,1)S(1)}, u32[]{:S(2)}, u32[]{:S(2)}) collective-permute-start(bf16[384,128]{1,0:T(8,128)(2,1)S(1)} %collective-permute-done.44.refs_1_), channel_id=1, source_target_pairs={{0,1},{1,0},{2,3},{3,2},{4,5},{5,4},{6,7},{7,6},{8,9},{9,8},{10,11... | collective-permute-start | bytes 294920 | tf_op jit(solution)/shard_map/ppermute | solution.py:25
  128.7 11.1 %collective-permute-start.49 = (bf16[384,128]{1,0:T(8,128)(2,1)S(1)}, bf16[384,128]{1,0:T(8,128)(2,1)S(1)}, u32[]{:S(2)}, u32[]{:S(2)}) collective-permute-start(bf16[384,128]{1,0:T(8,128)(2,1)S(1)} %collective-permute-done.45.refs_2_), channel_id=1, source_target_pairs={{0,1},{1,0},{2,3},{3,2},{4,5},{5,4},{6,7},{7,6},{8,9},{9,8},{10,11... | collective-permute-start | bytes 294920 | tf_op jit(solution)/shard_map/ppermute | solution.py:25
  132.8 10.3 %collective-permute-start.50 = (bf16[384,128]{1,0:T(8,128)(2,1)}, bf16[384,128]{1,0:T(8,128)(2,1)}, u32[]{:S(2)}, u32[]{:S(2)}) collective-permute-start(bf16[384,128]{1,0:T(8,128)(2,1)} %collective-permute-done.46.refs_3_), channel_id=1, source_target_pairs={{0,1},{1,0},{2,3},{3,2},{4,5},{5,4},{6,7},{7,6},{8,9},{9,8},{10,11... | collective-permute-start | bytes 294920 | tf_op jit(solution)/shard_map/ppermute | solution.py:25
  132.9 12.8 %collective-permute-start.33 = (bf16[512,256]{1,0:T(8,128)(2,1)}, bf16[512,256]{1,0:T(8,128)(2,1)}, u32[]{:S(2)}, u32[]{:S(2)}) collective-permute-start(bf16[512,256]{1,0:T(8,128)(2,1)} %get-tuple-element.33), channel_id=1, source_target_pairs={{2,4},{4,2},{3,5},{5,3},{10,12},{12,10},{11,13},{13,11},{18,20},{2... | collective-permute-start | bytes 786440 | tf_op jit(solution)/shard_map/ppermute | solution.py:35
  134.2 11.7 %collective-permute-start.31 = (bf16[512,256]{1,0:T(8,128)(2,1)}, bf16[512,256]{1,0:T(8,128)(2,1)}, u32[]{:S(2)}, u32[]{:S(2)}) collective-permute-start(bf16[512,256]{1,0:T(8,128)(2,1)} %get-tuple-element.34), channel_id=1, source_target_pairs={{8,16},{16,8},{24,32},{32,24},{40,48},{48,40},{56,64},{64,56},{72,... | collective-permute-start | bytes 786440 | tf_op jit(solution)/shard_map/ppermute | solution.py:35
  137.4 8.9 %collective-permute-start.29 = (bf16[512,256]{1,0:T(8,128)(2,1)}, bf16[512,256]{1,0:T(8,128)(2,1)}, u32[]{:S(2)}, u32[]{:S(2)}) collective-permute-start(bf16[512,256]{1,0:T(8,128)(2,1)} %get-tuple-element.35), channel_id=1, source_target_pairs={{0,2},{2,0},{1,3},{3,1},{4,6},{6,4},{5,7},{7,5},{8,10},{10,8},{9,1... | collective-permute-start | bytes 786440 | tf_op jit(solution)/shard_map/ppermute | solution.py:35
  (49 other events, 513.4 us)

commit v3 on v2

--- a/solution.py
+++ b/solution.py
@@ -35,31 +35,39 @@
     return lax.ppermute(array, axis, pairs)
 
 
-def rim(cells, row_even, col_even):
-    top, bottom = cells[0], cells[-1]
-    even = swap_pairs(jnp.where(row_even, bottom, top), "row", 0)
-    odd = swap_pairs(jnp.where(row_even, top, bottom), "row", 1)
+def rim(facing, away, ends, row_even, col_even):
+    even = swap_pairs(facing, "row", 0)
+    odd = swap_pairs(away, "row", 1)
     north, south = jnp.where(row_even, odd, even), jnp.where(row_even, even, odd)
-    left = jnp.concatenate([north[:1], cells[:, 0], south[:1]])
-    right = jnp.concatenate([north[-1:], cells[:, -1], south[-1:]])
+    left = jnp.concatenate([north[:1], ends[0], south[:1]])
+    right = jnp.concatenate([north[-1:], ends[1], south[-1:]])
     even = swap_pairs(jnp.where(col_even, right, left), "col", 0)
     odd = swap_pairs(jnp.where(col_even, left, right), "col", 1)
     west, east = jnp.where(col_even, odd, even), jnp.where(col_even, even, odd)
     return north, south, west, east
 
 
+def outer_columns(cells):
+    count = cells.shape[0]
+    line = lax.broadcasted_iota(jnp.int32, (32, count), 0)
+    cell = lax.broadcasted_iota(jnp.int32, (32, count), 1)
+    wanted = (line & 15) * 32 + (line >> 4) * 31
+    pick = (cell == wanted).astype(F32).astype(BF16)
+    return jnp.dot(pick, cells[...], preferred_element_type=F32).astype(BF16)
+
+
 def write_taps(taps, own, north, south, west, east, backwards):
     width = own.shape[1]
     line = north.shape[0]
-    taps[:line, width : 2 * width] = north[...]
+    taps[:line, width : 2 * width] = north
     taps[line:-line, width : 2 * width] = own[...]
-    taps[-line:, width : 2 * width] = south[...]
+    taps[-line:, width : 2 * width] = south
     middle = taps[:, width : 2 * width].astype(F32)
     place = lax.broadcasted_iota(jnp.int32, middle.shape, 0) % line
 
     def stretched(ends):
         shape = (ends.shape[0], line, width)
-        return jnp.broadcast_to(ends[...].astype(F32)[:, None], shape).reshape(middle.shape)
+        return jnp.broadcast_to(ends.astype(F32)[:, None], shape).reshape(middle.shape)
 
     left = jnp.where(place == 0, stretched(west), pltpu.roll(middle, 1, 0)).astype(BF16)
     right = jnp.where(
@@ -96,35 +104,37 @@
     )
 
 
-def early_kernel(
-    first, cotangent, north, south, west, east, back_weight, cot_taps, grad_motion, flipped
-):
+def pack_kernel(tile, cotangent, out):
+    cells = tile.shape[0]
+    out[:cells] = tile[...]
+    out[cells : cells + 32, :128] = cotangent[:32]
+    out[cells : cells + 32, 128:] = cotangent[cells - 32 :]
+    ends = outer_columns(cotangent)
+    out[cells + 32 :, :128] = ends[:16]
+    out[cells + 32 :, 128:] = ends[16:]
+
+
+def forward_kernel(info, first, context, cotangent, back_weight, corr_weight, *refs):
+    tiles, refs = refs[:18], refs[18:]
+    parts, motion, context_grad, facing, away, ends, weights_sent, weights_kept = refs[:8]
+    edges, cot_taps, taps, weight_grads, sems, edge_sems = refs[8:]
     cells = first.shape[0]
-    write_taps(cot_taps, cotangent, north, south, west, east, True)
-    total = jnp.zeros(grad_motion.shape, F32)
-    for a in range(3):
-        start = (2 - a) * 32
-        total += jnp.dot(
-            cot_taps[start : start + cells], back_weight[a], preferred_element_type=F32
-        )
-    grad_motion[...] = total
-    flip = flip_matrix()
-    for q in range(cells // GROUP):
-        at = slice(q * GROUP, (q + 1) * GROUP)
-        flipped[at] = jnp.dot(flip, first[at], preferred_element_type=F32).astype(BF16)
-
-
-def forward_kernel(info, flipped, context, cot_taps, grad_motion, corr_weight, *refs):
-    tiles, refs = refs[:18], refs[18:]
-    parts, motion, context_grad, weights_sent, weights_kept, taps, weight_grads, sems = refs
-    cells = flipped.shape[0]
     slots = parts.shape[0]
+    row_sides, chip_sides = (6, 12), (1, 3, 5)
+    options = [row_sides] * 2 + [chip_sides] * 2 + [[r + x for r in row_sides for x in chip_sides]] * 4
+    for n in range(8):
+        for t in options[n]:
+            @pl.when(info[8 + n] == t)
+            def _():
+                pltpu.make_async_copy(
+                    tiles[t].at[pl.ds(cells, 48)], edges.at[n], edge_sems.at[n]
+                ).start()
     for k in range(slots):
         for t in range(18):
             @pl.when(info[k] == t)
             def _():
                 pltpu.make_async_copy(
-                    tiles[t], parts.at[k, pl.ds(GROUP, cells)], sems.at[k]
+                    tiles[t].at[pl.ds(0, cells)], parts.at[k, pl.ds(GROUP, cells)], sems.at[k]
                 ).start()
         parts[k, :GROUP] = jnp.zeros((GROUP, parts.shape[2]), BF16)
         parts[k, GROUP + cells :] = jnp.zeros((GROUP, parts.shape[2]), BF16)
@@ -132,13 +142,39 @@
     flip = flip_matrix()
     gains = []
     for k in range(slots):
-        live = jnp.where(k < info[slots], 1.0 / math.sqrt(flipped.shape[1]), 0.0).astype(F32)
+        live = jnp.where(k < info[slots], 1.0 / math.sqrt(first.shape[1]), 0.0).astype(F32)
         gains.append(jnp.where(inside, live, 0.0))
+    for n in range(8):
+        pltpu.make_async_copy(tiles[0].at[pl.ds(cells, 48)], edges.at[n], edge_sems.at[n]).wait()
+    north, south = edges[0, :32, 128:], edges[1, :32, :128]
+    west = jnp.concatenate(
+        [
+            edges[4, :32, 128:].astype(F32)[31:],
+            edges[2, 32:, 128:].astype(F32),
+            edges[6, :32, :128].astype(F32)[31:],
+        ]
+    )
+    east = jnp.concatenate(
+        [
+            edges[5, :32, 128:].astype(F32)[:1],
+            edges[3, 32:, :128].astype(F32),
+            edges[7, :32, :128].astype(F32)[:1],
+        ]
+    )
+    write_taps(cot_taps, cotangent, north, south, west, east, True)
+    grad_motion = jnp.zeros(context_grad.shape, F32)
+    for a in range(3):
+        start = (2 - a) * 32
+        grad_motion += jnp.dot(
+            cot_taps[start : start + cells], back_weight[a], preferred_element_type=F32
+        )
     for k in range(slots):
-        pltpu.make_async_copy(tiles[0], parts.at[k, pl.ds(GROUP, cells)], sems.at[k]).wait()
+        pltpu.make_async_copy(
+            tiles[0].at[pl.ds(0, cells)], parts.at[k, pl.ds(GROUP, cells)], sems.at[k]
+        ).wait()
     for q in range(cells // GROUP):
         at = slice(q * GROUP, (q + 1) * GROUP)
-        features = flipped[at]
+        features = jnp.dot(flip, first[at], preferred_element_type=F32).astype(BF16)
         for k in range(slots):
             scores = lax.dot_general(
                 features,
@@ -161,7 +197,11 @@
     )
     sigma = jax.nn.sigmoid(pre)
     motion[...] = (pre * sigma).astype(BF16)
-    context_grad[...] = (grad_motion[...] * sigma * (1.0 + pre * (1.0 - sigma))).astype(BF16)
+    context_grad[...] = (grad_motion * sigma * (1.0 + pre * (1.0 - sigma))).astype(BF16)
+    row_odd = info[16]
+    facing[...] = motion[pl.ds(pl.multiple_of((1 - row_odd) * (cells - 32), 32), 32)]
+    away[...] = motion[pl.ds(pl.multiple_of(row_odd * (cells - 32), 32), 32)]
+    ends[...] = outer_columns(motion).reshape(ends.shape)
     over_cells = (((0,), (0,)), ((), ()))
     for a in range(3):
         start = (2 - a) * 32
@@ -233,33 +273,35 @@
 
         @pl.when(same)
         def _():
-            kept[place // 2] = value
+            kept[place % 6 // 2 * 3 + place // 6] = value
 
         @pl.when(jnp.logical_not(same))
         def _():
-            lent[place // 6 * 2 + (place % 6 > 1).astype(jnp.int32)] = value
+            lent[(place % 6 > 1).astype(jnp.int32) * 3 + place // 6] = value
 
 
 def features_kernel(motion, north, south, west, east, weight, out, taps):
     cells = out.shape[0]
-    write_taps(taps, motion, north, south, west, east, False)
+    write_taps(taps, motion, north[...], south[...], west[...], east[...], False)
     total = jnp.zeros(out.shape, F32)
     for a in range(3):
         total += jnp.dot(taps[a * 32 : a * 32 + cells], weight[a], preferred_element_type=F32)
     out[...] = total.astype(BF16)
 
 
-def finish_kernel(info, *refs):
-    shards, (conv, corr, whole) = refs[:8], refs[8:]
-    size = shards[0].shape[0]
-    core, chip = info[6], info[7]
+def finish_kernel(info, near, near_across, far, far_across, conv, corr, whole):
+    size = near.shape[0] // 2
+    core, low, high = info[6], info[7] & 1, info[7] >> 1
     half = whole.shape[0] // 2
-    for s in range(4):
-        other = chip ^ s
-        to = pl.multiple_of(core * half + other * size, size)
-        whole[pl.ds(to, size)] = shards[s][...].astype(F32)
-        to = pl.multiple_of((1 - core) * half + other * size, size)
-        whole[pl.ds(to, size)] = shards[4 + s][...].astype(F32)
+    for ref, owner, at in (
+        (near, core, low),
+        (near_across, core, 1 - low),
+        (far, 1 - core, low),
+        (far_across, 1 - core, 1 - low),
+    ):
+        for s in range(2):
+            to = owner * half + at * 2 * size + (high ^ s) * size
+            whole[pl.ds(pl.multiple_of(to, size), size)] = ref[s * size : (s + 1) * size].astype(F32)
     conv[...] = whole[: conv.shape[0]]
     base = conv.shape[0]
     for h in range(2):
@@ -278,22 +320,21 @@
     )
 
 
-def sum_weights(sent, kept):
+def sum_weights(sent, kept, chip):
     cur = kept + swap(sent, "col", 1).astype(F32)
-    size = cur.shape[0] // 4
-    chip = lax.axis_index("col") // 2
-    pieces = [
-        lax.dynamic_slice_in_dim(cur, (chip ^ s) * size, size, axis=0) for s in range(4)
-    ]
-    got = [swap(pieces[s].astype(BF16), "col", 2 * s).astype(F32) for s in (1, 2, 3)]
-    cur = (pieces[0] + got[0]) + (got[1] + got[2])
-    for unit in (1, 4):
+    for bit in (0, 1):
+        size = cur.shape[0] // 2
+        mine = (chip >> bit) & 1
+        gone = lax.dynamic_slice_in_dim(cur, (1 - mine) * size, size).astype(BF16)
+        cur = lax.dynamic_slice_in_dim(cur, mine * size, size)
+        cur = cur + swap(gone, "col", 2 << bit).astype(F32)
+    for bits in (1, 2, 4, 8):
         mine = cur.astype(BF16)
-        got = [swap(mine, "row", unit * s).astype(F32) for s in (1, 2, 3)]
-        cur = (mine.astype(F32) + got[0]) + (got[1] + got[2])
+        cur = mine.astype(F32) + swap(mine, "row", bits).astype(F32)
     mine = cur.astype(BF16)
-    shards = [mine] + [swap(mine, "col", 2 * s) for s in (1, 2, 3)]
-    return shards + [swap(shard, "col", 1) for shard in shards]
+    near = jnp.concatenate([mine, swap(mine, "col", 4)])
+    across = swap(near, "col", 2)
+    return near, across, swap(near, "col", 1), swap(across, "col", 1)
 
 
 def body(
@@ -309,16 +350,25 @@
     row_even, chip_even, col_even = row % 2 == 0, chip % 2 == 0, core == 0
 
     def role(step, even):
+        step = jnp.asarray(step)
         return jnp.where(step == 0, 0, jnp.where((step > 0) == even, 1, 2))
 
     down, across = partners[0, 0] // 5 - 1, partners[0, 0] % 5 - 2
     chip_step = (core + across) >> 1
     place = role(down, row_even) * 6 + role(chip_step, chip_even) * 2 + (across & 1)
+    north, south = role(-1, row_even) * 6, role(1, row_even) * 6
+    west = jnp.where(col_even, role(-1, chip_even), 0) * 2 + 1
+    east = jnp.where(col_even, 0, role(1, chip_even)) * 2 + 1
+    beside = [north, south, west, east, north + west, north + east, south + west, south + east]
     info = jnp.concatenate(
-        [place, counts[0], radius[0], core[None], chip[None]]
+        [place, counts[0], radius[0], jnp.stack([core, chip, *beside, row % 2])]
     ).astype(jnp.int32)
     first = frame_one.reshape(cells, channels)
-    own = frame_two.reshape(cells, channels)
+    shape = jax.ShapeDtypeStruct
+    cot = cotangent.reshape(cells, out_width)
+    own = call(pack_kernel, shape((cells + 48, channels), BF16), [VMEM] * 2)(
+        frame_two.reshape(cells, channels), cot
+    )
     tiles = {(0, 0): own}
     for r in (1, 2):
         tiles[r, 0] = swap_pairs(own, "row", r - 1)
@@ -340,41 +390,31 @@
         for lead in (LEAD, LEAD_BACK)
     )
     back_weight = conv_weight.transpose(0, 1, 3, 2).reshape(3, 3 * out_width, hidden)
-    shape = jax.ShapeDtypeStruct
     total_rows = 9 * hidden + 2 * 384
-    cot_taps, grad_motion, flipped = call(
-        early_kernel,
-        (
-            shape(((rows_tile + 2) * cols_tile, 3 * out_width), BF16),
-            shape((cells, hidden), F32),
-            shape((cells, channels), BF16),
-        ),
-        [VMEM] * 7,
-        flops=10**9,
-    )(
-        first,
-        cotangent.reshape(cells, out_width),
-        *rim(cotangent, row_even, col_even),
-        back_weight,
-    )
-    parts, motion, context_grad, weights_sent, weights_kept = call(
+    parts, motion, context_grad, facing, away, ends, weights_sent, weights_kept = call(
         forward_kernel,
         (
             shape((slots, cells + 2 * GROUP, channels), BF16),
             shape((cells, hidden), BF16),
             shape((cells, hidden), BF16),
+            shape((cols_tile, hidden), BF16),
+            shape((cols_tile, hidden), BF16),
+            shape((2, rows_tile, hidden), BF16),
             shape((total_rows // 2, 128), BF16),
             shape((total_rows // 2, 128), F32),
         ),
         [SMEM] + [VMEM] * 5 + [ANY] * 18,
         [
+            pltpu.VMEM((8, 48, channels), BF16),
+            pltpu.VMEM(((rows_tile + 2) * cols_tile, 3 * out_width), BF16),
             pltpu.VMEM((cells, slots * 128), BF16),
             pltpu.VMEM((total_rows, 128), F32),
             pltpu.SemaphoreType.DMA((slots,)),
+            pltpu.SemaphoreType.DMA((8,)),
         ],
         flops=3 * 10**9,
-    )(info, flipped, context.reshape(cells, hidden), cot_taps, grad_motion, spread, *around)
-    shards = sum_weights(weights_sent, weights_kept)
+    )(info, first, context.reshape(cells, hidden), cot, back_weight, spread, *around)
+    shards = sum_weights(weights_sent, weights_kept, chip)
     first_grad, kept, lent = call(
         backward_kernel,
         (
@@ -386,21 +426,16 @@
         [pltpu.VMEM((slots, cells + 2 * GROUP, channels), F32)],
         flops=3 * 10**9,
     )(info, first, context_grad, spread_back, parts)
-    lent = swap(lent, "col", 1).reshape(3, 2, cells, channels).astype(F32)
+    lent = swap(lent, "col", 1).reshape(2, 3, cells, channels).astype(F32)
     kept = kept.reshape(3, 3, cells, channels).astype(F32)
     side = jnp.where((core == 0) == chip_even, 1, 2)
-    sums = {}
-    for r in range(3):
-        sums[r, 0] = kept[r, 0] + lent[r, 0]
-        for x in (1, 2):
-            sums[r, x] = kept[r, x] + jnp.where(side == x, lent[r, 1], 0.0)
+    middle = kept[0] + lent[0]
+    for x in (1, 2):
+        out = kept[x] + jnp.where(side == x, lent[1], 0.0)
+        middle += swap_pairs(out.astype(BF16), "col", x - 1, 2).astype(F32)
+    second_grad = middle[0]
     for r in (1, 2):
-        sums[r, 0] += swap_pairs(sums[r, r].astype(BF16), "col", r - 1, 2).astype(F32)
-        sums[0, 3 - r] += swap_pairs(sums[r, 3 - r].astype(BF16), "row", r - 1).astype(F32)
-    second_grad = sums[0, 0]
-    for r in (1, 2):
-        second_grad += swap_pairs(sums[r, 0].astype(BF16), "row", r - 1).astype(F32)
-        second_grad += swap_pairs(sums[0, r].astype(BF16), "col", r - 1, 2).astype(F32)
+        second_grad += swap_pairs(middle[r].astype(BF16), "row", r - 1).astype(F32)
     features = call(
         features_kernel,
         shape((cells, out_width), BF16),
@@ -409,13 +444,13 @@
         flops=10**9,
     )(
         motion,
-        *rim(motion.reshape(rows_tile, cols_tile, hidden), row_even, col_even),
+        *rim(facing, away, ends, row_even, col_even),
         conv_weight.reshape(3, 3 * hidden, out_width),
     )
     conv_total, corr_total = call(
         finish_kernel,
         (shape((9 * hidden, out_width), F32), shape(corr_weight.shape, F32)),
-        [SMEM] + [VMEM] * 8,
+        [SMEM] + [VMEM] * 4,
         [pltpu.VMEM((total_rows, 128), F32)],
     )(info, *shards)
     return (

time: 151 us -> 133 us (0.88)
  starting transfers between devices: 78.4 us -> 59.1 us
  waiting for transfers between devices: 24.8 us -> 29.8 us
  other arithmetic: 9.15 us -> 6.19 us
    ppermute x24 -> x16, starting transfers between devices: 52.7 us -> 33.5 us  [swap_pairs(): return lax.ppermute(array, axis, pairs)]
    ppermute x27 -> x21, waiting for transfers between devices: 14.7 us -> 26 us  [swap(): lax.ppermute(array, axis, [(i, i ^ bits) for i in range(lax.axis_size(axi...]
    ppermute x24 -> x16, waiting for transfers between devices: 10.1 us -> 3.82 us  [swap_pairs(): return lax.ppermute(array, axis, pairs)]
    pallas_call x1, Pallas kernels: 10.1 us -> 11.8 us  [body(): call(forward_kernel, (shape((slots, cells + 2 * GROUP, channels), BF16),...]
    slice x5 -> x1, local copies, waits for them, and re-layouts: 1.71 us -> 0.01 us  [rim(): left = jnp.concatenate([north[:1], ends[0], south[:1]])]
    ppermute x27 -> x21, starting transfers between devices: 25.7 us -> 25.6 us  [swap(): lax.ppermute(array, axis, [(i, i ^ bits) for i in range(lax.axis_size(axi...]
  transfers between devices with their start and end apart: 51 -> 37, of which waited for: 16 -> 10; matrix products, arithmetic and copies ran while one was open for 9% -> 6% of each run, Pallas kernels for 11% -> 10%
where the time goes in v3:
time: 133 us; the launch traced here: 131 us
  starting transfers between devices  59.1 us (44%)
  waiting for transfers between devices  29.8 us (22%)
  Pallas kernels  27.2 us (20%)
  local copies, waits for them, and re-layouts  6.58 us (5%)
  other arithmetic  6.19 us (5%)
  between operations  2.45 us (2%)
    ppermute x16, starting transfers between devices, swap_pairs(): return lax.ppermute(array, axis, pairs)  33.5 us
    ppermute x21, waiting for transfers between devices, swap(): lax.ppermute(array, axis, [(i, i ^ bits) for i in range(lax.axis_size(axi...  26 us
    ppermute x21, starting transfers between devices, swap(): lax.ppermute(array, axis, [(i, i ^ bits) for i in range(lax.axis_size(axi...  25.6 us
    pallas_call x1, Pallas kernels, body(): call(forward_kernel, (shape((slots, cells + 2 * GROUP, channels), BF16),...  11.8 us
    pallas_call x1, Pallas kernels, body(): call(backward_kernel, (shape((cells, channels), F32), shape((9, cells, ch...  8.35 us
    ppermute x16, waiting for transfers between devices, swap_pairs(): return lax.ppermute(array, axis, pairs)  3.82 us
  transfers between devices with their start and end apart: 37, of which 10 were waited for; matrix products, arithmetic and copies ran while one was open for 6% of the time, Pallas kernels for 10%

profile of v3, /device:TPU:33, one launch (start us, length us, event | category | flops | bytes accessed | tf_op | source)
XLA Modules:
  0.0 131.3 jit_solution(8292506752043185770)
XLA Ops:
  0.6 1.9 %shard_map.136.refs_0_ = bf16[560,256]{1,0:T(8,128)(2,1)} custom-call(bf16[512,256]{1,0:T(8,128)(2,1)} %bitcast.72, bf16[512,128]{1,0:T(8,128)(2,1)} %bitcast.73), custom_call_target="tpu_custom_call" | custom-call | tf_op jit(solution)/shard_map/pallas_call | solution.py:369
  4.4 1.4 %collective-permute-start.5 = (bf16[560,256]{1,0:T(8,128)(2,1)}, bf16[560,256]{1,0:T(8,128)(2,1)S(1)}, u32[]{:S(2)}, u32[]{:S(2)}) collective-permute-start(bf16[560,256]{1,0:T(8,128)(2,1)} %shard_map.136.refs_0_), channel_id=1, source_target_pairs={{0,8},{8,0},{16,24},{24,16},{32,40},{40,32},{48,56},{56,48},{64,72... | collective-permute-start | bytes 860168 | tf_op jit(solution)/shard_map/ppermute | solution.py:35
  7.0 3.3 %collective-permute-start.11 = (bf16[560,256]{1,0:T(8,128)(2,1)}, bf16[560,256]{1,0:T(8,128)(2,1)S(1)}, u32[]{:S(2)}, u32[]{:S(2)}) collective-permute-start(bf16[560,256]{1,0:T(8,128)(2,1)} %shard_map.136.refs_0_), channel_id=1, source_target_pairs={{8,16},{16,8},{24,32},{32,24},{40,48},{48,40},{56,64},{64,56},{72,... | collective-permute-start | bytes 860168 | tf_op jit(solution)/shard_map/ppermute | solution.py:35
  10.4 1.5 %collective-permute-start.2 = (bf16[560,256]{1,0:T(8,128)(2,1)S(1)}, bf16[560,256]{1,0:T(8,128)(2,1)S(1)}, u32[]{:S(2)}, u32[]{:S(2)}) collective-permute-start(bf16[560,256]{1,0:T(8,128)(2,1)S(1)} %collective-permute-done.1.refs_2_), channel_id=1, source_target_pairs={{0,1},{1,0},{2,3},{3,2},{4,5},{5,4},{6,7},{7,6},{8,9},{9,8},{10,11... | collective-permute-start | bytes 860168 | tf_op jit(solution)/shard_map/ppermute | solution.py:25
  12.1 1.9 %collective-permute-start.6 = (bf16[560,256]{1,0:T(8,128)(2,1)S(1)}, bf16[560,256]{1,0:T(8,128)(2,1)S(1)}, u32[]{:S(2)}, u32[]{:S(2)}) collective-permute-start(bf16[560,256]{1,0:T(8,128)(2,1)S(1)} %collective-permute-done.5.refs_6_), channel_id=1, source_target_pairs={{0,1},{1,0},{2,3},{3,2},{4,5},{5,4},{6,7},{7,6},{8,9},{9,8},{10,11... | collective-permute-start | bytes 860168 | tf_op jit(solution)/shard_map/ppermute | solution.py:25
  13.9 3.4 %collective-permute-start.7 = (bf16[560,256]{1,0:T(8,128)(2,1)S(1)}, bf16[560,256]{1,0:T(8,128)(2,1)S(1)}, u32[]{:S(2)}, u32[]{:S(2)}) collective-permute-start(bf16[560,256]{1,0:T(8,128)(2,1)S(1)} %collective-permute-done.5.refs_6_), channel_id=1, source_target_pairs={{0,2},{2,0},{1,3},{3,1},{4,6},{6,4},{5,7},{7,5},{8,10},{10,8},{9,1... | collective-permute-start | bytes 860168 | tf_op jit(solution)/shard_map/ppermute | solution.py:35
  17.3 2.4 %collective-permute-done.11.refs_12_ = bf16[560,256]{1,0:T(8,128)(2,1)S(1)} collective-permute-done((bf16[560,256]{1,0:T(8,128)(2,1)}, bf16[560,256]{1,0:T(8,128)(2,1)S(1)}, u32[]{:S(2)}, u32[]{:S(2)}) %collective-permute-start.11) | collective-permute-done | bytes 286752 | tf_op jit(solution)/shard_map/ppermute | solution.py:35
  19.7 3.4 %collective-permute-start.13 = (bf16[560,256]{1,0:T(8,128)(2,1)S(1)}, bf16[560,256]{1,0:T(8,128)(2,1)}, u32[]{:S(2)}, u32[]{:S(2)}) collective-permute-start(bf16[560,256]{1,0:T(8,128)(2,1)S(1)} %collective-permute-done.1.refs_2_), channel_id=1, source_target_pairs={{8,16},{16,8},{24,32},{32,24},{40,48},{48,40},{56,64},{64,56},{72,... | collective-permute-start | bytes 860168 | tf_op jit(solution)/shard_map/ppermute | solution.py:35
  23.1 1.4 %collective-permute-start.15 = (bf16[560,256]{1,0:T(8,128)(2,1)S(1)}, bf16[560,256]{1,0:T(8,128)(2,1)}, u32[]{:S(2)}, u32[]{:S(2)}) collective-permute-start(bf16[560,256]{1,0:T(8,128)(2,1)S(1)} %collective-permute-done.11.refs_12_), channel_id=1, source_target_pairs={{2,4},{4,2},{3,5},{5,3},{10,12},{12,10},{11,13},{13,11},{18,20},{2... | collective-permute-start | bytes 860168 | tf_op jit(solution)/shard_map/ppermute | solution.py:35
  25.8 2.2 %copy.17 = bf16[3,3,128,256]{3,2,1,0:T(8,128)(2,1)} copy(bf16[3,3,128,256]{2,3,1,0:T(8,128)(2,1)} %bitcast.66) | data formatting | bytes 1179648 | tf_op jit(solution)/shard_map/transpose | solution.py:392
  30.0 1.4 %collective-permute-done.13.refs_14_ = bf16[560,256]{1,0:T(8,128)(2,1)} collective-permute-done((bf16[560,256]{1,0:T(8,128)(2,1)S(1)}, bf16[560,256]{1,0:T(8,128)(2,1)}, u32[]{:S(2)}, u32[]{:S(2)}) %collective-permute-start.13) | collective-permute-done | bytes 286752 | tf_op jit(solution)/shard_map/ppermute | solution.py:35
  31.4 1.7 %collective-permute-start.14 = (bf16[560,256]{1,0:T(8,128)(2,1)}, bf16[560,256]{1,0:T(8,128)(2,1)S(1)}, u32[]{:S(2)}, u32[]{:S(2)}) collective-permute-start(bf16[560,256]{1,0:T(8,128)(2,1)} %collective-permute-done.13.refs_14_), channel_id=1, source_target_pairs={{0,1},{1,0},{2,3},{3,2},{4,5},{5,4},{6,7},{7,6},{8,9},{9,8},{10,11... | collective-permute-start | bytes 860168 | tf_op jit(solution)/shard_map/ppermute | solution.py:25
  35.8 11.8 %shard_map.137 = (bf16[4,768,256]{2,1,0:T(8,128)(2,1)}, bf16[512,256]{1,0:T(8,128)(2,1)}, bf16[512,256]{1,0:T(8,128)(2,1)}, bf16[32,256]{1,0:T(8,128)(2,1)}, bf1...) custom-call(s32[17]{0:T(128)} %concatenate.12.info, ...), custom_call_target="tpu_custom_call" | custom-call | flops 3000000000 | bytes 10000000 | tf_op jit(solution)/shard_map/pallas_call | solution.py:394
  48.2 1.6 %collective-permute-done.26 = bf16[1536,128]{1,0:T(8,128)(2,1)S(1)} collective-permute-done((bf16[1536,128]{1,0:T(8,128)(2,1)}, bf16[1536,128]{1,0:T(8,128)(2,1)S(1)}, u32[]{:S(2)}, u32[]{:S(2)}) %collective-permute-start.26) | collective-permute-done | bytes 393248 | tf_op jit(solution)/shard_map/ppermute | solution.py:25
  51.0 5.1 %collective-permute-start.27 = (bf16[768,128]{1,0:T(8,128)(2,1)S(1)}, bf16[768,128]{1,0:T(8,128)(2,1)S(1)}, u32[]{:S(2)}, u32[]{:S(2)}) collective-permute-start(bf16[768,128]{1,0:T(8,128)(2,1)S(1)} %dynamic-slice_convert_fusion), channel_id=1, source_target_pairs={{0,2},{1,3},{2,0},{3,1},{4,6},{5,7},{6,4},{7,5},{8,10},{9,11},{10,... | collective-permute-start | bytes 589832 | tf_op jit(solution)/shard_map/ppermute | solution.py:25
  56.1 8.4 %shard_map.139 = (f32[512,256]{1,0:T(8,128)}, bf16[9,512,256]{2,1,0:T(8,128)(2,1)}, bf16[6,512,256]{2,1,0:T(8,128)(2,1)}) custom-call(s32[17]{0:T(128)} %concatenate.12.info, bf16[512,256]{1,0:T(8,128)(2,1)} %bitcast.78, bf16[512,256]{1,0:T(8,128)(2,1)} %get-tuple-element.23.context_grad, bf16[512,256]{1,0:T(8,128)(2,1)} %bitcast.70, ...), custom_call_target="tpu_custom_call" | custom-call | flops 3000000000 | bytes 10000000 | tf_op jit(solution)/shard_map/pallas_call | solution.py:418
  65.2 5.8 %collective-permute-done.28 = bf16[384,128]{1,0:T(8,128)(2,1)S(1)} collective-permute-done((bf16[384,128]{1,0:T(8,128)(2,1)S(1)}, bf16[384,128]{1,0:T(8,128)(2,1)S(1)}, u32[]{:S(2)}, u32[]{:S(2)}) %collective-permute-start.28) | collective-permute-done | bytes 98336 | tf_op jit(solution)/shard_map/ppermute | solution.py:25
  71.0 1.4 %collective-permute-start.29 = (bf16[384,128]{1,0:T(8,128)(2,1)S(1)}, bf16[384,128]{1,0:T(8,128)(2,1)S(1)}, u32[]{:S(2)}, u32[]{:S(2)}) collective-permute-start(bf16[384,128]{1,0:T(8,128)(2,1)S(1)} %add_convert_fusion.4), channel_id=1, source_target_pairs={{0,8},{8,0},{16,24},{24,16},{32,40},{40,32},{48,56},{56,48},{64,72... | collective-permute-start | bytes 294920 | tf_op jit(solution)/shard_map/ppermute | solution.py:25
  72.4 2.2 %collective-permute-done.29 = bf16[384,128]{1,0:T(8,128)(2,1)S(1)} collective-permute-done((bf16[384,128]{1,0:T(8,128)(2,1)S(1)}, bf16[384,128]{1,0:T(8,128)(2,1)S(1)}, u32[]{:S(2)}, u32[]{:S(2)}) %collective-permute-start.29) | collective-permute-done | bytes 98336 | tf_op jit(solution)/shard_map/ppermute | solution.py:25
  74.6 2.7 %collective-permute-start.30 = (bf16[384,128]{1,0:T(8,128)(2,1)S(1)}, bf16[384,128]{1,0:T(8,128)(2,1)S(1)}, u32[]{:S(2)}, u32[]{:S(2)}) collective-permute-start(bf16[384,128]{1,0:T(8,128)(2,1)S(1)} %add_convert_fusion.3), channel_id=1, source_target_pairs={{0,16},{8,24},{16,0},{24,8},{32,48},{40,56},{48,32},{56,40},{64,80... | collective-permute-start | bytes 294920 | tf_op jit(solution)/shard_map/ppermute | solution.py:25
  77.9 2.0 %collective-permute-start.17 = (bf16[32,256]{1,0:T(8,128)(2,1)S(1)}, bf16[32,256]{1,0:T(8,128)(2,1)S(1)}, u32[]{:S(2)}, u32[]{:S(2)}) collective-permute-start(bf16[32,256]{1,0:T(8,128)(2,1)S(1)} %copy-done.24), channel_id=1, source_target_pairs={{8,16},{16,8},{24,32},{32,24},{40,48},{48,40},{56,64},{64,56},{72,... | collective-permute-start | bytes 49160 | tf_op jit(solution)/shard_map/ppermute | solution.py:35
  80.0 2.1 %convert_element_type.94 = f32[9,512,256]{2,1,0:T(8,128)S(1)} convert(bf16[9,512,256]{2,1,0:T(8,128)(2,1)} %get-tuple-element.26) | non-fusion elementwise | flops 1179648 | bytes 7077888 | tf_op jit(solution)/shard_map/convert_element_type | solution.py:430
  82.1 1.3 %collective-permute-done.31 = bf16[384,128]{1,0:T(8,128)(2,1)S(1)} collective-permute-done((bf16[384,128]{1,0:T(8,128)(2,1)S(1)}, bf16[384,128]{1,0:T(8,128)(2,1)S(1)}, u32[]{:S(2)}, u32[]{:S(2)}) %collective-permute-start.31) | collective-permute-done | bytes 98336 | tf_op jit(solution)/shard_map/ppermute | solution.py:25
  83.5 3.3 %collective-permute-start.32 = (bf16[384,128]{1,0:T(8,128)(2,1)S(1)}, bf16[384,128]{1,0:T(8,128)(2,1)S(1)}, u32[]{:S(2)}, u32[]{:S(2)}) collective-permute-start(bf16[384,128]{1,0:T(8,128)(2,1)S(1)} %add_convert_fusion.1), channel_id=1, source_target_pairs={{0,64},{8,72},{16,80},{24,88},{32,96},{40,104},{48,112},{56,120},{... | collective-permute-start | bytes 294920 | tf_op jit(solution)/shard_map/ppermute | solution.py:25
  89.3 1.5 %collective-permute-start.33 = (bf16[384,128]{1,0:T(8,128)(2,1)S(1)}, bf16[384,128]{1,0:T(8,128)(2,1)S(1)}, u32[]{:S(2)}, u32[]{:S(2)}) collective-permute-start(bf16[384,128]{1,0:T(8,128)(2,1)S(1)} %add_convert_fusion), channel_id=1, source_target_pairs={{0,4},{1,5},{2,6},{3,7},{4,0},{5,1},{6,2},{7,3},{8,12},{9,13},{10,... | collective-permute-start | bytes 294920 | tf_op jit(solution)/shard_map/ppermute | solution.py:25
  90.8 14.6 %collective-permute-done.33 = bf16[384,128]{1,0:T(8,128)(2,1)S(1)} collective-permute-done((bf16[384,128]{1,0:T(8,128)(2,1)S(1)}, bf16[384,128]{1,0:T(8,128)(2,1)S(1)}, u32[]{:S(2)}, u32[]{:S(2)}) %collective-permute-start.33) | collective-permute-done | bytes 98336 | tf_op jit(solution)/shard_map/ppermute | solution.py:25
  106.2 8.5 %collective-permute-start.20 = (bf16[18,256]{1,0:T(8,128)(2,1)S(1)}, bf16[18,256]{1,0:T(8,128)(2,1)S(1)}, u32[]{:S(2)}, u32[]{:S(2)}) collective-permute-start(bf16[18,256]{1,0:T(8,128)(2,1)S(1)} %get-tuple-element.44), channel_id=1, source_target_pairs={{0,1},{1,0},{2,3},{3,2},{4,5},{5,4},{6,7},{7,6},{8,9},{9,8},{10,11... | collective-permute-start | bytes 27656 | tf_op jit(solution)/shard_map/ppermute | solution.py:35
  114.7 1.9 %collective-permute-start.19 = (bf16[18,256]{1,0:T(8,128)(2,1)S(1)}, bf16[18,256]{1,0:T(8,128)(2,1)S(1)}, u32[]{:S(2)}, u32[]{:S(2)}) collective-permute-start(bf16[18,256]{1,0:T(8,128)(2,1)S(1)} %get-tuple-element.45), channel_id=1, source_target_pairs={{1,2},{2,1},{3,4},{4,3},{5,6},{6,5},{9,10},{10,9},{11,12},{12,11},... | collective-permute-start | bytes 27656 | tf_op jit(solution)/shard_map/ppermute | solution.py:35
  116.6 1.6 %collective-permute-start.35 = (bf16[768,128]{1,0:T(8,128)(2,1)S(1)}, bf16[768,128]{1,0:T(8,128)(2,1)S(1)}, u32[]{:S(2)}, u32[]{:S(2)}) collective-permute-start(bf16[768,128]{1,0:T(8,128)(2,1)S(1)} %pad_maximum_fusion.near), channel_id=1, source_target_pairs={{0,1},{1,0},{2,3},{3,2},{4,5},{5,4},{6,7},{7,6},{8,9},{9,8},{10,11... | collective-permute-start | bytes 589832 | tf_op jit(solution)/shard_map/ppermute | solution.py:25
  118.8 4.3 %collective-permute-start.25 = (bf16[512,256]{1,0:T(8,128)(2,1)S(1)}, bf16[512,256]{1,0:T(8,128)(2,1)S(1)}, u32[]{:S(2)}, u32[]{:S(2)}) collective-permute-start(bf16[512,256]{1,0:T(8,128)(2,1)S(1)} %get-tuple-element.37), channel_id=1, source_target_pairs={{8,16},{16,8},{24,32},{32,24},{40,48},{48,40},{56,64},{64,56},{72,... | collective-permute-start | bytes 786440 | tf_op jit(solution)/shard_map/ppermute | solution.py:35
  123.9 2.7 %shard_map.138 = bf16[512,128]{1,0:T(8,128)(2,1)} custom-call(bf16[512,256]{1,0:T(8,128)(2,1)} %get-tuple-element.19.motion, bf16[32,256]{1,0:T(8,128)(2,1)} %copy-done.6, bf16[32,256]{1,0:T(8,128)(2,1)} %copy-done.5, bf16[18,256]{1,0:T(8,128)(2,1)} %get-tuple-element.43.west, bf16[18,256]{1,0:T(8,128)(2,1)} %get-tuple-element.42.east, ...), custom_call_target="tpu_custom_call" | custom-call | flops 1000000000 | bytes 3333333 | tf_op jit(solution)/shard_map/pallas_call | solution.py:439
  127.9 2.5 %shard_map.140 = (f32[2304,128]{1,0:T(8,128)}, f32[324,256]{1,0:T(8,128)}) custom-call(s32[17]{0:T(128)} %concatenate.12.info, bf16[768,128]{1,0:T(8,128)(2,1)} %copy-done, bf16[768,128]{1,0:T(8,128)(2,1)} %copy-done.1, bf16[768,128]{1,0:T(8,128)(2,1)} %copy-done.2, bf16[768,128]{1,0:T(8,128)(2,1)} %copy-done.3), custom_call_target="tpu_custom_call" | custom-call | tf_op jit(solution)/shard_map/pallas_call | solution.py:450
  (128 shorter events, 17.9 us)
Async XLA Ops:
  2.5 7.9 %collective-permute-start.1 = (bf16[560,256]{1,0:T(8,128)(2,1)}, bf16[560,256]{1,0:T(8,128)(2,1)S(1)}, u32[]{:S(2)}, u32[]{:S(2)}) collective-permute-start(bf16[560,256]{1,0:T(8,128)(2,1)} %shard_map.136.refs_0_), channel_id=1, source_target_pairs={{0,2},{2,0},{1,3},{3,1},{4,6},{6,4},{5,7},{7,5},{8,10},{10,8},{9,1... | collective-permute-start | bytes 860168 | tf_op jit(solution)/shard_map/ppermute | solution.py:35
  3.7 8.3 %collective-permute-start.3 = (bf16[560,256]{1,0:T(8,128)(2,1)}, bf16[560,256]{1,0:T(8,128)(2,1)S(1)}, u32[]{:S(2)}, u32[]{:S(2)}) collective-permute-start(bf16[560,256]{1,0:T(8,128)(2,1)} %shard_map.136.refs_0_), channel_id=1, source_target_pairs={{2,4},{4,2},{3,5},{5,3},{10,12},{12,10},{11,13},{13,11},{18,20},{2... | collective-permute-start | bytes 860168 | tf_op jit(solution)/shard_map/ppermute | solution.py:35
  4.4 7.7 %collective-permute-start.5 = (bf16[560,256]{1,0:T(8,128)(2,1)}, bf16[560,256]{1,0:T(8,128)(2,1)S(1)}, u32[]{:S(2)}, u32[]{:S(2)}) collective-permute-start(bf16[560,256]{1,0:T(8,128)(2,1)} %shard_map.136.refs_0_), channel_id=1, source_target_pairs={{0,8},{8,0},{16,24},{24,16},{32,40},{40,32},{48,56},{56,48},{64,72... | collective-permute-start | bytes 860168 | tf_op jit(solution)/shard_map/ppermute | solution.py:35
  5.8 8.2 %collective-permute-start = (bf16[560,256]{1,0:T(8,128)(2,1)}, bf16[560,256]{1,0:T(8,128)(2,1)S(1)}, u32[]{:S(2)}, u32[]{:S(2)}) collective-permute-start(bf16[560,256]{1,0:T(8,128)(2,1)} %shard_map.136.refs_0_), channel_id=1, source_target_pairs={{0,1},{1,0},{2,3},{3,2},{4,5},{5,4},{6,7},{7,6},{8,9},{9,8},{10,11... | collective-permute-start | bytes 860168 | tf_op jit(solution)/shard_map/ppermute | solution.py:25
  7.0 12.7 %collective-permute-start.11 = (bf16[560,256]{1,0:T(8,128)(2,1)}, bf16[560,256]{1,0:T(8,128)(2,1)S(1)}, u32[]{:S(2)}, u32[]{:S(2)}) collective-permute-start(bf16[560,256]{1,0:T(8,128)(2,1)} %shard_map.136.refs_0_), channel_id=1, source_target_pairs={{8,16},{16,8},{24,32},{32,24},{40,48},{48,40},{56,64},{64,56},{72,... | collective-permute-start | bytes 860168 | tf_op jit(solution)/shard_map/ppermute | solution.py:35
  10.4 9.3 %collective-permute-start.2 = (bf16[560,256]{1,0:T(8,128)(2,1)S(1)}, bf16[560,256]{1,0:T(8,128)(2,1)S(1)}, u32[]{:S(2)}, u32[]{:S(2)}) collective-permute-start(bf16[560,256]{1,0:T(8,128)(2,1)S(1)} %collective-permute-done.1.refs_2_), channel_id=1, source_target_pairs={{0,1},{1,0},{2,3},{3,2},{4,5},{5,4},{6,7},{7,6},{8,9},{9,8},{10,11... | collective-permute-start | bytes 860168 | tf_op jit(solution)/shard_map/ppermute | solution.py:25
  12.0 11.1 %collective-permute-start.4 = (bf16[560,256]{1,0:T(8,128)(2,1)S(1)}, bf16[560,256]{1,0:T(8,128)(2,1)S(1)}, u32[]{:S(2)}, u32[]{:S(2)}) collective-permute-start(bf16[560,256]{1,0:T(8,128)(2,1)S(1)} %collective-permute-done.3.refs_4_), channel_id=1, source_target_pairs={{0,1},{1,0},{2,3},{3,2},{4,5},{5,4},{6,7},{7,6},{8,9},{9,8},{10,11... | collective-permute-start | bytes 860168 | tf_op jit(solution)/shard_map/ppermute | solution.py:25
  12.1 16.2 %collective-permute-start.6 = (bf16[560,256]{1,0:T(8,128)(2,1)S(1)}, bf16[560,256]{1,0:T(8,128)(2,1)S(1)}, u32[]{:S(2)}, u32[]{:S(2)}) collective-permute-start(bf16[560,256]{1,0:T(8,128)(2,1)S(1)} %collective-permute-done.5.refs_6_), channel_id=1, source_target_pairs={{0,1},{1,0},{2,3},{3,2},{4,5},{5,4},{6,7},{7,6},{8,9},{9,8},{10,11... | collective-permute-start | bytes 860168 | tf_op jit(solution)/shard_map/ppermute | solution.py:25
  13.9 15.5 %collective-permute-start.7 = (bf16[560,256]{1,0:T(8,128)(2,1)S(1)}, bf16[560,256]{1,0:T(8,128)(2,1)S(1)}, u32[]{:S(2)}, u32[]{:S(2)}) collective-permute-start(bf16[560,256]{1,0:T(8,128)(2,1)S(1)} %collective-permute-done.5.refs_6_), channel_id=1, source_target_pairs={{0,2},{2,0},{1,3},{3,1},{4,6},{6,4},{5,7},{7,5},{8,10},{10,8},{9,1... | collective-permute-start | bytes 860168 | tf_op jit(solution)/shard_map/ppermute | solution.py:35
  19.7 9.9 %collective-permute-start.9 = (bf16[560,256]{1,0:T(8,128)(2,1)S(1)}, bf16[560,256]{1,0:T(8,128)(2,1)S(1)}, u32[]{:S(2)}, u32[]{:S(2)}) collective-permute-start(bf16[560,256]{1,0:T(8,128)(2,1)S(1)} %collective-permute-done.3.refs_4_), channel_id=1, source_target_pairs={{0,8},{8,0},{16,24},{24,16},{32,40},{40,32},{48,56},{56,48},{64,72... | collective-permute-start | bytes 860168 | tf_op jit(solution)/shard_map/ppermute | solution.py:35
  19.7 11.7 %collective-permute-start.13 = (bf16[560,256]{1,0:T(8,128)(2,1)S(1)}, bf16[560,256]{1,0:T(8,128)(2,1)}, u32[]{:S(2)}, u32[]{:S(2)}) collective-permute-start(bf16[560,256]{1,0:T(8,128)(2,1)S(1)} %collective-permute-done.1.refs_2_), channel_id=1, source_target_pairs={{8,16},{16,8},{24,32},{32,24},{40,48},{48,40},{56,64},{64,56},{72,... | collective-permute-start | bytes 860168 | tf_op jit(solution)/shard_map/ppermute | solution.py:35
  23.1 10.0 %collective-permute-start.15 = (bf16[560,256]{1,0:T(8,128)(2,1)S(1)}, bf16[560,256]{1,0:T(8,128)(2,1)}, u32[]{:S(2)}, u32[]{:S(2)}) collective-permute-start(bf16[560,256]{1,0:T(8,128)(2,1)S(1)} %collective-permute-done.11.refs_12_), channel_id=1, source_target_pairs={{2,4},{4,2},{3,5},{5,3},{10,12},{12,10},{11,13},{13,11},{18,20},{2... | collective-permute-start | bytes 860168 | tf_op jit(solution)/shard_map/ppermute | solution.py:35
  28.4 6.4 %collective-permute-start.12 = (bf16[560,256]{1,0:T(8,128)(2,1)S(1)}, bf16[560,256]{1,0:T(8,128)(2,1)S(1)}, u32[]{:S(2)}, u32[]{:S(2)}) collective-permute-start(bf16[560,256]{1,0:T(8,128)(2,1)S(1)} %collective-permute-done.11.refs_12_), channel_id=1, source_target_pairs={{0,1},{1,0},{2,3},{3,2},{4,5},{5,4},{6,7},{7,6},{8,9},{9,8},{10,11... | collective-permute-start | bytes 860168 | tf_op jit(solution)/shard_map/ppermute | solution.py:25
  29.5 5.2 %collective-permute-start.8 = (bf16[560,256]{1,0:T(8,128)(2,1)S(1)}, bf16[560,256]{1,0:T(8,128)(2,1)S(1)}, u32[]{:S(2)}, u32[]{:S(2)}) collective-permute-start(bf16[560,256]{1,0:T(8,128)(2,1)S(1)} %collective-permute-done.7.refs_8_), channel_id=1, source_target_pairs={{0,1},{1,0},{2,3},{3,2},{4,5},{5,4},{6,7},{7,6},{8,9},{9,8},{10,11... | collective-permute-start | bytes 860168 | tf_op jit(solution)/shard_map/ppermute | solution.py:25
  29.6 5.1 %collective-permute-start.10 = (bf16[560,256]{1,0:T(8,128)(2,1)S(1)}, bf16[560,256]{1,0:T(8,128)(2,1)S(1)}, u32[]{:S(2)}, u32[]{:S(2)}) collective-permute-start(bf16[560,256]{1,0:T(8,128)(2,1)S(1)} %collective-permute-done.9.refs_10_), channel_id=1, source_target_pairs={{0,1},{1,0},{2,3},{3,2},{4,5},{5,4},{6,7},{7,6},{8,9},{9,8},{10,11... | collective-permute-start | bytes 860168 | tf_op jit(solution)/shard_map/ppermute | solution.py:25
  51.0 14.0 %collective-permute-start.27 = (bf16[768,128]{1,0:T(8,128)(2,1)S(1)}, bf16[768,128]{1,0:T(8,128)(2,1)S(1)}, u32[]{:S(2)}, u32[]{:S(2)}) collective-permute-start(bf16[768,128]{1,0:T(8,128)(2,1)S(1)} %dynamic-slice_convert_fusion), channel_id=1, source_target_pairs={{0,2},{1,3},{2,0},{3,1},{4,6},{5,7},{6,4},{7,5},{8,10},{9,11},{10,... | collective-permute-start | bytes 589832 | tf_op jit(solution)/shard_map/ppermute | solution.py:25
  64.5 22.3 %collective-permute-start.21 = (bf16[6,512,256]{2,1,0:T(8,128)(2,1)}, bf16[6,512,256]{2,1,0:T(8,128)(2,1)S(1)}, u32[]{:S(2)}, u32[]{:S(2)}) collective-permute-start(bf16[6,512,256]{2,1,0:T(8,128)(2,1)} %get-tuple-element.27), channel_id=1, source_target_pairs={{0,1},{1,0},{2,3},{3,2},{4,5},{5,4},{6,7},{7,6},{8,9},{9,8},{10,11... | collective-permute-start | bytes 4718600 | tf_op jit(solution)/shard_map/ppermute | solution.py:25
  65.1 5.9 %collective-permute-start.28 = (bf16[384,128]{1,0:T(8,128)(2,1)S(1)}, bf16[384,128]{1,0:T(8,128)(2,1)S(1)}, u32[]{:S(2)}, u32[]{:S(2)}) collective-permute-start(bf16[384,128]{1,0:T(8,128)(2,1)S(1)} %dynamic-slice_convert_fusion.1), channel_id=1, source_target_pairs={{0,4},{1,5},{2,6},{3,7},{4,0},{5,1},{6,2},{7,3},{8,12},{9,13},{10,... | collective-permute-start | bytes 294920 | tf_op jit(solution)/shard_map/ppermute | solution.py:25
  74.6 5.3 %collective-permute-start.30 = (bf16[384,128]{1,0:T(8,128)(2,1)S(1)}, bf16[384,128]{1,0:T(8,128)(2,1)S(1)}, u32[]{:S(2)}, u32[]{:S(2)}) collective-permute-start(bf16[384,128]{1,0:T(8,128)(2,1)S(1)} %add_convert_fusion.3), channel_id=1, source_target_pairs={{0,16},{8,24},{16,0},{24,8},{32,48},{40,56},{48,32},{56,40},{64,80... | collective-permute-start | bytes 294920 | tf_op jit(solution)/shard_map/ppermute | solution.py:25
  77.3 13.5 %collective-permute-start.18 = (bf16[32,256]{1,0:T(8,128)(2,1)S(1)}, bf16[32,256]{1,0:T(8,128)(2,1)S(1)}, u32[]{:S(2)}, u32[]{:S(2)}) collective-permute-start(bf16[32,256]{1,0:T(8,128)(2,1)S(1)} %copy-done.25), channel_id=1, source_target_pairs={{0,8},{8,0},{16,24},{24,16},{32,40},{40,32},{48,56},{56,48},{64,72... | collective-permute-start | bytes 49160 | tf_op jit(solution)/shard_map/ppermute | solution.py:35
  77.9 12.9 %collective-permute-start.17 = (bf16[32,256]{1,0:T(8,128)(2,1)S(1)}, bf16[32,256]{1,0:T(8,128)(2,1)S(1)}, u32[]{:S(2)}, u32[]{:S(2)}) collective-permute-start(bf16[32,256]{1,0:T(8,128)(2,1)S(1)} %copy-done.24), channel_id=1, source_target_pairs={{8,16},{16,8},{24,32},{32,24},{40,48},{48,40},{56,64},{64,56},{72,... | collective-permute-start | bytes 49160 | tf_op jit(solution)/shard_map/ppermute | solution.py:35
  83.5 5.8 %collective-permute-start.32 = (bf16[384,128]{1,0:T(8,128)(2,1)S(1)}, bf16[384,128]{1,0:T(8,128)(2,1)S(1)}, u32[]{:S(2)}, u32[]{:S(2)}) collective-permute-start(bf16[384,128]{1,0:T(8,128)(2,1)S(1)} %add_convert_fusion.1), channel_id=1, source_target_pairs={{0,64},{8,72},{16,80},{24,88},{32,96},{40,104},{48,112},{56,120},{... | collective-permute-start | bytes 294920 | tf_op jit(solution)/shard_map/ppermute | solution.py:25
  87.5 30.7 %collective-permute-start.23 = (bf16[3,512,256]{2,1,0:T(8,128)(2,1)S(1)}, bf16[3,512,256]{2,1,0:T(8,128)(2,1)S(1)}, u32[]{:S(2)}, u32[]{:S(2)}) collective-permute-start(bf16[3,512,256]{2,1,0:T(8,128)(2,1)S(1)} %get-tuple-element.35), channel_id=1, source_target_pairs={{2,4},{4,2},{3,5},{5,3},{10,12},{12,10},{11,13},{13,11},{18,20},{2... | collective-permute-start | bytes 2359304 | tf_op jit(solution)/shard_map/ppermute | solution.py:35
  88.2 30.1 %collective-permute-start.22 = (bf16[3,512,256]{2,1,0:T(8,128)(2,1)S(1)}, bf16[3,512,256]{2,1,0:T(8,128)(2,1)S(1)}, u32[]{:S(2)}, u32[]{:S(2)}) collective-permute-start(bf16[3,512,256]{2,1,0:T(8,128)(2,1)S(1)} %get-tuple-element.34), channel_id=1, source_target_pairs={{0,2},{2,0},{1,3},{3,1},{4,6},{6,4},{5,7},{7,5},{8,10},{10,8},{9,1... | collective-permute-start | bytes 2359304 | tf_op jit(solution)/shard_map/ppermute | solution.py:35
  89.3 16.1 %collective-permute-start.33 = (bf16[384,128]{1,0:T(8,128)(2,1)S(1)}, bf16[384,128]{1,0:T(8,128)(2,1)S(1)}, u32[]{:S(2)}, u32[]{:S(2)}) collective-permute-start(bf16[384,128]{1,0:T(8,128)(2,1)S(1)} %add_convert_fusion), channel_id=1, source_target_pairs={{0,4},{1,5},{2,6},{3,7},{4,0},{5,1},{6,2},{7,3},{8,12},{9,13},{10,... | collective-permute-start | bytes 294920 | tf_op jit(solution)/shard_map/ppermute | solution.py:25
  105.5 11.2 %collective-permute-start.34 = (bf16[768,128]{1,0:T(8,128)(2,1)S(1)}, bf16[768,128]{1,0:T(8,128)(2,1)S(1)}, u32[]{:S(2)}, u32[]{:S(2)}) collective-permute-start(bf16[768,128]{1,0:T(8,128)(2,1)S(1)} %pad_maximum_fusion.near), channel_id=1, source_target_pairs={{0,2},{1,3},{2,0},{3,1},{4,6},{5,7},{6,4},{7,5},{8,10},{9,11},{10,... | collective-permute-start | bytes 589832 | tf_op jit(solution)/shard_map/ppermute | solution.py:25
  106.2 17.0 %collective-permute-start.20 = (bf16[18,256]{1,0:T(8,128)(2,1)S(1)}, bf16[18,256]{1,0:T(8,128)(2,1)S(1)}, u32[]{:S(2)}, u32[]{:S(2)}) collective-permute-start(bf16[18,256]{1,0:T(8,128)(2,1)S(1)} %get-tuple-element.44), channel_id=1, source_target_pairs={{0,1},{1,0},{2,3},{3,2},{4,5},{5,4},{6,7},{7,6},{8,9},{9,8},{10,11... | collective-permute-start | bytes 27656 | tf_op jit(solution)/shard_map/ppermute | solution.py:35
  114.7 8.6 %collective-permute-start.19 = (bf16[18,256]{1,0:T(8,128)(2,1)S(1)}, bf16[18,256]{1,0:T(8,128)(2,1)S(1)}, u32[]{:S(2)}, u32[]{:S(2)}) collective-permute-start(bf16[18,256]{1,0:T(8,128)(2,1)S(1)} %get-tuple-element.45), channel_id=1, source_target_pairs={{1,2},{2,1},{3,4},{4,3},{5,6},{6,5},{9,10},{10,9},{11,12},{12,11},... | collective-permute-start | bytes 27656 | tf_op jit(solution)/shard_map/ppermute | solution.py:35
  116.6 9.9 %collective-permute-start.35 = (bf16[768,128]{1,0:T(8,128)(2,1)S(1)}, bf16[768,128]{1,0:T(8,128)(2,1)S(1)}, u32[]{:S(2)}, u32[]{:S(2)}) collective-permute-start(bf16[768,128]{1,0:T(8,128)(2,1)S(1)} %pad_maximum_fusion.near), channel_id=1, source_target_pairs={{0,1},{1,0},{2,3},{3,2},{4,5},{5,4},{6,7},{7,6},{8,9},{9,8},{10,11... | collective-permute-start | bytes 589832 | tf_op jit(solution)/shard_map/ppermute | solution.py:25
  118.2 8.3 %collective-permute-start.36 = (bf16[768,128]{1,0:T(8,128)(2,1)S(1)}, bf16[768,128]{1,0:T(8,128)(2,1)S(1)}, u32[]{:S(2)}, u32[]{:S(2)}) collective-permute-start(bf16[768,128]{1,0:T(8,128)(2,1)S(1)} %collective-permute-done.34.near_across), channel_id=1, source_target_pairs={{0,1},{1,0},{2,3},{3,2},{4,5},{5,4},{6,7},{7,6},{8,9},{9,8},{10,11... | collective-permute-start | bytes 589832 | tf_op jit(solution)/shard_map/ppermute | solution.py:25
  118.8 11.6 %collective-permute-start.25 = (bf16[512,256]{1,0:T(8,128)(2,1)S(1)}, bf16[512,256]{1,0:T(8,128)(2,1)S(1)}, u32[]{:S(2)}, u32[]{:S(2)}) collective-permute-start(bf16[512,256]{1,0:T(8,128)(2,1)S(1)} %get-tuple-element.37), channel_id=1, source_target_pairs={{8,16},{16,8},{24,32},{32,24},{40,48},{48,40},{56,64},{64,56},{72,... | collective-permute-start | bytes 786440 | tf_op jit(solution)/shard_map/ppermute | solution.py:35
  123.2 7.3 %collective-permute-start.24 = (bf16[512,256]{1,0:T(8,128)(2,1)S(1)}, bf16[512,256]{1,0:T(8,128)(2,1)S(1)}, u32[]{:S(2)}, u32[]{:S(2)}) collective-permute-start(bf16[512,256]{1,0:T(8,128)(2,1)S(1)} %get-tuple-element.36), channel_id=1, source_target_pairs={{0,8},{8,0},{16,24},{24,16},{32,40},{40,32},{48,56},{56,48},{64,72... | collective-permute-start | bytes 786440 | tf_op jit(solution)/shard_map/ppermute | solution.py:35
  (31 other events, 272.3 us)

commit v4 on v3

--- a/solution.py
+++ b/solution.py
@@ -114,7 +114,45 @@
     out[cells + 32 :, 128:] = ends[16:]
 
 
-def forward_kernel(info, first, context, cotangent, back_weight, corr_weight, *refs):
+def role(step, even):
+    step = jnp.asarray(step)
+    return jnp.where(step == 0, 0, jnp.where((step > 0) == even, 1, 2))
+
+
+def position():
+    col = lax.axis_index("col")
+    return lax.axis_index("row"), col >> 1, col & 1
+
+
+def tile_of(offset):
+    row, chip, core = position()
+    down, across = offset // 5 - 1, offset % 5 - 2
+    return (
+        role(down, row % 2 == 0) * 6 + role((core + across) >> 1, chip % 2 == 0) * 2 + (across & 1)
+    )
+
+
+def tiles_beside():
+    row, chip, core = position()
+    row_even, chip_even = row % 2 == 0, chip % 2 == 0
+    north, south = role(-1, row_even) * 6, role(1, row_even) * 6
+    west = jnp.where(core == 0, role(-1, chip_even), 0) * 2 + 1
+    east = jnp.where(core == 0, 0, role(1, chip_even)) * 2 + 1
+    return [north, south, west, east, north + west, north + east, south + west, south + east]
+
+
+def spread_kernel(weight, out, out_back, wide):
+    for lead, ref in ((LEAD, out), (LEAD_BACK, out_back)):
+        wide[...] = jnp.zeros_like(wide)
+        for k in range(4):
+            for u in range(SPAN):
+                row = k * 128 + (u % 4) * 32 + (u // 4) * SPAN + lead
+                at = (k * SPAN + u) * SPAN
+                wide[row : row + SPAN] = weight[at : at + SPAN]
+        ref[...] = wide[...].astype(BF16)
+
+
+def forward_kernel(partners, counts, radius, first, context, cotangent, conv_weight, corr_weight, *refs):
     tiles, refs = refs[:18], refs[18:]
     parts, motion, context_grad, facing, away, ends, weights_sent, weights_kept = refs[:8]
     edges, cot_taps, taps, weight_grads, sems, edge_sems = refs[8:]
@@ -122,27 +160,28 @@
     slots = parts.shape[0]
     row_sides, chip_sides = (6, 12), (1, 3, 5)
     options = [row_sides] * 2 + [chip_sides] * 2 + [[r + x for r in row_sides for x in chip_sides]] * 4
-    for n in range(8):
+    for n, tile in enumerate(tiles_beside()):
         for t in options[n]:
-            @pl.when(info[8 + n] == t)
+            @pl.when(tile == t)
             def _():
                 pltpu.make_async_copy(
                     tiles[t].at[pl.ds(cells, 48)], edges.at[n], edge_sems.at[n]
                 ).start()
     for k in range(slots):
+        tile = tile_of(partners[0, 0, k])
         for t in range(18):
-            @pl.when(info[k] == t)
+            @pl.when(tile == t)
             def _():
                 pltpu.make_async_copy(
                     tiles[t].at[pl.ds(0, cells)], parts.at[k, pl.ds(GROUP, cells)], sems.at[k]
                 ).start()
         parts[k, :GROUP] = jnp.zeros((GROUP, parts.shape[2]), BF16)
         parts[k, GROUP + cells :] = jnp.zeros((GROUP, parts.shape[2]), BF16)
-    inside = tap_mask(info[slots + 1], LEAD, True)
+    inside = tap_mask(radius[0, 0], LEAD, True)
     flip = flip_matrix()
     gains = []
     for k in range(slots):
-        live = jnp.where(k < info[slots], 1.0 / math.sqrt(first.shape[1]), 0.0).astype(F32)
+        live = jnp.where(k < counts[0, 0], 1.0 / math.sqrt(first.shape[1]), 0.0).astype(F32)
         gains.append(jnp.where(inside, live, 0.0))
     for n in range(8):
         pltpu.make_async_copy(tiles[0].at[pl.ds(cells, 48)], edges.at[n], edge_sems.at[n]).wait()
@@ -165,9 +204,13 @@
     grad_motion = jnp.zeros(context_grad.shape, F32)
     for a in range(3):
         start = (2 - a) * 32
-        grad_motion += jnp.dot(
-            cot_taps[start : start + cells], back_weight[a], preferred_element_type=F32
-        )
+        for b in range(3):
+            grad_motion += lax.dot_general(
+                cot_taps[start : start + cells, b * 128 : (b + 1) * 128],
+                conv_weight[a, b],
+                (((1,), (1,)), ((), ())),
+                preferred_element_type=F32,
+            )
     for k in range(slots):
         pltpu.make_async_copy(
             tiles[0].at[pl.ds(0, cells)], parts.at[k, pl.ds(GROUP, cells)], sems.at[k]
@@ -198,7 +241,8 @@
     sigma = jax.nn.sigmoid(pre)
     motion[...] = (pre * sigma).astype(BF16)
     context_grad[...] = (grad_motion * sigma * (1.0 + pre * (1.0 - sigma))).astype(BF16)
-    row_odd = info[16]
+    row, _, core = position()
+    row_odd = row % 2
     facing[...] = motion[pl.ds(pl.multiple_of((1 - row_odd) * (cells - 32), 32), 32)]
     away[...] = motion[pl.ds(pl.multiple_of(row_odd * (cells - 32), 32), 32)]
     ends[...] = outer_columns(motion).reshape(ends.shape)
@@ -222,7 +266,6 @@
                 to = base + h * 384 + (k * SPAN + u) * SPAN
                 weight_grads[to : to + SPAN] = term[row : row + SPAN, h * 128 : (h + 1) * 128]
     half = weight_grads.shape[0] // 2
-    core = info[slots + 2]
     weights_kept[...] = weight_grads[pl.ds(pl.multiple_of(core * half, half), half)]
     weights_sent[...] = weight_grads[pl.ds(pl.multiple_of((1 - core) * half, half), half)].astype(
         BF16
@@ -230,15 +273,15 @@
 
 
 def backward_kernel(
-    info, first, context_grad, corr_weight, parts, first_grad, kept, lent, totals
+    partners, counts, radius, first, context_grad, corr_weight, parts, first_grad, *refs
 ):
     cells = first.shape[0]
     slots = parts.shape[0]
     scale = 1.0 / math.sqrt(first.shape[1])
-    inside = tap_mask(info[slots + 1], LEAD_BACK, False)
-    totals[...] = jnp.zeros_like(totals)
-    kept[...] = jnp.zeros_like(kept)
-    lent[...] = jnp.zeros_like(lent)
+    inside = tap_mask(radius[0, 0], LEAD_BACK, False)
+    *kept, lent, totals = refs
+    for ref in refs:
+        ref[...] = jnp.zeros_like(ref)
     for q in range(cells // GROUP):
         at = slice(q * GROUP, (q + 1) * GROUP)
         packed = (
@@ -258,7 +301,7 @@
                 [mine, pltpu.roll(mine, 128 - SPAN, 1), pltpu.roll(mine, 128 - 2 * SPAN, 1)],
                 axis=1,
             )
-            band = jnp.where(inside & (k < info[slots]), band, 0.0)
+            band = jnp.where(inside & (k < counts[0, 0]), band, 0.0)
             scores = pltpu.roll(band, WINDOW - REACH - LEAD_BACK, 1, stride=1, stride_axis=0).astype(BF16)
             window = slice(q * GROUP, q * GROUP + WINDOW)
             first_here += jnp.dot(scores, parts[k, window], preferred_element_type=F32)
@@ -268,14 +311,13 @@
         first_grad[at] = first_here * scale
     for k in range(slots):
         value = (totals[k, GROUP : GROUP + cells] * scale).astype(BF16)
-        place = info[k]
-        same = place % 2 == 0
-
-        @pl.when(same)
-        def _():
-            kept[place % 6 // 2 * 3 + place // 6] = value
-
-        @pl.when(jnp.logical_not(same))
+        place = tile_of(partners[0, 0, k])
+        for x in range(3):
+            @pl.when(place % 6 == 2 * x)
+            def _():
+                kept[x][place // 6] = value
+
+        @pl.when(place % 2 == 1)
         def _():
             lent[(place % 6 > 1).astype(jnp.int32) * 3 + place // 6] = value
 
@@ -289,19 +331,15 @@
     out[...] = total.astype(BF16)
 
 
-def finish_kernel(info, near, near_across, far, far_across, conv, corr, whole):
-    size = near.shape[0] // 2
-    core, low, high = info[6], info[7] & 1, info[7] >> 1
+def finish_kernel(*refs):
+    shards, (conv, corr, whole) = refs[:8], refs[8:]
+    size = shards[0].shape[0]
+    _, chip, core = position()
     half = whole.shape[0] // 2
-    for ref, owner, at in (
-        (near, core, low),
-        (near_across, core, 1 - low),
-        (far, 1 - core, low),
-        (far_across, 1 - core, 1 - low),
-    ):
-        for s in range(2):
-            to = owner * half + at * 2 * size + (high ^ s) * size
-            whole[pl.ds(pl.multiple_of(to, size), size)] = ref[s * size : (s + 1) * size].astype(F32)
+    for n, ref in enumerate(shards):
+        owner = core if n < 4 else 1 - core
+        to = owner * half + (chip ^ (n % 4)) * size
+        whole[pl.ds(pl.multiple_of(to, size), size)] = ref[...].astype(F32)
     conv[...] = whole[: conv.shape[0]]
     base = conv.shape[0]
     for h in range(2):
@@ -320,21 +358,16 @@
     )
 
 
-def sum_weights(sent, kept, chip):
-    cur = kept + swap(sent, "col", 1).astype(F32)
-    for bit in (0, 1):
-        size = cur.shape[0] // 2
-        mine = (chip >> bit) & 1
-        gone = lax.dynamic_slice_in_dim(cur, (1 - mine) * size, size).astype(BF16)
-        cur = lax.dynamic_slice_in_dim(cur, mine * size, size)
-        cur = cur + swap(gone, "col", 2 << bit).astype(F32)
-    for bits in (1, 2, 4, 8):
-        mine = cur.astype(BF16)
-        cur = mine.astype(F32) + swap(mine, "row", bits).astype(F32)
+def halve(cur, mine, axis, bits):
+    size = cur.shape[0] // 2
+    gone = lax.dynamic_slice_in_dim(cur, (1 - mine) * size, size).astype(BF16)
+    return lax.dynamic_slice_in_dim(cur, mine * size, size), swap(gone, axis, bits)
+
+
+def sum_everywhere(cur, axis, unit):
     mine = cur.astype(BF16)
-    near = jnp.concatenate([mine, swap(mine, "col", 4)])
-    across = swap(near, "col", 2)
-    return near, across, swap(near, "col", 1), swap(across, "col", 1)
+    got = [swap(mine, axis, unit * s).astype(F32) for s in (1, 2, 3)]
+    return (mine.astype(F32) + got[0]) + (got[1] + got[2])
 
 
 def body(
@@ -348,21 +381,7 @@
     row, col = lax.axis_index("row"), lax.axis_index("col")
     core, chip = col % 2, col // 2
     row_even, chip_even, col_even = row % 2 == 0, chip % 2 == 0, core == 0
-
-    def role(step, even):
-        step = jnp.asarray(step)
-        return jnp.where(step == 0, 0, jnp.where((step > 0) == even, 1, 2))
-
-    down, across = partners[0, 0] // 5 - 1, partners[0, 0] % 5 - 2
-    chip_step = (core + across) >> 1
-    place = role(down, row_even) * 6 + role(chip_step, chip_even) * 2 + (across & 1)
-    north, south = role(-1, row_even) * 6, role(1, row_even) * 6
-    west = jnp.where(col_even, role(-1, chip_even), 0) * 2 + 1
-    east = jnp.where(col_even, 0, role(1, chip_even)) * 2 + 1
-    beside = [north, south, west, east, north + west, north + east, south + west, south + east]
-    info = jnp.concatenate(
-        [place, counts[0], radius[0], jnp.stack([core, chip, *beside, row % 2])]
-    ).astype(jnp.int32)
+    tables = (partners, counts, radius)
     first = frame_one.reshape(cells, channels)
     shape = jax.ShapeDtypeStruct
     cot = cotangent.reshape(cells, out_width)
@@ -380,16 +399,12 @@
     for r in range(3):
         for x in range(3):
             around += [tiles[r, x], swap(tiles[r, x], "col", 1)]
-    spread = jnp.pad(
-        corr_weight.reshape(slots, SPAN, SPAN, hidden), ((0, 0), (0, 3), (0, 0), (0, 0))
-    )
-    spread = spread.reshape(slots, 3, 4, SPAN, hidden).transpose(0, 2, 1, 3, 4)
-    spread = spread.reshape(slots, 4, 3 * SPAN, hidden)
-    spread, spread_back = (
-        jnp.pad(spread, ((0, 0), (0, 0), (lead, 5 - lead), (0, 0))).reshape(slots * 128, hidden)
-        for lead in (LEAD, LEAD_BACK)
-    )
-    back_weight = conv_weight.transpose(0, 1, 3, 2).reshape(3, 3 * out_width, hidden)
+    spread, spread_back = call(
+        spread_kernel,
+        (shape((slots * 128, hidden), BF16), shape((slots * 128, hidden), BF16)),
+        [VMEM],
+        [pltpu.VMEM((slots * 128, hidden), F32)],
+    )(corr_weight.astype(F32))
     total_rows = 9 * hidden + 2 * 384
     parts, motion, context_grad, facing, away, ends, weights_sent, weights_kept = call(
         forward_kernel,
@@ -403,7 +418,7 @@
             shape((total_rows // 2, 128), BF16),
             shape((total_rows // 2, 128), F32),
         ),
-        [SMEM] + [VMEM] * 5 + [ANY] * 18,
+        [SMEM] * 3 + [VMEM] * 5 + [ANY] * 18,
         [
             pltpu.VMEM((8, 48, channels), BF16),
             pltpu.VMEM(((rows_tile + 2) * cols_tile, 3 * out_width), BF16),
@@ -413,26 +428,42 @@
             pltpu.SemaphoreType.DMA((8,)),
         ],
         flops=3 * 10**9,
-    )(info, first, context.reshape(cells, hidden), cot, back_weight, spread, *around)
-    shards = sum_weights(weights_sent, weights_kept, chip)
-    first_grad, kept, lent = call(
+    )(
+        *tables,
+        first,
+        context.reshape(cells, hidden),
+        cot,
+        conv_weight,
+        spread,
+        *around,
+    )
+    total = weights_kept + swap(weights_sent, "col", 1).astype(F32)
+    total, got = halve(total, chip >> 1, "col", 4)
+    first_grad, *kept, lent = call(
         backward_kernel,
         (
             shape((cells, channels), F32),
-            shape((9, cells, channels), BF16),
+            *[shape((3, cells, channels), BF16)] * 3,
             shape((6, cells, channels), BF16),
         ),
-        [SMEM] + [VMEM] * 4,
+        [SMEM] * 3 + [VMEM] * 4,
         [pltpu.VMEM((slots, cells + 2 * GROUP, channels), F32)],
         flops=3 * 10**9,
-    )(info, first, context_grad, spread_back, parts)
-    lent = swap(lent, "col", 1).reshape(2, 3, cells, channels).astype(F32)
-    kept = kept.reshape(3, 3, cells, channels).astype(F32)
+    )(*tables, first, context_grad, spread_back, parts)
+    lent = swap(lent, "col", 1)
     side = jnp.where((core == 0) == chip_even, 1, 2)
-    middle = kept[0] + lent[0]
+    sent = [
+        (kept[x].astype(F32) + jnp.where(side == x, lent[3:].astype(F32), 0.0)).astype(BF16)
+        for x in (1, 2)
+    ]
+    total, got = halve(total + got.astype(F32), chip & 1, "col", 2)
+    total, sent[0], sent[1] = lax.optimization_barrier((total + got.astype(F32), *sent))
+    middle = kept[0].astype(F32) + lent[:3].astype(F32)
     for x in (1, 2):
-        out = kept[x] + jnp.where(side == x, lent[1], 0.0)
-        middle += swap_pairs(out.astype(BF16), "col", x - 1, 2).astype(F32)
+        middle += swap_pairs(sent[x - 1], "col", x - 1, 2).astype(F32)
+    total = sum_everywhere(sum_everywhere(total, "row", 1), "row", 4).astype(BF16)
+    shards = [total] + [swap(total, "col", 2 * s) for s in (1, 2, 3)]
+    shards += [swap(shard, "col", 1) for shard in shards]
     second_grad = middle[0]
     for r in (1, 2):
         second_grad += swap_pairs(middle[r].astype(BF16), "row", r - 1).astype(F32)
@@ -450,9 +481,9 @@
     conv_total, corr_total = call(
         finish_kernel,
         (shape((9 * hidden, out_width), F32), shape(corr_weight.shape, F32)),
-        [SMEM] + [VMEM] * 4,
+        [VMEM] * 8,
         [pltpu.VMEM((total_rows, 128), F32)],
-    )(info, *shards)
+    )(*shards)
     return (
         features.reshape(rows_tile, cols_tile, out_width),
         context_grad.reshape(rows_tile, cols_tile, hidden),

time: 133 us -> 122 us (0.917)
  waiting for transfers between devices: 29.8 us -> 12.7 us
  starting transfers between devices: 59.1 us -> 67.9 us
  local copies, waits for them, and re-layouts: 6.58 us -> 2.37 us
  Pallas kernels: 27.2 us -> 30.2 us
  other arithmetic: 6.19 us -> 4.32 us
    ppermute x21 -> x26, waiting for transfers between devices: 26 us -> 9.54 us  [swap(): lax.ppermute(array, axis, [(i, i ^ bits) for i in range(lax.axis_size(axi...]
    ppermute x21 -> x26, starting transfers between devices: 25.6 us -> 34.8 us  [swap(): lax.ppermute(array, axis, [(i, i ^ bits) for i in range(lax.axis_size(axi...]
    transpose x1 -> x0, local copies, waits for them, and re-layouts: 2.18 us -> none  [body(): conv_weight.transpose(0, 1, 3, 2).reshape(3, 3 * out_width, hidden)]
    pallas_call x1 -> x2, Pallas kernels: 8.35 us -> 10.4 us  [the longest x1 8.48 us: body(): call(backward_kernel, (shape((cells, channels), F32), *[shape((3, cells,...]
    convert_element_type x8 -> x4, other arithmetic: 3.01 us -> 2.26 us  [the longest x1 1.68 us: body(): corr_weight.astype(F32)]
  transfers between devices with their start and end apart: 37 -> 42, of which waited for: 10 -> 8; matrix products, arithmetic and copies ran while one was open for 6% -> 3% of each run, Pallas kernels for 10% -> 13%
where the time goes in v4:
time: 122 us; the launch traced here: 120 us
  starting transfers between devices  67.9 us (56%)
  Pallas kernels  30.2 us (25%)
  waiting for transfers between devices  12.7 us (10%)
  other arithmetic  4.32 us (4%)
  between operations  2.55 us (2%)
  local copies, waits for them, and re-layouts  2.37 us (2%)
    ppermute x26, starting transfers between devices, swap(): lax.ppermute(array, axis, [(i, i ^ bits) for i in range(lax.axis_size(axi...  34.8 us
    ppermute x16, starting transfers between devices, swap_pairs(): return lax.ppermute(array, axis, pairs)  33.2 us
    pallas_call x1, Pallas kernels, body(): call(forward_kernel, (shape((slots, cells + 2 * GROUP, channels), BF16),...  12.7 us
    ppermute x26, waiting for transfers between devices, swap(): lax.ppermute(array, axis, [(i, i ^ bits) for i in range(lax.axis_size(axi...  9.54 us
    pallas_call x1, Pallas kernels, body(): call(backward_kernel, (shape((cells, channels), F32), *[shape((3, cells,...  8.48 us
    ppermute x16, waiting for transfers between devices, swap_pairs(): return lax.ppermute(array, axis, pairs)  3.2 us
    pallas_call x1, Pallas kernels, body(): call(features_kernel, shape((cells, out_width), BF16), [VMEM] * 6, [pltpu...  2.66 us
    pallas_call x1, Pallas kernels, body(): call(finish_kernel, (shape((9 * hidden, out_width), F32), shape(corr_weig...  2.51 us
  transfers between devices with their start and end apart: 42, of which 8 were waited for; matrix products, arithmetic and copies ran while one was open for 3% of the time, Pallas kernels for 13%

profile of v4, /device:TPU:33, one launch (start us, length us, event | category | flops | bytes accessed | tf_op | source)
XLA Modules:
  0.0 120.1 jit_solution(5788440966286716336)
XLA Ops:
  0.6 1.8 %shard_map.137.refs_0_ = bf16[560,256]{1,0:T(8,128)(2,1)} custom-call(bf16[512,256]{1,0:T(8,128)(2,1)} %bitcast.25, bf16[512,128]{1,0:T(8,128)(2,1)} %bitcast.26), custom_call_target="tpu_custom_call" | custom-call | tf_op jit(solution)/shard_map/pallas_call | solution.py:388
  3.1 3.7 %collective-permute-start.1 = (bf16[560,256]{1,0:T(8,128)(2,1)}, bf16[560,256]{1,0:T(8,128)(2,1)S(1)}, u32[]{:S(2)}, u32[]{:S(2)}) collective-permute-start(bf16[560,256]{1,0:T(8,128)(2,1)} %shard_map.137.refs_0_), channel_id=1, source_target_pairs={{0,2},{2,0},{1,3},{3,1},{4,6},{6,4},{5,7},{7,5},{8,10},{10,8},{9,1... | collective-permute-start | bytes 860168 | tf_op jit(solution)/shard_map/ppermute | solution.py:35
  6.9 4.2 %collective-permute-start.11 = (bf16[560,256]{1,0:T(8,128)(2,1)}, bf16[560,256]{1,0:T(8,128)(2,1)S(1)}, u32[]{:S(2)}, u32[]{:S(2)}) collective-permute-start(bf16[560,256]{1,0:T(8,128)(2,1)} %shard_map.137.refs_0_), channel_id=1, source_target_pairs={{8,16},{16,8},{24,32},{32,24},{40,48},{48,40},{56,64},{64,56},{72,... | collective-permute-start | bytes 860168 | tf_op jit(solution)/shard_map/ppermute | solution.py:35
  11.4 1.8 %collective-permute-start = (bf16[560,256]{1,0:T(8,128)(2,1)}, bf16[560,256]{1,0:T(8,128)(2,1)S(1)}, u32[]{:S(2)}, u32[]{:S(2)}) collective-permute-start(bf16[560,256]{1,0:T(8,128)(2,1)} %shard_map.137.refs_0_), channel_id=1, source_target_pairs={{0,1},{1,0},{2,3},{3,2},{4,5},{5,4},{6,7},{7,6},{8,9},{9,8},{10,11... | collective-permute-start | bytes 860168 | tf_op jit(solution)/shard_map/ppermute | solution.py:25
  13.3 1.2 collective-permute-start.9
  14.4 3.2 %collective-permute-start.13 = (bf16[560,256]{1,0:T(8,128)(2,1)S(1)}, bf16[560,256]{1,0:T(8,128)(2,1)S(1)}, u32[]{:S(2)}, u32[]{:S(2)}) collective-permute-start(bf16[560,256]{1,0:T(8,128)(2,1)S(1)} %collective-permute-done.1.refs_2_), channel_id=1, source_target_pairs={{8,16},{16,8},{24,32},{32,24},{40,48},{48,40},{56,64},{64,56},{72,... | collective-permute-start | bytes 860168 | tf_op jit(solution)/shard_map/ppermute | solution.py:35
  18.9 2.5 %collective-permute-start.7 = (bf16[560,256]{1,0:T(8,128)(2,1)S(1)}, bf16[560,256]{1,0:T(8,128)(2,1)S(1)}, u32[]{:S(2)}, u32[]{:S(2)}) collective-permute-start(bf16[560,256]{1,0:T(8,128)(2,1)S(1)} %collective-permute-done.5.refs_6_), channel_id=1, source_target_pairs={{0,2},{2,0},{1,3},{3,1},{4,6},{6,4},{5,7},{7,5},{8,10},{10,8},{9,1... | collective-permute-start | bytes 860168 | tf_op jit(solution)/shard_map/ppermute | solution.py:35
  21.4 2.7 %collective-permute-start.12 = (bf16[560,256]{1,0:T(8,128)(2,1)S(1)}, bf16[560,256]{1,0:T(8,128)(2,1)S(1)}, u32[]{:S(2)}, u32[]{:S(2)}) collective-permute-start(bf16[560,256]{1,0:T(8,128)(2,1)S(1)} %collective-permute-done.11.refs_12_), channel_id=1, source_target_pairs={{0,1},{1,0},{2,3},{3,2},{4,5},{5,4},{6,7},{7,6},{8,9},{9,8},{10,11... | collective-permute-start | bytes 860168 | tf_op jit(solution)/shard_map/ppermute | solution.py:25
  24.3 2.4 %collective-permute-start.2 = (bf16[560,256]{1,0:T(8,128)(2,1)S(1)}, bf16[560,256]{1,0:T(8,128)(2,1)S(1)}, u32[]{:S(2)}, u32[]{:S(2)}) collective-permute-start(bf16[560,256]{1,0:T(8,128)(2,1)S(1)} %collective-permute-done.1.refs_2_), channel_id=1, source_target_pairs={{0,1},{1,0},{2,3},{3,2},{4,5},{5,4},{6,7},{7,6},{8,9},{9,8},{10,11... | collective-permute-start | bytes 860168 | tf_op jit(solution)/shard_map/ppermute | solution.py:25
  27.8 1.5 %collective-permute-start.10 = (bf16[560,256]{1,0:T(8,128)(2,1)S(1)}, bf16[560,256]{1,0:T(8,128)(2,1)S(1)}, u32[]{:S(2)}, u32[]{:S(2)}) collective-permute-start(bf16[560,256]{1,0:T(8,128)(2,1)S(1)} %collective-permute-done.9.refs_10_), channel_id=1, source_target_pairs={{0,1},{1,0},{2,3},{3,2},{4,5},{5,4},{6,7},{7,6},{8,9},{9,8},{10,11... | collective-permute-start | bytes 860168 | tf_op jit(solution)/shard_map/ppermute | solution.py:25
  29.9 1.7 %convert_element_type.93.weight = f32[324,256]{1,0:T(8,128)} convert(bf16[324,256]{1,0:T(8,128)(2,1)} %param.13) | non-fusion elementwise | flops 82944 | bytes 497664 | tf_op jit(solution)/shard_map/convert_element_type | solution.py:407
  31.6 2.0 %shard_map.136 = (bf16[512,256]{1,0:T(8,128)(2,1)}, bf16[512,256]{1,0:T(8,128)(2,1)}) custom-call(f32[324,256]{1,0:T(8,128)} %convert_element_type.93.weight), custom_call_target="tpu_custom_call" | custom-call | tf_op jit(solution)/shard_map/pallas_call | solution.py:402
  35.9 12.7 %shard_map.138 = (bf16[4,768,256]{2,1,0:T(8,128)(2,1)}, bf16[512,256]{1,0:T(8,128)(2,1)}, bf16[512,256]{1,0:T(8,128)(2,1)}, bf16[32,256]{1,0:T(8,128)(2,1)}, bf1...) custom-call(s32[1,1,4]{2,1,0:T(1,128)} %partners.3, ...), custom_call_target="tpu_custom_call" | custom-call | flops 3000000000 | bytes 10000000 | tf_op jit(solution)/shard_map/pallas_call | solution.py:409
  49.3 8.5 %shard_map.140 = (f32[512,256]{1,0:T(8,128)}, bf16[3,512,256]{2,1,0:T(8,128)(2,1)}, bf16[3,512,256]{2,1,0:T(8,128)(2,1)}, bf16[3,512,256]{2,1,0:T(8,128)(2,1)}, bf16[6,512,256]{2,1,0:T(8,128)(2,1)}) custom-call(s32[1,1,4]{2,1,0:T(1,128)} %partners.3, s32[1,1]{1,0:T(1,128)S(6)} %copy.15.counts, s32[1,1]{1,0:T(1,128)S(6)} %copy.16.radius, ...), custom_call_target="tpu_custom_call" | custom-call | flops 3000000000 | bytes 10000000 | tf_op jit(solution)/shard_map/pallas_call | solution.py:442
  57.9 3.9 %collective-permute-start.17 = (bf16[32,256]{1,0:T(8,128)(2,1)S(1)}, bf16[32,256]{1,0:T(8,128)(2,1)S(1)}, u32[]{:S(2)}, u32[]{:S(2)}) collective-permute-start(bf16[32,256]{1,0:T(8,128)(2,1)S(1)} %copy-done.33), channel_id=1, source_target_pairs={{8,16},{16,8},{24,32},{32,24},{40,48},{48,40},{56,64},{64,56},{72,... | collective-permute-start | bytes 49160 | tf_op jit(solution)/shard_map/ppermute | solution.py:35
  62.1 2.6 %collective-permute-start.23 = (bf16[768,128]{1,0:T(8,128)(2,1)S(1)}, bf16[768,128]{1,0:T(8,128)(2,1)S(1)}, u32[]{:S(2)}, u32[]{:S(2)}) collective-permute-start(bf16[768,128]{1,0:T(8,128)(2,1)S(1)} %dynamic-slice_convert_fusion), channel_id=1, source_target_pairs={{0,4},{1,5},{2,6},{3,7},{4,0},{5,1},{6,2},{7,3},{8,12},{9,13},{10,... | collective-permute-start | bytes 589832 | tf_op jit(solution)/shard_map/ppermute | solution.py:25
  64.7 4.9 %collective-permute-done.23 = bf16[768,128]{1,0:T(8,128)(2,1)S(1)} collective-permute-done((bf16[768,128]{1,0:T(8,128)(2,1)S(1)}, bf16[768,128]{1,0:T(8,128)(2,1)S(1)}, u32[]{:S(2)}, u32[]{:S(2)}) %collective-permute-start.23) | collective-permute-done | bytes 196640 | tf_op jit(solution)/shard_map/ppermute | solution.py:25
  69.7 1.6 %collective-permute-start.24 = (bf16[384,128]{1,0:T(8,128)(2,1)S(1)}, bf16[384,128]{1,0:T(8,128)(2,1)S(1)}, u32[]{:S(2)}, u32[]{:S(2)}) collective-permute-start(bf16[384,128]{1,0:T(8,128)(2,1)S(1)} %dynamic-slice_convert_fusion.1), channel_id=1, source_target_pairs={{0,2},{1,3},{2,0},{3,1},{4,6},{5,7},{6,4},{7,5},{8,10},{9,11},{10,... | collective-permute-start | bytes 294920 | tf_op jit(solution)/shard_map/ppermute | solution.py:25
  71.3 2.0 %collective-permute-done.24 = bf16[384,128]{1,0:T(8,128)(2,1)S(1)} collective-permute-done((bf16[384,128]{1,0:T(8,128)(2,1)S(1)}, bf16[384,128]{1,0:T(8,128)(2,1)S(1)}, u32[]{:S(2)}, u32[]{:S(2)}) %collective-permute-start.24) | collective-permute-done | bytes 98336 | tf_op jit(solution)/shard_map/ppermute | solution.py:25
  73.8 1.2 collective-permute-start.29
  75.0 2.0 %collective-permute-start.30 = (bf16[384,128]{1,0:T(8,128)(2,1)S(1)}, bf16[384,128]{1,0:T(8,128)(2,1)S(1)}, u32[]{:S(2)}, u32[]{:S(2)}) collective-permute-start(bf16[384,128]{1,0:T(8,128)(2,1)S(1)} %convert_add_fusion.3), channel_id=1, source_target_pairs={{0,16},{8,24},{16,0},{24,8},{32,48},{40,56},{48,32},{56,40},{64,80... | collective-permute-start | bytes 294920 | tf_op jit(solution)/shard_map/ppermute | solution.py:25
  77.8 1.5 %collective-permute-start.25 = (bf16[3,512,256]{2,1,0:T(8,128)(2,1)S(1)}, bf16[3,512,256]{2,1,0:T(8,128)(2,1)S(1)}, u32[]{:S(2)}, u32[]{:S(2)}) collective-permute-start(bf16[3,512,256]{2,1,0:T(8,128)(2,1)S(1)} %get-tuple-element.41), channel_id=1, source_target_pairs={{0,2},{2,0},{1,3},{3,1},{4,6},{6,4},{5,7},{7,5},{8,10},{10,8},{9,1... | collective-permute-start | bytes 2359304 | tf_op jit(solution)/shard_map/ppermute | solution.py:35
  80.1 1.6 %collective-permute-done.31 = bf16[384,128]{1,0:T(8,128)(2,1)S(1)} collective-permute-done((bf16[384,128]{1,0:T(8,128)(2,1)S(1)}, bf16[384,128]{1,0:T(8,128)(2,1)S(1)}, u32[]{:S(2)}, u32[]{:S(2)}) %collective-permute-start.31) | collective-permute-done | bytes 98336 | tf_op jit(solution)/shard_map/ppermute | solution.py:25
  81.8 2.8 %collective-permute-start.33 = (bf16[384,128]{1,0:T(8,128)(2,1)S(1)}, bf16[384,128]{1,0:T(8,128)(2,1)S(1)}, u32[]{:S(2)}, u32[]{:S(2)}) collective-permute-start(bf16[384,128]{1,0:T(8,128)(2,1)S(1)} %add_convert_fusion.1), channel_id=1, source_target_pairs={{0,64},{8,72},{16,80},{24,88},{32,96},{40,104},{48,112},{56,120},{... | collective-permute-start | bytes 294920 | tf_op jit(solution)/shard_map/ppermute | solution.py:25
  85.6 8.3 %collective-permute-start.19 = (bf16[18,256]{1,0:T(8,128)(2,1)S(1)}, bf16[18,256]{1,0:T(8,128)(2,1)S(1)}, u32[]{:S(2)}, u32[]{:S(2)}) collective-permute-start(bf16[18,256]{1,0:T(8,128)(2,1)S(1)} %get-tuple-element.57), channel_id=1, source_target_pairs={{1,2},{2,1},{3,4},{4,3},{5,6},{6,5},{9,10},{10,9},{11,12},{12,11},... | collective-permute-start | bytes 27656 | tf_op jit(solution)/shard_map/ppermute | solution.py:35
  95.8 2.2 %collective-permute-start.37 = (bf16[384,128]{1,0:T(8,128)(2,1)S(1)}, bf16[384,128]{1,0:T(8,128)(2,1)S(1)}, u32[]{:S(2)}, u32[]{:S(2)}) collective-permute-start(bf16[384,128]{1,0:T(8,128)(2,1)S(1)} %add_convert_fusion.refs_0_), channel_id=1, source_target_pairs={{0,6},{1,7},{2,4},{3,5},{4,2},{5,3},{6,0},{7,1},{8,14},{9,15},{10,... | collective-permute-start | bytes 294920 | tf_op jit(solution)/shard_map/ppermute | solution.py:25
  98.5 5.5 %collective-permute-start.38 = (bf16[384,128]{1,0:T(8,128)(2,1)S(1)}, bf16[384,128]{1,0:T(8,128)(2,1)S(1)}, u32[]{:S(2)}, u32[]{:S(2)}) collective-permute-start(bf16[384,128]{1,0:T(8,128)(2,1)S(1)} %add_convert_fusion.refs_0_), channel_id=1, source_target_pairs={{0,1},{1,0},{2,3},{3,2},{4,5},{5,4},{6,7},{7,6},{8,9},{9,8},{10,11... | collective-permute-start | bytes 294920 | tf_op jit(solution)/shard_map/ppermute | solution.py:25
  104.7 2.9 %collective-permute-start.41 = (bf16[384,128]{1,0:T(8,128)(2,1)S(1)}, bf16[384,128]{1,0:T(8,128)(2,1)S(1)}, u32[]{:S(2)}, u32[]{:S(2)}) collective-permute-start(bf16[384,128]{1,0:T(8,128)(2,1)S(1)} %collective-permute-done.37.refs_3_), channel_id=1, source_target_pairs={{0,1},{1,0},{2,3},{3,2},{4,5},{5,4},{6,7},{7,6},{8,9},{9,8},{10,11... | collective-permute-start | bytes 294920 | tf_op jit(solution)/shard_map/ppermute | solution.py:25
  107.7 2.0 %collective-permute-start.28 = (bf16[512,256]{1,0:T(8,128)(2,1)S(1)}, bf16[512,256]{1,0:T(8,128)(2,1)S(1)}, u32[]{:S(2)}, u32[]{:S(2)}) collective-permute-start(bf16[512,256]{1,0:T(8,128)(2,1)S(1)} %get-tuple-element.51), channel_id=1, source_target_pairs={{8,16},{16,8},{24,32},{32,24},{40,48},{48,40},{56,64},{64,56},{72,... | collective-permute-start | bytes 786440 | tf_op jit(solution)/shard_map/ppermute | solution.py:35
  110.3 2.7 %shard_map.139 = bf16[512,128]{1,0:T(8,128)(2,1)} custom-call(bf16[512,256]{1,0:T(8,128)(2,1)} %get-tuple-element.27.motion, bf16[32,256]{1,0:T(8,128)(2,1)} %copy-done.13, bf16[32,256]{1,0:T(8,128)(2,1)} %copy-done.12, bf16[18,256]{1,0:T(8,128)(2,1)} %get-tuple-element.55.west, bf16[18,256]{1,0:T(8,128)(2,1)} %get-tuple-element.54.east, ...), custom_call_target="tpu_custom_call" | custom-call | flops 1000000000 | bytes 3333333 | tf_op jit(solution)/shard_map/pallas_call | solution.py:470
  114.3 2.5 %shard_map.141 = (f32[2304,128]{1,0:T(8,128)}, f32[324,256]{1,0:T(8,128)}) custom-call(bf16[384,128]{1,0:T(8,128)(2,1)} %copy-done.4, bf16[384,128]{1,0:T(8,128)(2,1)} %copy-done.5, bf16[384,128]{1,0:T(8,128)(2,1)} %copy-done.6, bf16[384,128]{1,0:T(8,128)(2,1)} %copy-done.7, bf16[384,128]{1,0:T(8,128)(2,1)} %copy-done.8, bf16[384,128]{1,0:T(8,128)(2,1)} %copy-done.9, ...), custom_call_target="tpu_custom_call" | custom-call | tf_op jit(solution)/shard_map/pallas_call | solution.py:481
  116.8 2.4 %collective-permute-done.28 = bf16[512,256]{1,0:T(8,128)(2,1)S(1)} collective-permute-done((bf16[512,256]{1,0:T(8,128)(2,1)S(1)}, bf16[512,256]{1,0:T(8,128)(2,1)S(1)}, u32[]{:S(2)}, u32[]{:S(2)}) %collective-permute-start.28) | collective-permute-done | bytes 262176 | tf_op jit(solution)/shard_map/ppermute | solution.py:35
  (143 shorter events, 15.2 us)
Async XLA Ops:
  2.5 10.8 %collective-permute-start.3 = (bf16[560,256]{1,0:T(8,128)(2,1)}, bf16[560,256]{1,0:T(8,128)(2,1)S(1)}, u32[]{:S(2)}, u32[]{:S(2)}) collective-permute-start(bf16[560,256]{1,0:T(8,128)(2,1)} %shard_map.137.refs_0_), channel_id=1, source_target_pairs={{2,4},{4,2},{3,5},{5,3},{10,12},{12,10},{11,13},{13,11},{18,20},{2... | collective-permute-start | bytes 860168 | tf_op jit(solution)/shard_map/ppermute | solution.py:35
  3.1 11.3 %collective-permute-start.1 = (bf16[560,256]{1,0:T(8,128)(2,1)}, bf16[560,256]{1,0:T(8,128)(2,1)S(1)}, u32[]{:S(2)}, u32[]{:S(2)}) collective-permute-start(bf16[560,256]{1,0:T(8,128)(2,1)} %shard_map.137.refs_0_), channel_id=1, source_target_pairs={{0,2},{2,0},{1,3},{3,1},{4,6},{6,4},{5,7},{7,5},{8,10},{10,8},{9,1... | collective-permute-start | bytes 860168 | tf_op jit(solution)/shard_map/ppermute | solution.py:35
  6.9 11.3 %collective-permute-start.11 = (bf16[560,256]{1,0:T(8,128)(2,1)}, bf16[560,256]{1,0:T(8,128)(2,1)S(1)}, u32[]{:S(2)}, u32[]{:S(2)}) collective-permute-start(bf16[560,256]{1,0:T(8,128)(2,1)} %shard_map.137.refs_0_), channel_id=1, source_target_pairs={{8,16},{16,8},{24,32},{32,24},{40,48},{48,40},{56,64},{64,56},{72,... | collective-permute-start | bytes 860168 | tf_op jit(solution)/shard_map/ppermute | solution.py:35
  11.1 7.8 %collective-permute-start.5 = (bf16[560,256]{1,0:T(8,128)(2,1)}, bf16[560,256]{1,0:T(8,128)(2,1)S(1)}, u32[]{:S(2)}, u32[]{:S(2)}) collective-permute-start(bf16[560,256]{1,0:T(8,128)(2,1)} %shard_map.137.refs_0_), channel_id=1, source_target_pairs={{0,8},{8,0},{16,24},{24,16},{32,40},{40,32},{48,56},{56,48},{64,72... | collective-permute-start | bytes 860168 | tf_op jit(solution)/shard_map/ppermute | solution.py:35
  11.4 9.9 %collective-permute-start = (bf16[560,256]{1,0:T(8,128)(2,1)}, bf16[560,256]{1,0:T(8,128)(2,1)S(1)}, u32[]{:S(2)}, u32[]{:S(2)}) collective-permute-start(bf16[560,256]{1,0:T(8,128)(2,1)} %shard_map.137.refs_0_), channel_id=1, source_target_pairs={{0,1},{1,0},{2,3},{3,2},{4,5},{5,4},{6,7},{7,6},{8,9},{9,8},{10,11... | collective-permute-start | bytes 860168 | tf_op jit(solution)/shard_map/ppermute | solution.py:25
  13.3 11.0 %collective-permute-start.9 = (bf16[560,256]{1,0:T(8,128)(2,1)S(1)}, bf16[560,256]{1,0:T(8,128)(2,1)S(1)}, u32[]{:S(2)}, u32[]{:S(2)}) collective-permute-start(bf16[560,256]{1,0:T(8,128)(2,1)S(1)} %collective-permute-done.3.refs_4_), channel_id=1, source_target_pairs={{0,8},{8,0},{16,24},{24,16},{32,40},{40,32},{48,56},{56,48},{64,72... | collective-permute-start | bytes 860168 | tf_op jit(solution)/shard_map/ppermute | solution.py:35
  14.4 12.3 %collective-permute-start.13 = (bf16[560,256]{1,0:T(8,128)(2,1)S(1)}, bf16[560,256]{1,0:T(8,128)(2,1)S(1)}, u32[]{:S(2)}, u32[]{:S(2)}) collective-permute-start(bf16[560,256]{1,0:T(8,128)(2,1)S(1)} %collective-permute-done.1.refs_2_), channel_id=1, source_target_pairs={{8,16},{16,8},{24,32},{32,24},{40,48},{48,40},{56,64},{64,56},{72,... | collective-permute-start | bytes 860168 | tf_op jit(solution)/shard_map/ppermute | solution.py:35
  18.2 9.5 %collective-permute-start.15 = (bf16[560,256]{1,0:T(8,128)(2,1)S(1)}, bf16[560,256]{1,0:T(8,128)(2,1)S(1)}, u32[]{:S(2)}, u32[]{:S(2)}) collective-permute-start(bf16[560,256]{1,0:T(8,128)(2,1)S(1)} %collective-permute-done.11.refs_12_), channel_id=1, source_target_pairs={{2,4},{4,2},{3,5},{5,3},{10,12},{12,10},{11,13},{13,11},{18,20},{2... | collective-permute-start | bytes 860168 | tf_op jit(solution)/shard_map/ppermute | solution.py:35
  18.9 8.9 %collective-permute-start.7 = (bf16[560,256]{1,0:T(8,128)(2,1)S(1)}, bf16[560,256]{1,0:T(8,128)(2,1)S(1)}, u32[]{:S(2)}, u32[]{:S(2)}) collective-permute-start(bf16[560,256]{1,0:T(8,128)(2,1)S(1)} %collective-permute-done.5.refs_6_), channel_id=1, source_target_pairs={{0,2},{2,0},{1,3},{3,1},{4,6},{6,4},{5,7},{7,5},{8,10},{10,8},{9,1... | collective-permute-start | bytes 860168 | tf_op jit(solution)/shard_map/ppermute | solution.py:35
  21.4 7.9 %collective-permute-start.12 = (bf16[560,256]{1,0:T(8,128)(2,1)S(1)}, bf16[560,256]{1,0:T(8,128)(2,1)S(1)}, u32[]{:S(2)}, u32[]{:S(2)}) collective-permute-start(bf16[560,256]{1,0:T(8,128)(2,1)S(1)} %collective-permute-done.11.refs_12_), channel_id=1, source_target_pairs={{0,1},{1,0},{2,3},{3,2},{4,5},{5,4},{6,7},{7,6},{8,9},{9,8},{10,11... | collective-permute-start | bytes 860168 | tf_op jit(solution)/shard_map/ppermute | solution.py:25
  27.7 7.2 %collective-permute-start.6 = (bf16[560,256]{1,0:T(8,128)(2,1)S(1)}, bf16[560,256]{1,0:T(8,128)(2,1)S(1)}, u32[]{:S(2)}, u32[]{:S(2)}) collective-permute-start(bf16[560,256]{1,0:T(8,128)(2,1)S(1)} %collective-permute-done.5.refs_6_), channel_id=1, source_target_pairs={{0,1},{1,0},{2,3},{3,2},{4,5},{5,4},{6,7},{7,6},{8,9},{9,8},{10,11... | collective-permute-start | bytes 860168 | tf_op jit(solution)/shard_map/ppermute | solution.py:25
  27.8 7.1 %collective-permute-start.10 = (bf16[560,256]{1,0:T(8,128)(2,1)S(1)}, bf16[560,256]{1,0:T(8,128)(2,1)S(1)}, u32[]{:S(2)}, u32[]{:S(2)}) collective-permute-start(bf16[560,256]{1,0:T(8,128)(2,1)S(1)} %collective-permute-done.9.refs_10_), channel_id=1, source_target_pairs={{0,1},{1,0},{2,3},{3,2},{4,5},{5,4},{6,7},{7,6},{8,9},{9,8},{10,11... | collective-permute-start | bytes 860168 | tf_op jit(solution)/shard_map/ppermute | solution.py:25
  48.7 13.3 %collective-permute-start.22 = (bf16[1536,128]{1,0:T(8,128)(2,1)}, bf16[1536,128]{1,0:T(8,128)(2,1)S(1)}, u32[]{:S(2)}, u32[]{:S(2)}) collective-permute-start(bf16[1536,128]{1,0:T(8,128)(2,1)} %get-tuple-element.38), channel_id=1, source_target_pairs={{0,1},{1,0},{2,3},{3,2},{4,5},{5,4},{6,7},{7,6},{8,9},{9,8},{10,11... | collective-permute-start | bytes 1179656 | tf_op jit(solution)/shard_map/ppermute | solution.py:25
  57.8 15.5 %collective-permute-start.21 = (bf16[6,512,256]{2,1,0:T(8,128)(2,1)}, bf16[6,512,256]{2,1,0:T(8,128)(2,1)S(1)}, u32[]{:S(2)}, u32[]{:S(2)}) collective-permute-start(bf16[6,512,256]{2,1,0:T(8,128)(2,1)} %get-tuple-element.36), channel_id=1, source_target_pairs={{0,1},{1,0},{2,3},{3,2},{4,5},{5,4},{6,7},{7,6},{8,9},{9,8},{10,11... | collective-permute-start | bytes 4718600 | tf_op jit(solution)/shard_map/ppermute | solution.py:25
  57.9 13.3 %collective-permute-start.17 = (bf16[32,256]{1,0:T(8,128)(2,1)S(1)}, bf16[32,256]{1,0:T(8,128)(2,1)S(1)}, u32[]{:S(2)}, u32[]{:S(2)}) collective-permute-start(bf16[32,256]{1,0:T(8,128)(2,1)S(1)} %copy-done.33), channel_id=1, source_target_pairs={{8,16},{16,8},{24,32},{32,24},{40,48},{48,40},{56,64},{64,56},{72,... | collective-permute-start | bytes 49160 | tf_op jit(solution)/shard_map/ppermute | solution.py:35
  61.9 9.4 %collective-permute-start.18 = (bf16[32,256]{1,0:T(8,128)(2,1)S(1)}, bf16[32,256]{1,0:T(8,128)(2,1)S(1)}, u32[]{:S(2)}, u32[]{:S(2)}) collective-permute-start(bf16[32,256]{1,0:T(8,128)(2,1)S(1)} %copy-done.32), channel_id=1, source_target_pairs={{0,8},{8,0},{16,24},{24,16},{32,40},{40,32},{48,56},{56,48},{64,72... | collective-permute-start | bytes 49160 | tf_op jit(solution)/shard_map/ppermute | solution.py:35
  62.1 7.5 %collective-permute-start.23 = (bf16[768,128]{1,0:T(8,128)(2,1)S(1)}, bf16[768,128]{1,0:T(8,128)(2,1)S(1)}, u32[]{:S(2)}, u32[]{:S(2)}) collective-permute-start(bf16[768,128]{1,0:T(8,128)(2,1)S(1)} %dynamic-slice_convert_fusion), channel_id=1, source_target_pairs={{0,4},{1,5},{2,6},{3,7},{4,0},{5,1},{6,2},{7,3},{8,12},{9,13},{10,... | collective-permute-start | bytes 589832 | tf_op jit(solution)/shard_map/ppermute | solution.py:25
  77.8 17.2 %collective-permute-start.25 = (bf16[3,512,256]{2,1,0:T(8,128)(2,1)S(1)}, bf16[3,512,256]{2,1,0:T(8,128)(2,1)S(1)}, u32[]{:S(2)}, u32[]{:S(2)}) collective-permute-start(bf16[3,512,256]{2,1,0:T(8,128)(2,1)S(1)} %get-tuple-element.41), channel_id=1, source_target_pairs={{0,2},{2,0},{1,3},{3,1},{4,6},{6,4},{5,7},{7,5},{8,10},{10,8},{9,1... | collective-permute-start | bytes 2359304 | tf_op jit(solution)/shard_map/ppermute | solution.py:35
  79.2 16.6 %collective-permute-start.26 = (bf16[3,512,256]{2,1,0:T(8,128)(2,1)S(1)}, bf16[3,512,256]{2,1,0:T(8,128)(2,1)S(1)}, u32[]{:S(2)}, u32[]{:S(2)}) collective-permute-start(bf16[3,512,256]{2,1,0:T(8,128)(2,1)S(1)} %get-tuple-element.42), channel_id=1, source_target_pairs={{2,4},{4,2},{3,5},{5,3},{10,12},{12,10},{11,13},{13,11},{18,20},{2... | collective-permute-start | bytes 2359304 | tf_op jit(solution)/shard_map/ppermute | solution.py:35
  81.8 12.0 %collective-permute-start.33 = (bf16[384,128]{1,0:T(8,128)(2,1)S(1)}, bf16[384,128]{1,0:T(8,128)(2,1)S(1)}, u32[]{:S(2)}, u32[]{:S(2)}) collective-permute-start(bf16[384,128]{1,0:T(8,128)(2,1)S(1)} %add_convert_fusion.1), channel_id=1, source_target_pairs={{0,64},{8,72},{16,80},{24,88},{32,96},{40,104},{48,112},{56,120},{... | collective-permute-start | bytes 294920 | tf_op jit(solution)/shard_map/ppermute | solution.py:25
  84.6 9.4 %collective-permute-start.34 = (bf16[384,128]{1,0:T(8,128)(2,1)S(1)}, bf16[384,128]{1,0:T(8,128)(2,1)S(1)}, u32[]{:S(2)}, u32[]{:S(2)}) collective-permute-start(bf16[384,128]{1,0:T(8,128)(2,1)S(1)} %add_convert_fusion.1), channel_id=1, source_target_pairs={{0,96},{8,104},{16,112},{24,120},{32,64},{40,72},{48,80},{56,88},{... | collective-permute-start | bytes 294920 | tf_op jit(solution)/shard_map/ppermute | solution.py:25
  85.6 12.9 %collective-permute-start.19 = (bf16[18,256]{1,0:T(8,128)(2,1)S(1)}, bf16[18,256]{1,0:T(8,128)(2,1)S(1)}, u32[]{:S(2)}, u32[]{:S(2)}) collective-permute-start(bf16[18,256]{1,0:T(8,128)(2,1)S(1)} %get-tuple-element.57), channel_id=1, source_target_pairs={{1,2},{2,1},{3,4},{4,3},{5,6},{6,5},{9,10},{10,9},{11,12},{12,11},... | collective-permute-start | bytes 27656 | tf_op jit(solution)/shard_map/ppermute | solution.py:35
  93.9 13.7 %collective-permute-start.20 = (bf16[18,256]{1,0:T(8,128)(2,1)S(1)}, bf16[18,256]{1,0:T(8,128)(2,1)S(1)}, u32[]{:S(2)}, u32[]{:S(2)}) collective-permute-start(bf16[18,256]{1,0:T(8,128)(2,1)S(1)} %get-tuple-element.56), channel_id=1, source_target_pairs={{0,1},{1,0},{2,3},{3,2},{4,5},{5,4},{6,7},{7,6},{8,9},{9,8},{10,11... | collective-permute-start | bytes 27656 | tf_op jit(solution)/shard_map/ppermute | solution.py:35
  94.1 10.0 %collective-permute-start.35 = (bf16[384,128]{1,0:T(8,128)(2,1)S(1)}, bf16[384,128]{1,0:T(8,128)(2,1)S(1)}, u32[]{:S(2)}, u32[]{:S(2)}) collective-permute-start(bf16[384,128]{1,0:T(8,128)(2,1)S(1)} %add_convert_fusion.refs_0_), channel_id=1, source_target_pairs={{0,2},{1,3},{2,0},{3,1},{4,6},{5,7},{6,4},{7,5},{8,10},{9,11},{10,... | collective-permute-start | bytes 294920 | tf_op jit(solution)/shard_map/ppermute | solution.py:25
  95.0 9.2 %collective-permute-start.36 = (bf16[384,128]{1,0:T(8,128)(2,1)S(1)}, bf16[384,128]{1,0:T(8,128)(2,1)S(1)}, u32[]{:S(2)}, u32[]{:S(2)}) collective-permute-start(bf16[384,128]{1,0:T(8,128)(2,1)S(1)} %add_convert_fusion.refs_0_), channel_id=1, source_target_pairs={{0,4},{1,5},{2,6},{3,7},{4,0},{5,1},{6,2},{7,3},{8,12},{9,13},{10,... | collective-permute-start | bytes 294920 | tf_op jit(solution)/shard_map/ppermute | solution.py:25
  95.8 8.8 %collective-permute-start.37 = (bf16[384,128]{1,0:T(8,128)(2,1)S(1)}, bf16[384,128]{1,0:T(8,128)(2,1)S(1)}, u32[]{:S(2)}, u32[]{:S(2)}) collective-permute-start(bf16[384,128]{1,0:T(8,128)(2,1)S(1)} %add_convert_fusion.refs_0_), channel_id=1, source_target_pairs={{0,6},{1,7},{2,4},{3,5},{4,2},{5,3},{6,0},{7,1},{8,14},{9,15},{10,... | collective-permute-start | bytes 294920 | tf_op jit(solution)/shard_map/ppermute | solution.py:25
  98.5 9.2 %collective-permute-start.38 = (bf16[384,128]{1,0:T(8,128)(2,1)S(1)}, bf16[384,128]{1,0:T(8,128)(2,1)S(1)}, u32[]{:S(2)}, u32[]{:S(2)}) collective-permute-start(bf16[384,128]{1,0:T(8,128)(2,1)S(1)} %add_convert_fusion.refs_0_), channel_id=1, source_target_pairs={{0,1},{1,0},{2,3},{3,2},{4,5},{5,4},{6,7},{7,6},{8,9},{9,8},{10,11... | collective-permute-start | bytes 294920 | tf_op jit(solution)/shard_map/ppermute | solution.py:25
  104.1 9.0 %collective-permute-start.39 = (bf16[384,128]{1,0:T(8,128)(2,1)S(1)}, bf16[384,128]{1,0:T(8,128)(2,1)S(1)}, u32[]{:S(2)}, u32[]{:S(2)}) collective-permute-start(bf16[384,128]{1,0:T(8,128)(2,1)S(1)} %collective-permute-done.35.refs_1_), channel_id=1, source_target_pairs={{0,1},{1,0},{2,3},{3,2},{4,5},{5,4},{6,7},{7,6},{8,9},{9,8},{10,11... | collective-permute-start | bytes 294920 | tf_op jit(solution)/shard_map/ppermute | solution.py:25
  104.2 8.9 %collective-permute-start.40 = (bf16[384,128]{1,0:T(8,128)(2,1)S(1)}, bf16[384,128]{1,0:T(8,128)(2,1)S(1)}, u32[]{:S(2)}, u32[]{:S(2)}) collective-permute-start(bf16[384,128]{1,0:T(8,128)(2,1)S(1)} %collective-permute-done.36.refs_2_), channel_id=1, source_target_pairs={{0,1},{1,0},{2,3},{3,2},{4,5},{5,4},{6,7},{7,6},{8,9},{9,8},{10,11... | collective-permute-start | bytes 294920 | tf_op jit(solution)/shard_map/ppermute | solution.py:25
  104.7 8.4 %collective-permute-start.41 = (bf16[384,128]{1,0:T(8,128)(2,1)S(1)}, bf16[384,128]{1,0:T(8,128)(2,1)S(1)}, u32[]{:S(2)}, u32[]{:S(2)}) collective-permute-start(bf16[384,128]{1,0:T(8,128)(2,1)S(1)} %collective-permute-done.37.refs_3_), channel_id=1, source_target_pairs={{0,1},{1,0},{2,3},{3,2},{4,5},{5,4},{6,7},{7,6},{8,9},{9,8},{10,11... | collective-permute-start | bytes 294920 | tf_op jit(solution)/shard_map/ppermute | solution.py:25
  107.6 9.3 %collective-permute-start.27 = (bf16[512,256]{1,0:T(8,128)(2,1)S(1)}, bf16[512,256]{1,0:T(8,128)(2,1)S(1)}, u32[]{:S(2)}, u32[]{:S(2)}) collective-permute-start(bf16[512,256]{1,0:T(8,128)(2,1)S(1)} %get-tuple-element.50), channel_id=1, source_target_pairs={{0,8},{8,0},{16,24},{24,16},{32,40},{40,32},{48,56},{56,48},{64,72... | collective-permute-start | bytes 786440 | tf_op jit(solution)/shard_map/ppermute | solution.py:35
  107.7 11.5 %collective-permute-start.28 = (bf16[512,256]{1,0:T(8,128)(2,1)S(1)}, bf16[512,256]{1,0:T(8,128)(2,1)S(1)}, u32[]{:S(2)}, u32[]{:S(2)}) collective-permute-start(bf16[512,256]{1,0:T(8,128)(2,1)S(1)} %get-tuple-element.51), channel_id=1, source_target_pairs={{8,16},{16,8},{24,32},{32,24},{40,48},{48,40},{56,64},{64,56},{72,... | collective-permute-start | bytes 786440 | tf_op jit(solution)/shard_map/ppermute | solution.py:35
  (44 other events, 334.5 us)

commit v5 on v4

--- a/solution.py
+++ b/solution.py
@@ -141,21 +141,21 @@
     return [north, south, west, east, north + west, north + east, south + west, south + east]
 
 
-def spread_kernel(weight, out, out_back, wide):
-    for lead, ref in ((LEAD, out), (LEAD_BACK, out_back)):
-        wide[...] = jnp.zeros_like(wide)
-        for k in range(4):
-            for u in range(SPAN):
-                row = k * 128 + (u % 4) * 32 + (u // 4) * SPAN + lead
-                at = (k * SPAN + u) * SPAN
-                wide[row : row + SPAN] = weight[at : at + SPAN]
-        ref[...] = wide[...].astype(BF16)
+def spread_rows(weight, narrow, wide, lead):
+    narrow[...] = weight[...].astype(F32)
+    wide[...] = jnp.zeros_like(wide)
+    for k in range(wide.shape[0] // 128):
+        for u in range(SPAN):
+            row = k * 128 + (u % 4) * 32 + (u // 4) * SPAN + lead
+            at = (k * SPAN + u) * SPAN
+            wide[row : row + SPAN] = narrow[at : at + SPAN]
 
 
 def forward_kernel(partners, counts, radius, first, context, cotangent, conv_weight, corr_weight, *refs):
     tiles, refs = refs[:18], refs[18:]
-    parts, motion, context_grad, facing, away, ends, weights_sent, weights_kept = refs[:8]
-    edges, cot_taps, taps, weight_grads, sems, edge_sems = refs[8:]
+    motion, context_grad, facing, away, ends, weights_sent, weights_kept, parts = refs[:8]
+    edges, cot_taps, taps_back, taps, flipped, narrow, wide, spread, weight_grads = refs[8:17]
+    sems, edge_sems = refs[17:]
     cells = first.shape[0]
     slots = parts.shape[0]
     row_sides, chip_sides = (6, 12), (1, 3, 5)
@@ -183,6 +183,11 @@
     for k in range(slots):
         live = jnp.where(k < counts[0, 0], 1.0 / math.sqrt(first.shape[1]), 0.0).astype(F32)
         gains.append(jnp.where(inside, live, 0.0))
+    for q in range(cells // GROUP):
+        at = slice(q * GROUP, (q + 1) * GROUP)
+        flipped[at] = jnp.dot(flip, first[at], preferred_element_type=F32).astype(BF16)
+    spread_rows(corr_weight, narrow, wide, LEAD)
+    spread[...] = wide[...].astype(BF16)
     for n in range(8):
         pltpu.make_async_copy(tiles[0].at[pl.ds(cells, 48)], edges.at[n], edge_sems.at[n]).wait()
     north, south = edges[0, :32, 128:], edges[1, :32, :128]
@@ -217,7 +222,7 @@
         ).wait()
     for q in range(cells // GROUP):
         at = slice(q * GROUP, (q + 1) * GROUP)
-        features = jnp.dot(flip, first[at], preferred_element_type=F32).astype(BF16)
+        features = flipped[at]
         for k in range(slots):
             scores = lax.dot_general(
                 features,
@@ -232,10 +237,11 @@
                 + pltpu.roll(band[:, 128:256], SPAN, 1)
                 + pltpu.roll(band[:, 256:], 2 * SPAN, 1)
             )
-            taps[at, k * 128 : (k + 1) * 128] = jnp.dot(
-                flip, packed.astype(BF16), preferred_element_type=F32
-            ).astype(BF16)
-    pre = jnp.dot(taps[...], corr_weight[...], preferred_element_type=F32) + context[...].astype(
+            taps_back[at, k * 128 : (k + 1) * 128] = packed.astype(BF16)
+    for q in range(cells // GROUP):
+        at = slice(q * GROUP, (q + 1) * GROUP)
+        taps[at] = jnp.dot(flip, taps_back[at], preferred_element_type=F32).astype(BF16)
+    pre = jnp.dot(taps[...], spread[...], preferred_element_type=F32) + context[...].astype(
         F32
     )
     sigma = jax.nn.sigmoid(pre)
@@ -273,21 +279,24 @@
 
 
 def backward_kernel(
-    partners, counts, radius, first, context_grad, corr_weight, parts, first_grad, *refs
+    partners, counts, radius, first, context_grad, corr_weight, parts, *refs
 ):
     cells = first.shape[0]
     slots = parts.shape[0]
     scale = 1.0 / math.sqrt(first.shape[1])
     inside = tap_mask(radius[0, 0], LEAD_BACK, False)
-    *kept, lent, totals = refs
-    for ref in refs:
+    first_grad, *kept, lent, totals, narrow, wide, spread = refs[-9:]
+    for ref in (*kept, lent, totals):
         ref[...] = jnp.zeros_like(ref)
+    spread_rows(corr_weight, narrow, wide, LEAD_BACK)
+    spread[...] = wide[...].astype(BF16)
+    across = first[...].T
     for q in range(cells // GROUP):
         at = slice(q * GROUP, (q + 1) * GROUP)
         packed = (
             lax.dot_general(
                 context_grad[at],
-                corr_weight[...],
+                spread[...],
                 (((1,), (1,)), ((), ())),
                 preferred_element_type=F32,
             )
@@ -305,12 +314,12 @@
             scores = pltpu.roll(band, WINDOW - REACH - LEAD_BACK, 1, stride=1, stride_axis=0).astype(BF16)
             window = slice(q * GROUP, q * GROUP + WINDOW)
             first_here += jnp.dot(scores, parts[k, window], preferred_element_type=F32)
-            totals[k, window] += lax.dot_general(
-                scores, first[at], (((0,), (0,)), ((), ())), preferred_element_type=F32
+            totals[k, :, window] += jnp.dot(
+                across[:, at], scores, preferred_element_type=F32
             )
         first_grad[at] = first_here * scale
     for k in range(slots):
-        value = (totals[k, GROUP : GROUP + cells] * scale).astype(BF16)
+        value = (totals[k, :, GROUP : GROUP + cells] * scale).astype(BF16).T
         place = tile_of(partners[0, 0, k])
         for x in range(3):
             @pl.when(place % 6 == 2 * x)
@@ -361,13 +370,71 @@
 def halve(cur, mine, axis, bits):
     size = cur.shape[0] // 2
     gone = lax.dynamic_slice_in_dim(cur, (1 - mine) * size, size).astype(BF16)
-    return lax.dynamic_slice_in_dim(cur, mine * size, size), swap(gone, axis, bits)
+    return lax.dynamic_slice_in_dim(cur, mine * size, size), gone, swap(gone, axis, bits)
 
 
 def sum_everywhere(cur, axis, unit):
     mine = cur.astype(BF16)
     got = [swap(mine, axis, unit * s).astype(F32) for s in (1, 2, 3)]
     return (mine.astype(F32) + got[0]) + (got[1] + got[2])
+
+
+def forward(tables, first, context, cotangent, conv_weight, corr_weight, around):
+    cells, channels = first.shape
+    hidden = context.shape[1]
+    slots = tables[0].shape[-1]
+    shape = jax.ShapeDtypeStruct
+    total_rows = 9 * hidden + 2 * 384
+    return call(
+        forward_kernel,
+        (
+            shape((cells, hidden), BF16),
+            shape((cells, hidden), BF16),
+            shape((32, hidden), BF16),
+            shape((32, hidden), BF16),
+            shape((2, 16, hidden), BF16),
+            shape((total_rows // 2, 128), BF16),
+            shape((total_rows // 2, 128), F32),
+            shape((slots, cells + 2 * GROUP, channels), BF16),
+        ),
+        [SMEM] * 3 + [VMEM] * 5 + [ANY] * 18,
+        [
+            pltpu.VMEM((8, 48, channels), BF16),
+            pltpu.VMEM((cells + 64, 384), BF16),
+            pltpu.VMEM((cells, slots * 128), BF16),
+            pltpu.VMEM((cells, slots * 128), BF16),
+            pltpu.VMEM((cells, channels), BF16),
+            pltpu.VMEM(corr_weight.shape, F32),
+            pltpu.VMEM((slots * 128, hidden), F32),
+            pltpu.VMEM((slots * 128, hidden), BF16),
+            pltpu.VMEM((total_rows, 128), F32),
+            pltpu.SemaphoreType.DMA((slots,)),
+            pltpu.SemaphoreType.DMA((8,)),
+        ],
+        flops=3 * 10**9,
+    )(*tables, first, context, cotangent, conv_weight, corr_weight, *around)
+
+
+def backward(tables, first, context_grad, corr_weight, parts, after=()):
+    cells, channels = first.shape
+    slots, hidden = parts.shape[0], context_grad.shape[1]
+    shape = jax.ShapeDtypeStruct
+    return call(
+        backward_kernel,
+        (
+            shape((cells, channels), F32),
+            *[shape((3, cells, channels), BF16)] * 3,
+            shape((6, cells, channels), BF16),
+        ),
+        [SMEM] * 3 + [VMEM] * 4 + [ANY] * len(after),
+        [
+            pltpu.VMEM((slots, channels, cells + 2 * GROUP), F32),
+            pltpu.VMEM(corr_weight.shape, F32),
+            pltpu.VMEM((slots * 128, hidden), F32),
+            pltpu.VMEM((slots * 128, hidden), BF16),
+        ],
+        flops=3 * 10**9,
+    )(*tables, first, context_grad, corr_weight, parts, *after)
 
 
 def body(
@@ -399,65 +466,30 @@
     for r in range(3):
         for x in range(3):
             around += [tiles[r, x], swap(tiles[r, x], "col", 1)]
-    spread, spread_back = call(
-        spread_kernel,
-        (shape((slots * 128, hidden), BF16), shape((slots * 128, hidden), BF16)),
-        [VMEM],
-        [pltpu.VMEM((slots * 128, hidden), F32)],
-    )(corr_weight.astype(F32))
-    total_rows = 9 * hidden + 2 * 384
-    parts, motion, context_grad, facing, away, ends, weights_sent, weights_kept = call(
-        forward_kernel,
-        (
-            shape((slots, cells + 2 * GROUP, channels), BF16),
-            shape((cells, hidden), BF16),
-            shape((cells, hidden), BF16),
-            shape((cols_tile, hidden), BF16),
-            shape((cols_tile, hidden), BF16),
-            shape((2, rows_tile, hidden), BF16),
-            shape((total_rows // 2, 128), BF16),
-            shape((total_rows // 2, 128), F32),
-        ),
-        [SMEM] * 3 + [VMEM] * 5 + [ANY] * 18,
-        [
-            pltpu.VMEM((8, 48, channels), BF16),
-            pltpu.VMEM(((rows_tile + 2) * cols_tile, 3 * out_width), BF16),
-            pltpu.VMEM((cells, slots * 128), BF16),
-            pltpu.VMEM((total_rows, 128), F32),
-            pltpu.SemaphoreType.DMA((slots,)),
-            pltpu.SemaphoreType.DMA((8,)),
-        ],
-        flops=3 * 10**9,
-    )(
-        *tables,
-        first,
-        context.reshape(cells, hidden),
-        cot,
-        conv_weight,
-        spread,
-        *around,
+    motion, context_grad, facing, away, ends, weights_sent, weights_kept, parts = forward(
+        tables, first, context.reshape(cells, hidden), cot, conv_weight, corr_weight, around
     )
     total = weights_kept + swap(weights_sent, "col", 1).astype(F32)
-    total, got = halve(total, chip >> 1, "col", 4)
-    first_grad, *kept, lent = call(
-        backward_kernel,
-        (
-            shape((cells, channels), F32),
-            *[shape((3, cells, channels), BF16)] * 3,
-            shape((6, cells, channels), BF16),
-        ),
-        [SMEM] * 3 + [VMEM] * 4,
-        [pltpu.VMEM((slots, cells + 2 * GROUP, channels), F32)],
-        flops=3 * 10**9,
-    )(*tables, first, context_grad, spread_back, parts)
+    total, gone, got = halve(total, chip >> 1, "col", 4)
+    around_motion = rim(facing, away, ends, row_even, col_even)
+    first_grad, *kept, lent = backward(
+        tables, first, context_grad, corr_weight, parts, (gone, *around_motion)
+    )
     lent = swap(lent, "col", 1)
     side = jnp.where((core == 0) == chip_even, 1, 2)
     sent = [
         (kept[x].astype(F32) + jnp.where(side == x, lent[3:].astype(F32), 0.0)).astype(BF16)
         for x in (1, 2)
     ]
-    total, got = halve(total + got.astype(F32), chip & 1, "col", 2)
-    total, sent[0], sent[1] = lax.optimization_barrier((total + got.astype(F32), *sent))
+    total, _, got = halve(total + got.astype(F32), chip & 1, "col", 2)
+    features = call(
+        features_kernel,
+        shape((cells, out_width), BF16),
+        [VMEM] * 6,
+        [pltpu.VMEM(((rows_tile + 2) * cols_tile, 3 * hidden), BF16)],
+        flops=10**9,
+    )(motion, *around_motion, conv_weight.reshape(3, 3 * hidden, out_width))
+    total, features, *sent = lax.optimization_barrier((total + got.astype(F32), features, *sent))
     middle = kept[0].astype(F32) + lent[:3].astype(F32)
     for x in (1, 2):
         middle += swap_pairs(sent[x - 1], "col", x - 1, 2).astype(F32)
@@ -467,22 +499,11 @@
     second_grad = middle[0]
     for r in (1, 2):
         second_grad += swap_pairs(middle[r].astype(BF16), "row", r - 1).astype(F32)
-    features = call(
-        features_kernel,
-        shape((cells, out_width), BF16),
-        [VMEM] * 6,
-        [pltpu.VMEM(((rows_tile + 2) * cols_tile, 3 * hidden), BF16)],
-        flops=10**9,
-    )(
-        motion,
-        *rim(facing, away, ends, row_even, col_even),
-        conv_weight.reshape(3, 3 * hidden, out_width),
-    )
     conv_total, corr_total = call(
         finish_kernel,
         (shape((9 * hidden, out_width), F32), shape(corr_weight.shape, F32)),
         [VMEM] * 8,
-        [pltpu.VMEM((total_rows, 128), F32)],
+        [pltpu.VMEM((9 * hidden + 2 * 384, 128), F32)],
     )(*shards)
     return (
         features.reshape(rows_tile, cols_tile, out_width),

time: 122 us -> 128 us (1.049)
  waiting for transfers between devices: 12.7 us -> 25.6 us
  Pallas kernels: 30.2 us -> 23.6 us
    ppermute x16, waiting for transfers between devices: 3.2 us -> 12 us  [swap_pairs(): return lax.ppermute(array, axis, pairs)]
    pallas_call x3 -> x2, Pallas kernels: 23.2 us -> 16.5 us  [the longest x1 8.87 us: forward(): call(forward_kernel, (shape((cells, hidden), BF16), shape((cells, hidden)...]
    ppermute x26, waiting for transfers between devices: 9.54 us -> 13.6 us  [swap(): lax.ppermute(array, axis, [(i, i ^ bits) for i in range(lax.axis_size(axi...]
    convert_element_type x1 -> x0, other arithmetic: 1.68 us -> none  [body(): corr_weight.astype(F32)]
    ppermute x26, starting transfers between devices: 34.8 us -> 36.1 us  [swap(): lax.ppermute(array, axis, [(i, i ^ bits) for i in range(lax.axis_size(axi...]
    unnamed x68 -> x52, local copies, waits for them, and re-layouts: 2.27 us -> 0.98 us
  transfers between devices with their start and end apart: 42 -> 42, of which waited for: 8 -> 17; matrix products, arithmetic and copies ran while one was open for 3% -> 2% of each run, Pallas kernels for 13% -> 4%
where the time goes in v5:
time: 128 us; the launch traced here: 126 us
  starting transfers between devices  68.5 us (54%)
  waiting for transfers between devices  25.6 us (20%)
  Pallas kernels  23.6 us (18%)
  other arithmetic  3.7 us (3%)
  local copies, waits for them, and re-layouts  2.47 us (2%)
  between operations  2.4 us (2%)
    ppermute x26, starting transfers between devices, swap(): lax.ppermute(array, axis, [(i, i ^ bits) for i in range(lax.axis_size(axi...  36.1 us
    ppermute x16, starting transfers between devices, swap_pairs(): return lax.ppermute(array, axis, pairs)  32.3 us
    ppermute x26, waiting for transfers between devices, swap(): lax.ppermute(array, axis, [(i, i ^ bits) for i in range(lax.axis_size(axi...  13.6 us
    ppermute x16, waiting for transfers between devices, swap_pairs(): return lax.ppermute(array, axis, pairs)  12 us
    pallas_call x1, Pallas kernels, forward(): call(forward_kernel, (shape((cells, hidden), BF16), shape((cells, hidden)...  8.87 us
    pallas_call x1, Pallas kernels, backward(): call(backward_kernel, (shape((cells, channels), F32), *[shape((3, cells,...  7.58 us
    pallas_call x1, Pallas kernels, body(): call(features_kernel, shape((cells, out_width), BF16), [VMEM] * 6, [pltpu...  2.77 us
  transfers between devices with their start and end apart: 42, of which 17 were waited for; matrix products, arithmetic and copies ran while one was open for 2% of the time, Pallas kernels for 4%

profile of v5, /device:TPU:33, one launch (start us, length us, event | category | flops | bytes accessed | tf_op | source)
XLA Modules:
  0.0 126.2 jit_solution(8178125050491189371)
XLA Ops:
  0.6 1.8 %shard_map.136.refs_0_ = bf16[560,256]{1,0:T(8,128)(2,1)} custom-call(bf16[512,256]{1,0:T(8,128)(2,1)} %bitcast.25, bf16[512,128]{1,0:T(8,128)(2,1)} %bitcast.26), custom_call_target="tpu_custom_call" | custom-call | tf_op jit(solution)/shard_map/pallas_call | solution.py:455
  7.0 3.3 %collective-permute-start.11 = (bf16[560,256]{1,0:T(8,128)(2,1)}, bf16[560,256]{1,0:T(8,128)(2,1)S(1)}, u32[]{:S(2)}, u32[]{:S(2)}) collective-permute-start(bf16[560,256]{1,0:T(8,128)(2,1)} %shard_map.136.refs_0_), channel_id=1, source_target_pairs={{8,16},{16,8},{24,32},{32,24},{40,48},{48,40},{56,64},{64,56},{72,... | collective-permute-start | bytes 860168 | tf_op jit(solution)/shard_map/ppermute | solution.py:35
  10.4 1.5 %collective-permute-start.2 = (bf16[560,256]{1,0:T(8,128)(2,1)S(1)}, bf16[560,256]{1,0:T(8,128)(2,1)S(1)}, u32[]{:S(2)}, u32[]{:S(2)}) collective-permute-start(bf16[560,256]{1,0:T(8,128)(2,1)S(1)} %collective-permute-done.1.refs_2_), channel_id=1, source_target_pairs={{0,1},{1,0},{2,3},{3,2},{4,5},{5,4},{6,7},{7,6},{8,9},{9,8},{10,11... | collective-permute-start | bytes 860168 | tf_op jit(solution)/shard_map/ppermute | solution.py:25
  12.0 1.9 %collective-permute-start.6 = (bf16[560,256]{1,0:T(8,128)(2,1)S(1)}, bf16[560,256]{1,0:T(8,128)(2,1)S(1)}, u32[]{:S(2)}, u32[]{:S(2)}) collective-permute-start(bf16[560,256]{1,0:T(8,128)(2,1)S(1)} %collective-permute-done.5.refs_6_), channel_id=1, source_target_pairs={{0,1},{1,0},{2,3},{3,2},{4,5},{5,4},{6,7},{7,6},{8,9},{9,8},{10,11... | collective-permute-start | bytes 860168 | tf_op jit(solution)/shard_map/ppermute | solution.py:25
  13.9 3.4 %collective-permute-start.7 = (bf16[560,256]{1,0:T(8,128)(2,1)S(1)}, bf16[560,256]{1,0:T(8,128)(2,1)S(1)}, u32[]{:S(2)}, u32[]{:S(2)}) collective-permute-start(bf16[560,256]{1,0:T(8,128)(2,1)S(1)} %collective-permute-done.5.refs_6_), channel_id=1, source_target_pairs={{0,2},{2,0},{1,3},{3,1},{4,6},{6,4},{5,7},{7,5},{8,10},{10,8},{9,1... | collective-permute-start | bytes 860168 | tf_op jit(solution)/shard_map/ppermute | solution.py:35
  17.3 2.4 %collective-permute-done.11.refs_12_ = bf16[560,256]{1,0:T(8,128)(2,1)S(1)} collective-permute-done((bf16[560,256]{1,0:T(8,128)(2,1)}, bf16[560,256]{1,0:T(8,128)(2,1)S(1)}, u32[]{:S(2)}, u32[]{:S(2)}) %collective-permute-start.11) | collective-permute-done | bytes 286752 | tf_op jit(solution)/shard_map/ppermute | solution.py:35
  19.7 3.4 %collective-permute-start.13 = (bf16[560,256]{1,0:T(8,128)(2,1)S(1)}, bf16[560,256]{1,0:T(8,128)(2,1)S(1)}, u32[]{:S(2)}, u32[]{:S(2)}) collective-permute-start(bf16[560,256]{1,0:T(8,128)(2,1)S(1)} %collective-permute-done.1.refs_2_), channel_id=1, source_target_pairs={{8,16},{16,8},{24,32},{32,24},{40,48},{48,40},{56,64},{64,56},{72,... | collective-permute-start | bytes 860168 | tf_op jit(solution)/shard_map/ppermute | solution.py:35
  25.0 2.2 %collective-permute-done.9.refs_10_ = bf16[560,256]{1,0:T(8,128)(2,1)S(1)} collective-permute-done((bf16[560,256]{1,0:T(8,128)(2,1)S(1)}, bf16[560,256]{1,0:T(8,128)(2,1)S(1)}, u32[]{:S(2)}, u32[]{:S(2)}) %collective-permute-start.9) | collective-permute-done | bytes 286752 | tf_op jit(solution)/shard_map/ppermute | solution.py:35
  27.2 1.7 %collective-permute-start.10 = (bf16[560,256]{1,0:T(8,128)(2,1)S(1)}, bf16[560,256]{1,0:T(8,128)(2,1)}, u32[]{:S(2)}, u32[]{:S(2)}) collective-permute-start(bf16[560,256]{1,0:T(8,128)(2,1)S(1)} %collective-permute-done.9.refs_10_), channel_id=1, source_target_pairs={{0,1},{1,0},{2,3},{3,2},{4,5},{5,4},{6,7},{7,6},{8,9},{9,8},{10,11... | collective-permute-start | bytes 860168 | tf_op jit(solution)/shard_map/ppermute | solution.py:25
  28.9 2.3 %collective-permute-done.13.refs_14_ = bf16[560,256]{1,0:T(8,128)(2,1)S(1)} collective-permute-done((bf16[560,256]{1,0:T(8,128)(2,1)S(1)}, bf16[560,256]{1,0:T(8,128)(2,1)S(1)}, u32[]{:S(2)}, u32[]{:S(2)}) %collective-permute-start.13) | collective-permute-done | bytes 286752 | tf_op jit(solution)/shard_map/ppermute | solution.py:35
  31.2 1.7 %collective-permute-start.14 = (bf16[560,256]{1,0:T(8,128)(2,1)S(1)}, bf16[560,256]{1,0:T(8,128)(2,1)}, u32[]{:S(2)}, u32[]{:S(2)}) collective-permute-start(bf16[560,256]{1,0:T(8,128)(2,1)S(1)} %collective-permute-done.13.refs_14_), channel_id=1, source_target_pairs={{0,1},{1,0},{2,3},{3,2},{4,5},{5,4},{6,7},{7,6},{8,9},{9,8},{10,11... | collective-permute-start | bytes 860168 | tf_op jit(solution)/shard_map/ppermute | solution.py:25
  34.7 8.9 %shard_map.137 = (bf16[512,256]{1,0:T(8,128)(2,1)}, bf16[512,256]{1,0:T(8,128)(2,1)}, bf16[32,256]{1,0:T(8,128)(2,1)}, bf16[32,256]{1,0:T(8,128)(2,1)}, bf16[2,1...) custom-call(s32[1,1,4]{2,1,0:T(1,128)} %partners.3, ...), custom_call_target="tpu_custom_call" | custom-call | flops 3000000000 | bytes 10000000 | tf_op jit(solution)/shard_map/pallas_call | solution.py:388
  44.0 3.4 %collective-permute-start.20 = (bf16[32,256]{1,0:T(8,128)(2,1)}, bf16[32,256]{1,0:T(8,128)(2,1)S(1)}, u32[]{:S(2)}, u32[]{:S(2)}) collective-permute-start(bf16[32,256]{1,0:T(8,128)(2,1)} %get-tuple-element.28), channel_id=1, source_target_pairs={{8,16},{16,8},{24,32},{32,24},{40,48},{48,40},{56,64},{64,56},{72,... | collective-permute-start | bytes 49160 | tf_op jit(solution)/shard_map/ppermute | solution.py:35
  48.1 2.7 %collective-permute-done.20 = bf16[32,256]{1,0:T(8,128)(2,1)S(1)} collective-permute-done((bf16[32,256]{1,0:T(8,128)(2,1)}, bf16[32,256]{1,0:T(8,128)(2,1)S(1)}, u32[]{:S(2)}, u32[]{:S(2)}) %collective-permute-start.20) | collective-permute-done | bytes 16416 | tf_op jit(solution)/shard_map/ppermute | solution.py:35
  52.3 8.1 %collective-permute-start.22 = (bf16[18,256]{1,0:T(8,128)(2,1)S(1)}, bf16[18,256]{1,0:T(8,128)(2,1)S(1)}, u32[]{:S(2)}, u32[]{:S(2)}) collective-permute-start(bf16[18,256]{1,0:T(8,128)(2,1)S(1)} %get-tuple-element.55), channel_id=1, source_target_pairs={{1,2},{2,1},{3,4},{4,3},{5,6},{6,5},{9,10},{10,9},{11,12},{12,11},... | collective-permute-start | bytes 27656 | tf_op jit(solution)/shard_map/ppermute | solution.py:35
  64.1 7.6 %shard_map.139 = (f32[512,256]{1,0:T(8,128)}, bf16[3,512,256]{2,1,0:T(8,128)(2,1)}, bf16[3,512,256]{2,1,0:T(8,128)(2,1)}, bf16[3,512,256]{2,1,0:T(8,128)(2,1)}, bf16[6,512,256]{2,1,0:T(8,128)(2,1)}) custom-call(s32[1,1,4]{2,1,0:T(1,128)} %partners.3, s32[1,1]{1,0:T(1,128)S(6)} %copy.15.counts, s32[1,1]{1,0:T(1,128)S(6)} %copy.16.radius, ...), custom_call_target="tpu_custom_call" | custom-call | flops 3000000000 | bytes 10000000 | tf_op jit(solution)/shard_map/pallas_call | solution.py:422
  71.7 2.3 %collective-permute-start.18 = (bf16[768,128]{1,0:T(8,128)(2,1)S(1)}, bf16[768,128]{1,0:T(8,128)(2,1)S(1)}, u32[]{:S(2)}, u32[]{:S(2)}) collective-permute-start(bf16[768,128]{1,0:T(8,128)(2,1)S(1)} %copy-done.4), channel_id=1, source_target_pairs={{0,4},{1,5},{2,6},{3,7},{4,0},{5,1},{6,2},{7,3},{8,12},{9,13},{10,... | collective-permute-start | bytes 589832 | tf_op jit(solution)/shard_map/ppermute | solution.py:25
  74.0 5.4 %collective-permute-done.18 = bf16[768,128]{1,0:T(8,128)(2,1)S(1)} collective-permute-done((bf16[768,128]{1,0:T(8,128)(2,1)S(1)}, bf16[768,128]{1,0:T(8,128)(2,1)S(1)}, u32[]{:S(2)}, u32[]{:S(2)}) %collective-permute-start.18) | collective-permute-done | bytes 196640 | tf_op jit(solution)/shard_map/ppermute | solution.py:25
  79.4 1.9 %collective-permute-start.19 = (bf16[384,128]{1,0:T(8,128)(2,1)S(1)}, bf16[384,128]{1,0:T(8,128)(2,1)S(1)}, u32[]{:S(2)}, u32[]{:S(2)}) collective-permute-start(bf16[384,128]{1,0:T(8,128)(2,1)S(1)} %dynamic-slice_convert_fusion.1), channel_id=1, source_target_pairs={{0,2},{1,3},{2,0},{3,1},{4,6},{5,7},{6,4},{7,5},{8,10},{9,11},{10,... | collective-permute-start | bytes 294920 | tf_op jit(solution)/shard_map/ppermute | solution.py:25
  81.3 2.8 %shard_map.138 = bf16[512,128]{1,0:T(8,128)(2,1)} custom-call(bf16[512,256]{1,0:T(8,128)(2,1)} %get-tuple-element.27.motion, bf16[32,256]{1,0:T(8,128)(2,1)} %copy-done.13, bf16[32,256]{1,0:T(8,128)(2,1)} %copy-done.12, bf16[18,256]{1,0:T(8,128)(2,1)} %get-tuple-element.53.west.refs_3_, bf16[18,256]{1,0:T(8,128)(2,1)} %get-tuple-element.52.east.refs_4_, ...), custom_call_target="tpu_custom_call" | custom-call | flops 1000000000 | bytes 3333333 | tf_op jit(solution)/shard_map/pallas_call | solution.py:485
  85.3 2.0 %collective-permute-start.25 = (bf16[3,512,256]{2,1,0:T(8,128)(2,1)S(1)}, bf16[3,512,256]{2,1,0:T(8,128)(2,1)S(1)}, u32[]{:S(2)}, u32[]{:S(2)}) collective-permute-start(bf16[3,512,256]{2,1,0:T(8,128)(2,1)S(1)} %get-tuple-element.39), channel_id=1, source_target_pairs={{0,2},{2,0},{1,3},{3,1},{4,6},{6,4},{5,7},{7,5},{8,10},{10,8},{9,1... | collective-permute-start | bytes 2359304 | tf_op jit(solution)/shard_map/ppermute | solution.py:35
  88.4 2.2 %collective-permute-start.29 = (bf16[384,128]{1,0:T(8,128)(2,1)S(1)}, bf16[384,128]{1,0:T(8,128)(2,1)S(1)}, u32[]{:S(2)}, u32[]{:S(2)}) collective-permute-start(bf16[384,128]{1,0:T(8,128)(2,1)S(1)} %convert_add_fusion.3), channel_id=1, source_target_pairs={{0,8},{8,0},{16,24},{24,16},{32,40},{40,32},{48,56},{56,48},{64,72... | collective-permute-start | bytes 294920 | tf_op jit(solution)/shard_map/ppermute | solution.py:25
  90.6 1.4 %collective-permute-done.31 = bf16[384,128]{1,0:T(8,128)(2,1)S(1)} collective-permute-done((bf16[384,128]{1,0:T(8,128)(2,1)S(1)}, bf16[384,128]{1,0:T(8,128)(2,1)S(1)}, u32[]{:S(2)}, u32[]{:S(2)}) %collective-permute-start.31) | collective-permute-done | bytes 98336 | tf_op jit(solution)/shard_map/ppermute | solution.py:25
  94.0 1.8 %collective-permute-start.34 = (bf16[384,128]{1,0:T(8,128)(2,1)S(1)}, bf16[384,128]{1,0:T(8,128)(2,1)S(1)}, u32[]{:S(2)}, u32[]{:S(2)}) collective-permute-start(bf16[384,128]{1,0:T(8,128)(2,1)S(1)} %add_convert_fusion.1), channel_id=1, source_target_pairs={{0,96},{8,104},{16,112},{24,120},{32,64},{40,72},{48,80},{56,88},{... | collective-permute-start | bytes 294920 | tf_op jit(solution)/shard_map/ppermute | solution.py:25
  95.8 1.9 %collective-permute-start.32 = (bf16[384,128]{1,0:T(8,128)(2,1)S(1)}, bf16[384,128]{1,0:T(8,128)(2,1)S(1)}, u32[]{:S(2)}, u32[]{:S(2)}) collective-permute-start(bf16[384,128]{1,0:T(8,128)(2,1)S(1)} %add_convert_fusion.1), channel_id=1, source_target_pairs={{0,32},{8,40},{16,48},{24,56},{32,0},{40,8},{48,16},{56,24},{64,96... | collective-permute-start | bytes 294920 | tf_op jit(solution)/shard_map/ppermute | solution.py:25
  98.1 2.7 %collective-permute-done.33 = bf16[384,128]{1,0:T(8,128)(2,1)S(1)} collective-permute-done((bf16[384,128]{1,0:T(8,128)(2,1)S(1)}, bf16[384,128]{1,0:T(8,128)(2,1)S(1)}, u32[]{:S(2)}, u32[]{:S(2)}) %collective-permute-start.33) | collective-permute-done | bytes 98336 | tf_op jit(solution)/shard_map/ppermute | solution.py:25
  103.0 2.6 %collective-permute-start.28 = (bf16[512,256]{1,0:T(8,128)(2,1)S(1)}, bf16[512,256]{1,0:T(8,128)(2,1)S(1)}, u32[]{:S(2)}, u32[]{:S(2)}) collective-permute-start(bf16[512,256]{1,0:T(8,128)(2,1)S(1)} %get-tuple-element.49), channel_id=1, source_target_pairs={{8,16},{16,8},{24,32},{32,24},{40,48},{48,40},{56,64},{64,56},{72,... | collective-permute-start | bytes 786440 | tf_op jit(solution)/shard_map/ppermute | solution.py:35
  105.7 2.9 %collective-permute-start.36 = (bf16[384,128]{1,0:T(8,128)(2,1)S(1)}, bf16[384,128]{1,0:T(8,128)(2,1)S(1)}, u32[]{:S(2)}, u32[]{:S(2)}) collective-permute-start(bf16[384,128]{1,0:T(8,128)(2,1)S(1)} %add_convert_fusion.refs_0_), channel_id=1, source_target_pairs={{0,4},{1,5},{2,6},{3,7},{4,0},{5,1},{6,2},{7,3},{8,12},{9,13},{10,... | collective-permute-start | bytes 294920 | tf_op jit(solution)/shard_map/ppermute | solution.py:25
  109.3 6.4 %collective-permute-start.38 = (bf16[384,128]{1,0:T(8,128)(2,1)S(1)}, bf16[384,128]{1,0:T(8,128)(2,1)S(1)}, u32[]{:S(2)}, u32[]{:S(2)}) collective-permute-start(bf16[384,128]{1,0:T(8,128)(2,1)S(1)} %add_convert_fusion.refs_0_), channel_id=1, source_target_pairs={{0,1},{1,0},{2,3},{3,2},{4,5},{5,4},{6,7},{7,6},{8,9},{9,8},{10,11... | collective-permute-start | bytes 294920 | tf_op jit(solution)/shard_map/ppermute | solution.py:25
  115.8 1.6 %collective-permute-start.39 = (bf16[384,128]{1,0:T(8,128)(2,1)S(1)}, bf16[384,128]{1,0:T(8,128)(2,1)S(1)}, u32[]{:S(2)}, u32[]{:S(2)}) collective-permute-start(bf16[384,128]{1,0:T(8,128)(2,1)S(1)} %collective-permute-done.35.refs_1_), channel_id=1, source_target_pairs={{0,1},{1,0},{2,3},{3,2},{4,5},{5,4},{6,7},{7,6},{8,9},{9,8},{10,11... | collective-permute-start | bytes 294920 | tf_op jit(solution)/shard_map/ppermute | solution.py:25
  117.4 3.2 %collective-permute-start.40 = (bf16[384,128]{1,0:T(8,128)(2,1)S(1)}, bf16[384,128]{1,0:T(8,128)(2,1)S(1)}, u32[]{:S(2)}, u32[]{:S(2)}) collective-permute-start(bf16[384,128]{1,0:T(8,128)(2,1)S(1)} %collective-permute-done.36.refs_2_), channel_id=1, source_target_pairs={{0,1},{1,0},{2,3},{3,2},{4,5},{5,4},{6,7},{7,6},{8,9},{9,8},{10,11... | collective-permute-start | bytes 294920 | tf_op jit(solution)/shard_map/ppermute | solution.py:25
  122.8 2.5 %shard_map.140 = (f32[2304,128]{1,0:T(8,128)}, f32[324,256]{1,0:T(8,128)}) custom-call(bf16[384,128]{1,0:T(8,128)(2,1)} %copy-done.3, bf16[384,128]{1,0:T(8,128)(2,1)} %copy-done.5, bf16[384,128]{1,0:T(8,128)(2,1)} %copy-done.6, bf16[384,128]{1,0:T(8,128)(2,1)} %copy-done.7, bf16[384,128]{1,0:T(8,128)(2,1)} %copy-done.8, bf16[384,128]{1,0:T(8,128)(2,1)} %copy-done.9, ...), custom_call_target="tpu_custom_call" | custom-call | tf_op jit(solution)/shard_map/pallas_call | solution.py:502
  (125 shorter events, 24.2 us)
Async XLA Ops:
  2.5 7.9 %collective-permute-start.1 = (bf16[560,256]{1,0:T(8,128)(2,1)}, bf16[560,256]{1,0:T(8,128)(2,1)S(1)}, u32[]{:S(2)}, u32[]{:S(2)}) collective-permute-start(bf16[560,256]{1,0:T(8,128)(2,1)} %shard_map.136.refs_0_), channel_id=1, source_target_pairs={{0,2},{2,0},{1,3},{3,1},{4,6},{6,4},{5,7},{7,5},{8,10},{10,8},{9,1... | collective-permute-start | bytes 860168 | tf_op jit(solution)/shard_map/ppermute | solution.py:35
  3.7 8.3 %collective-permute-start.3 = (bf16[560,256]{1,0:T(8,128)(2,1)}, bf16[560,256]{1,0:T(8,128)(2,1)S(1)}, u32[]{:S(2)}, u32[]{:S(2)}) collective-permute-start(bf16[560,256]{1,0:T(8,128)(2,1)} %shard_map.136.refs_0_), channel_id=1, source_target_pairs={{2,4},{4,2},{3,5},{5,3},{10,12},{12,10},{11,13},{13,11},{18,20},{2... | collective-permute-start | bytes 860168 | tf_op jit(solution)/shard_map/ppermute | solution.py:35
  4.4 7.7 %collective-permute-start.5 = (bf16[560,256]{1,0:T(8,128)(2,1)}, bf16[560,256]{1,0:T(8,128)(2,1)S(1)}, u32[]{:S(2)}, u32[]{:S(2)}) collective-permute-start(bf16[560,256]{1,0:T(8,128)(2,1)} %shard_map.136.refs_0_), channel_id=1, source_target_pairs={{0,8},{8,0},{16,24},{24,16},{32,40},{40,32},{48,56},{56,48},{64,72... | collective-permute-start | bytes 860168 | tf_op jit(solution)/shard_map/ppermute | solution.py:35
  5.7 8.2 %collective-permute-start = (bf16[560,256]{1,0:T(8,128)(2,1)}, bf16[560,256]{1,0:T(8,128)(2,1)S(1)}, u32[]{:S(2)}, u32[]{:S(2)}) collective-permute-start(bf16[560,256]{1,0:T(8,128)(2,1)} %shard_map.136.refs_0_), channel_id=1, source_target_pairs={{0,1},{1,0},{2,3},{3,2},{4,5},{5,4},{6,7},{7,6},{8,9},{9,8},{10,11... | collective-permute-start | bytes 860168 | tf_op jit(solution)/shard_map/ppermute | solution.py:25
  7.0 12.7 %collective-permute-start.11 = (bf16[560,256]{1,0:T(8,128)(2,1)}, bf16[560,256]{1,0:T(8,128)(2,1)S(1)}, u32[]{:S(2)}, u32[]{:S(2)}) collective-permute-start(bf16[560,256]{1,0:T(8,128)(2,1)} %shard_map.136.refs_0_), channel_id=1, source_target_pairs={{8,16},{16,8},{24,32},{32,24},{40,48},{48,40},{56,64},{64,56},{72,... | collective-permute-start | bytes 860168 | tf_op jit(solution)/shard_map/ppermute | solution.py:35
  10.4 9.3 %collective-permute-start.2 = (bf16[560,256]{1,0:T(8,128)(2,1)S(1)}, bf16[560,256]{1,0:T(8,128)(2,1)S(1)}, u32[]{:S(2)}, u32[]{:S(2)}) collective-permute-start(bf16[560,256]{1,0:T(8,128)(2,1)S(1)} %collective-permute-done.1.refs_2_), channel_id=1, source_target_pairs={{0,1},{1,0},{2,3},{3,2},{4,5},{5,4},{6,7},{7,6},{8,9},{9,8},{10,11... | collective-permute-start | bytes 860168 | tf_op jit(solution)/shard_map/ppermute | solution.py:25
  11.9 11.1 %collective-permute-start.4 = (bf16[560,256]{1,0:T(8,128)(2,1)S(1)}, bf16[560,256]{1,0:T(8,128)(2,1)S(1)}, u32[]{:S(2)}, u32[]{:S(2)}) collective-permute-start(bf16[560,256]{1,0:T(8,128)(2,1)S(1)} %collective-permute-done.3.refs_4_), channel_id=1, source_target_pairs={{0,1},{1,0},{2,3},{3,2},{4,5},{5,4},{6,7},{7,6},{8,9},{9,8},{10,11... | collective-permute-start | bytes 860168 | tf_op jit(solution)/shard_map/ppermute | solution.py:25
  12.0 11.7 %collective-permute-start.6 = (bf16[560,256]{1,0:T(8,128)(2,1)S(1)}, bf16[560,256]{1,0:T(8,128)(2,1)S(1)}, u32[]{:S(2)}, u32[]{:S(2)}) collective-permute-start(bf16[560,256]{1,0:T(8,128)(2,1)S(1)} %collective-permute-done.5.refs_6_), channel_id=1, source_target_pairs={{0,1},{1,0},{2,3},{3,2},{4,5},{5,4},{6,7},{7,6},{8,9},{9,8},{10,11... | collective-permute-start | bytes 860168 | tf_op jit(solution)/shard_map/ppermute | solution.py:25
  13.9 11.0 %collective-permute-start.7 = (bf16[560,256]{1,0:T(8,128)(2,1)S(1)}, bf16[560,256]{1,0:T(8,128)(2,1)S(1)}, u32[]{:S(2)}, u32[]{:S(2)}) collective-permute-start(bf16[560,256]{1,0:T(8,128)(2,1)S(1)} %collective-permute-done.5.refs_6_), channel_id=1, source_target_pairs={{0,2},{2,0},{1,3},{3,1},{4,6},{6,4},{5,7},{7,5},{8,10},{10,8},{9,1... | collective-permute-start | bytes 860168 | tf_op jit(solution)/shard_map/ppermute | solution.py:35
  19.6 7.6 %collective-permute-start.9 = (bf16[560,256]{1,0:T(8,128)(2,1)S(1)}, bf16[560,256]{1,0:T(8,128)(2,1)S(1)}, u32[]{:S(2)}, u32[]{:S(2)}) collective-permute-start(bf16[560,256]{1,0:T(8,128)(2,1)S(1)} %collective-permute-done.3.refs_4_), channel_id=1, source_target_pairs={{0,8},{8,0},{16,24},{24,16},{32,40},{40,32},{48,56},{56,48},{64,72... | collective-permute-start | bytes 860168 | tf_op jit(solution)/shard_map/ppermute | solution.py:35
  19.7 11.6 %collective-permute-start.13 = (bf16[560,256]{1,0:T(8,128)(2,1)S(1)}, bf16[560,256]{1,0:T(8,128)(2,1)S(1)}, u32[]{:S(2)}, u32[]{:S(2)}) collective-permute-start(bf16[560,256]{1,0:T(8,128)(2,1)S(1)} %collective-permute-done.1.refs_2_), channel_id=1, source_target_pairs={{8,16},{16,8},{24,32},{32,24},{40,48},{48,40},{56,64},{64,56},{72,... | collective-permute-start | bytes 860168 | tf_op jit(solution)/shard_map/ppermute | solution.py:35
  23.0 9.9 %collective-permute-start.15 = (bf16[560,256]{1,0:T(8,128)(2,1)S(1)}, bf16[560,256]{1,0:T(8,128)(2,1)S(1)}, u32[]{:S(2)}, u32[]{:S(2)}) collective-permute-start(bf16[560,256]{1,0:T(8,128)(2,1)S(1)} %collective-permute-done.11.refs_12_), channel_id=1, source_target_pairs={{2,4},{4,2},{3,5},{5,3},{10,12},{12,10},{11,13},{13,11},{18,20},{2... | collective-permute-start | bytes 860168 | tf_op jit(solution)/shard_map/ppermute | solution.py:35
  23.7 10.6 %collective-permute-start.12 = (bf16[560,256]{1,0:T(8,128)(2,1)S(1)}, bf16[560,256]{1,0:T(8,128)(2,1)}, u32[]{:S(2)}, u32[]{:S(2)}) collective-permute-start(bf16[560,256]{1,0:T(8,128)(2,1)S(1)} %collective-permute-done.11.refs_12_), channel_id=1, source_target_pairs={{0,1},{1,0},{2,3},{3,2},{4,5},{5,4},{6,7},{7,6},{8,9},{9,8},{10,11... | collective-permute-start | bytes 860168 | tf_op jit(solution)/shard_map/ppermute | solution.py:25
  24.9 9.5 %collective-permute-start.8 = (bf16[560,256]{1,0:T(8,128)(2,1)S(1)}, bf16[560,256]{1,0:T(8,128)(2,1)}, u32[]{:S(2)}, u32[]{:S(2)}) collective-permute-start(bf16[560,256]{1,0:T(8,128)(2,1)S(1)} %collective-permute-done.7.refs_8_), channel_id=1, source_target_pairs={{0,1},{1,0},{2,3},{3,2},{4,5},{5,4},{6,7},{7,6},{8,9},{9,8},{10,11... | collective-permute-start | bytes 860168 | tf_op jit(solution)/shard_map/ppermute | solution.py:25
  27.2 7.2 %collective-permute-start.10 = (bf16[560,256]{1,0:T(8,128)(2,1)S(1)}, bf16[560,256]{1,0:T(8,128)(2,1)}, u32[]{:S(2)}, u32[]{:S(2)}) collective-permute-start(bf16[560,256]{1,0:T(8,128)(2,1)S(1)} %collective-permute-done.9.refs_10_), channel_id=1, source_target_pairs={{0,1},{1,0},{2,3},{3,2},{4,5},{5,4},{6,7},{7,6},{8,9},{9,8},{10,11... | collective-permute-start | bytes 860168 | tf_op jit(solution)/shard_map/ppermute | solution.py:25
  43.6 18.6 %collective-permute-start.17 = (bf16[1536,128]{1,0:T(8,128)(2,1)}, bf16[1536,128]{1,0:T(8,128)(2,1)S(1)}, u32[]{:S(2)}, u32[]{:S(2)}) collective-permute-start(bf16[1536,128]{1,0:T(8,128)(2,1)} %get-tuple-element.26), channel_id=1, source_target_pairs={{0,1},{1,0},{2,3},{3,2},{4,5},{5,4},{6,7},{7,6},{8,9},{9,8},{10,11... | collective-permute-start | bytes 1179656 | tf_op jit(solution)/shard_map/ppermute | solution.py:25
  44.0 6.8 %collective-permute-start.20 = (bf16[32,256]{1,0:T(8,128)(2,1)}, bf16[32,256]{1,0:T(8,128)(2,1)S(1)}, u32[]{:S(2)}, u32[]{:S(2)}) collective-permute-start(bf16[32,256]{1,0:T(8,128)(2,1)} %get-tuple-element.28), channel_id=1, source_target_pairs={{8,16},{16,8},{24,32},{32,24},{40,48},{48,40},{56,64},{64,56},{72,... | collective-permute-start | bytes 49160 | tf_op jit(solution)/shard_map/ppermute | solution.py:35
  50.9 9.6 %collective-permute-start.23 = (bf16[18,256]{1,0:T(8,128)(2,1)S(1)}, bf16[18,256]{1,0:T(8,128)(2,1)S(1)}, u32[]{:S(2)}, u32[]{:S(2)}) collective-permute-start(bf16[18,256]{1,0:T(8,128)(2,1)S(1)} %get-tuple-element.54), channel_id=1, source_target_pairs={{0,1},{1,0},{2,3},{3,2},{4,5},{5,4},{6,7},{7,6},{8,9},{9,8},{10,11... | collective-permute-start | bytes 27656 | tf_op jit(solution)/shard_map/ppermute | solution.py:35
  52.3 9.3 %collective-permute-start.22 = (bf16[18,256]{1,0:T(8,128)(2,1)S(1)}, bf16[18,256]{1,0:T(8,128)(2,1)S(1)}, u32[]{:S(2)}, u32[]{:S(2)}) collective-permute-start(bf16[18,256]{1,0:T(8,128)(2,1)S(1)} %get-tuple-element.55), channel_id=1, source_target_pairs={{1,2},{2,1},{3,4},{4,3},{5,6},{6,5},{9,10},{10,9},{11,12},{12,11},... | collective-permute-start | bytes 27656 | tf_op jit(solution)/shard_map/ppermute | solution.py:35
  71.7 12.4 %collective-permute-start.24 = (bf16[6,512,256]{2,1,0:T(8,128)(2,1)}, bf16[6,512,256]{2,1,0:T(8,128)(2,1)S(1)}, u32[]{:S(2)}, u32[]{:S(2)}) collective-permute-start(bf16[6,512,256]{2,1,0:T(8,128)(2,1)} %get-tuple-element.34), channel_id=1, source_target_pairs={{0,1},{1,0},{2,3},{3,2},{4,5},{5,4},{6,7},{7,6},{8,9},{9,8},{10,11... | collective-permute-start | bytes 4718600 | tf_op jit(solution)/shard_map/ppermute | solution.py:25
  71.7 7.6 %collective-permute-start.18 = (bf16[768,128]{1,0:T(8,128)(2,1)S(1)}, bf16[768,128]{1,0:T(8,128)(2,1)S(1)}, u32[]{:S(2)}, u32[]{:S(2)}) collective-permute-start(bf16[768,128]{1,0:T(8,128)(2,1)S(1)} %copy-done.4), channel_id=1, source_target_pairs={{0,4},{1,5},{2,6},{3,7},{4,0},{5,1},{6,2},{7,3},{8,12},{9,13},{10,... | collective-permute-start | bytes 589832 | tf_op jit(solution)/shard_map/ppermute | solution.py:25
  84.6 16.6 %collective-permute-start.26 = (bf16[3,512,256]{2,1,0:T(8,128)(2,1)S(1)}, bf16[3,512,256]{2,1,0:T(8,128)(2,1)S(1)}, u32[]{:S(2)}, u32[]{:S(2)}) collective-permute-start(bf16[3,512,256]{2,1,0:T(8,128)(2,1)S(1)} %get-tuple-element.40), channel_id=1, source_target_pairs={{2,4},{4,2},{3,5},{5,3},{10,12},{12,10},{11,13},{13,11},{18,20},{2... | collective-permute-start | bytes 2359304 | tf_op jit(solution)/shard_map/ppermute | solution.py:35
  85.3 17.2 %collective-permute-start.25 = (bf16[3,512,256]{2,1,0:T(8,128)(2,1)S(1)}, bf16[3,512,256]{2,1,0:T(8,128)(2,1)S(1)}, u32[]{:S(2)}, u32[]{:S(2)}) collective-permute-start(bf16[3,512,256]{2,1,0:T(8,128)(2,1)S(1)} %get-tuple-element.39), channel_id=1, source_target_pairs={{0,2},{2,0},{1,3},{3,1},{4,6},{6,4},{5,7},{7,5},{8,10},{10,8},{9,1... | collective-permute-start | bytes 2359304 | tf_op jit(solution)/shard_map/ppermute | solution.py:35
  88.4 5.0 %collective-permute-start.30 = (bf16[384,128]{1,0:T(8,128)(2,1)S(1)}, bf16[384,128]{1,0:T(8,128)(2,1)S(1)}, u32[]{:S(2)}, u32[]{:S(2)}) collective-permute-start(bf16[384,128]{1,0:T(8,128)(2,1)S(1)} %convert_add_fusion.3), channel_id=1, source_target_pairs={{0,16},{8,24},{16,0},{24,8},{32,48},{40,56},{48,32},{56,40},{64,80... | collective-permute-start | bytes 294920 | tf_op jit(solution)/shard_map/ppermute | solution.py:25
  88.4 5.5 %collective-permute-start.29 = (bf16[384,128]{1,0:T(8,128)(2,1)S(1)}, bf16[384,128]{1,0:T(8,128)(2,1)S(1)}, u32[]{:S(2)}, u32[]{:S(2)}) collective-permute-start(bf16[384,128]{1,0:T(8,128)(2,1)S(1)} %convert_add_fusion.3), channel_id=1, source_target_pairs={{0,8},{8,0},{16,24},{24,16},{32,40},{40,32},{48,56},{56,48},{64,72... | collective-permute-start | bytes 294920 | tf_op jit(solution)/shard_map/ppermute | solution.py:25
  95.8 5.2 %collective-permute-start.32 = (bf16[384,128]{1,0:T(8,128)(2,1)S(1)}, bf16[384,128]{1,0:T(8,128)(2,1)S(1)}, u32[]{:S(2)}, u32[]{:S(2)}) collective-permute-start(bf16[384,128]{1,0:T(8,128)(2,1)S(1)} %add_convert_fusion.1), channel_id=1, source_target_pairs={{0,32},{8,40},{16,48},{24,56},{32,0},{40,8},{48,16},{56,24},{64,96... | collective-permute-start | bytes 294920 | tf_op jit(solution)/shard_map/ppermute | solution.py:25
  101.1 8.3 %collective-permute-start.35 = (bf16[384,128]{1,0:T(8,128)(2,1)S(1)}, bf16[384,128]{1,0:T(8,128)(2,1)S(1)}, u32[]{:S(2)}, u32[]{:S(2)}) collective-permute-start(bf16[384,128]{1,0:T(8,128)(2,1)S(1)} %add_convert_fusion.refs_0_), channel_id=1, source_target_pairs={{0,2},{1,3},{2,0},{3,1},{4,6},{5,7},{6,4},{7,5},{8,10},{9,11},{10,... | collective-permute-start | bytes 294920 | tf_op jit(solution)/shard_map/ppermute | solution.py:25
  103.0 22.4 %collective-permute-start.28 = (bf16[512,256]{1,0:T(8,128)(2,1)S(1)}, bf16[512,256]{1,0:T(8,128)(2,1)S(1)}, u32[]{:S(2)}, u32[]{:S(2)}) collective-permute-start(bf16[512,256]{1,0:T(8,128)(2,1)S(1)} %get-tuple-element.49), channel_id=1, source_target_pairs={{8,16},{16,8},{24,32},{32,24},{40,48},{48,40},{56,64},{64,56},{72,... | collective-permute-start | bytes 786440 | tf_op jit(solution)/shard_map/ppermute | solution.py:35
  105.6 19.7 %collective-permute-start.27 = (bf16[512,256]{1,0:T(8,128)(2,1)S(1)}, bf16[512,256]{1,0:T(8,128)(2,1)S(1)}, u32[]{:S(2)}, u32[]{:S(2)}) collective-permute-start(bf16[512,256]{1,0:T(8,128)(2,1)S(1)} %get-tuple-element.48), channel_id=1, source_target_pairs={{0,8},{8,0},{16,24},{24,16},{32,40},{40,32},{48,56},{56,48},{64,72... | collective-permute-start | bytes 786440 | tf_op jit(solution)/shard_map/ppermute | solution.py:35
  105.7 10.1 %collective-permute-start.36 = (bf16[384,128]{1,0:T(8,128)(2,1)S(1)}, bf16[384,128]{1,0:T(8,128)(2,1)S(1)}, u32[]{:S(2)}, u32[]{:S(2)}) collective-permute-start(bf16[384,128]{1,0:T(8,128)(2,1)S(1)} %add_convert_fusion.refs_0_), channel_id=1, source_target_pairs={{0,4},{1,5},{2,6},{3,7},{4,0},{5,1},{6,2},{7,3},{8,12},{9,13},{10,... | collective-permute-start | bytes 294920 | tf_op jit(solution)/shard_map/ppermute | solution.py:25
  108.5 8.8 %collective-permute-start.37 = (bf16[384,128]{1,0:T(8,128)(2,1)S(1)}, bf16[384,128]{1,0:T(8,128)(2,1)S(1)}, u32[]{:S(2)}, u32[]{:S(2)}) collective-permute-start(bf16[384,128]{1,0:T(8,128)(2,1)S(1)} %add_convert_fusion.refs_0_), channel_id=1, source_target_pairs={{0,6},{1,7},{2,4},{3,5},{4,2},{5,3},{6,0},{7,1},{8,14},{9,15},{10,... | collective-permute-start | bytes 294920 | tf_op jit(solution)/shard_map/ppermute | solution.py:25
  109.3 11.2 %collective-permute-start.38 = (bf16[384,128]{1,0:T(8,128)(2,1)S(1)}, bf16[384,128]{1,0:T(8,128)(2,1)S(1)}, u32[]{:S(2)}, u32[]{:S(2)}) collective-permute-start(bf16[384,128]{1,0:T(8,128)(2,1)S(1)} %add_convert_fusion.refs_0_), channel_id=1, source_target_pairs={{0,1},{1,0},{2,3},{3,2},{4,5},{5,4},{6,7},{7,6},{8,9},{9,8},{10,11... | collective-permute-start | bytes 294920 | tf_op jit(solution)/shard_map/ppermute | solution.py:25
  (36 other events, 296.9 us)

commit v6 on v5

--- a/solution.py
+++ b/solution.py
@@ -278,19 +278,14 @@
     )
 
 
-def backward_kernel(
-    partners, counts, radius, first, context_grad, corr_weight, parts, *refs
+def scores_kernel(
+    counts, radius, context_grad, corr_weight, parts, first_grad, scores, narrow, wide, spread
 ):
-    cells = first.shape[0]
+    cells = context_grad.shape[0]
     slots = parts.shape[0]
-    scale = 1.0 / math.sqrt(first.shape[1])
     inside = tap_mask(radius[0, 0], LEAD_BACK, False)
-    first_grad, *kept, lent, totals, narrow, wide, spread = refs[-9:]
-    for ref in (*kept, lent, totals):
-        ref[...] = jnp.zeros_like(ref)
     spread_rows(corr_weight, narrow, wide, LEAD_BACK)
     spread[...] = wide[...].astype(BF16)
-    across = first[...].T
     for q in range(cells // GROUP):
         at = slice(q * GROUP, (q + 1) * GROUP)
         packed = (
@@ -303,7 +298,7 @@
             .astype(BF16)
             .astype(F32)
         )
-        first_here = jnp.zeros((GROUP, first.shape[1]), F32)
+        first_here = jnp.zeros((GROUP, parts.shape[2]), F32)
         for k in range(slots):
             mine = packed[:, k * 128 : (k + 1) * 128]
             band = jnp.concatenate(
@@ -311,14 +306,27 @@
                 axis=1,
             )
             band = jnp.where(inside & (k < counts[0, 0]), band, 0.0)
-            scores = pltpu.roll(band, WINDOW - REACH - LEAD_BACK, 1, stride=1, stride_axis=0).astype(BF16)
+            turn = WINDOW - REACH - LEAD_BACK
+            here = pltpu.roll(band, turn, 1, stride=1, stride_axis=0).astype(BF16)
+            scores[k, at] = here
             window = slice(q * GROUP, q * GROUP + WINDOW)
-            first_here += jnp.dot(scores, parts[k, window], preferred_element_type=F32)
-            totals[k, :, window] += jnp.dot(
-                across[:, at], scores, preferred_element_type=F32
+            first_here += jnp.dot(here, parts[k, window], preferred_element_type=F32)
+        first_grad[at] = first_here * (1.0 / math.sqrt(parts.shape[2]))
+
+
+def partners_kernel(partners, first, scores, *refs):
+    *kept, lent, totals = refs[-5:]
+    cells, channels = first.shape
+    scale = 1.0 / math.sqrt(channels)
+    for ref in (*kept, lent, totals):
+        ref[...] = jnp.zeros_like(ref)
+    across = first[...].T
+    for k in range(scores.shape[0]):
+        for q in range(cells // GROUP):
+            at = slice(q * GROUP, (q + 1) * GROUP)
+            totals[k, :, q * GROUP : q * GROUP + WINDOW] += jnp.dot(
+                across[:, at], scores[k, at], preferred_element_type=F32
             )
-        first_grad[at] = first_here * scale
-    for k in range(slots):
         value = (totals[k, :, GROUP : GROUP + cells] * scale).astype(BF16).T
         place = tile_of(partners[0, 0, k])
         for x in range(3):
@@ -355,7 +363,7 @@
         corr[:, h * 128 : (h + 1) * 128] = whole[base + h * 384 : base + h * 384 + corr.shape[0]]
 
 
-def call(kernel, out_shape, in_specs, scratch=(), flops=0):
+def call(kernel, out_shape, in_specs, scratch=(), flops=1000):
     return pl.pallas_call(
         kernel,
         out_shape=out_shape,
@@ -365,12 +373,6 @@
         compiler_params=pltpu.CompilerParams(vmem_limit_bytes=VMEM_LIMIT),
         cost_estimate=pl.CostEstimate(flops=flops, bytes_accessed=flops // 300, transcendentals=0),
     )
-
-
-def halve(cur, mine, axis, bits):
-    size = cur.shape[0] // 2
-    gone = lax.dynamic_slice_in_dim(cur, (1 - mine) * size, size).astype(BF16)
-    return lax.dynamic_slice_in_dim(cur, mine * size, size), gone, swap(gone, axis, bits)
 
 
 def sum_everywhere(cur, axis, unit):
@@ -415,26 +417,33 @@
     )(*tables, first, context, cotangent, conv_weight, corr_weight, *around)
 
 
-def backward(tables, first, context_grad, corr_weight, parts, after=()):
-    cells, channels = first.shape
-    slots, hidden = parts.shape[0], context_grad.shape[1]
+def backward_scores(tables, context_grad, corr_weight, parts):
+    cells, hidden = context_grad.shape
+    slots, _, channels = parts.shape
     shape = jax.ShapeDtypeStruct
     return call(
-        backward_kernel,
-        (
-            shape((cells, channels), F32),
-            *[shape((3, cells, channels), BF16)] * 3,
-            shape((6, cells, channels), BF16),
-        ),
-        [SMEM] * 3 + [VMEM] * 4 + [ANY] * len(after),
+        scores_kernel,
+        (shape((cells, channels), F32), shape((slots, cells, WINDOW), BF16)),
+        [SMEM] * 2 + [VMEM] * 3,
         [
-            pltpu.VMEM((slots, channels, cells + 2 * GROUP), F32),
             pltpu.VMEM(corr_weight.shape, F32),
             pltpu.VMEM((slots * 128, hidden), F32),
             pltpu.VMEM((slots * 128, hidden), BF16),
         ],
-        flops=3 * 10**9,
-    )(*tables, first, context_grad, corr_weight, parts, *after)
+        flops=4 * 10**9,
+    )(*tables[1:], context_grad, corr_weight, parts)
+
+
+def backward_partners(tables, first, scores, after=()):
+    cells, channels = first.shape
+    shape = jax.ShapeDtypeStruct
+    return call(
+        partners_kernel,
+        (*[shape((3, cells, channels), BF16)] * 3, shape((6, cells, channels), BF16)),
+        [SMEM] + [VMEM] * 2 + [ANY] * len(after),
+        [pltpu.VMEM((scores.shape[0], channels, cells + 2 * GROUP), F32)],
+        flops=4 * 10**9,
+    )(tables[0], first, scores, *after)
 
 
 def body(
@@ -470,10 +479,14 @@
         tables, first, context.reshape(cells, hidden), cot, conv_weight, corr_weight, around
     )
     total = weights_kept + swap(weights_sent, "col", 1).astype(F32)
-    total, gone, got = halve(total, chip >> 1, "col", 4)
+    size = total.shape[0] // 4
+    pieces = [lax.dynamic_slice_in_dim(total, (chip ^ s) * size, size) for s in range(4)]
+    gone = [piece.astype(BF16) for piece in pieces[1:]]
+    got = [swap(piece, "col", 2 * s) for s, piece in zip((1, 2, 3), gone)]
     around_motion = rim(facing, away, ends, row_even, col_even)
-    first_grad, *kept, lent = backward(
-        tables, first, context_grad, corr_weight, parts, (gone, *around_motion)
+    first_grad, scores = backward_scores(tables, context_grad, corr_weight, parts)
+    *kept, lent = backward_partners(
+        tables, first, scores, (*got, *around_motion[:2])
     )
     lent = swap(lent, "col", 1)
     side = jnp.where((core == 0) == chip_even, 1, 2)
@@ -481,20 +494,21 @@
         (kept[x].astype(F32) + jnp.where(side == x, lent[3:].astype(F32), 0.0)).astype(BF16)
         for x in (1, 2)
     ]
-    total, _, got = halve(total + got.astype(F32), chip & 1, "col", 2)
+    total = (pieces[0] + got[0].astype(F32)) + (got[1].astype(F32) + got[2].astype(F32))
+    total, *ready = lax.optimization_barrier((total, *sent, *around_motion))
+    sent, around_motion = ready[:2], ready[2:]
+    middle = kept[0].astype(F32) + lent[:3].astype(F32)
+    for x in (1, 2):
+        middle += swap_pairs(sent[x - 1], "col", x - 1, 2).astype(F32)
+    total = sum_everywhere(sum_everywhere(total, "row", 1), "row", 4).astype(BF16)
+    shards = [total] + [swap(total, "col", 2 * s) for s in (1, 2, 3)]
     features = call(
         features_kernel,
         shape((cells, out_width), BF16),
         [VMEM] * 6,
         [pltpu.VMEM(((rows_tile + 2) * cols_tile, 3 * hidden), BF16)],
-        flops=10**9,
     )(motion, *around_motion, conv_weight.reshape(3, 3 * hidden, out_width))
-    total, features, *sent = lax.optimization_barrier((total + got.astype(F32), features, *sent))
-    middle = kept[0].astype(F32) + lent[:3].astype(F32)
-    for x in (1, 2):
-        middle += swap_pairs(sent[x - 1], "col", x - 1, 2).astype(F32)
-    total = sum_everywhere(sum_everywhere(total, "row", 1), "row", 4).astype(BF16)
-    shards = [total] + [swap(total, "col", 2 * s) for s in (1, 2, 3)]
+    features, *shards = lax.optimization_barrier((features, *shards))
     shards += [swap(shard, "col", 1) for shard in shards]
     second_grad = middle[0]
     for r in (1, 2):

time: 128 us -> 124 us (0.969)
  waiting for transfers between devices: 25.6 us -> 20.6 us
  starting transfers between devices: 68.5 us -> 64.8 us
  Pallas kernels: 23.6 us -> 26.2 us
  other arithmetic: 3.7 us -> 5.61 us
    ppermute x16, waiting for transfers between devices: 12 us -> 8.28 us  [swap_pairs(): return lax.ppermute(array, axis, pairs)]
    pallas_call x1 -> x2, Pallas kernels: 7.58 us -> 10.4 us  [the longest x1 5.55 us: backward_partners(): call(partners_kernel, (*[shape((3, cells, channels), BF16)] * 3, shape((6...]
    ppermute x16, starting transfers between devices: 32.3 us -> 30.2 us  [swap_pairs(): return lax.ppermute(array, axis, pairs)]
    ppermute x26 -> x27, starting transfers between devices: 36.1 us -> 34.6 us  [swap(): lax.ppermute(array, axis, [(i, i ^ bits) for i in range(lax.axis_size(axi...]
    convert_element_type x1, other arithmetic: 0.41 us -> 1.86 us  [body(): (kept[x].astype(F32) + jnp.where(side == x, lent[3:].astype(F32), 0.0)).a...]
    ppermute x26 -> x27, waiting for transfers between devices: 13.6 us -> 12.3 us  [swap(): lax.ppermute(array, axis, [(i, i ^ bits) for i in range(lax.axis_size(axi...]
  transfers between devices with their start and end apart: 42 -> 43, of which waited for: 17 -> 16; matrix products, arithmetic and copies ran while one was open for 2% -> 3% of each run, Pallas kernels for 4% -> 8%
where the time goes in v6:
time: 124 us; the launch traced here: 123 us
  starting transfers between devices  64.8 us (52%)
  Pallas kernels  26.2 us (21%)
  waiting for transfers between devices  20.6 us (17%)
  other arithmetic  5.61 us (5%)
  local copies, waits for them, and re-layouts  3 us (2%)
  between operations  2.47 us (2%)
    ppermute x27, starting transfers between devices, swap(): lax.ppermute(array, axis, [(i, i ^ bits) for i in range(lax.axis_size(axi...  34.6 us
    ppermute x16, starting transfers between devices, swap_pairs(): return lax.ppermute(array, axis, pairs)  30.2 us
    ppermute x27, waiting for transfers between devices, swap(): lax.ppermute(array, axis, [(i, i ^ bits) for i in range(lax.axis_size(axi...  12.3 us
    pallas_call x1, Pallas kernels, forward(): call(forward_kernel, (shape((cells, hidden), BF16), shape((cells, hidden)...  8.79 us
    ppermute x16, waiting for transfers between devices, swap_pairs(): return lax.ppermute(array, axis, pairs)  8.28 us
    pallas_call x1, Pallas kernels, backward_partners(): call(partners_kernel, (*[shape((3, cells, channels), BF16)] * 3, shape((6...  5.55 us
    pallas_call x1, Pallas kernels, backward_scores(): call(scores_kernel, (shape((cells, channels), F32), shape((slots, cells,...  4.85 us
    pallas_call x1, Pallas kernels, body(): call(features_kernel, shape((cells, out_width), BF16), [VMEM] * 6, [pltpu...  2.66 us
  transfers between devices with their start and end apart: 43, of which 16 were waited for; matrix products, arithmetic and copies ran while one was open for 3% of the time, Pallas kernels for 8%

profile of v6, /device:TPU:33, one launch (start us, length us, event | category | flops | bytes accessed | tf_op | source)
XLA Modules:
  0.0 122.6 jit_solution(5950060055410852730)
XLA Ops:
  0.6 1.8 %shard_map.136.refs_0_ = bf16[560,256]{1,0:T(8,128)(2,1)} custom-call(bf16[512,256]{1,0:T(8,128)(2,1)} %bitcast.26, bf16[512,128]{1,0:T(8,128)(2,1)} %bitcast.27), custom_call_target="tpu_custom_call" | custom-call | flops 1000 | bytes 3 | tf_op jit(solution)/shard_map/pallas_call | solution.py:464
  4.4 1.4 %collective-permute-start.5 = (bf16[560,256]{1,0:T(8,128)(2,1)}, bf16[560,256]{1,0:T(8,128)(2,1)S(1)}, u32[]{:S(2)}, u32[]{:S(2)}) collective-permute-start(bf16[560,256]{1,0:T(8,128)(2,1)} %shard_map.136.refs_0_), channel_id=1, source_target_pairs={{0,8},{8,0},{16,24},{24,16},{32,40},{40,32},{48,56},{56,48},{64,72... | collective-permute-start | bytes 860168 | tf_op jit(solution)/shard_map/ppermute | solution.py:35
  7.0 3.3 %collective-permute-start.11 = (bf16[560,256]{1,0:T(8,128)(2,1)}, bf16[560,256]{1,0:T(8,128)(2,1)S(1)}, u32[]{:S(2)}, u32[]{:S(2)}) collective-permute-start(bf16[560,256]{1,0:T(8,128)(2,1)} %shard_map.136.refs_0_), channel_id=1, source_target_pairs={{8,16},{16,8},{24,32},{32,24},{40,48},{48,40},{56,64},{64,56},{72,... | collective-permute-start | bytes 860168 | tf_op jit(solution)/shard_map/ppermute | solution.py:35
  10.4 1.5 %collective-permute-start.2 = (bf16[560,256]{1,0:T(8,128)(2,1)S(1)}, bf16[560,256]{1,0:T(8,128)(2,1)S(1)}, u32[]{:S(2)}, u32[]{:S(2)}) collective-permute-start(bf16[560,256]{1,0:T(8,128)(2,1)S(1)} %collective-permute-done.1.refs_2_), channel_id=1, source_target_pairs={{0,1},{1,0},{2,3},{3,2},{4,5},{5,4},{6,7},{7,6},{8,9},{9,8},{10,11... | collective-permute-start | bytes 860168 | tf_op jit(solution)/shard_map/ppermute | solution.py:25
  12.0 1.9 %collective-permute-start.6 = (bf16[560,256]{1,0:T(8,128)(2,1)S(1)}, bf16[560,256]{1,0:T(8,128)(2,1)S(1)}, u32[]{:S(2)}, u32[]{:S(2)}) collective-permute-start(bf16[560,256]{1,0:T(8,128)(2,1)S(1)} %collective-permute-done.5.refs_6_), channel_id=1, source_target_pairs={{0,1},{1,0},{2,3},{3,2},{4,5},{5,4},{6,7},{7,6},{8,9},{9,8},{10,11... | collective-permute-start | bytes 860168 | tf_op jit(solution)/shard_map/ppermute | solution.py:25
  13.9 3.4 %collective-permute-start.7 = (bf16[560,256]{1,0:T(8,128)(2,1)S(1)}, bf16[560,256]{1,0:T(8,128)(2,1)S(1)}, u32[]{:S(2)}, u32[]{:S(2)}) collective-permute-start(bf16[560,256]{1,0:T(8,128)(2,1)S(1)} %collective-permute-done.5.refs_6_), channel_id=1, source_target_pairs={{0,2},{2,0},{1,3},{3,1},{4,6},{6,4},{5,7},{7,5},{8,10},{10,8},{9,1... | collective-permute-start | bytes 860168 | tf_op jit(solution)/shard_map/ppermute | solution.py:35
  17.3 2.4 %collective-permute-done.11.refs_12_ = bf16[560,256]{1,0:T(8,128)(2,1)S(1)} collective-permute-done((bf16[560,256]{1,0:T(8,128)(2,1)}, bf16[560,256]{1,0:T(8,128)(2,1)S(1)}, u32[]{:S(2)}, u32[]{:S(2)}) %collective-permute-start.11) | collective-permute-done | bytes 286752 | tf_op jit(solution)/shard_map/ppermute | solution.py:35
  19.7 3.4 %collective-permute-start.13 = (bf16[560,256]{1,0:T(8,128)(2,1)S(1)}, bf16[560,256]{1,0:T(8,128)(2,1)S(1)}, u32[]{:S(2)}, u32[]{:S(2)}) collective-permute-start(bf16[560,256]{1,0:T(8,128)(2,1)S(1)} %collective-permute-done.1.refs_2_), channel_id=1, source_target_pairs={{8,16},{16,8},{24,32},{32,24},{40,48},{48,40},{56,64},{64,56},{72,... | collective-permute-start | bytes 860168 | tf_op jit(solution)/shard_map/ppermute | solution.py:35
  25.0 2.2 %collective-permute-done.9.refs_10_ = bf16[560,256]{1,0:T(8,128)(2,1)S(1)} collective-permute-done((bf16[560,256]{1,0:T(8,128)(2,1)S(1)}, bf16[560,256]{1,0:T(8,128)(2,1)S(1)}, u32[]{:S(2)}, u32[]{:S(2)}) %collective-permute-start.9) | collective-permute-done | bytes 286752 | tf_op jit(solution)/shard_map/ppermute | solution.py:35
  27.2 1.7 %collective-permute-start.10 = (bf16[560,256]{1,0:T(8,128)(2,1)S(1)}, bf16[560,256]{1,0:T(8,128)(2,1)S(1)}, u32[]{:S(2)}, u32[]{:S(2)}) collective-permute-start(bf16[560,256]{1,0:T(8,128)(2,1)S(1)} %collective-permute-done.9.refs_10_), channel_id=1, source_target_pairs={{0,1},{1,0},{2,3},{3,2},{4,5},{5,4},{6,7},{7,6},{8,9},{9,8},{10,11... | collective-permute-start | bytes 860168 | tf_op jit(solution)/shard_map/ppermute | solution.py:25
  28.9 2.3 %collective-permute-done.13.refs_14_ = bf16[560,256]{1,0:T(8,128)(2,1)S(1)} collective-permute-done((bf16[560,256]{1,0:T(8,128)(2,1)S(1)}, bf16[560,256]{1,0:T(8,128)(2,1)S(1)}, u32[]{:S(2)}, u32[]{:S(2)}) %collective-permute-start.13) | collective-permute-done | bytes 286752 | tf_op jit(solution)/shard_map/ppermute | solution.py:35
  31.2 1.7 %collective-permute-start.14 = (bf16[560,256]{1,0:T(8,128)(2,1)S(1)}, bf16[560,256]{1,0:T(8,128)(2,1)S(1)}, u32[]{:S(2)}, u32[]{:S(2)}) collective-permute-start(bf16[560,256]{1,0:T(8,128)(2,1)S(1)} %collective-permute-done.13.refs_14_), channel_id=1, source_target_pairs={{0,1},{1,0},{2,3},{3,2},{4,5},{5,4},{6,7},{7,6},{8,9},{9,8},{10,11... | collective-permute-start | bytes 860168 | tf_op jit(solution)/shard_map/ppermute | solution.py:25
  35.5 8.8 %shard_map.137 = (bf16[512,256]{1,0:T(8,128)(2,1)}, bf16[512,256]{1,0:T(8,128)(2,1)}, bf16[32,256]{1,0:T(8,128)(2,1)}, bf16[32,256]{1,0:T(8,128)(2,1)}, bf16[2,1...) custom-call(s32[1,1,4]{2,1,0:T(1,128)} %partners.3, ...), custom_call_target="tpu_custom_call" | custom-call | flops 3000000000 | bytes 10000000 | tf_op jit(solution)/shard_map/pallas_call | solution.py:390
  44.7 3.3 %collective-permute-start.21 = (bf16[32,256]{1,0:T(8,128)(2,1)}, bf16[32,256]{1,0:T(8,128)(2,1)S(1)}, u32[]{:S(2)}, u32[]{:S(2)}) collective-permute-start(bf16[32,256]{1,0:T(8,128)(2,1)} %get-tuple-element.40), channel_id=1, source_target_pairs={{8,16},{16,8},{24,32},{32,24},{40,48},{48,40},{56,64},{64,56},{72,... | collective-permute-start | bytes 49160 | tf_op jit(solution)/shard_map/ppermute | solution.py:35
  48.1 4.9 %shard_map.138 = (f32[512,256]{1,0:T(8,128)}, bf16[4,512,384]{2,1,0:T(8,128)(2,1)}) custom-call(s32[1,1]{1,0:T(1,128)S(6)} %copy.15.counts, s32[1,1]{1,0:T(1,128)S(6)} %copy.16.radius, bf16[512,256]{1,0:T(8,128)(2,1)} %get-tuple-element.37.context_grad, bf16[324,256]{1,0:T(8,128)(2,1)} %corr_weight.3, bf16[4,768,256]{2,1,0:T(8,128)(2,1)} %get-tuple-element.38.parts), custom_call_target="tpu_custom_call" | custom-call | flops 4000000000 | bytes 13333333 | tf_op jit(solution)/shard_map/pallas_call | solution.py:424
  53.1 1.9 %collective-permute-start.20 = (bf16[384,128]{1,0:T(8,128)(2,1)S(1)}, bf16[384,128]{1,0:T(8,128)(2,1)S(1)}, u32[]{:S(2)}, u32[]{:S(2)}) collective-permute-start(bf16[384,128]{1,0:T(8,128)(2,1)S(1)} %get-tuple-element.69), channel_id=1, source_target_pairs={{0,6},{1,7},{2,4},{3,5},{4,2},{5,3},{6,0},{7,1},{8,14},{9,15},{10,... | collective-permute-start | bytes 294920 | tf_op jit(solution)/shard_map/ppermute | solution.py:25
  55.0 5.3 %collective-permute-start.19 = (bf16[384,128]{1,0:T(8,128)(2,1)S(1)}, bf16[384,128]{1,0:T(8,128)(2,1)S(1)}, u32[]{:S(2)}, u32[]{:S(2)}) collective-permute-start(bf16[384,128]{1,0:T(8,128)(2,1)S(1)} %get-tuple-element.70), channel_id=1, source_target_pairs={{0,4},{1,5},{2,6},{3,7},{4,0},{5,1},{6,2},{7,3},{8,12},{9,13},{10,... | collective-permute-start | bytes 294920 | tf_op jit(solution)/shard_map/ppermute | solution.py:25
  62.3 1.7 %collective-permute-done.18.refs_0_ = bf16[384,128]{1,0:T(8,128)(2,1)S(1)} collective-permute-done((bf16[384,128]{1,0:T(8,128)(2,1)S(1)}, bf16[384,128]{1,0:T(8,128)(2,1)S(1)}, u32[]{:S(2)}, u32[]{:S(2)}) %collective-permute-start.18) | collective-permute-done | bytes 98336 | tf_op jit(solution)/shard_map/ppermute | solution.py:25
  64.6 5.5 %shard_map.139 = (bf16[3,512,256]{2,1,0:T(8,128)(2,1)}, bf16[3,512,256]{2,1,0:T(8,128)(2,1)}, bf16[3,512,256]{2,1,0:T(8,128)(2,1)}, bf16[6,512,256]{2,1,0:T(8,128)(2,1)}) custom-call(s32[1,1,4]{2,1,0:T(1,128)} %partners.3, bf16[512,256]{1,0:T(8,128)(2,1)} %bitcast.33, bf16[4,512,384]{2,1,0:T(8,128)(2,1)} %get-tuple-element.39.scores, ...), custom_call_target="tpu_custom_call" | custom-call | flops 4000000000 | bytes 13333333 | tf_op jit(solution)/shard_map/pallas_call | solution.py:440
  70.1 2.1 %collective-permute-start.23 = (bf16[6,512,256]{2,1,0:T(8,128)(2,1)}, bf16[6,512,256]{2,1,0:T(8,128)(2,1)S(1)}, u32[]{:S(2)}, u32[]{:S(2)}) collective-permute-start(bf16[6,512,256]{2,1,0:T(8,128)(2,1)} %get-tuple-element.43), channel_id=1, source_target_pairs={{0,1},{1,0},{2,3},{3,2},{4,5},{5,4},{6,7},{7,6},{8,9},{9,8},{10,11... | collective-permute-start | bytes 4718600 | tf_op jit(solution)/shard_map/ppermute | solution.py:25
  73.1 3.8 %collective-permute-start.24 = (bf16[18,256]{1,0:T(8,128)(2,1)S(1)}, bf16[18,256]{1,0:T(8,128)(2,1)S(1)}, u32[]{:S(2)}, u32[]{:S(2)}) collective-permute-start(bf16[18,256]{1,0:T(8,128)(2,1)S(1)} %get-tuple-element.76), channel_id=1, source_target_pairs={{1,2},{2,1},{3,4},{4,3},{5,6},{6,5},{9,10},{10,9},{11,12},{12,11},... | collective-permute-start | bytes 27656 | tf_op jit(solution)/shard_map/ppermute | solution.py:35
  79.9 1.9 %fusion.3 = (bf16[3,512,256]{2,1,0:T(8,128)(2,1)S(1)}, bf16[3,512,256]{2,1,0:T(8,128)(2,1)S(1)}) fusion(bf16[3,512,256]{2,1,0:T(8,128)(2,1)} %get-tuple-element.44, pred[]{:T(512)S(6)} %eq.28, bf16[6,512,256]{2,1,0:T(8,128)(2,1)S(1)} %collective-permute-done.23, pred[]{:T(512)S(6)} %eq.27, bf16[3,512,256]{2,1,0:T(8,128)(2,1)} %get-tuple-element.42), kind=kLoop, calls=%fused_computation.5 | loop fusion | flops 3538944 | bytes 3932162 | tf_op jit(solution)/shard_map/convert_element_type | solution.py:494
  82.5 2.9 %collective-permute-start.35 = (bf16[3,512,256]{2,1,0:T(8,128)(2,1)S(1)}, bf16[3,512,256]{2,1,0:T(8,128)(2,1)S(1)}, u32[]{:S(2)}, u32[]{:S(2)}) collective-permute-start(bf16[3,512,256]{2,1,0:T(8,128)(2,1)S(1)} %get-tuple-element.54), channel_id=1, source_target_pairs={{0,2},{2,0},{1,3},{3,1},{4,6},{6,4},{5,7},{7,5},{8,10},{10,8},{9,1... | collective-permute-start | bytes 2359304 | tf_op jit(solution)/shard_map/ppermute | solution.py:35
  85.4 3.1 %collective-permute-start.28 = (bf16[384,128]{1,0:T(8,128)(2,1)S(1)}, bf16[384,128]{1,0:T(8,128)(2,1)S(1)}, u32[]{:S(2)}, u32[]{:S(2)}) collective-permute-start(bf16[384,128]{1,0:T(8,128)(2,1)S(1)} %add_add_fusion), channel_id=1, source_target_pairs={{0,24},{8,16},{16,8},{24,0},{32,56},{40,48},{48,40},{56,32},{64,88... | collective-permute-start | bytes 294920 | tf_op jit(solution)/shard_map/ppermute | solution.py:25
  89.1 3.1 %collective-permute-done.28 = bf16[384,128]{1,0:T(8,128)(2,1)S(1)} collective-permute-done((bf16[384,128]{1,0:T(8,128)(2,1)S(1)}, bf16[384,128]{1,0:T(8,128)(2,1)S(1)}, u32[]{:S(2)}, u32[]{:S(2)}) %collective-permute-start.28) | collective-permute-done | bytes 98336 | tf_op jit(solution)/shard_map/ppermute | solution.py:25
  94.1 1.9 %collective-permute-start.30 = (bf16[384,128]{1,0:T(8,128)(2,1)S(1)}, bf16[384,128]{1,0:T(8,128)(2,1)S(1)}, u32[]{:S(2)}, u32[]{:S(2)}) collective-permute-start(bf16[384,128]{1,0:T(8,128)(2,1)S(1)} %add_convert_fusion.1), channel_id=1, source_target_pairs={{0,64},{8,72},{16,80},{24,88},{32,96},{40,104},{48,112},{56,120},{... | collective-permute-start | bytes 294920 | tf_op jit(solution)/shard_map/ppermute | solution.py:25
  97.4 1.7 %collective-permute-done.30 = bf16[384,128]{1,0:T(8,128)(2,1)S(1)} collective-permute-done((bf16[384,128]{1,0:T(8,128)(2,1)S(1)}, bf16[384,128]{1,0:T(8,128)(2,1)S(1)}, u32[]{:S(2)}, u32[]{:S(2)}) %collective-permute-start.30) | collective-permute-done | bytes 98336 | tf_op jit(solution)/shard_map/ppermute | solution.py:25
  100.6 2.9 %collective-permute-start.33 = (bf16[384,128]{1,0:T(8,128)(2,1)S(1)}, bf16[384,128]{1,0:T(8,128)(2,1)S(1)}, u32[]{:S(2)}, u32[]{:S(2)}) collective-permute-start(bf16[384,128]{1,0:T(8,128)(2,1)S(1)} %add_convert_fusion.refs_0_), channel_id=1, source_target_pairs={{0,4},{1,5},{2,6},{3,7},{4,0},{5,1},{6,2},{7,3},{8,12},{9,13},{10,... | collective-permute-start | bytes 294920 | tf_op jit(solution)/shard_map/ppermute | solution.py:25
  104.7 5.3 %collective-permute-start.38 = (bf16[512,256]{1,0:T(8,128)(2,1)S(1)}, bf16[512,256]{1,0:T(8,128)(2,1)S(1)}, u32[]{:S(2)}, u32[]{:S(2)}) collective-permute-start(bf16[512,256]{1,0:T(8,128)(2,1)S(1)} %get-tuple-element.67), channel_id=1, source_target_pairs={{8,16},{16,8},{24,32},{32,24},{40,48},{48,40},{56,64},{64,56},{72,... | collective-permute-start | bytes 786440 | tf_op jit(solution)/shard_map/ppermute | solution.py:35
  110.1 2.7 %shard_map.140 = bf16[512,128]{1,0:T(8,128)(2,1)} custom-call(bf16[512,256]{1,0:T(8,128)(2,1)} %get-tuple-element.34.motion, bf16[32,256]{1,0:T(8,128)(2,1)} %get-tuple-element.46.refs_3_.north, bf16[32,256]{1,0:T(8,128)(2,1)} %get-tuple-element.47.refs_4_.south, bf16[18,256]{1,0:T(8,128)(2,1)} %get-tuple-element.48.west, ...), custom_call_target="tpu_custom_call" | custom-call | flops 1000 | bytes 3 | tf_op jit(solution)/shard_map/pallas_call | solution.py:505
  112.9 3.5 %collective-permute-start.39 = (bf16[384,128]{1,0:T(8,128)(2,1)S(1)}, bf16[384,128]{1,0:T(8,128)(2,1)S(1)}, u32[]{:S(2)}, u32[]{:S(2)}) collective-permute-start(bf16[384,128]{1,0:T(8,128)(2,1)S(1)} %add_convert_fusion.refs_0_), channel_id=1, source_target_pairs={{0,1},{1,0},{2,3},{3,2},{4,5},{5,4},{6,7},{7,6},{8,9},{9,8},{10,11... | collective-permute-start | bytes 294920 | tf_op jit(solution)/shard_map/ppermute | solution.py:25
  119.3 2.5 %shard_map.141 = (f32[2304,128]{1,0:T(8,128)}, f32[324,256]{1,0:T(8,128)}) custom-call(bf16[384,128]{1,0:T(8,128)(2,1)} %copy-done.2, bf16[384,128]{1,0:T(8,128)(2,1)} %copy-done.3, bf16[384,128]{1,0:T(8,128)(2,1)} %copy-done.4, bf16[384,128]{1,0:T(8,128)(2,1)} %copy-done.5, bf16[384,128]{1,0:T(8,128)(2,1)} %copy-done.6, bf16[384,128]{1,0:T(8,128)(2,1)} %copy-done.7, ...), custom_call_target="tpu_custom_call" | custom-call | flops 1000 | bytes 3 | tf_op jit(solution)/shard_map/pallas_call | solution.py:516
  (136 shorter events, 24.6 us)
Async XLA Ops:
  2.5 7.9 %collective-permute-start.1 = (bf16[560,256]{1,0:T(8,128)(2,1)}, bf16[560,256]{1,0:T(8,128)(2,1)S(1)}, u32[]{:S(2)}, u32[]{:S(2)}) collective-permute-start(bf16[560,256]{1,0:T(8,128)(2,1)} %shard_map.136.refs_0_), channel_id=1, source_target_pairs={{0,2},{2,0},{1,3},{3,1},{4,6},{6,4},{5,7},{7,5},{8,10},{10,8},{9,1... | collective-permute-start | bytes 860168 | tf_op jit(solution)/shard_map/ppermute | solution.py:35
  3.7 8.3 %collective-permute-start.3 = (bf16[560,256]{1,0:T(8,128)(2,1)}, bf16[560,256]{1,0:T(8,128)(2,1)S(1)}, u32[]{:S(2)}, u32[]{:S(2)}) collective-permute-start(bf16[560,256]{1,0:T(8,128)(2,1)} %shard_map.136.refs_0_), channel_id=1, source_target_pairs={{2,4},{4,2},{3,5},{5,3},{10,12},{12,10},{11,13},{13,11},{18,20},{2... | collective-permute-start | bytes 860168 | tf_op jit(solution)/shard_map/ppermute | solution.py:35
  4.4 7.7 %collective-permute-start.5 = (bf16[560,256]{1,0:T(8,128)(2,1)}, bf16[560,256]{1,0:T(8,128)(2,1)S(1)}, u32[]{:S(2)}, u32[]{:S(2)}) collective-permute-start(bf16[560,256]{1,0:T(8,128)(2,1)} %shard_map.136.refs_0_), channel_id=1, source_target_pairs={{0,8},{8,0},{16,24},{24,16},{32,40},{40,32},{48,56},{56,48},{64,72... | collective-permute-start | bytes 860168 | tf_op jit(solution)/shard_map/ppermute | solution.py:35
  5.7 8.2 %collective-permute-start = (bf16[560,256]{1,0:T(8,128)(2,1)}, bf16[560,256]{1,0:T(8,128)(2,1)S(1)}, u32[]{:S(2)}, u32[]{:S(2)}) collective-permute-start(bf16[560,256]{1,0:T(8,128)(2,1)} %shard_map.136.refs_0_), channel_id=1, source_target_pairs={{0,1},{1,0},{2,3},{3,2},{4,5},{5,4},{6,7},{7,6},{8,9},{9,8},{10,11... | collective-permute-start | bytes 860168 | tf_op jit(solution)/shard_map/ppermute | solution.py:25
  7.0 12.7 %collective-permute-start.11 = (bf16[560,256]{1,0:T(8,128)(2,1)}, bf16[560,256]{1,0:T(8,128)(2,1)S(1)}, u32[]{:S(2)}, u32[]{:S(2)}) collective-permute-start(bf16[560,256]{1,0:T(8,128)(2,1)} %shard_map.136.refs_0_), channel_id=1, source_target_pairs={{8,16},{16,8},{24,32},{32,24},{40,48},{48,40},{56,64},{64,56},{72,... | collective-permute-start | bytes 860168 | tf_op jit(solution)/shard_map/ppermute | solution.py:35
  10.4 9.3 %collective-permute-start.2 = (bf16[560,256]{1,0:T(8,128)(2,1)S(1)}, bf16[560,256]{1,0:T(8,128)(2,1)S(1)}, u32[]{:S(2)}, u32[]{:S(2)}) collective-permute-start(bf16[560,256]{1,0:T(8,128)(2,1)S(1)} %collective-permute-done.1.refs_2_), channel_id=1, source_target_pairs={{0,1},{1,0},{2,3},{3,2},{4,5},{5,4},{6,7},{7,6},{8,9},{9,8},{10,11... | collective-permute-start | bytes 860168 | tf_op jit(solution)/shard_map/ppermute | solution.py:25
  11.9 11.1 %collective-permute-start.4 = (bf16[560,256]{1,0:T(8,128)(2,1)S(1)}, bf16[560,256]{1,0:T(8,128)(2,1)S(1)}, u32[]{:S(2)}, u32[]{:S(2)}) collective-permute-start(bf16[560,256]{1,0:T(8,128)(2,1)S(1)} %collective-permute-done.3.refs_4_), channel_id=1, source_target_pairs={{0,1},{1,0},{2,3},{3,2},{4,5},{5,4},{6,7},{7,6},{8,9},{9,8},{10,11... | collective-permute-start | bytes 860168 | tf_op jit(solution)/shard_map/ppermute | solution.py:25
  12.0 11.7 %collective-permute-start.6 = (bf16[560,256]{1,0:T(8,128)(2,1)S(1)}, bf16[560,256]{1,0:T(8,128)(2,1)S(1)}, u32[]{:S(2)}, u32[]{:S(2)}) collective-permute-start(bf16[560,256]{1,0:T(8,128)(2,1)S(1)} %collective-permute-done.5.refs_6_), channel_id=1, source_target_pairs={{0,1},{1,0},{2,3},{3,2},{4,5},{5,4},{6,7},{7,6},{8,9},{9,8},{10,11... | collective-permute-start | bytes 860168 | tf_op jit(solution)/shard_map/ppermute | solution.py:25
  13.9 11.0 %collective-permute-start.7 = (bf16[560,256]{1,0:T(8,128)(2,1)S(1)}, bf16[560,256]{1,0:T(8,128)(2,1)S(1)}, u32[]{:S(2)}, u32[]{:S(2)}) collective-permute-start(bf16[560,256]{1,0:T(8,128)(2,1)S(1)} %collective-permute-done.5.refs_6_), channel_id=1, source_target_pairs={{0,2},{2,0},{1,3},{3,1},{4,6},{6,4},{5,7},{7,5},{8,10},{10,8},{9,1... | collective-permute-start | bytes 860168 | tf_op jit(solution)/shard_map/ppermute | solution.py:35
  19.6 7.6 %collective-permute-start.9 = (bf16[560,256]{1,0:T(8,128)(2,1)S(1)}, bf16[560,256]{1,0:T(8,128)(2,1)S(1)}, u32[]{:S(2)}, u32[]{:S(2)}) collective-permute-start(bf16[560,256]{1,0:T(8,128)(2,1)S(1)} %collective-permute-done.3.refs_4_), channel_id=1, source_target_pairs={{0,8},{8,0},{16,24},{24,16},{32,40},{40,32},{48,56},{56,48},{64,72... | collective-permute-start | bytes 860168 | tf_op jit(solution)/shard_map/ppermute | solution.py:35
  19.7 11.6 %collective-permute-start.13 = (bf16[560,256]{1,0:T(8,128)(2,1)S(1)}, bf16[560,256]{1,0:T(8,128)(2,1)S(1)}, u32[]{:S(2)}, u32[]{:S(2)}) collective-permute-start(bf16[560,256]{1,0:T(8,128)(2,1)S(1)} %collective-permute-done.1.refs_2_), channel_id=1, source_target_pairs={{8,16},{16,8},{24,32},{32,24},{40,48},{48,40},{56,64},{64,56},{72,... | collective-permute-start | bytes 860168 | tf_op jit(solution)/shard_map/ppermute | solution.py:35
  23.0 9.9 %collective-permute-start.15 = (bf16[560,256]{1,0:T(8,128)(2,1)S(1)}, bf16[560,256]{1,0:T(8,128)(2,1)S(1)}, u32[]{:S(2)}, u32[]{:S(2)}) collective-permute-start(bf16[560,256]{1,0:T(8,128)(2,1)S(1)} %collective-permute-done.11.refs_12_), channel_id=1, source_target_pairs={{2,4},{4,2},{3,5},{5,3},{10,12},{12,10},{11,13},{13,11},{18,20},{2... | collective-permute-start | bytes 860168 | tf_op jit(solution)/shard_map/ppermute | solution.py:35
  23.7 10.6 %collective-permute-start.12 = (bf16[560,256]{1,0:T(8,128)(2,1)S(1)}, bf16[560,256]{1,0:T(8,128)(2,1)S(1)}, u32[]{:S(2)}, u32[]{:S(2)}) collective-permute-start(bf16[560,256]{1,0:T(8,128)(2,1)S(1)} %collective-permute-done.11.refs_12_), channel_id=1, source_target_pairs={{0,1},{1,0},{2,3},{3,2},{4,5},{5,4},{6,7},{7,6},{8,9},{9,8},{10,11... | collective-permute-start | bytes 860168 | tf_op jit(solution)/shard_map/ppermute | solution.py:25
  24.9 9.5 %collective-permute-start.8 = (bf16[560,256]{1,0:T(8,128)(2,1)S(1)}, bf16[560,256]{1,0:T(8,128)(2,1)S(1)}, u32[]{:S(2)}, u32[]{:S(2)}) collective-permute-start(bf16[560,256]{1,0:T(8,128)(2,1)S(1)} %collective-permute-done.7.refs_8_), channel_id=1, source_target_pairs={{0,1},{1,0},{2,3},{3,2},{4,5},{5,4},{6,7},{7,6},{8,9},{9,8},{10,11... | collective-permute-start | bytes 860168 | tf_op jit(solution)/shard_map/ppermute | solution.py:25
  27.2 7.2 %collective-permute-start.10 = (bf16[560,256]{1,0:T(8,128)(2,1)S(1)}, bf16[560,256]{1,0:T(8,128)(2,1)S(1)}, u32[]{:S(2)}, u32[]{:S(2)}) collective-permute-start(bf16[560,256]{1,0:T(8,128)(2,1)S(1)} %collective-permute-done.9.refs_10_), channel_id=1, source_target_pairs={{0,1},{1,0},{2,3},{3,2},{4,5},{5,4},{6,7},{7,6},{8,9},{9,8},{10,11... | collective-permute-start | bytes 860168 | tf_op jit(solution)/shard_map/ppermute | solution.py:25
  44.3 8.7 %collective-permute-start.17 = (bf16[1536,128]{1,0:T(8,128)(2,1)}, bf16[1536,128]{1,0:T(8,128)(2,1)S(1)}, u32[]{:S(2)}, u32[]{:S(2)}) collective-permute-start(bf16[1536,128]{1,0:T(8,128)(2,1)} %get-tuple-element.36), channel_id=1, source_target_pairs={{0,1},{1,0},{2,3},{3,2},{4,5},{5,4},{6,7},{7,6},{8,9},{9,8},{10,11... | collective-permute-start | bytes 1179656 | tf_op jit(solution)/shard_map/ppermute | solution.py:25
  44.7 15.5 %collective-permute-start.22 = (bf16[32,256]{1,0:T(8,128)(2,1)}, bf16[32,256]{1,0:T(8,128)(2,1)S(1)}, u32[]{:S(2)}, u32[]{:S(2)}) collective-permute-start(bf16[32,256]{1,0:T(8,128)(2,1)} %get-tuple-element.41), channel_id=1, source_target_pairs={{0,8},{8,0},{16,24},{24,16},{32,40},{40,32},{48,56},{56,48},{64,72... | collective-permute-start | bytes 49160 | tf_op jit(solution)/shard_map/ppermute | solution.py:35
  44.7 15.5 %collective-permute-start.21 = (bf16[32,256]{1,0:T(8,128)(2,1)}, bf16[32,256]{1,0:T(8,128)(2,1)S(1)}, u32[]{:S(2)}, u32[]{:S(2)}) collective-permute-start(bf16[32,256]{1,0:T(8,128)(2,1)} %get-tuple-element.40), channel_id=1, source_target_pairs={{8,16},{16,8},{24,32},{32,24},{40,48},{48,40},{56,64},{64,56},{72,... | collective-permute-start | bytes 49160 | tf_op jit(solution)/shard_map/ppermute | solution.py:35
  53.1 7.8 %collective-permute-start.20 = (bf16[384,128]{1,0:T(8,128)(2,1)S(1)}, bf16[384,128]{1,0:T(8,128)(2,1)S(1)}, u32[]{:S(2)}, u32[]{:S(2)}) collective-permute-start(bf16[384,128]{1,0:T(8,128)(2,1)S(1)} %get-tuple-element.69), channel_id=1, source_target_pairs={{0,6},{1,7},{2,4},{3,5},{4,2},{5,3},{6,0},{7,1},{8,14},{9,15},{10,... | collective-permute-start | bytes 294920 | tf_op jit(solution)/shard_map/ppermute | solution.py:25
  55.0 7.3 %collective-permute-start.19 = (bf16[384,128]{1,0:T(8,128)(2,1)S(1)}, bf16[384,128]{1,0:T(8,128)(2,1)S(1)}, u32[]{:S(2)}, u32[]{:S(2)}) collective-permute-start(bf16[384,128]{1,0:T(8,128)(2,1)S(1)} %get-tuple-element.70), channel_id=1, source_target_pairs={{0,4},{1,5},{2,6},{3,7},{4,0},{5,1},{6,2},{7,3},{8,12},{9,13},{10,... | collective-permute-start | bytes 294920 | tf_op jit(solution)/shard_map/ppermute | solution.py:25
  70.1 9.8 %collective-permute-start.23 = (bf16[6,512,256]{2,1,0:T(8,128)(2,1)}, bf16[6,512,256]{2,1,0:T(8,128)(2,1)S(1)}, u32[]{:S(2)}, u32[]{:S(2)}) collective-permute-start(bf16[6,512,256]{2,1,0:T(8,128)(2,1)} %get-tuple-element.43), channel_id=1, source_target_pairs={{0,1},{1,0},{2,3},{3,2},{4,5},{5,4},{6,7},{7,6},{8,9},{9,8},{10,11... | collective-permute-start | bytes 4718600 | tf_op jit(solution)/shard_map/ppermute | solution.py:25
  73.1 5.2 %collective-permute-start.24 = (bf16[18,256]{1,0:T(8,128)(2,1)S(1)}, bf16[18,256]{1,0:T(8,128)(2,1)S(1)}, u32[]{:S(2)}, u32[]{:S(2)}) collective-permute-start(bf16[18,256]{1,0:T(8,128)(2,1)S(1)} %get-tuple-element.76), channel_id=1, source_target_pairs={{1,2},{2,1},{3,4},{4,3},{5,6},{6,5},{9,10},{10,9},{11,12},{12,11},... | collective-permute-start | bytes 27656 | tf_op jit(solution)/shard_map/ppermute | solution.py:35
  81.8 22.5 %collective-permute-start.36 = (bf16[3,512,256]{2,1,0:T(8,128)(2,1)S(1)}, bf16[3,512,256]{2,1,0:T(8,128)(2,1)S(1)}, u32[]{:S(2)}, u32[]{:S(2)}) collective-permute-start(bf16[3,512,256]{2,1,0:T(8,128)(2,1)S(1)} %get-tuple-element.55), channel_id=1, source_target_pairs={{2,4},{4,2},{3,5},{5,3},{10,12},{12,10},{11,13},{13,11},{18,20},{2... | collective-permute-start | bytes 2359304 | tf_op jit(solution)/shard_map/ppermute | solution.py:35
  82.5 21.8 %collective-permute-start.35 = (bf16[3,512,256]{2,1,0:T(8,128)(2,1)S(1)}, bf16[3,512,256]{2,1,0:T(8,128)(2,1)S(1)}, u32[]{:S(2)}, u32[]{:S(2)}) collective-permute-start(bf16[3,512,256]{2,1,0:T(8,128)(2,1)S(1)} %get-tuple-element.54), channel_id=1, source_target_pairs={{0,2},{2,0},{1,3},{3,1},{4,6},{6,4},{5,7},{7,5},{8,10},{10,8},{9,1... | collective-permute-start | bytes 2359304 | tf_op jit(solution)/shard_map/ppermute | solution.py:35
  85.4 6.8 %collective-permute-start.28 = (bf16[384,128]{1,0:T(8,128)(2,1)S(1)}, bf16[384,128]{1,0:T(8,128)(2,1)S(1)}, u32[]{:S(2)}, u32[]{:S(2)}) collective-permute-start(bf16[384,128]{1,0:T(8,128)(2,1)S(1)} %add_add_fusion), channel_id=1, source_target_pairs={{0,24},{8,16},{16,8},{24,0},{32,56},{40,48},{48,40},{56,32},{64,88... | collective-permute-start | bytes 294920 | tf_op jit(solution)/shard_map/ppermute | solution.py:25
  88.5 5.0 %collective-permute-start.27 = (bf16[384,128]{1,0:T(8,128)(2,1)S(1)}, bf16[384,128]{1,0:T(8,128)(2,1)S(1)}, u32[]{:S(2)}, u32[]{:S(2)}) collective-permute-start(bf16[384,128]{1,0:T(8,128)(2,1)S(1)} %add_add_fusion), channel_id=1, source_target_pairs={{0,16},{8,24},{16,0},{24,8},{32,48},{40,56},{48,32},{56,40},{64,80... | collective-permute-start | bytes 294920 | tf_op jit(solution)/shard_map/ppermute | solution.py:25
  88.5 5.0 %collective-permute-start.26 = (bf16[384,128]{1,0:T(8,128)(2,1)S(1)}, bf16[384,128]{1,0:T(8,128)(2,1)S(1)}, u32[]{:S(2)}, u32[]{:S(2)}) collective-permute-start(bf16[384,128]{1,0:T(8,128)(2,1)S(1)} %add_add_fusion), channel_id=1, source_target_pairs={{0,8},{8,0},{16,24},{24,16},{32,40},{40,32},{48,56},{56,48},{64,72... | collective-permute-start | bytes 294920 | tf_op jit(solution)/shard_map/ppermute | solution.py:25
  100.3 12.5 %collective-permute-start.32 = (bf16[384,128]{1,0:T(8,128)(2,1)S(1)}, bf16[384,128]{1,0:T(8,128)(2,1)S(1)}, u32[]{:S(2)}, u32[]{:S(2)}) collective-permute-start(bf16[384,128]{1,0:T(8,128)(2,1)S(1)} %add_convert_fusion.refs_0_), channel_id=1, source_target_pairs={{0,2},{1,3},{2,0},{3,1},{4,6},{5,7},{6,4},{7,5},{8,10},{9,11},{10,... | collective-permute-start | bytes 294920 | tf_op jit(solution)/shard_map/ppermute | solution.py:25
  100.6 12.3 %collective-permute-start.33 = (bf16[384,128]{1,0:T(8,128)(2,1)S(1)}, bf16[384,128]{1,0:T(8,128)(2,1)S(1)}, u32[]{:S(2)}, u32[]{:S(2)}) collective-permute-start(bf16[384,128]{1,0:T(8,128)(2,1)S(1)} %add_convert_fusion.refs_0_), channel_id=1, source_target_pairs={{0,4},{1,5},{2,6},{3,7},{4,0},{5,1},{6,2},{7,3},{8,12},{9,13},{10,... | collective-permute-start | bytes 294920 | tf_op jit(solution)/shard_map/ppermute | solution.py:25
  103.5 9.4 %collective-permute-start.34 = (bf16[384,128]{1,0:T(8,128)(2,1)S(1)}, bf16[384,128]{1,0:T(8,128)(2,1)S(1)}, u32[]{:S(2)}, u32[]{:S(2)}) collective-permute-start(bf16[384,128]{1,0:T(8,128)(2,1)S(1)} %add_convert_fusion.refs_0_), channel_id=1, source_target_pairs={{0,6},{1,7},{2,4},{3,5},{4,2},{5,3},{6,0},{7,1},{8,14},{9,15},{10,... | collective-permute-start | bytes 294920 | tf_op jit(solution)/shard_map/ppermute | solution.py:25
  104.7 17.0 %collective-permute-start.38 = (bf16[512,256]{1,0:T(8,128)(2,1)S(1)}, bf16[512,256]{1,0:T(8,128)(2,1)S(1)}, u32[]{:S(2)}, u32[]{:S(2)}) collective-permute-start(bf16[512,256]{1,0:T(8,128)(2,1)S(1)} %get-tuple-element.67), channel_id=1, source_target_pairs={{8,16},{16,8},{24,32},{32,24},{40,48},{48,40},{56,64},{64,56},{72,... | collective-permute-start | bytes 786440 | tf_op jit(solution)/shard_map/ppermute | solution.py:35
  110.1 11.7 %collective-permute-start.37 = (bf16[512,256]{1,0:T(8,128)(2,1)S(1)}, bf16[512,256]{1,0:T(8,128)(2,1)S(1)}, u32[]{:S(2)}, u32[]{:S(2)}) collective-permute-start(bf16[512,256]{1,0:T(8,128)(2,1)S(1)} %get-tuple-element.66), channel_id=1, source_target_pairs={{0,8},{8,0},{16,24},{24,16},{32,40},{40,32},{48,56},{56,48},{64,72... | collective-permute-start | bytes 786440 | tf_op jit(solution)/shard_map/ppermute | solution.py:35
  (42 other events, 278.2 us)

commit v7 on v6

--- a/solution.py
+++ b/solution.py
@@ -35,16 +35,18 @@
     return lax.ppermute(array, axis, pairs)
 
 
-def rim(facing, away, ends, row_even, col_even):
+def rim_rows(facing, away, row_even):
     even = swap_pairs(facing, "row", 0)
     odd = swap_pairs(away, "row", 1)
-    north, south = jnp.where(row_even, odd, even), jnp.where(row_even, even, odd)
+    return jnp.where(row_even, odd, even), jnp.where(row_even, even, odd)
+
+
+def rim_columns(north, south, ends, col_even):
     left = jnp.concatenate([north[:1], ends[0], south[:1]])
     right = jnp.concatenate([north[-1:], ends[1], south[-1:]])
     even = swap_pairs(jnp.where(col_even, right, left), "col", 0)
     odd = swap_pairs(jnp.where(col_even, left, right), "col", 1)
-    west, east = jnp.where(col_even, odd, even), jnp.where(col_even, even, odd)
-    return north, south, west, east
+    return jnp.where(col_even, odd, even), jnp.where(col_even, even, odd)
 
 
 def outer_columns(cells):
@@ -152,12 +154,20 @@
 
 
 def forward_kernel(partners, counts, radius, first, context, cotangent, conv_weight, corr_weight, *refs):
-    tiles, refs = refs[:18], refs[18:]
+    around, refs = refs[:14], refs[14:]
     motion, context_grad, facing, away, ends, weights_sent, weights_kept, parts = refs[:8]
     edges, cot_taps, taps_back, taps, flipped, narrow, wide, spread, weight_grads = refs[8:17]
     sems, edge_sems = refs[17:]
     cells = first.shape[0]
     slots = parts.shape[0]
+    height = cells + 48
+
+    def tile_rows(t, start, size):
+        r, x, other = t // 6, t // 2 % 3, t % 2
+        which = r if x == 0 else 2 + x + (2 if r else 0)
+        lead = (r - 1) * height if r and x else 0
+        return around[2 * which + other].at[pl.ds(lead + start, size)]
+
     row_sides, chip_sides = (6, 12), (1, 3, 5)
     options = [row_sides] * 2 + [chip_sides] * 2 + [[r + x for r in row_sides for x in chip_sides]] * 4
     for n, tile in enumerate(tiles_beside()):
@@ -165,7 +175,7 @@
             @pl.when(tile == t)
             def _():
                 pltpu.make_async_copy(
-                    tiles[t].at[pl.ds(cells, 48)], edges.at[n], edge_sems.at[n]
+                    tile_rows(t, cells, 48), edges.at[n], edge_sems.at[n]
                 ).start()
     for k in range(slots):
         tile = tile_of(partners[0, 0, k])
@@ -173,7 +183,7 @@
             @pl.when(tile == t)
             def _():
                 pltpu.make_async_copy(
-                    tiles[t].at[pl.ds(0, cells)], parts.at[k, pl.ds(GROUP, cells)], sems.at[k]
+                    tile_rows(t, 0, cells), parts.at[k, pl.ds(GROUP, cells)], sems.at[k]
                 ).start()
         parts[k, :GROUP] = jnp.zeros((GROUP, parts.shape[2]), BF16)
         parts[k, GROUP + cells :] = jnp.zeros((GROUP, parts.shape[2]), BF16)
@@ -189,7 +199,7 @@
     spread_rows(corr_weight, narrow, wide, LEAD)
     spread[...] = wide[...].astype(BF16)
     for n in range(8):
-        pltpu.make_async_copy(tiles[0].at[pl.ds(cells, 48)], edges.at[n], edge_sems.at[n]).wait()
+        pltpu.make_async_copy(tile_rows(0, cells, 48), edges.at[n], edge_sems.at[n]).wait()
     north, south = edges[0, :32, 128:], edges[1, :32, :128]
     west = jnp.concatenate(
         [
@@ -218,7 +228,7 @@
             )
     for k in range(slots):
         pltpu.make_async_copy(
-            tiles[0].at[pl.ds(0, cells)], parts.at[k, pl.ds(GROUP, cells)], sems.at[k]
+            tile_rows(0, 0, cells), parts.at[k, pl.ds(GROUP, cells)], sems.at[k]
         ).wait()
     for q in range(cells // GROUP):
         at = slice(q * GROUP, (q + 1) * GROUP)
@@ -399,7 +409,7 @@
             shape((total_rows // 2, 128), F32),
             shape((slots, cells + 2 * GROUP, channels), BF16),
         ),
-        [SMEM] * 3 + [VMEM] * 5 + [ANY] * 18,
+        [SMEM] * 3 + [VMEM] * 5 + [ANY] * 14,
         [
             pltpu.VMEM((8, 48, channels), BF16),
             pltpu.VMEM((cells + 64, 384), BF16),
@@ -464,30 +474,27 @@
     own = call(pack_kernel, shape((cells + 48, channels), BF16), [VMEM] * 2)(
         frame_two.reshape(cells, channels), cot
     )
-    tiles = {(0, 0): own}
-    for r in (1, 2):
-        tiles[r, 0] = swap_pairs(own, "row", r - 1)
-        tiles[0, r] = swap_pairs(own, "col", r - 1, 2)
-    for r in (1, 2):
-        tiles[r, r] = swap_pairs(tiles[r, 0], "col", r - 1, 2)
-        tiles[r, 3 - r] = swap_pairs(tiles[0, 3 - r], "row", r - 1)
+    rows = [swap_pairs(own, "row", odd) for odd in (1, 0)][::-1]
+    sides = [swap_pairs(own, "col", odd, 2) for odd in (0, 1)]
+    both = jnp.concatenate(rows)
+    corners = [swap_pairs(both, "col", odd, 2) for odd in (0, 1)]
     around = []
-    for r in range(3):
-        for x in range(3):
-            around += [tiles[r, x], swap(tiles[r, x], "col", 1)]
+    for tile in (own, *rows, *sides, *corners):
+        around += [tile, swap(tile, "col", 1)]
     motion, context_grad, facing, away, ends, weights_sent, weights_kept, parts = forward(
         tables, first, context.reshape(cells, hidden), cot, conv_weight, corr_weight, around
     )
     total = weights_kept + swap(weights_sent, "col", 1).astype(F32)
     size = total.shape[0] // 4
     pieces = [lax.dynamic_slice_in_dim(total, (chip ^ s) * size, size) for s in range(4)]
-    gone = [piece.astype(BF16) for piece in pieces[1:]]
+    north, south = rim_rows(facing, away, row_even)
+    north, south, *gone = lax.optimization_barrier(
+        (north, south, *[piece.astype(BF16) for piece in pieces[1:]])
+    )
     got = [swap(piece, "col", 2 * s) for s, piece in zip((1, 2, 3), gone)]
-    around_motion = rim(facing, away, ends, row_even, col_even)
+    around_motion = (north, south, *rim_columns(north, south, ends, col_even))
     first_grad, scores = backward_scores(tables, context_grad, corr_weight, parts)
-    *kept, lent = backward_partners(
-        tables, first, scores, (*got, *around_motion[:2])
-    )
+    *kept, lent = backward_partners(tables, first, scores, got)
     lent = swap(lent, "col", 1)
     side = jnp.where((core == 0) == chip_even, 1, 2)
     sent = [

time: 124 us -> 128 us (1.032)
  waiting for transfers between devices: 20.6 us -> 26.2 us
  starting transfers between devices: 64.8 us -> 63.2 us
    ppermute x16 -> x14, waiting for transfers between devices: 8.28 us -> 17.6 us  [swap_pairs(): return lax.ppermute(array, axis, pairs)]
    ppermute x27 -> x25, waiting for transfers between devices: 12.3 us -> 8.64 us  [swap(): lax.ppermute(array, axis, [(i, i ^ bits) for i in range(lax.axis_size(axi...]
    ppermute x16 -> x14, starting transfers between devices: 30.2 us -> 26.9 us  [swap_pairs(): return lax.ppermute(array, axis, pairs)]
    ppermute x27 -> x25, starting transfers between devices: 34.6 us -> 36.3 us  [swap(): lax.ppermute(array, axis, [(i, i ^ bits) for i in range(lax.axis_size(axi...]
  transfers between devices with their start and end apart: 43 -> 39, of which waited for: 16 -> 14; matrix products, arithmetic and copies ran while one was open for 3% -> 2% of each run, Pallas kernels for 8% -> 8%
where the time goes in v7:
time: 128 us; the launch traced here: 127 us
  starting transfers between devices  63.2 us (49%)
  Pallas kernels  26.3 us (21%)
  waiting for transfers between devices  26.2 us (20%)
  other arithmetic  6.13 us (5%)
  local copies, waits for them, and re-layouts  2.55 us (2%)
  between operations  2.46 us (2%)
    ppermute x25, starting transfers between devices, swap(): lax.ppermute(array, axis, [(i, i ^ bits) for i in range(lax.axis_size(axi...  36.3 us
    ppermute x14, starting transfers between devices, swap_pairs(): return lax.ppermute(array, axis, pairs)  26.9 us
    ppermute x14, waiting for transfers between devices, swap_pairs(): return lax.ppermute(array, axis, pairs)  17.6 us
    pallas_call x1, Pallas kernels, forward(): call(forward_kernel, (shape((cells, hidden), BF16), shape((cells, hidden)...  8.75 us
    ppermute x25, waiting for transfers between devices, swap(): lax.ppermute(array, axis, [(i, i ^ bits) for i in range(lax.axis_size(axi...  8.64 us
    pallas_call x1, Pallas kernels, backward_partners(): call(partners_kernel, (*[shape((3, cells, channels), BF16)] * 3, shape((6...  5.73 us
    pallas_call x1, Pallas kernels, backward_scores(): call(scores_kernel, (shape((cells, channels), F32), shape((slots, cells,...  4.79 us
    pallas_call x1, Pallas kernels, body(): call(features_kernel, shape((cells, out_width), BF16), [VMEM] * 6, [pltpu...  2.66 us
  transfers between devices with their start and end apart: 39, of which 14 were waited for; matrix products, arithmetic and copies ran while one was open for 2% of the time, Pallas kernels for 8%

profile of v7, /device:TPU:33, one launch (start us, length us, event | category | flops | bytes accessed | tf_op | source)
XLA Modules:
  0.0 126.8 jit_solution(9513675668136116891)
XLA Ops:
  0.6 1.8 %shard_map.136.refs_0_ = bf16[560,256]{1,0:T(8,128)(2,1)} custom-call(bf16[512,256]{1,0:T(8,128)(2,1)} %bitcast.26, bf16[512,128]{1,0:T(8,128)(2,1)} %bitcast.27), custom_call_target="tpu_custom_call" | custom-call | flops 1000 | bytes 3 | tf_op jit(solution)/shard_map/pallas_call | solution.py:474
  3.8 3.3 %collective-permute-start.3 = (bf16[560,256]{1,0:T(8,128)(2,1)}, bf16[560,256]{1,0:T(8,128)(2,1)S(1)}, u32[]{:S(2)}, u32[]{:S(2)}) collective-permute-start(bf16[560,256]{1,0:T(8,128)(2,1)} %shard_map.136.refs_0_), channel_id=1, source_target_pairs={{8,16},{16,8},{24,32},{32,24},{40,48},{48,40},{56,64},{64,56},{72,... | collective-permute-start | bytes 860168 | tf_op jit(solution)/shard_map/ppermute | solution.py:35
  7.1 3.3 %collective-permute-done.1.refs_2_ = bf16[560,256]{1,0:T(8,128)(2,1)S(1)} collective-permute-done((bf16[560,256]{1,0:T(8,128)(2,1)}, bf16[560,256]{1,0:T(8,128)(2,1)S(1)}, u32[]{:S(2)}, u32[]{:S(2)}) %collective-permute-start.1) | collective-permute-done | bytes 286752 | tf_op jit(solution)/shard_map/ppermute | solution.py:35
  10.4 4.9 %collective-permute-done.3.refs_4_ = bf16[560,256]{1,0:T(8,128)(2,1)S(1)} collective-permute-done((bf16[560,256]{1,0:T(8,128)(2,1)}, bf16[560,256]{1,0:T(8,128)(2,1)S(1)}, u32[]{:S(2)}, u32[]{:S(2)}) %collective-permute-start.3) | collective-permute-done | bytes 286752 | tf_op jit(solution)/shard_map/ppermute | solution.py:35
  17.4 2.2 %collective-permute-start = (bf16[560,256]{1,0:T(8,128)(2,1)}, bf16[560,256]{1,0:T(8,128)(2,1)S(1)}, u32[]{:S(2)}, u32[]{:S(2)}) collective-permute-start(bf16[560,256]{1,0:T(8,128)(2,1)} %shard_map.136.refs_0_), channel_id=1, source_target_pairs={{0,1},{1,0},{2,3},{3,2},{4,5},{5,4},{6,7},{7,6},{8,9},{9,8},{10,11... | collective-permute-start | bytes 860168 | tf_op jit(solution)/shard_map/ppermute | solution.py:25
  19.6 3.6 %collective-permute-start.5 = (bf16[560,256]{1,0:T(8,128)(2,1)}, bf16[560,256]{1,0:T(8,128)(2,1)S(1)}, u32[]{:S(2)}, u32[]{:S(2)}) collective-permute-start(bf16[560,256]{1,0:T(8,128)(2,1)} %shard_map.136.refs_0_), channel_id=1, source_target_pairs={{0,2},{2,0},{1,3},{3,1},{4,6},{6,4},{5,7},{7,5},{8,10},{10,8},{9,1... | collective-permute-start | bytes 860168 | tf_op jit(solution)/shard_map/ppermute | solution.py:35
  24.4 3.7 %collective-permute-done.9.refs_10_ = bf16[1120,256]{1,0:T(8,128)(2,1)S(1)} collective-permute-done((bf16[1120,256]{1,0:T(8,128)(2,1)S(1)}, bf16[1120,256]{1,0:T(8,128)(2,1)S(1)}, u32[]{:S(2)}, u32[]{:S(2)}) %collective-permute-start.9) | collective-permute-done | bytes 573472 | tf_op jit(solution)/shard_map/ppermute | solution.py:35
  28.1 5.2 %collective-permute-start.10 = (bf16[1120,256]{1,0:T(8,128)(2,1)S(1)}, bf16[1120,256]{1,0:T(8,128)(2,1)S(1)}, u32[]{:S(2)}, u32[]{:S(2)}) collective-permute-start(bf16[1120,256]{1,0:T(8,128)(2,1)S(1)} %collective-permute-done.9.refs_10_), channel_id=1, source_target_pairs={{0,1},{1,0},{2,3},{3,2},{4,5},{5,4},{6,7},{7,6},{8,9},{9,8},{10,11... | collective-permute-start | bytes 1720328 | tf_op jit(solution)/shard_map/ppermute | solution.py:25
  34.2 2.8 %collective-permute-start.4 = (bf16[560,256]{1,0:T(8,128)(2,1)S(1)}, bf16[560,256]{1,0:T(8,128)(2,1)S(1)}, u32[]{:S(2)}, u32[]{:S(2)}) collective-permute-start(bf16[560,256]{1,0:T(8,128)(2,1)S(1)} %collective-permute-done.3.refs_4_), channel_id=1, source_target_pairs={{0,1},{1,0},{2,3},{3,2},{4,5},{5,4},{6,7},{7,6},{8,9},{9,8},{10,11... | collective-permute-start | bytes 860168 | tf_op jit(solution)/shard_map/ppermute | solution.py:25
  40.1 8.8 %shard_map.137 = (bf16[512,256]{1,0:T(8,128)(2,1)}, bf16[512,256]{1,0:T(8,128)(2,1)}, bf16[32,256]{1,0:T(8,128)(2,1)}, bf16[32,256]{1,0:T(8,128)(2,1)}, bf16[2,1...) custom-call(s32[1,1,4]{2,1,0:T(1,128)} %partners.3, ...), custom_call_target="tpu_custom_call" | custom-call | flops 3000000000 | bytes 10000000 | tf_op jit(solution)/shard_map/pallas_call | solution.py:400
  49.4 3.3 %collective-permute-start.14 = (bf16[32,256]{1,0:T(8,128)(2,1)}, bf16[32,256]{1,0:T(8,128)(2,1)S(1)}, u32[]{:S(2)}, u32[]{:S(2)}) collective-permute-start(bf16[32,256]{1,0:T(8,128)(2,1)} %get-tuple-element.42), channel_id=1, source_target_pairs={{8,16},{16,8},{24,32},{32,24},{40,48},{48,40},{56,64},{64,56},{72,... | collective-permute-start | bytes 49160 | tf_op jit(solution)/shard_map/ppermute | solution.py:35
  52.8 3.4 %collective-permute-done.14 = bf16[32,256]{1,0:T(8,128)(2,1)S(1)} collective-permute-done((bf16[32,256]{1,0:T(8,128)(2,1)}, bf16[32,256]{1,0:T(8,128)(2,1)S(1)}, u32[]{:S(2)}, u32[]{:S(2)}) %collective-permute-start.14) | collective-permute-done | bytes 16416 | tf_op jit(solution)/shard_map/ppermute | solution.py:35
  57.5 2.5 %collective-permute-start.18 = (bf16[384,128]{1,0:T(8,128)(2,1)S(1)}, bf16[384,128]{1,0:T(8,128)(2,1)S(1)}, u32[]{:S(2)}, u32[]{:S(2)}) collective-permute-start(bf16[384,128]{1,0:T(8,128)(2,1)S(1)} %get-tuple-element.46), channel_id=1, source_target_pairs={{0,6},{1,7},{2,4},{3,5},{4,2},{5,3},{6,0},{7,1},{8,14},{9,15},{10,... | collective-permute-start | bytes 294920 | tf_op jit(solution)/shard_map/ppermute | solution.py:25
  60.1 2.7 %collective-permute-start.17 = (bf16[384,128]{1,0:T(8,128)(2,1)S(1)}, bf16[384,128]{1,0:T(8,128)(2,1)S(1)}, u32[]{:S(2)}, u32[]{:S(2)}) collective-permute-start(bf16[384,128]{1,0:T(8,128)(2,1)S(1)} %get-tuple-element.45), channel_id=1, source_target_pairs={{0,4},{1,5},{2,6},{3,7},{4,0},{5,1},{6,2},{7,3},{8,12},{9,13},{10,... | collective-permute-start | bytes 294920 | tf_op jit(solution)/shard_map/ppermute | solution.py:25
  62.7 4.8 %shard_map.138 = (f32[512,256]{1,0:T(8,128)}, bf16[4,512,384]{2,1,0:T(8,128)(2,1)}) custom-call(s32[1,1]{1,0:T(1,128)S(6)} %copy.16.counts, s32[1,1]{1,0:T(1,128)S(6)} %copy.17.radius, bf16[512,256]{1,0:T(8,128)(2,1)} %get-tuple-element.47.context_grad, bf16[324,256]{1,0:T(8,128)(2,1)} %corr_weight.3, bf16[4,768,256]{2,1,0:T(8,128)(2,1)} %get-tuple-element.48.parts), custom_call_target="tpu_custom_call" | custom-call | flops 4000000000 | bytes 13333333 | tf_op jit(solution)/shard_map/pallas_call | solution.py:434
  68.2 5.7 %shard_map.139 = (bf16[3,512,256]{2,1,0:T(8,128)(2,1)}, bf16[3,512,256]{2,1,0:T(8,128)(2,1)}, bf16[3,512,256]{2,1,0:T(8,128)(2,1)}, bf16[6,512,256]{2,1,0:T(8,128)(2,1)}) custom-call(s32[1,1,4]{2,1,0:T(1,128)} %partners.3, bf16[512,256]{1,0:T(8,128)(2,1)} %bitcast.33, bf16[4,512,384]{2,1,0:T(8,128)(2,1)} %get-tuple-element.49.scores, ...), custom_call_target="tpu_custom_call" | custom-call | flops 4000000000 | bytes 13333333 | tf_op jit(solution)/shard_map/pallas_call | solution.py:450
  74.0 1.9 %collective-permute-start.19 = (bf16[6,512,256]{2,1,0:T(8,128)(2,1)}, bf16[6,512,256]{2,1,0:T(8,128)(2,1)S(1)}, u32[]{:S(2)}, u32[]{:S(2)}) collective-permute-start(bf16[6,512,256]{2,1,0:T(8,128)(2,1)} %get-tuple-element.51), channel_id=1, source_target_pairs={{0,1},{1,0},{2,3},{3,2},{4,5},{5,4},{6,7},{7,6},{8,9},{9,8},{10,11... | collective-permute-start | bytes 4718600 | tf_op jit(solution)/shard_map/ppermute | solution.py:25
  76.0 4.0 %collective-permute-start.20 = (bf16[18,256]{1,0:T(8,128)(2,1)S(1)}, bf16[18,256]{1,0:T(8,128)(2,1)S(1)}, u32[]{:S(2)}, u32[]{:S(2)}) collective-permute-start(bf16[18,256]{1,0:T(8,128)(2,1)S(1)} %get-tuple-element.86), channel_id=1, source_target_pairs={{1,2},{2,1},{3,4},{4,3},{5,6},{6,5},{9,10},{10,9},{11,12},{12,11},... | collective-permute-start | bytes 27656 | tf_op jit(solution)/shard_map/ppermute | solution.py:35
  83.0 1.9 %fusion.3 = (bf16[3,512,256]{2,1,0:T(8,128)(2,1)S(1)}, bf16[3,512,256]{2,1,0:T(8,128)(2,1)S(1)}) fusion(bf16[3,512,256]{2,1,0:T(8,128)(2,1)} %get-tuple-element.52, pred[]{:T(512)S(6)} %eq.28, bf16[6,512,256]{2,1,0:T(8,128)(2,1)S(1)} %collective-permute-done.19, pred[]{:T(512)S(6)} %eq.27, bf16[3,512,256]{2,1,0:T(8,128)(2,1)} %get-tuple-element.50), kind=kLoop, calls=%fused_computation.5 | loop fusion | flops 3538944 | bytes 3932162 | tf_op jit(solution)/shard_map/convert_element_type | solution.py:501
  85.6 4.2 %collective-permute-start.31 = (bf16[3,512,256]{2,1,0:T(8,128)(2,1)S(1)}, bf16[3,512,256]{2,1,0:T(8,128)(2,1)S(1)}, u32[]{:S(2)}, u32[]{:S(2)}) collective-permute-start(bf16[3,512,256]{2,1,0:T(8,128)(2,1)S(1)} %get-tuple-element.64), channel_id=1, source_target_pairs={{0,2},{2,0},{1,3},{3,1},{4,6},{6,4},{5,7},{7,5},{8,10},{10,8},{9,1... | collective-permute-start | bytes 2359304 | tf_op jit(solution)/shard_map/ppermute | solution.py:35
  89.8 1.9 %collective-permute-start.24 = (bf16[384,128]{1,0:T(8,128)(2,1)S(1)}, bf16[384,128]{1,0:T(8,128)(2,1)S(1)}, u32[]{:S(2)}, u32[]{:S(2)}) collective-permute-start(bf16[384,128]{1,0:T(8,128)(2,1)S(1)} %add_add_fusion), channel_id=1, source_target_pairs={{0,24},{8,16},{16,8},{24,0},{32,56},{40,48},{48,40},{56,32},{64,88... | collective-permute-start | bytes 294920 | tf_op jit(solution)/shard_map/ppermute | solution.py:25
  93.1 1.4 %collective-permute-done.24 = bf16[384,128]{1,0:T(8,128)(2,1)S(1)} collective-permute-done((bf16[384,128]{1,0:T(8,128)(2,1)S(1)}, bf16[384,128]{1,0:T(8,128)(2,1)S(1)}, u32[]{:S(2)}, u32[]{:S(2)}) %collective-permute-start.24) | collective-permute-done | bytes 98336 | tf_op jit(solution)/shard_map/ppermute | solution.py:25
  94.5 2.3 %collective-permute-done.23 = bf16[384,128]{1,0:T(8,128)(2,1)S(1)} collective-permute-done((bf16[384,128]{1,0:T(8,128)(2,1)S(1)}, bf16[384,128]{1,0:T(8,128)(2,1)S(1)}, u32[]{:S(2)}, u32[]{:S(2)}) %collective-permute-start.23) | collective-permute-done | bytes 98336 | tf_op jit(solution)/shard_map/ppermute | solution.py:25
  96.8 1.7 %collective-permute-start.27 = (bf16[384,128]{1,0:T(8,128)(2,1)S(1)}, bf16[384,128]{1,0:T(8,128)(2,1)S(1)}, u32[]{:S(2)}, u32[]{:S(2)}) collective-permute-start(bf16[384,128]{1,0:T(8,128)(2,1)S(1)} %add_convert_fusion.1), channel_id=1, source_target_pairs={{0,96},{8,104},{16,112},{24,120},{32,64},{40,72},{48,80},{56,88},{... | collective-permute-start | bytes 294920 | tf_op jit(solution)/shard_map/ppermute | solution.py:25
  98.6 1.8 %collective-permute-start.26 = (bf16[384,128]{1,0:T(8,128)(2,1)S(1)}, bf16[384,128]{1,0:T(8,128)(2,1)S(1)}, u32[]{:S(2)}, u32[]{:S(2)}) collective-permute-start(bf16[384,128]{1,0:T(8,128)(2,1)S(1)} %add_convert_fusion.1), channel_id=1, source_target_pairs={{0,64},{8,72},{16,80},{24,88},{32,96},{40,104},{48,112},{56,120},{... | collective-permute-start | bytes 294920 | tf_op jit(solution)/shard_map/ppermute | solution.py:25
  101.2 2.5 %collective-permute-done.26 = bf16[384,128]{1,0:T(8,128)(2,1)S(1)} collective-permute-done((bf16[384,128]{1,0:T(8,128)(2,1)S(1)}, bf16[384,128]{1,0:T(8,128)(2,1)S(1)}, u32[]{:S(2)}, u32[]{:S(2)}) %collective-permute-start.26) | collective-permute-done | bytes 98336 | tf_op jit(solution)/shard_map/ppermute | solution.py:25
  104.7 1.8 %collective-permute-start.29 = (bf16[384,128]{1,0:T(8,128)(2,1)S(1)}, bf16[384,128]{1,0:T(8,128)(2,1)S(1)}, u32[]{:S(2)}, u32[]{:S(2)}) collective-permute-start(bf16[384,128]{1,0:T(8,128)(2,1)S(1)} %add_convert_fusion.refs_0_), channel_id=1, source_target_pairs={{0,4},{1,5},{2,6},{3,7},{4,0},{5,1},{6,2},{7,3},{8,12},{9,13},{10,... | collective-permute-start | bytes 294920 | tf_op jit(solution)/shard_map/ppermute | solution.py:25
  106.5 2.0 %collective-permute-start.30 = (bf16[384,128]{1,0:T(8,128)(2,1)S(1)}, bf16[384,128]{1,0:T(8,128)(2,1)S(1)}, u32[]{:S(2)}, u32[]{:S(2)}) collective-permute-start(bf16[384,128]{1,0:T(8,128)(2,1)S(1)} %add_convert_fusion.refs_0_), channel_id=1, source_target_pairs={{0,6},{1,7},{2,4},{3,5},{4,2},{5,3},{6,0},{7,1},{8,14},{9,15},{10,... | collective-permute-start | bytes 294920 | tf_op jit(solution)/shard_map/ppermute | solution.py:25
  109.0 3.3 %collective-permute-start.34 = (bf16[512,256]{1,0:T(8,128)(2,1)S(1)}, bf16[512,256]{1,0:T(8,128)(2,1)S(1)}, u32[]{:S(2)}, u32[]{:S(2)}) collective-permute-start(bf16[512,256]{1,0:T(8,128)(2,1)S(1)} %get-tuple-element.77), channel_id=1, source_target_pairs={{8,16},{16,8},{24,32},{32,24},{40,48},{48,40},{56,64},{64,56},{72,... | collective-permute-start | bytes 786440 | tf_op jit(solution)/shard_map/ppermute | solution.py:35
  112.6 2.7 %shard_map.140 = bf16[512,128]{1,0:T(8,128)(2,1)} custom-call(bf16[512,256]{1,0:T(8,128)(2,1)} %get-tuple-element.39.motion, bf16[32,256]{1,0:T(8,128)(2,1)} %copy-done.15, bf16[32,256]{1,0:T(8,128)(2,1)} %copy-done.14, bf16[18,256]{1,0:T(8,128)(2,1)} %get-tuple-element.58.west, bf16[18,256]{1,0:T(8,128)(2,1)} %get-tuple-element.59.east, ...), custom_call_target="tpu_custom_call" | custom-call | flops 1000 | bytes 3 | tf_op jit(solution)/shard_map/pallas_call | solution.py:512
  115.4 5.1 %collective-permute-start.35 = (bf16[384,128]{1,0:T(8,128)(2,1)S(1)}, bf16[384,128]{1,0:T(8,128)(2,1)S(1)}, u32[]{:S(2)}, u32[]{:S(2)}) collective-permute-start(bf16[384,128]{1,0:T(8,128)(2,1)S(1)} %add_convert_fusion.refs_0_), channel_id=1, source_target_pairs={{0,1},{1,0},{2,3},{3,2},{4,5},{5,4},{6,7},{7,6},{8,9},{9,8},{10,11... | collective-permute-start | bytes 294920 | tf_op jit(solution)/shard_map/ppermute | solution.py:25
  123.4 2.5 %shard_map.141 = (f32[2304,128]{1,0:T(8,128)}, f32[324,256]{1,0:T(8,128)}) custom-call(bf16[384,128]{1,0:T(8,128)(2,1)} %copy-done.1, bf16[384,128]{1,0:T(8,128)(2,1)} %copy-done.4, bf16[384,128]{1,0:T(8,128)(2,1)} %copy-done.5, bf16[384,128]{1,0:T(8,128)(2,1)} %copy-done.6, bf16[384,128]{1,0:T(8,128)(2,1)} %copy-done.7, bf16[384,128]{1,0:T(8,128)(2,1)} %copy-done.8, ...), custom_call_target="tpu_custom_call" | custom-call | flops 1000 | bytes 3 | tf_op jit(solution)/shard_map/pallas_call | solution.py:523
  (124 shorter events, 21.2 us)
Async XLA Ops:
  2.5 7.9 %collective-permute-start.1 = (bf16[560,256]{1,0:T(8,128)(2,1)}, bf16[560,256]{1,0:T(8,128)(2,1)S(1)}, u32[]{:S(2)}, u32[]{:S(2)}) collective-permute-start(bf16[560,256]{1,0:T(8,128)(2,1)} %shard_map.136.refs_0_), channel_id=1, source_target_pairs={{0,8},{8,0},{16,24},{24,16},{32,40},{40,32},{48,56},{56,48},{64,72... | collective-permute-start | bytes 860168 | tf_op jit(solution)/shard_map/ppermute | solution.py:35
  3.8 11.6 %collective-permute-start.3 = (bf16[560,256]{1,0:T(8,128)(2,1)}, bf16[560,256]{1,0:T(8,128)(2,1)S(1)}, u32[]{:S(2)}, u32[]{:S(2)}) collective-permute-start(bf16[560,256]{1,0:T(8,128)(2,1)} %shard_map.136.refs_0_), channel_id=1, source_target_pairs={{8,16},{16,8},{24,32},{32,24},{40,48},{48,40},{56,64},{64,56},{72,... | collective-permute-start | bytes 860168 | tf_op jit(solution)/shard_map/ppermute | solution.py:35
  15.4 12.7 %collective-permute-start.9 = (bf16[1120,256]{1,0:T(8,128)(2,1)S(1)}, bf16[1120,256]{1,0:T(8,128)(2,1)S(1)}, u32[]{:S(2)}, u32[]{:S(2)}) collective-permute-start(bf16[1120,256]{1,0:T(8,128)(2,1)S(1)} %constant_dynamic-update-slice_fusion), channel_id=1, source_target_pairs={{0,2},{2,0},{1,3},{3,1},{4,6},{6,4},{5,7},{7,5},{8,10},{10,8},{9,1... | collective-permute-start | bytes 1720328 | tf_op jit(solution)/shard_map/ppermute | solution.py:35
  16.7 16.6 %collective-permute-start.11 = (bf16[1120,256]{1,0:T(8,128)(2,1)S(1)}, bf16[1120,256]{1,0:T(8,128)(2,1)S(1)}, u32[]{:S(2)}, u32[]{:S(2)}) collective-permute-start(bf16[1120,256]{1,0:T(8,128)(2,1)S(1)} %constant_dynamic-update-slice_fusion), channel_id=1, source_target_pairs={{2,4},{4,2},{3,5},{5,3},{10,12},{12,10},{11,13},{13,11},{18,20},{2... | collective-permute-start | bytes 1720328 | tf_op jit(solution)/shard_map/ppermute | solution.py:35
  17.4 6.5 %collective-permute-start = (bf16[560,256]{1,0:T(8,128)(2,1)}, bf16[560,256]{1,0:T(8,128)(2,1)S(1)}, u32[]{:S(2)}, u32[]{:S(2)}) collective-permute-start(bf16[560,256]{1,0:T(8,128)(2,1)} %shard_map.136.refs_0_), channel_id=1, source_target_pairs={{0,1},{1,0},{2,3},{3,2},{4,5},{5,4},{6,7},{7,6},{8,9},{9,8},{10,11... | collective-permute-start | bytes 860168 | tf_op jit(solution)/shard_map/ppermute | solution.py:25
  19.6 14.6 %collective-permute-start.5 = (bf16[560,256]{1,0:T(8,128)(2,1)}, bf16[560,256]{1,0:T(8,128)(2,1)S(1)}, u32[]{:S(2)}, u32[]{:S(2)}) collective-permute-start(bf16[560,256]{1,0:T(8,128)(2,1)} %shard_map.136.refs_0_), channel_id=1, source_target_pairs={{0,2},{2,0},{1,3},{3,1},{4,6},{6,4},{5,7},{7,5},{8,10},{10,8},{9,1... | collective-permute-start | bytes 860168 | tf_op jit(solution)/shard_map/ppermute | solution.py:35
  23.2 13.8 %collective-permute-start.7 = (bf16[560,256]{1,0:T(8,128)(2,1)}, bf16[560,256]{1,0:T(8,128)(2,1)S(1)}, u32[]{:S(2)}, u32[]{:S(2)}) collective-permute-start(bf16[560,256]{1,0:T(8,128)(2,1)} %shard_map.136.refs_0_), channel_id=1, source_target_pairs={{2,4},{4,2},{3,5},{5,3},{10,12},{12,10},{11,13},{13,11},{18,20},{2... | collective-permute-start | bytes 860168 | tf_op jit(solution)/shard_map/ppermute | solution.py:35
  23.9 13.2 %collective-permute-start.2 = (bf16[560,256]{1,0:T(8,128)(2,1)S(1)}, bf16[560,256]{1,0:T(8,128)(2,1)S(1)}, u32[]{:S(2)}, u32[]{:S(2)}) collective-permute-start(bf16[560,256]{1,0:T(8,128)(2,1)S(1)} %collective-permute-done.1.refs_2_), channel_id=1, source_target_pairs={{0,1},{1,0},{2,3},{3,2},{4,5},{5,4},{6,7},{7,6},{8,9},{9,8},{10,11... | collective-permute-start | bytes 860168 | tf_op jit(solution)/shard_map/ppermute | solution.py:25
  28.1 11.0 %collective-permute-start.10 = (bf16[1120,256]{1,0:T(8,128)(2,1)S(1)}, bf16[1120,256]{1,0:T(8,128)(2,1)S(1)}, u32[]{:S(2)}, u32[]{:S(2)}) collective-permute-start(bf16[1120,256]{1,0:T(8,128)(2,1)S(1)} %collective-permute-done.9.refs_10_), channel_id=1, source_target_pairs={{0,1},{1,0},{2,3},{3,2},{4,5},{5,4},{6,7},{7,6},{8,9},{9,8},{10,11... | collective-permute-start | bytes 1720328 | tf_op jit(solution)/shard_map/ppermute | solution.py:25
  33.2 5.8 %collective-permute-start.12 = (bf16[1120,256]{1,0:T(8,128)(2,1)S(1)}, bf16[1120,256]{1,0:T(8,128)(2,1)S(1)}, u32[]{:S(2)}, u32[]{:S(2)}) collective-permute-start(bf16[1120,256]{1,0:T(8,128)(2,1)S(1)} %collective-permute-done.11.refs_12_), channel_id=1, source_target_pairs={{0,1},{1,0},{2,3},{3,2},{4,5},{5,4},{6,7},{7,6},{8,9},{9,8},{10,11... | collective-permute-start | bytes 1720328 | tf_op jit(solution)/shard_map/ppermute | solution.py:25
  34.2 4.6 %collective-permute-start.4 = (bf16[560,256]{1,0:T(8,128)(2,1)S(1)}, bf16[560,256]{1,0:T(8,128)(2,1)S(1)}, u32[]{:S(2)}, u32[]{:S(2)}) collective-permute-start(bf16[560,256]{1,0:T(8,128)(2,1)S(1)} %collective-permute-done.3.refs_4_), channel_id=1, source_target_pairs={{0,1},{1,0},{2,3},{3,2},{4,5},{5,4},{6,7},{7,6},{8,9},{9,8},{10,11... | collective-permute-start | bytes 860168 | tf_op jit(solution)/shard_map/ppermute | solution.py:25
  48.9 7.3 %collective-permute-start.13 = (bf16[1536,128]{1,0:T(8,128)(2,1)}, bf16[1536,128]{1,0:T(8,128)(2,1)S(1)}, u32[]{:S(2)}, u32[]{:S(2)}) collective-permute-start(bf16[1536,128]{1,0:T(8,128)(2,1)} %get-tuple-element.41), channel_id=1, source_target_pairs={{0,1},{1,0},{2,3},{3,2},{4,5},{5,4},{6,7},{7,6},{8,9},{9,8},{10,11... | collective-permute-start | bytes 1179656 | tf_op jit(solution)/shard_map/ppermute | solution.py:25
  49.4 6.8 %collective-permute-start.14 = (bf16[32,256]{1,0:T(8,128)(2,1)}, bf16[32,256]{1,0:T(8,128)(2,1)S(1)}, u32[]{:S(2)}, u32[]{:S(2)}) collective-permute-start(bf16[32,256]{1,0:T(8,128)(2,1)} %get-tuple-element.42), channel_id=1, source_target_pairs={{8,16},{16,8},{24,32},{32,24},{40,48},{48,40},{56,64},{64,56},{72,... | collective-permute-start | bytes 49160 | tf_op jit(solution)/shard_map/ppermute | solution.py:35
  57.5 10.0 %collective-permute-start.18 = (bf16[384,128]{1,0:T(8,128)(2,1)S(1)}, bf16[384,128]{1,0:T(8,128)(2,1)S(1)}, u32[]{:S(2)}, u32[]{:S(2)}) collective-permute-start(bf16[384,128]{1,0:T(8,128)(2,1)S(1)} %get-tuple-element.46), channel_id=1, source_target_pairs={{0,6},{1,7},{2,4},{3,5},{4,2},{5,3},{6,0},{7,1},{8,14},{9,15},{10,... | collective-permute-start | bytes 294920 | tf_op jit(solution)/shard_map/ppermute | solution.py:25
  60.1 7.5 %collective-permute-start.17 = (bf16[384,128]{1,0:T(8,128)(2,1)S(1)}, bf16[384,128]{1,0:T(8,128)(2,1)S(1)}, u32[]{:S(2)}, u32[]{:S(2)}) collective-permute-start(bf16[384,128]{1,0:T(8,128)(2,1)S(1)} %get-tuple-element.45), channel_id=1, source_target_pairs={{0,4},{1,5},{2,6},{3,7},{4,0},{5,1},{6,2},{7,3},{8,12},{9,13},{10,... | collective-permute-start | bytes 294920 | tf_op jit(solution)/shard_map/ppermute | solution.py:25
  62.7 4.8 %collective-permute-start.16 = (bf16[384,128]{1,0:T(8,128)(2,1)S(1)}, bf16[384,128]{1,0:T(8,128)(2,1)S(1)}, u32[]{:S(2)}, u32[]{:S(2)}) collective-permute-start(bf16[384,128]{1,0:T(8,128)(2,1)S(1)} %get-tuple-element.44), channel_id=1, source_target_pairs={{0,2},{1,3},{2,0},{3,1},{4,6},{5,7},{6,4},{7,5},{8,10},{9,11},{10,... | collective-permute-start | bytes 294920 | tf_op jit(solution)/shard_map/ppermute | solution.py:25
  74.0 9.1 %collective-permute-start.19 = (bf16[6,512,256]{2,1,0:T(8,128)(2,1)}, bf16[6,512,256]{2,1,0:T(8,128)(2,1)S(1)}, u32[]{:S(2)}, u32[]{:S(2)}) collective-permute-start(bf16[6,512,256]{2,1,0:T(8,128)(2,1)} %get-tuple-element.51), channel_id=1, source_target_pairs={{0,1},{1,0},{2,3},{3,2},{4,5},{5,4},{6,7},{7,6},{8,9},{9,8},{10,11... | collective-permute-start | bytes 4718600 | tf_op jit(solution)/shard_map/ppermute | solution.py:25
  75.9 4.2 %collective-permute-start.21 = (bf16[18,256]{1,0:T(8,128)(2,1)S(1)}, bf16[18,256]{1,0:T(8,128)(2,1)S(1)}, u32[]{:S(2)}, u32[]{:S(2)}) collective-permute-start(bf16[18,256]{1,0:T(8,128)(2,1)S(1)} %get-tuple-element.85), channel_id=1, source_target_pairs={{0,1},{1,0},{2,3},{3,2},{4,5},{5,4},{6,7},{7,6},{8,9},{9,8},{10,11... | collective-permute-start | bytes 27656 | tf_op jit(solution)/shard_map/ppermute | solution.py:35
  76.0 5.4 %collective-permute-start.20 = (bf16[18,256]{1,0:T(8,128)(2,1)S(1)}, bf16[18,256]{1,0:T(8,128)(2,1)S(1)}, u32[]{:S(2)}, u32[]{:S(2)}) collective-permute-start(bf16[18,256]{1,0:T(8,128)(2,1)S(1)} %get-tuple-element.86), channel_id=1, source_target_pairs={{1,2},{2,1},{3,4},{4,3},{5,6},{6,5},{9,10},{10,9},{11,12},{12,11},... | collective-permute-start | bytes 27656 | tf_op jit(solution)/shard_map/ppermute | solution.py:35
  84.9 23.6 %collective-permute-start.32 = (bf16[3,512,256]{2,1,0:T(8,128)(2,1)S(1)}, bf16[3,512,256]{2,1,0:T(8,128)(2,1)S(1)}, u32[]{:S(2)}, u32[]{:S(2)}) collective-permute-start(bf16[3,512,256]{2,1,0:T(8,128)(2,1)S(1)} %get-tuple-element.65), channel_id=1, source_target_pairs={{2,4},{4,2},{3,5},{5,3},{10,12},{12,10},{11,13},{13,11},{18,20},{2... | collective-permute-start | bytes 2359304 | tf_op jit(solution)/shard_map/ppermute | solution.py:35
  85.6 22.9 %collective-permute-start.31 = (bf16[3,512,256]{2,1,0:T(8,128)(2,1)S(1)}, bf16[3,512,256]{2,1,0:T(8,128)(2,1)S(1)}, u32[]{:S(2)}, u32[]{:S(2)}) collective-permute-start(bf16[3,512,256]{2,1,0:T(8,128)(2,1)S(1)} %get-tuple-element.64), channel_id=1, source_target_pairs={{0,2},{2,0},{1,3},{3,1},{4,6},{6,4},{5,7},{7,5},{8,10},{10,8},{9,1... | collective-permute-start | bytes 2359304 | tf_op jit(solution)/shard_map/ppermute | solution.py:35
  89.8 4.7 %collective-permute-start.24 = (bf16[384,128]{1,0:T(8,128)(2,1)S(1)}, bf16[384,128]{1,0:T(8,128)(2,1)S(1)}, u32[]{:S(2)}, u32[]{:S(2)}) collective-permute-start(bf16[384,128]{1,0:T(8,128)(2,1)S(1)} %add_add_fusion), channel_id=1, source_target_pairs={{0,24},{8,16},{16,8},{24,0},{32,56},{40,48},{48,40},{56,32},{64,88... | collective-permute-start | bytes 294920 | tf_op jit(solution)/shard_map/ppermute | solution.py:25
  91.7 5.1 %collective-permute-start.23 = (bf16[384,128]{1,0:T(8,128)(2,1)S(1)}, bf16[384,128]{1,0:T(8,128)(2,1)S(1)}, u32[]{:S(2)}, u32[]{:S(2)}) collective-permute-start(bf16[384,128]{1,0:T(8,128)(2,1)S(1)} %add_add_fusion), channel_id=1, source_target_pairs={{0,16},{8,24},{16,0},{24,8},{32,48},{40,56},{48,32},{56,40},{64,80... | collective-permute-start | bytes 294920 | tf_op jit(solution)/shard_map/ppermute | solution.py:25
  91.7 5.1 %collective-permute-start.22 = (bf16[384,128]{1,0:T(8,128)(2,1)S(1)}, bf16[384,128]{1,0:T(8,128)(2,1)S(1)}, u32[]{:S(2)}, u32[]{:S(2)}) collective-permute-start(bf16[384,128]{1,0:T(8,128)(2,1)S(1)} %add_add_fusion), channel_id=1, source_target_pairs={{0,8},{8,0},{16,24},{24,16},{32,40},{40,32},{48,56},{56,48},{64,72... | collective-permute-start | bytes 294920 | tf_op jit(solution)/shard_map/ppermute | solution.py:25
  96.8 4.3 %collective-permute-start.27 = (bf16[384,128]{1,0:T(8,128)(2,1)S(1)}, bf16[384,128]{1,0:T(8,128)(2,1)S(1)}, u32[]{:S(2)}, u32[]{:S(2)}) collective-permute-start(bf16[384,128]{1,0:T(8,128)(2,1)S(1)} %add_convert_fusion.1), channel_id=1, source_target_pairs={{0,96},{8,104},{16,112},{24,120},{32,64},{40,72},{48,80},{56,88},{... | collective-permute-start | bytes 294920 | tf_op jit(solution)/shard_map/ppermute | solution.py:25
  98.6 5.1 %collective-permute-start.26 = (bf16[384,128]{1,0:T(8,128)(2,1)S(1)}, bf16[384,128]{1,0:T(8,128)(2,1)S(1)}, u32[]{:S(2)}, u32[]{:S(2)}) collective-permute-start(bf16[384,128]{1,0:T(8,128)(2,1)S(1)} %add_convert_fusion.1), channel_id=1, source_target_pairs={{0,64},{8,72},{16,80},{24,88},{32,96},{40,104},{48,112},{56,120},{... | collective-permute-start | bytes 294920 | tf_op jit(solution)/shard_map/ppermute | solution.py:25
  104.6 10.7 %collective-permute-start.28 = (bf16[384,128]{1,0:T(8,128)(2,1)S(1)}, bf16[384,128]{1,0:T(8,128)(2,1)S(1)}, u32[]{:S(2)}, u32[]{:S(2)}) collective-permute-start(bf16[384,128]{1,0:T(8,128)(2,1)S(1)} %add_convert_fusion.refs_0_), channel_id=1, source_target_pairs={{0,2},{1,3},{2,0},{3,1},{4,6},{5,7},{6,4},{7,5},{8,10},{9,11},{10,... | collective-permute-start | bytes 294920 | tf_op jit(solution)/shard_map/ppermute | solution.py:25
  104.7 10.6 %collective-permute-start.29 = (bf16[384,128]{1,0:T(8,128)(2,1)S(1)}, bf16[384,128]{1,0:T(8,128)(2,1)S(1)}, u32[]{:S(2)}, u32[]{:S(2)}) collective-permute-start(bf16[384,128]{1,0:T(8,128)(2,1)S(1)} %add_convert_fusion.refs_0_), channel_id=1, source_target_pairs={{0,4},{1,5},{2,6},{3,7},{4,0},{5,1},{6,2},{7,3},{8,12},{9,13},{10,... | collective-permute-start | bytes 294920 | tf_op jit(solution)/shard_map/ppermute | solution.py:25
  106.5 8.8 %collective-permute-start.30 = (bf16[384,128]{1,0:T(8,128)(2,1)S(1)}, bf16[384,128]{1,0:T(8,128)(2,1)S(1)}, u32[]{:S(2)}, u32[]{:S(2)}) collective-permute-start(bf16[384,128]{1,0:T(8,128)(2,1)S(1)} %add_convert_fusion.refs_0_), channel_id=1, source_target_pairs={{0,6},{1,7},{2,4},{3,5},{4,2},{5,3},{6,0},{7,1},{8,14},{9,15},{10,... | collective-permute-start | bytes 294920 | tf_op jit(solution)/shard_map/ppermute | solution.py:25
  109.0 16.9 %collective-permute-start.34 = (bf16[512,256]{1,0:T(8,128)(2,1)S(1)}, bf16[512,256]{1,0:T(8,128)(2,1)S(1)}, u32[]{:S(2)}, u32[]{:S(2)}) collective-permute-start(bf16[512,256]{1,0:T(8,128)(2,1)S(1)} %get-tuple-element.77), channel_id=1, source_target_pairs={{8,16},{16,8},{24,32},{32,24},{40,48},{48,40},{56,64},{64,56},{72,... | collective-permute-start | bytes 786440 | tf_op jit(solution)/shard_map/ppermute | solution.py:35
  112.3 13.6 %collective-permute-start.33 = (bf16[512,256]{1,0:T(8,128)(2,1)S(1)}, bf16[512,256]{1,0:T(8,128)(2,1)S(1)}, u32[]{:S(2)}, u32[]{:S(2)}) collective-permute-start(bf16[512,256]{1,0:T(8,128)(2,1)S(1)} %get-tuple-element.76), channel_id=1, source_target_pairs={{0,8},{8,0},{16,24},{24,16},{32,40},{40,32},{48,56},{56,48},{64,72... | collective-permute-start | bytes 786440 | tf_op jit(solution)/shard_map/ppermute | solution.py:35
  115.4 6.1 %collective-permute-start.35 = (bf16[384,128]{1,0:T(8,128)(2,1)S(1)}, bf16[384,128]{1,0:T(8,128)(2,1)S(1)}, u32[]{:S(2)}, u32[]{:S(2)}) collective-permute-start(bf16[384,128]{1,0:T(8,128)(2,1)S(1)} %add_convert_fusion.refs_0_), channel_id=1, source_target_pairs={{0,1},{1,0},{2,3},{3,2},{4,5},{5,4},{6,7},{7,6},{8,9},{9,8},{10,11... | collective-permute-start | bytes 294920 | tf_op jit(solution)/shard_map/ppermute | solution.py:25
  (35 other events, 224.0 us)

commit v8 on v4

--- a/solution.py
+++ b/solution.py
@@ -141,21 +141,22 @@
     return [north, south, west, east, north + west, north + east, south + west, south + east]
 
 
-def spread_kernel(weight, out, out_back, wide):
+def spread_kernel(weight, out, out_back, narrow, wide):
+    narrow[...] = weight[...].astype(F32)
     for lead, ref in ((LEAD, out), (LEAD_BACK, out_back)):
         wide[...] = jnp.zeros_like(wide)
         for k in range(4):
             for u in range(SPAN):
                 row = k * 128 + (u % 4) * 32 + (u // 4) * SPAN + lead
                 at = (k * SPAN + u) * SPAN
-                wide[row : row + SPAN] = weight[at : at + SPAN]
+                wide[row : row + SPAN] = narrow[at : at + SPAN]
         ref[...] = wide[...].astype(BF16)
 
 
 def forward_kernel(partners, counts, radius, first, context, cotangent, conv_weight, corr_weight, *refs):
     tiles, refs = refs[:18], refs[18:]
     parts, motion, context_grad, facing, away, ends, weights_sent, weights_kept = refs[:8]
-    edges, cot_taps, taps, weight_grads, sems, edge_sems = refs[8:]
+    edges, cot_taps, taps_back, taps, flipped, weight_grads, sems, edge_sems = refs[8:]
     cells = first.shape[0]
     slots = parts.shape[0]
     row_sides, chip_sides = (6, 12), (1, 3, 5)
@@ -183,6 +184,9 @@
     for k in range(slots):
         live = jnp.where(k < counts[0, 0], 1.0 / math.sqrt(first.shape[1]), 0.0).astype(F32)
         gains.append(jnp.where(inside, live, 0.0))
+    for q in range(cells // GROUP):
+        at = slice(q * GROUP, (q + 1) * GROUP)
+        flipped[at] = jnp.dot(flip, first[at], preferred_element_type=F32).astype(BF16)
     for n in range(8):
         pltpu.make_async_copy(tiles[0].at[pl.ds(cells, 48)], edges.at[n], edge_sems.at[n]).wait()
     north, south = edges[0, :32, 128:], edges[1, :32, :128]
@@ -217,7 +221,7 @@
         ).wait()
     for q in range(cells // GROUP):
         at = slice(q * GROUP, (q + 1) * GROUP)
-        features = jnp.dot(flip, first[at], preferred_element_type=F32).astype(BF16)
+        features = flipped[at]
         for k in range(slots):
             scores = lax.dot_general(
                 features,
@@ -232,9 +236,10 @@
                 + pltpu.roll(band[:, 128:256], SPAN, 1)
                 + pltpu.roll(band[:, 256:], 2 * SPAN, 1)
             )
-            taps[at, k * 128 : (k + 1) * 128] = jnp.dot(
-                flip, packed.astype(BF16), preferred_element_type=F32
-            ).astype(BF16)
+            taps_back[at, k * 128 : (k + 1) * 128] = packed.astype(BF16)
+    for q in range(cells // GROUP):
+        at = slice(q * GROUP, (q + 1) * GROUP)
+        taps[at] = jnp.dot(flip, taps_back[at], preferred_element_type=F32).astype(BF16)
     pre = jnp.dot(taps[...], corr_weight[...], preferred_element_type=F32) + context[...].astype(
         F32
     )
@@ -282,6 +287,7 @@
     *kept, lent, totals = refs
     for ref in refs:
         ref[...] = jnp.zeros_like(ref)
+    across = first[...].T
     for q in range(cells // GROUP):
         at = slice(q * GROUP, (q + 1) * GROUP)
         packed = (
@@ -305,12 +311,12 @@
             scores = pltpu.roll(band, WINDOW - REACH - LEAD_BACK, 1, stride=1, stride_axis=0).astype(BF16)
             window = slice(q * GROUP, q * GROUP + WINDOW)
             first_here += jnp.dot(scores, parts[k, window], preferred_element_type=F32)
-            totals[k, window] += lax.dot_general(
-                scores, first[at], (((0,), (0,)), ((), ())), preferred_element_type=F32
+            totals[k, :, window] += jnp.dot(
+                across[:, at], scores, preferred_element_type=F32
             )
         first_grad[at] = first_here * scale
     for k in range(slots):
-        value = (totals[k, GROUP : GROUP + cells] * scale).astype(BF16)
+        value = (totals[k, :, GROUP : GROUP + cells] * scale).astype(BF16).T
         place = tile_of(partners[0, 0, k])
         for x in range(3):
             @pl.when(place % 6 == 2 * x)
@@ -356,12 +362,6 @@
         compiler_params=pltpu.CompilerParams(vmem_limit_bytes=VMEM_LIMIT),
         cost_estimate=pl.CostEstimate(flops=flops, bytes_accessed=flops // 300, transcendentals=0),
     )
-
-
-def halve(cur, mine, axis, bits):
-    size = cur.shape[0] // 2
-    gone = lax.dynamic_slice_in_dim(cur, (1 - mine) * size, size).astype(BF16)
-    return lax.dynamic_slice_in_dim(cur, mine * size, size), swap(gone, axis, bits)
 
 
 def sum_everywhere(cur, axis, unit):
@@ -403,8 +403,8 @@
         spread_kernel,
         (shape((slots * 128, hidden), BF16), shape((slots * 128, hidden), BF16)),
         [VMEM],
-        [pltpu.VMEM((slots * 128, hidden), F32)],
-    )(corr_weight.astype(F32))
+        [pltpu.VMEM(corr_weight.shape, F32), pltpu.VMEM((slots * 128, hidden), F32)],
+    )(corr_weight)
     total_rows = 9 * hidden + 2 * 384
     parts, motion, context_grad, facing, away, ends, weights_sent, weights_kept = call(
         forward_kernel,
@@ -423,6 +423,8 @@
             pltpu.VMEM((8, 48, channels), BF16),
             pltpu.VMEM(((rows_tile + 2) * cols_tile, 3 * out_width), BF16),
             pltpu.VMEM((cells, slots * 128), BF16),
+            pltpu.VMEM((cells, slots * 128), BF16),
+            pltpu.VMEM((cells, channels), BF16),
             pltpu.VMEM((total_rows, 128), F32),
             pltpu.SemaphoreType.DMA((slots,)),
             pltpu.SemaphoreType.DMA((8,)),
@@ -438,7 +440,9 @@
         *around,
     )
     total = weights_kept + swap(weights_sent, "col", 1).astype(F32)
-    total, got = halve(total, chip >> 1, "col", 4)
+    size = total.shape[0] // 4
+    pieces = [lax.dynamic_slice_in_dim(total, (chip ^ s) * size, size) for s in range(4)]
+    got = [swap(pieces[s].astype(BF16), "col", 2 * s) for s in (1, 2, 3)]
     first_grad, *kept, lent = call(
         backward_kernel,
         (
@@ -447,7 +451,7 @@
             shape((6, cells, channels), BF16),
         ),
         [SMEM] * 3 + [VMEM] * 4,
-        [pltpu.VMEM((slots, cells + 2 * GROUP, channels), F32)],
+        [pltpu.VMEM((slots, channels, cells + 2 * GROUP), F32)],
         flops=3 * 10**9,
     )(*tables, first, context_grad, spread_back, parts)
     lent = swap(lent, "col", 1)
@@ -456,8 +460,10 @@
         (kept[x].astype(F32) + jnp.where(side == x, lent[3:].astype(F32), 0.0)).astype(BF16)
         for x in (1, 2)
     ]
-    total, got = halve(total + got.astype(F32), chip & 1, "col", 2)
-    total, sent[0], sent[1] = lax.optimization_barrier((total + got.astype(F32), *sent))
+    total = (pieces[0] + got[0].astype(F32)) + (got[1].astype(F32) + got[2].astype(F32))
+    around_motion = rim(facing, away, ends, row_even, col_even)
+    total, *ready = lax.optimization_barrier((total, *sent, *around_motion))
+    sent, around_motion = ready[:2], ready[2:]
     middle = kept[0].astype(F32) + lent[:3].astype(F32)
     for x in (1, 2):
         middle += swap_pairs(sent[x - 1], "col", x - 1, 2).astype(F32)
@@ -475,7 +481,7 @@
         flops=10**9,
     )(
         motion,
-        *rim(facing, away, ends, row_even, col_even),
+        *around_motion,
         conv_weight.reshape(3, 3 * hidden, out_width),
     )
     conv_total, corr_total = call(

time: 122 us -> 116 us (0.951)
  waiting for transfers between devices: 12.7 us -> 19 us
  Pallas kernels: 30.2 us -> 25.4 us
  starting transfers between devices: 67.9 us -> 64 us
  other arithmetic: 4.32 us -> 2.64 us
    ppermute x26 -> x27, waiting for transfers between devices: 9.54 us -> 18.2 us  [swap(): lax.ppermute(array, axis, [(i, i ^ bits) for i in range(lax.axis_size(axi...]
    pallas_call x1, Pallas kernels: 12.7 us -> 8.84 us  [body(): call(forward_kernel, (shape((slots, cells + 2 * GROUP, channels), BF16),...]
    ppermute x16, starting transfers between devices: 33.2 us -> 30.7 us  [swap_pairs(): return lax.ppermute(array, axis, pairs)]
    ppermute x16, waiting for transfers between devices: 3.2 us -> 0.82 us  [swap_pairs(): return lax.ppermute(array, axis, pairs)]
    convert_element_type x1 -> x0, other arithmetic: 1.68 us -> none  [body(): corr_weight.astype(F32)]
    ppermute x26 -> x27, starting transfers between devices: 34.8 us -> 33.3 us  [swap(): lax.ppermute(array, axis, [(i, i ^ bits) for i in range(lax.axis_size(axi...]
  transfers between devices with their start and end apart: 42 -> 43, of which waited for: 8 -> 10; matrix products, arithmetic and copies ran while one was open for 3% -> 1% of each run, Pallas kernels for 13% -> 13%
where the time goes in v8:
time: 116 us; the launch traced here: 115 us
  starting transfers between devices  64 us (55%)
  Pallas kernels  25.4 us (22%)
  waiting for transfers between devices  19 us (16%)
  other arithmetic  2.64 us (2%)
  between operations  2.51 us (2%)
  local copies, waits for them, and re-layouts  1.47 us (1%)
    ppermute x27, starting transfers between devices, swap(): lax.ppermute(array, axis, [(i, i ^ bits) for i in range(lax.axis_size(axi...  33.3 us
    ppermute x16, starting transfers between devices, swap_pairs(): return lax.ppermute(array, axis, pairs)  30.7 us
    ppermute x27, waiting for transfers between devices, swap(): lax.ppermute(array, axis, [(i, i ^ bits) for i in range(lax.axis_size(axi...  18.2 us
    pallas_call x1, Pallas kernels, body(): call(forward_kernel, (shape((slots, cells + 2 * GROUP, channels), BF16),...  8.84 us
    pallas_call x1, Pallas kernels, body(): call(backward_kernel, (shape((cells, channels), F32), *[shape((3, cells,...  7.57 us
    pallas_call x1, Pallas kernels, body(): call(features_kernel, shape((cells, out_width), BF16), [VMEM] * 6, [pltpu...  2.66 us
    pallas_call x1, Pallas kernels, body(): call(finish_kernel, (shape((9 * hidden, out_width), F32), shape(corr_weig...  2.51 us
  transfers between devices with their start and end apart: 43, of which 10 were waited for; matrix products, arithmetic and copies ran while one was open for 1% of the time, Pallas kernels for 13%

profile of v8, /device:TPU:33, one launch (start us, length us, event | category | flops | bytes accessed | tf_op | source)
XLA Modules:
  0.0 115.1 jit_solution(12885927703931527729)
XLA Ops:
  0.6 1.8 %shard_map.137.refs_0_ = bf16[560,256]{1,0:T(8,128)(2,1)} custom-call(bf16[512,256]{1,0:T(8,128)(2,1)} %bitcast.25, bf16[512,128]{1,0:T(8,128)(2,1)} %bitcast.26), custom_call_target="tpu_custom_call" | custom-call | tf_op jit(solution)/shard_map/pallas_call | solution.py:388
  3.1 3.7 %collective-permute-start.1 = (bf16[560,256]{1,0:T(8,128)(2,1)}, bf16[560,256]{1,0:T(8,128)(2,1)S(1)}, u32[]{:S(2)}, u32[]{:S(2)}) collective-permute-start(bf16[560,256]{1,0:T(8,128)(2,1)} %shard_map.137.refs_0_), channel_id=1, source_target_pairs={{0,2},{2,0},{1,3},{3,1},{4,6},{6,4},{5,7},{7,5},{8,10},{10,8},{9,1... | collective-permute-start | bytes 860168 | tf_op jit(solution)/shard_map/ppermute | solution.py:35
  6.9 4.2 %collective-permute-start.11 = (bf16[560,256]{1,0:T(8,128)(2,1)}, bf16[560,256]{1,0:T(8,128)(2,1)S(1)}, u32[]{:S(2)}, u32[]{:S(2)}) collective-permute-start(bf16[560,256]{1,0:T(8,128)(2,1)} %shard_map.137.refs_0_), channel_id=1, source_target_pairs={{8,16},{16,8},{24,32},{32,24},{40,48},{48,40},{56,64},{64,56},{72,... | collective-permute-start | bytes 860168 | tf_op jit(solution)/shard_map/ppermute | solution.py:35
  11.4 1.8 %collective-permute-start = (bf16[560,256]{1,0:T(8,128)(2,1)}, bf16[560,256]{1,0:T(8,128)(2,1)S(1)}, u32[]{:S(2)}, u32[]{:S(2)}) collective-permute-start(bf16[560,256]{1,0:T(8,128)(2,1)} %shard_map.137.refs_0_), channel_id=1, source_target_pairs={{0,1},{1,0},{2,3},{3,2},{4,5},{5,4},{6,7},{7,6},{8,9},{9,8},{10,11... | collective-permute-start | bytes 860168 | tf_op jit(solution)/shard_map/ppermute | solution.py:25
  14.4 3.2 %collective-permute-start.13 = (bf16[560,256]{1,0:T(8,128)(2,1)S(1)}, bf16[560,256]{1,0:T(8,128)(2,1)S(1)}, u32[]{:S(2)}, u32[]{:S(2)}) collective-permute-start(bf16[560,256]{1,0:T(8,128)(2,1)S(1)} %collective-permute-done.1.refs_2_), channel_id=1, source_target_pairs={{8,16},{16,8},{24,32},{32,24},{40,48},{48,40},{56,64},{64,56},{72,... | collective-permute-start | bytes 860168 | tf_op jit(solution)/shard_map/ppermute | solution.py:35
  18.9 2.5 %collective-permute-start.7 = (bf16[560,256]{1,0:T(8,128)(2,1)S(1)}, bf16[560,256]{1,0:T(8,128)(2,1)S(1)}, u32[]{:S(2)}, u32[]{:S(2)}) collective-permute-start(bf16[560,256]{1,0:T(8,128)(2,1)S(1)} %collective-permute-done.5.refs_6_), channel_id=1, source_target_pairs={{0,2},{2,0},{1,3},{3,1},{4,6},{6,4},{5,7},{7,5},{8,10},{10,8},{9,1... | collective-permute-start | bytes 860168 | tf_op jit(solution)/shard_map/ppermute | solution.py:35
  21.4 2.7 %collective-permute-start.12 = (bf16[560,256]{1,0:T(8,128)(2,1)S(1)}, bf16[560,256]{1,0:T(8,128)(2,1)S(1)}, u32[]{:S(2)}, u32[]{:S(2)}) collective-permute-start(bf16[560,256]{1,0:T(8,128)(2,1)S(1)} %collective-permute-done.11.refs_12_), channel_id=1, source_target_pairs={{0,1},{1,0},{2,3},{3,2},{4,5},{5,4},{6,7},{7,6},{8,9},{9,8},{10,11... | collective-permute-start | bytes 860168 | tf_op jit(solution)/shard_map/ppermute | solution.py:25
  24.3 2.4 %collective-permute-start.2 = (bf16[560,256]{1,0:T(8,128)(2,1)S(1)}, bf16[560,256]{1,0:T(8,128)(2,1)S(1)}, u32[]{:S(2)}, u32[]{:S(2)}) collective-permute-start(bf16[560,256]{1,0:T(8,128)(2,1)S(1)} %collective-permute-done.1.refs_2_), channel_id=1, source_target_pairs={{0,1},{1,0},{2,3},{3,2},{4,5},{5,4},{6,7},{7,6},{8,9},{9,8},{10,11... | collective-permute-start | bytes 860168 | tf_op jit(solution)/shard_map/ppermute | solution.py:25
  27.8 1.5 %collective-permute-start.10 = (bf16[560,256]{1,0:T(8,128)(2,1)S(1)}, bf16[560,256]{1,0:T(8,128)(2,1)}, u32[]{:S(2)}, u32[]{:S(2)}) collective-permute-start(bf16[560,256]{1,0:T(8,128)(2,1)S(1)} %collective-permute-done.9.refs_10_), channel_id=1, source_target_pairs={{0,1},{1,0},{2,3},{3,2},{4,5},{5,4},{6,7},{7,6},{8,9},{9,8},{10,11... | collective-permute-start | bytes 860168 | tf_op jit(solution)/shard_map/ppermute | solution.py:25
  29.9 2.0 %shard_map.136 = (bf16[512,256]{1,0:T(8,128)(2,1)}, bf16[512,256]{1,0:T(8,128)(2,1)}) custom-call(bf16[324,256]{1,0:T(8,128)(2,1)} %weight.1), custom_call_target="tpu_custom_call" | custom-call | tf_op jit(solution)/shard_map/pallas_call | solution.py:402
  33.4 8.8 %shard_map.138 = (bf16[4,768,256]{2,1,0:T(8,128)(2,1)}, bf16[512,256]{1,0:T(8,128)(2,1)}, bf16[512,256]{1,0:T(8,128)(2,1)}, bf16[32,256]{1,0:T(8,128)(2,1)}, bf1...) custom-call(s32[1,1,4]{2,1,0:T(1,128)} %partners.3, ...), custom_call_target="tpu_custom_call" | custom-call | flops 3000000000 | bytes 10000000 | tf_op jit(solution)/shard_map/pallas_call | solution.py:409
  42.2 4.0 %collective-permute-start.22 = (bf16[32,256]{1,0:T(8,128)(2,1)}, bf16[32,256]{1,0:T(8,128)(2,1)S(1)}, u32[]{:S(2)}, u32[]{:S(2)}) collective-permute-start(bf16[32,256]{1,0:T(8,128)(2,1)} %get-tuple-element.40), channel_id=1, source_target_pairs={{8,16},{16,8},{24,32},{32,24},{40,48},{48,40},{56,64},{64,56},{72,... | collective-permute-start | bytes 49160 | tf_op jit(solution)/shard_map/ppermute | solution.py:35
  46.6 7.6 %shard_map.139 = (f32[512,256]{1,0:T(8,128)}, bf16[3,512,256]{2,1,0:T(8,128)(2,1)}, bf16[3,512,256]{2,1,0:T(8,128)(2,1)}, bf16[3,512,256]{2,1,0:T(8,128)(2,1)}, bf16[6,512,256]{2,1,0:T(8,128)(2,1)}) custom-call(s32[1,1,4]{2,1,0:T(1,128)} %partners.3, s32[1,1]{1,0:T(1,128)S(6)} %copy.15.counts, s32[1,1]{1,0:T(1,128)S(6)} %copy.16.radius, ...), custom_call_target="tpu_custom_call" | custom-call | flops 3000000000 | bytes 10000000 | tf_op jit(solution)/shard_map/pallas_call | solution.py:446
  55.0 3.7 %collective-permute-start.24 = (bf16[18,256]{1,0:T(8,128)(2,1)S(1)}, bf16[18,256]{1,0:T(8,128)(2,1)S(1)}, u32[]{:S(2)}, u32[]{:S(2)}) collective-permute-start(bf16[18,256]{1,0:T(8,128)(2,1)S(1)} %get-tuple-element.68), channel_id=1, source_target_pairs={{1,2},{2,1},{3,4},{4,3},{5,6},{6,5},{9,10},{10,9},{11,12},{12,11},... | collective-permute-start | bytes 27656 | tf_op jit(solution)/shard_map/ppermute | solution.py:35
  60.0 1.6 %collective-permute-start.19 = (bf16[384,128]{1,0:T(8,128)(2,1)S(1)}, bf16[384,128]{1,0:T(8,128)(2,1)S(1)}, u32[]{:S(2)}, u32[]{:S(2)}) collective-permute-start(bf16[384,128]{1,0:T(8,128)(2,1)S(1)} %get-tuple-element.62), channel_id=1, source_target_pairs={{0,4},{1,5},{2,6},{3,7},{4,0},{5,1},{6,2},{7,3},{8,12},{9,13},{10,... | collective-permute-start | bytes 294920 | tf_op jit(solution)/shard_map/ppermute | solution.py:25
  63.5 3.1 %collective-permute-done.19 = bf16[384,128]{1,0:T(8,128)(2,1)S(1)} collective-permute-done((bf16[384,128]{1,0:T(8,128)(2,1)S(1)}, bf16[384,128]{1,0:T(8,128)(2,1)S(1)}, u32[]{:S(2)}, u32[]{:S(2)}) %collective-permute-start.19) | collective-permute-done | bytes 98336 | tf_op jit(solution)/shard_map/ppermute | solution.py:25
  66.6 2.4 %collective-permute-done.20 = bf16[384,128]{1,0:T(8,128)(2,1)S(1)} collective-permute-done((bf16[384,128]{1,0:T(8,128)(2,1)S(1)}, bf16[384,128]{1,0:T(8,128)(2,1)S(1)}, u32[]{:S(2)}, u32[]{:S(2)}) %collective-permute-start.20) | collective-permute-done | bytes 98336 | tf_op jit(solution)/shard_map/ppermute | solution.py:25
  70.5 1.8 %collective-permute-start.30 = (bf16[384,128]{1,0:T(8,128)(2,1)S(1)}, bf16[384,128]{1,0:T(8,128)(2,1)S(1)}, u32[]{:S(2)}, u32[]{:S(2)}) collective-permute-start(bf16[384,128]{1,0:T(8,128)(2,1)S(1)} %add_add_fusion), channel_id=1, source_target_pairs={{0,8},{8,0},{16,24},{24,16},{32,40},{40,32},{48,56},{56,48},{64,72... | collective-permute-start | bytes 294920 | tf_op jit(solution)/shard_map/ppermute | solution.py:25
  72.2 1.8 %collective-permute-start.31 = (bf16[384,128]{1,0:T(8,128)(2,1)S(1)}, bf16[384,128]{1,0:T(8,128)(2,1)S(1)}, u32[]{:S(2)}, u32[]{:S(2)}) collective-permute-start(bf16[384,128]{1,0:T(8,128)(2,1)S(1)} %add_add_fusion), channel_id=1, source_target_pairs={{0,16},{8,24},{16,0},{24,8},{32,48},{40,56},{48,32},{56,40},{64,80... | collective-permute-start | bytes 294920 | tf_op jit(solution)/shard_map/ppermute | solution.py:25
  74.9 3.8 %collective-permute-done.31 = bf16[384,128]{1,0:T(8,128)(2,1)S(1)} collective-permute-done((bf16[384,128]{1,0:T(8,128)(2,1)S(1)}, bf16[384,128]{1,0:T(8,128)(2,1)S(1)}, u32[]{:S(2)}, u32[]{:S(2)}) %collective-permute-start.31) | collective-permute-done | bytes 98336 | tf_op jit(solution)/shard_map/ppermute | solution.py:25
  78.7 2.7 %collective-permute-done.32 = bf16[384,128]{1,0:T(8,128)(2,1)S(1)} collective-permute-done((bf16[384,128]{1,0:T(8,128)(2,1)S(1)}, bf16[384,128]{1,0:T(8,128)(2,1)S(1)}, u32[]{:S(2)}, u32[]{:S(2)}) %collective-permute-start.32) | collective-permute-done | bytes 98336 | tf_op jit(solution)/shard_map/ppermute | solution.py:25
  81.6 2.7 %collective-permute-start.34 = (bf16[384,128]{1,0:T(8,128)(2,1)S(1)}, bf16[384,128]{1,0:T(8,128)(2,1)S(1)}, u32[]{:S(2)}, u32[]{:S(2)}) collective-permute-start(bf16[384,128]{1,0:T(8,128)(2,1)S(1)} %add_convert_fusion.1), channel_id=1, source_target_pairs={{0,64},{8,72},{16,80},{24,88},{32,96},{40,104},{48,112},{56,120},{... | collective-permute-start | bytes 294920 | tf_op jit(solution)/shard_map/ppermute | solution.py:25
  85.4 3.3 %collective-permute-done.34 = bf16[384,128]{1,0:T(8,128)(2,1)S(1)} collective-permute-done((bf16[384,128]{1,0:T(8,128)(2,1)S(1)}, bf16[384,128]{1,0:T(8,128)(2,1)S(1)}, u32[]{:S(2)}, u32[]{:S(2)}) %collective-permute-start.34) | collective-permute-done | bytes 98336 | tf_op jit(solution)/shard_map/ppermute | solution.py:25
  88.7 1.4 %collective-permute-done.35 = bf16[384,128]{1,0:T(8,128)(2,1)S(1)} collective-permute-done((bf16[384,128]{1,0:T(8,128)(2,1)S(1)}, bf16[384,128]{1,0:T(8,128)(2,1)S(1)}, u32[]{:S(2)}, u32[]{:S(2)}) %collective-permute-start.35) | collective-permute-done | bytes 98336 | tf_op jit(solution)/shard_map/ppermute | solution.py:25
  90.3 1.4 %collective-permute-start.36 = (bf16[384,128]{1,0:T(8,128)(2,1)S(1)}, bf16[384,128]{1,0:T(8,128)(2,1)S(1)}, u32[]{:S(2)}, u32[]{:S(2)}) collective-permute-start(bf16[384,128]{1,0:T(8,128)(2,1)S(1)} %add_convert_fusion.refs_0_), channel_id=1, source_target_pairs={{0,2},{1,3},{2,0},{3,1},{4,6},{5,7},{6,4},{7,5},{8,10},{9,11},{10,... | collective-permute-start | bytes 294920 | tf_op jit(solution)/shard_map/ppermute | solution.py:25
  92.2 5.3 %collective-permute-start.29 = (bf16[512,256]{1,0:T(8,128)(2,1)S(1)}, bf16[512,256]{1,0:T(8,128)(2,1)S(1)}, u32[]{:S(2)}, u32[]{:S(2)}) collective-permute-start(bf16[512,256]{1,0:T(8,128)(2,1)S(1)} %get-tuple-element.59), channel_id=1, source_target_pairs={{8,16},{16,8},{24,32},{32,24},{40,48},{48,40},{56,64},{64,56},{72,... | collective-permute-start | bytes 786440 | tf_op jit(solution)/shard_map/ppermute | solution.py:35
  97.5 1.5 %collective-permute-start.37 = (bf16[384,128]{1,0:T(8,128)(2,1)S(1)}, bf16[384,128]{1,0:T(8,128)(2,1)S(1)}, u32[]{:S(2)}, u32[]{:S(2)}) collective-permute-start(bf16[384,128]{1,0:T(8,128)(2,1)S(1)} %add_convert_fusion.refs_0_), channel_id=1, source_target_pairs={{0,4},{1,5},{2,6},{3,7},{4,0},{5,1},{6,2},{7,3},{8,12},{9,13},{10,... | collective-permute-start | bytes 294920 | tf_op jit(solution)/shard_map/ppermute | solution.py:25
  99.0 1.7 %collective-permute-start.38 = (bf16[384,128]{1,0:T(8,128)(2,1)S(1)}, bf16[384,128]{1,0:T(8,128)(2,1)S(1)}, u32[]{:S(2)}, u32[]{:S(2)}) collective-permute-start(bf16[384,128]{1,0:T(8,128)(2,1)S(1)} %add_convert_fusion.refs_0_), channel_id=1, source_target_pairs={{0,6},{1,7},{2,4},{3,5},{4,2},{5,3},{6,0},{7,1},{8,14},{9,15},{10,... | collective-permute-start | bytes 294920 | tf_op jit(solution)/shard_map/ppermute | solution.py:25
  100.8 2.4 %collective-permute-start.39 = (bf16[384,128]{1,0:T(8,128)(2,1)S(1)}, bf16[384,128]{1,0:T(8,128)(2,1)S(1)}, u32[]{:S(2)}, u32[]{:S(2)}) collective-permute-start(bf16[384,128]{1,0:T(8,128)(2,1)S(1)} %add_convert_fusion.refs_0_), channel_id=1, source_target_pairs={{0,1},{1,0},{2,3},{3,2},{4,5},{5,4},{6,7},{7,6},{8,9},{9,8},{10,11... | collective-permute-start | bytes 294920 | tf_op jit(solution)/shard_map/ppermute | solution.py:25
  103.1 3.3 %collective-permute-start.40 = (bf16[384,128]{1,0:T(8,128)(2,1)S(1)}, bf16[384,128]{1,0:T(8,128)(2,1)S(1)}, u32[]{:S(2)}, u32[]{:S(2)}) collective-permute-start(bf16[384,128]{1,0:T(8,128)(2,1)S(1)} %collective-permute-done.36.refs_1_), channel_id=1, source_target_pairs={{0,1},{1,0},{2,3},{3,2},{4,5},{5,4},{6,7},{7,6},{8,9},{9,8},{10,11... | collective-permute-start | bytes 294920 | tf_op jit(solution)/shard_map/ppermute | solution.py:25
  107.7 2.7 %shard_map.140 = bf16[512,128]{1,0:T(8,128)(2,1)} custom-call(bf16[512,256]{1,0:T(8,128)(2,1)} %get-tuple-element.31.motion, bf16[32,256]{1,0:T(8,128)(2,1)} %copy-done.13, bf16[32,256]{1,0:T(8,128)(2,1)} %copy-done.12, bf16[18,256]{1,0:T(8,128)(2,1)} %get-tuple-element.45.west, bf16[18,256]{1,0:T(8,128)(2,1)} %get-tuple-element.46.east, ...), custom_call_target="tpu_custom_call" | custom-call | flops 1000000000 | bytes 3333333 | tf_op jit(solution)/shard_map/pallas_call | solution.py:476
  111.7 2.5 %shard_map.141 = (f32[2304,128]{1,0:T(8,128)}, f32[324,256]{1,0:T(8,128)}) custom-call(bf16[384,128]{1,0:T(8,128)(2,1)} %copy-done.4, bf16[384,128]{1,0:T(8,128)(2,1)} %copy-done.5, bf16[384,128]{1,0:T(8,128)(2,1)} %copy-done.6, bf16[384,128]{1,0:T(8,128)(2,1)} %copy-done.7, bf16[384,128]{1,0:T(8,128)(2,1)} %copy-done.8, bf16[384,128]{1,0:T(8,128)(2,1)} %copy-done.9, ...), custom_call_target="tpu_custom_call" | custom-call | tf_op jit(solution)/shard_map/pallas_call | solution.py:487
  (130 shorter events, 17.2 us)
Async XLA Ops:
  2.5 10.8 %collective-permute-start.3 = (bf16[560,256]{1,0:T(8,128)(2,1)}, bf16[560,256]{1,0:T(8,128)(2,1)S(1)}, u32[]{:S(2)}, u32[]{:S(2)}) collective-permute-start(bf16[560,256]{1,0:T(8,128)(2,1)} %shard_map.137.refs_0_), channel_id=1, source_target_pairs={{2,4},{4,2},{3,5},{5,3},{10,12},{12,10},{11,13},{13,11},{18,20},{2... | collective-permute-start | bytes 860168 | tf_op jit(solution)/shard_map/ppermute | solution.py:35
  3.1 11.3 %collective-permute-start.1 = (bf16[560,256]{1,0:T(8,128)(2,1)}, bf16[560,256]{1,0:T(8,128)(2,1)S(1)}, u32[]{:S(2)}, u32[]{:S(2)}) collective-permute-start(bf16[560,256]{1,0:T(8,128)(2,1)} %shard_map.137.refs_0_), channel_id=1, source_target_pairs={{0,2},{2,0},{1,3},{3,1},{4,6},{6,4},{5,7},{7,5},{8,10},{10,8},{9,1... | collective-permute-start | bytes 860168 | tf_op jit(solution)/shard_map/ppermute | solution.py:35
  6.9 11.3 %collective-permute-start.11 = (bf16[560,256]{1,0:T(8,128)(2,1)}, bf16[560,256]{1,0:T(8,128)(2,1)S(1)}, u32[]{:S(2)}, u32[]{:S(2)}) collective-permute-start(bf16[560,256]{1,0:T(8,128)(2,1)} %shard_map.137.refs_0_), channel_id=1, source_target_pairs={{8,16},{16,8},{24,32},{32,24},{40,48},{48,40},{56,64},{64,56},{72,... | collective-permute-start | bytes 860168 | tf_op jit(solution)/shard_map/ppermute | solution.py:35
  11.1 7.8 %collective-permute-start.5 = (bf16[560,256]{1,0:T(8,128)(2,1)}, bf16[560,256]{1,0:T(8,128)(2,1)S(1)}, u32[]{:S(2)}, u32[]{:S(2)}) collective-permute-start(bf16[560,256]{1,0:T(8,128)(2,1)} %shard_map.137.refs_0_), channel_id=1, source_target_pairs={{0,8},{8,0},{16,24},{24,16},{32,40},{40,32},{48,56},{56,48},{64,72... | collective-permute-start | bytes 860168 | tf_op jit(solution)/shard_map/ppermute | solution.py:35
  11.4 9.9 %collective-permute-start = (bf16[560,256]{1,0:T(8,128)(2,1)}, bf16[560,256]{1,0:T(8,128)(2,1)S(1)}, u32[]{:S(2)}, u32[]{:S(2)}) collective-permute-start(bf16[560,256]{1,0:T(8,128)(2,1)} %shard_map.137.refs_0_), channel_id=1, source_target_pairs={{0,1},{1,0},{2,3},{3,2},{4,5},{5,4},{6,7},{7,6},{8,9},{9,8},{10,11... | collective-permute-start | bytes 860168 | tf_op jit(solution)/shard_map/ppermute | solution.py:25
  13.3 11.0 %collective-permute-start.9 = (bf16[560,256]{1,0:T(8,128)(2,1)S(1)}, bf16[560,256]{1,0:T(8,128)(2,1)S(1)}, u32[]{:S(2)}, u32[]{:S(2)}) collective-permute-start(bf16[560,256]{1,0:T(8,128)(2,1)S(1)} %collective-permute-done.3.refs_4_), channel_id=1, source_target_pairs={{0,8},{8,0},{16,24},{24,16},{32,40},{40,32},{48,56},{56,48},{64,72... | collective-permute-start | bytes 860168 | tf_op jit(solution)/shard_map/ppermute | solution.py:35
  14.4 12.3 %collective-permute-start.13 = (bf16[560,256]{1,0:T(8,128)(2,1)S(1)}, bf16[560,256]{1,0:T(8,128)(2,1)S(1)}, u32[]{:S(2)}, u32[]{:S(2)}) collective-permute-start(bf16[560,256]{1,0:T(8,128)(2,1)S(1)} %collective-permute-done.1.refs_2_), channel_id=1, source_target_pairs={{8,16},{16,8},{24,32},{32,24},{40,48},{48,40},{56,64},{64,56},{72,... | collective-permute-start | bytes 860168 | tf_op jit(solution)/shard_map/ppermute | solution.py:35
  18.2 9.5 %collective-permute-start.15 = (bf16[560,256]{1,0:T(8,128)(2,1)S(1)}, bf16[560,256]{1,0:T(8,128)(2,1)S(1)}, u32[]{:S(2)}, u32[]{:S(2)}) collective-permute-start(bf16[560,256]{1,0:T(8,128)(2,1)S(1)} %collective-permute-done.11.refs_12_), channel_id=1, source_target_pairs={{2,4},{4,2},{3,5},{5,3},{10,12},{12,10},{11,13},{13,11},{18,20},{2... | collective-permute-start | bytes 860168 | tf_op jit(solution)/shard_map/ppermute | solution.py:35
  18.9 8.9 %collective-permute-start.7 = (bf16[560,256]{1,0:T(8,128)(2,1)S(1)}, bf16[560,256]{1,0:T(8,128)(2,1)S(1)}, u32[]{:S(2)}, u32[]{:S(2)}) collective-permute-start(bf16[560,256]{1,0:T(8,128)(2,1)S(1)} %collective-permute-done.5.refs_6_), channel_id=1, source_target_pairs={{0,2},{2,0},{1,3},{3,1},{4,6},{6,4},{5,7},{7,5},{8,10},{10,8},{9,1... | collective-permute-start | bytes 860168 | tf_op jit(solution)/shard_map/ppermute | solution.py:35
  21.4 7.9 %collective-permute-start.12 = (bf16[560,256]{1,0:T(8,128)(2,1)S(1)}, bf16[560,256]{1,0:T(8,128)(2,1)S(1)}, u32[]{:S(2)}, u32[]{:S(2)}) collective-permute-start(bf16[560,256]{1,0:T(8,128)(2,1)S(1)} %collective-permute-done.11.refs_12_), channel_id=1, source_target_pairs={{0,1},{1,0},{2,3},{3,2},{4,5},{5,4},{6,7},{7,6},{8,9},{9,8},{10,11... | collective-permute-start | bytes 860168 | tf_op jit(solution)/shard_map/ppermute | solution.py:25
  24.3 5.1 %collective-permute-start.2 = (bf16[560,256]{1,0:T(8,128)(2,1)S(1)}, bf16[560,256]{1,0:T(8,128)(2,1)S(1)}, u32[]{:S(2)}, u32[]{:S(2)}) collective-permute-start(bf16[560,256]{1,0:T(8,128)(2,1)S(1)} %collective-permute-done.1.refs_2_), channel_id=1, source_target_pairs={{0,1},{1,0},{2,3},{3,2},{4,5},{5,4},{6,7},{7,6},{8,9},{9,8},{10,11... | collective-permute-start | bytes 860168 | tf_op jit(solution)/shard_map/ppermute | solution.py:25
  27.7 5.5 %collective-permute-start.6 = (bf16[560,256]{1,0:T(8,128)(2,1)S(1)}, bf16[560,256]{1,0:T(8,128)(2,1)}, u32[]{:S(2)}, u32[]{:S(2)}) collective-permute-start(bf16[560,256]{1,0:T(8,128)(2,1)S(1)} %collective-permute-done.5.refs_6_), channel_id=1, source_target_pairs={{0,1},{1,0},{2,3},{3,2},{4,5},{5,4},{6,7},{7,6},{8,9},{9,8},{10,11... | collective-permute-start | bytes 860168 | tf_op jit(solution)/shard_map/ppermute | solution.py:25
  27.8 5.5 %collective-permute-start.10 = (bf16[560,256]{1,0:T(8,128)(2,1)S(1)}, bf16[560,256]{1,0:T(8,128)(2,1)}, u32[]{:S(2)}, u32[]{:S(2)}) collective-permute-start(bf16[560,256]{1,0:T(8,128)(2,1)S(1)} %collective-permute-done.9.refs_10_), channel_id=1, source_target_pairs={{0,1},{1,0},{2,3},{3,2},{4,5},{5,4},{6,7},{7,6},{8,9},{9,8},{10,11... | collective-permute-start | bytes 860168 | tf_op jit(solution)/shard_map/ppermute | solution.py:25
  42.2 12.7 %collective-permute-start.22 = (bf16[32,256]{1,0:T(8,128)(2,1)}, bf16[32,256]{1,0:T(8,128)(2,1)S(1)}, u32[]{:S(2)}, u32[]{:S(2)}) collective-permute-start(bf16[32,256]{1,0:T(8,128)(2,1)} %get-tuple-element.40), channel_id=1, source_target_pairs={{8,16},{16,8},{24,32},{32,24},{40,48},{48,40},{56,64},{64,56},{72,... | collective-permute-start | bytes 49160 | tf_op jit(solution)/shard_map/ppermute | solution.py:35
  46.2 8.7 %collective-permute-start.23 = (bf16[32,256]{1,0:T(8,128)(2,1)}, bf16[32,256]{1,0:T(8,128)(2,1)S(1)}, u32[]{:S(2)}, u32[]{:S(2)}) collective-permute-start(bf16[32,256]{1,0:T(8,128)(2,1)} %get-tuple-element.41), channel_id=1, source_target_pairs={{0,8},{8,0},{16,24},{24,16},{32,40},{40,32},{48,56},{56,48},{64,72... | collective-permute-start | bytes 49160 | tf_op jit(solution)/shard_map/ppermute | solution.py:35
  54.1 15.0 %collective-permute-start.21 = (bf16[6,512,256]{2,1,0:T(8,128)(2,1)}, bf16[6,512,256]{2,1,0:T(8,128)(2,1)S(1)}, u32[]{:S(2)}, u32[]{:S(2)}) collective-permute-start(bf16[6,512,256]{2,1,0:T(8,128)(2,1)} %get-tuple-element.38), channel_id=1, source_target_pairs={{0,1},{1,0},{2,3},{3,2},{4,5},{5,4},{6,7},{7,6},{8,9},{9,8},{10,11... | collective-permute-start | bytes 4718600 | tf_op jit(solution)/shard_map/ppermute | solution.py:25
  55.0 6.6 %collective-permute-start.24 = (bf16[18,256]{1,0:T(8,128)(2,1)S(1)}, bf16[18,256]{1,0:T(8,128)(2,1)S(1)}, u32[]{:S(2)}, u32[]{:S(2)}) collective-permute-start(bf16[18,256]{1,0:T(8,128)(2,1)S(1)} %get-tuple-element.68), channel_id=1, source_target_pairs={{1,2},{2,1},{3,4},{4,3},{5,6},{6,5},{9,10},{10,9},{11,12},{12,11},... | collective-permute-start | bytes 27656 | tf_op jit(solution)/shard_map/ppermute | solution.py:35
  60.0 6.6 %collective-permute-start.19 = (bf16[384,128]{1,0:T(8,128)(2,1)S(1)}, bf16[384,128]{1,0:T(8,128)(2,1)S(1)}, u32[]{:S(2)}, u32[]{:S(2)}) collective-permute-start(bf16[384,128]{1,0:T(8,128)(2,1)S(1)} %get-tuple-element.62), channel_id=1, source_target_pairs={{0,4},{1,5},{2,6},{3,7},{4,0},{5,1},{6,2},{7,3},{8,12},{9,13},{10,... | collective-permute-start | bytes 294920 | tf_op jit(solution)/shard_map/ppermute | solution.py:25
  61.6 7.5 %collective-permute-start.20 = (bf16[384,128]{1,0:T(8,128)(2,1)S(1)}, bf16[384,128]{1,0:T(8,128)(2,1)S(1)}, u32[]{:S(2)}, u32[]{:S(2)}) collective-permute-start(bf16[384,128]{1,0:T(8,128)(2,1)S(1)} %get-tuple-element.61), channel_id=1, source_target_pairs={{0,6},{1,7},{2,4},{3,5},{4,2},{5,3},{6,0},{7,1},{8,14},{9,15},{10,... | collective-permute-start | bytes 294920 | tf_op jit(solution)/shard_map/ppermute | solution.py:25
  69.6 22.0 %collective-permute-start.26 = (bf16[3,512,256]{2,1,0:T(8,128)(2,1)S(1)}, bf16[3,512,256]{2,1,0:T(8,128)(2,1)S(1)}, u32[]{:S(2)}, u32[]{:S(2)}) collective-permute-start(bf16[3,512,256]{2,1,0:T(8,128)(2,1)S(1)} %get-tuple-element.49), channel_id=1, source_target_pairs={{0,2},{2,0},{1,3},{3,1},{4,6},{6,4},{5,7},{7,5},{8,10},{10,8},{9,1... | collective-permute-start | bytes 2359304 | tf_op jit(solution)/shard_map/ppermute | solution.py:35
  69.7 21.9 %collective-permute-start.27 = (bf16[3,512,256]{2,1,0:T(8,128)(2,1)S(1)}, bf16[3,512,256]{2,1,0:T(8,128)(2,1)S(1)}, u32[]{:S(2)}, u32[]{:S(2)}) collective-permute-start(bf16[3,512,256]{2,1,0:T(8,128)(2,1)S(1)} %get-tuple-element.50), channel_id=1, source_target_pairs={{2,4},{4,2},{3,5},{5,3},{10,12},{12,10},{11,13},{13,11},{18,20},{2... | collective-permute-start | bytes 2359304 | tf_op jit(solution)/shard_map/ppermute | solution.py:35
  72.2 6.5 %collective-permute-start.31 = (bf16[384,128]{1,0:T(8,128)(2,1)S(1)}, bf16[384,128]{1,0:T(8,128)(2,1)S(1)}, u32[]{:S(2)}, u32[]{:S(2)}) collective-permute-start(bf16[384,128]{1,0:T(8,128)(2,1)S(1)} %add_add_fusion), channel_id=1, source_target_pairs={{0,16},{8,24},{16,0},{24,8},{32,48},{40,56},{48,32},{56,40},{64,80... | collective-permute-start | bytes 294920 | tf_op jit(solution)/shard_map/ppermute | solution.py:25
  74.0 7.4 %collective-permute-start.32 = (bf16[384,128]{1,0:T(8,128)(2,1)S(1)}, bf16[384,128]{1,0:T(8,128)(2,1)S(1)}, u32[]{:S(2)}, u32[]{:S(2)}) collective-permute-start(bf16[384,128]{1,0:T(8,128)(2,1)S(1)} %add_add_fusion), channel_id=1, source_target_pairs={{0,24},{8,16},{16,8},{24,0},{32,56},{40,48},{48,40},{56,32},{64,88... | collective-permute-start | bytes 294920 | tf_op jit(solution)/shard_map/ppermute | solution.py:25
  81.6 7.2 %collective-permute-start.34 = (bf16[384,128]{1,0:T(8,128)(2,1)S(1)}, bf16[384,128]{1,0:T(8,128)(2,1)S(1)}, u32[]{:S(2)}, u32[]{:S(2)}) collective-permute-start(bf16[384,128]{1,0:T(8,128)(2,1)S(1)} %add_convert_fusion.1), channel_id=1, source_target_pairs={{0,64},{8,72},{16,80},{24,88},{32,96},{40,104},{48,112},{56,120},{... | collective-permute-start | bytes 294920 | tf_op jit(solution)/shard_map/ppermute | solution.py:25
  84.2 5.9 %collective-permute-start.35 = (bf16[384,128]{1,0:T(8,128)(2,1)S(1)}, bf16[384,128]{1,0:T(8,128)(2,1)S(1)}, u32[]{:S(2)}, u32[]{:S(2)}) collective-permute-start(bf16[384,128]{1,0:T(8,128)(2,1)S(1)} %add_convert_fusion.1), channel_id=1, source_target_pairs={{0,96},{8,104},{16,112},{24,120},{32,64},{40,72},{48,80},{56,88},{... | collective-permute-start | bytes 294920 | tf_op jit(solution)/shard_map/ppermute | solution.py:25
  90.3 10.5 %collective-permute-start.36 = (bf16[384,128]{1,0:T(8,128)(2,1)S(1)}, bf16[384,128]{1,0:T(8,128)(2,1)S(1)}, u32[]{:S(2)}, u32[]{:S(2)}) collective-permute-start(bf16[384,128]{1,0:T(8,128)(2,1)S(1)} %add_convert_fusion.refs_0_), channel_id=1, source_target_pairs={{0,2},{1,3},{2,0},{3,1},{4,6},{5,7},{6,4},{7,5},{8,10},{9,11},{10,... | collective-permute-start | bytes 294920 | tf_op jit(solution)/shard_map/ppermute | solution.py:25
  92.1 22.1 %collective-permute-start.28 = (bf16[512,256]{1,0:T(8,128)(2,1)S(1)}, bf16[512,256]{1,0:T(8,128)(2,1)S(1)}, u32[]{:S(2)}, u32[]{:S(2)}) collective-permute-start(bf16[512,256]{1,0:T(8,128)(2,1)S(1)} %get-tuple-element.58), channel_id=1, source_target_pairs={{0,8},{8,0},{16,24},{24,16},{32,40},{40,32},{48,56},{56,48},{64,72... | collective-permute-start | bytes 786440 | tf_op jit(solution)/shard_map/ppermute | solution.py:35
  92.2 22.0 %collective-permute-start.29 = (bf16[512,256]{1,0:T(8,128)(2,1)S(1)}, bf16[512,256]{1,0:T(8,128)(2,1)S(1)}, u32[]{:S(2)}, u32[]{:S(2)}) collective-permute-start(bf16[512,256]{1,0:T(8,128)(2,1)S(1)} %get-tuple-element.59), channel_id=1, source_target_pairs={{8,16},{16,8},{24,32},{32,24},{40,48},{48,40},{56,64},{64,56},{72,... | collective-permute-start | bytes 786440 | tf_op jit(solution)/shard_map/ppermute | solution.py:35
  97.5 5.6 %collective-permute-start.37 = (bf16[384,128]{1,0:T(8,128)(2,1)S(1)}, bf16[384,128]{1,0:T(8,128)(2,1)S(1)}, u32[]{:S(2)}, u32[]{:S(2)}) collective-permute-start(bf16[384,128]{1,0:T(8,128)(2,1)S(1)} %add_convert_fusion.refs_0_), channel_id=1, source_target_pairs={{0,4},{1,5},{2,6},{3,7},{4,0},{5,1},{6,2},{7,3},{8,12},{9,13},{10,... | collective-permute-start | bytes 294920 | tf_op jit(solution)/shard_map/ppermute | solution.py:25
  99.0 7.4 %collective-permute-start.38 = (bf16[384,128]{1,0:T(8,128)(2,1)S(1)}, bf16[384,128]{1,0:T(8,128)(2,1)S(1)}, u32[]{:S(2)}, u32[]{:S(2)}) collective-permute-start(bf16[384,128]{1,0:T(8,128)(2,1)S(1)} %add_convert_fusion.refs_0_), channel_id=1, source_target_pairs={{0,6},{1,7},{2,4},{3,5},{4,2},{5,3},{6,0},{7,1},{8,14},{9,15},{10,... | collective-permute-start | bytes 294920 | tf_op jit(solution)/shard_map/ppermute | solution.py:25
  100.8 6.8 %collective-permute-start.39 = (bf16[384,128]{1,0:T(8,128)(2,1)S(1)}, bf16[384,128]{1,0:T(8,128)(2,1)S(1)}, u32[]{:S(2)}, u32[]{:S(2)}) collective-permute-start(bf16[384,128]{1,0:T(8,128)(2,1)S(1)} %add_convert_fusion.refs_0_), channel_id=1, source_target_pairs={{0,1},{1,0},{2,3},{3,2},{4,5},{5,4},{6,7},{7,6},{8,9},{9,8},{10,11... | collective-permute-start | bytes 294920 | tf_op jit(solution)/shard_map/ppermute | solution.py:25
  103.1 7.2 %collective-permute-start.40 = (bf16[384,128]{1,0:T(8,128)(2,1)S(1)}, bf16[384,128]{1,0:T(8,128)(2,1)S(1)}, u32[]{:S(2)}, u32[]{:S(2)}) collective-permute-start(bf16[384,128]{1,0:T(8,128)(2,1)S(1)} %collective-permute-done.36.refs_1_), channel_id=1, source_target_pairs={{0,1},{1,0},{2,3},{3,2},{4,5},{5,4},{6,7},{7,6},{8,9},{9,8},{10,11... | collective-permute-start | bytes 294920 | tf_op jit(solution)/shard_map/ppermute | solution.py:25
  (39 other events, 296.7 us)

commit v9 on v8

--- a/solution.py
+++ b/solution.py
@@ -338,18 +338,21 @@
 
 
 def finish_kernel(*refs):
-    shards, (conv, corr, whole) = refs[:8], refs[8:]
+    shards, (conv, corr) = refs[:8], refs[8:]
     size = shards[0].shape[0]
+    blocks = conv.shape[0] // size
     _, chip, core = position()
-    half = whole.shape[0] // 2
     for n, ref in enumerate(shards):
-        owner = core if n < 4 else 1 - core
-        to = owner * half + (chip ^ (n % 4)) * size
-        whole[pl.ds(pl.multiple_of(to, size), size)] = ref[...].astype(F32)
-    conv[...] = whole[: conv.shape[0]]
-    base = conv.shape[0]
-    for h in range(2):
-        corr[:, h * 128 : (h + 1) * 128] = whole[base + h * 384 : base + h * 384 + corr.shape[0]]
+        block = (core if n < 4 else 1 - core) * 4 + (chip ^ (n % 4))
+
+        @pl.when(block < blocks)
+        def _():
+            conv[pl.ds(pl.multiple_of(block * size, size), size)] = ref[...].astype(F32)
+
+        for h in range(2):
+            @pl.when(block == blocks + h)
+            def _():
+                corr[:, h * 128 : (h + 1) * 128] = ref[...].astype(F32)[: corr.shape[0]]
 
 
 def call(kernel, out_shape, in_specs, scratch=(), flops=0):
@@ -469,10 +472,6 @@
         middle += swap_pairs(sent[x - 1], "col", x - 1, 2).astype(F32)
     total = sum_everywhere(sum_everywhere(total, "row", 1), "row", 4).astype(BF16)
     shards = [total] + [swap(total, "col", 2 * s) for s in (1, 2, 3)]
-    shards += [swap(shard, "col", 1) for shard in shards]
-    second_grad = middle[0]
-    for r in (1, 2):
-        second_grad += swap_pairs(middle[r].astype(BF16), "row", r - 1).astype(F32)
     features = call(
         features_kernel,
         shape((cells, out_width), BF16),
@@ -484,11 +483,15 @@
         *around_motion,
         conv_weight.reshape(3, 3 * hidden, out_width),
     )
+    features, *shards = lax.optimization_barrier((features, *shards))
+    shards += [swap(shard, "col", 1) for shard in shards]
+    second_grad = middle[0]
+    for r in (1, 2):
+        second_grad += swap_pairs(middle[r].astype(BF16), "row", r - 1).astype(F32)
     conv_total, corr_total = call(
         finish_kernel,
         (shape((9 * hidden, out_width), F32), shape(corr_weight.shape, F32)),
         [VMEM] * 8,
-        [pltpu.VMEM((total_rows, 128), F32)],
     )(*shards)
     return (
         features.reshape(rows_tile, cols_tile, out_width),

time: 116 us -> 113 us (0.974)
  starting transfers between devices: 64 us -> 60.4 us
  waiting for transfers between devices: 19 us -> 20.3 us
    ppermute x27, starting transfers between devices: 33.3 us -> 29.2 us  [swap(): lax.ppermute(array, axis, [(i, i ^ bits) for i in range(lax.axis_size(axi...]
    ppermute x27, waiting for transfers between devices: 18.2 us -> 19.5 us  [swap(): lax.ppermute(array, axis, [(i, i ^ bits) for i in range(lax.axis_size(axi...]
  transfers between devices with their start and end apart: 43 -> 43, of which waited for: 10 -> 13; matrix products, arithmetic and copies ran while one was open for 1% -> 1% of each run, Pallas kernels for 13% -> 13%
where the time goes in v9:
time: 113 us; the launch traced here: 112 us
  starting transfers between devices  60.4 us (53%)
  Pallas kernels  25.4 us (22%)
  waiting for transfers between devices  20.3 us (18%)
  other arithmetic  2.64 us (2%)
  between operations  2.53 us (2%)
    ppermute x16, starting transfers between devices, swap_pairs(): return lax.ppermute(array, axis, pairs)  31.1 us
    ppermute x27, starting transfers between devices, swap(): lax.ppermute(array, axis, [(i, i ^ bits) for i in range(lax.axis_size(axi...  29.2 us
    ppermute x27, waiting for transfers between devices, swap(): lax.ppermute(array, axis, [(i, i ^ bits) for i in range(lax.axis_size(axi...  19.5 us
    pallas_call x1, Pallas kernels, body(): call(forward_kernel, (shape((slots, cells + 2 * GROUP, channels), BF16),...  8.84 us
    pallas_call x1, Pallas kernels, body(): call(backward_kernel, (shape((cells, channels), F32), *[shape((3, cells,...  7.57 us
    pallas_call x1, Pallas kernels, body(): call(features_kernel, shape((cells, out_width), BF16), [VMEM] * 6, [pltpu...  2.66 us
    pallas_call x1, Pallas kernels, body(): call(finish_kernel, (shape((9 * hidden, out_width), F32), shape(corr_weig...  2.52 us
  transfers between devices with their start and end apart: 43, of which 13 were waited for; matrix products, arithmetic and copies ran while one was open for 1% of the time, Pallas kernels for 13%

profile of v9, /device:TPU:33, one launch (start us, length us, event | category | flops | bytes accessed | tf_op | source)
XLA Modules:
  0.0 112.1 jit_solution(833572446679536492)
XLA Ops:
  0.6 1.8 %shard_map.137.refs_0_ = bf16[560,256]{1,0:T(8,128)(2,1)} custom-call(bf16[512,256]{1,0:T(8,128)(2,1)} %bitcast.25, bf16[512,128]{1,0:T(8,128)(2,1)} %bitcast.26), custom_call_target="tpu_custom_call" | custom-call | tf_op jit(solution)/shard_map/pallas_call | solution.py:391
  3.1 3.7 %collective-permute-start.1 = (bf16[560,256]{1,0:T(8,128)(2,1)}, bf16[560,256]{1,0:T(8,128)(2,1)S(1)}, u32[]{:S(2)}, u32[]{:S(2)}) collective-permute-start(bf16[560,256]{1,0:T(8,128)(2,1)} %shard_map.137.refs_0_), channel_id=1, source_target_pairs={{0,2},{2,0},{1,3},{3,1},{4,6},{6,4},{5,7},{7,5},{8,10},{10,8},{9,1... | collective-permute-start | bytes 860168 | tf_op jit(solution)/shard_map/ppermute | solution.py:35
  6.9 4.2 %collective-permute-start.11 = (bf16[560,256]{1,0:T(8,128)(2,1)}, bf16[560,256]{1,0:T(8,128)(2,1)S(1)}, u32[]{:S(2)}, u32[]{:S(2)}) collective-permute-start(bf16[560,256]{1,0:T(8,128)(2,1)} %shard_map.137.refs_0_), channel_id=1, source_target_pairs={{8,16},{16,8},{24,32},{32,24},{40,48},{48,40},{56,64},{64,56},{72,... | collective-permute-start | bytes 860168 | tf_op jit(solution)/shard_map/ppermute | solution.py:35
  11.4 1.8 %collective-permute-start = (bf16[560,256]{1,0:T(8,128)(2,1)}, bf16[560,256]{1,0:T(8,128)(2,1)S(1)}, u32[]{:S(2)}, u32[]{:S(2)}) collective-permute-start(bf16[560,256]{1,0:T(8,128)(2,1)} %shard_map.137.refs_0_), channel_id=1, source_target_pairs={{0,1},{1,0},{2,3},{3,2},{4,5},{5,4},{6,7},{7,6},{8,9},{9,8},{10,11... | collective-permute-start | bytes 860168 | tf_op jit(solution)/shard_map/ppermute | solution.py:25
  13.3 1.2 %collective-permute-start.9 = (bf16[560,256]{1,0:T(8,128)(2,1)S(1)}, bf16[560,256]{1,0:T(8,128)(2,1)S(1)}, u32[]{:S(2)}, u32[]{:S(2)}) collective-permute-start(bf16[560,256]{1,0:T(8,128)(2,1)S(1)} %collective-permute-done.3.refs_4_), channel_id=1, source_target_pairs={{0,8},{8,0},{16,24},{24,16},{32,40},{40,32},{48,56},{56,48},{64,72... | collective-permute-start | bytes 860168 | tf_op jit(solution)/shard_map/ppermute | solution.py:35
  14.4 3.2 %collective-permute-start.13 = (bf16[560,256]{1,0:T(8,128)(2,1)S(1)}, bf16[560,256]{1,0:T(8,128)(2,1)S(1)}, u32[]{:S(2)}, u32[]{:S(2)}) collective-permute-start(bf16[560,256]{1,0:T(8,128)(2,1)S(1)} %collective-permute-done.1.refs_2_), channel_id=1, source_target_pairs={{8,16},{16,8},{24,32},{32,24},{40,48},{48,40},{56,64},{64,56},{72,... | collective-permute-start | bytes 860168 | tf_op jit(solution)/shard_map/ppermute | solution.py:35
  18.9 2.5 %collective-permute-start.7 = (bf16[560,256]{1,0:T(8,128)(2,1)S(1)}, bf16[560,256]{1,0:T(8,128)(2,1)S(1)}, u32[]{:S(2)}, u32[]{:S(2)}) collective-permute-start(bf16[560,256]{1,0:T(8,128)(2,1)S(1)} %collective-permute-done.5.refs_6_), channel_id=1, source_target_pairs={{0,2},{2,0},{1,3},{3,1},{4,6},{6,4},{5,7},{7,5},{8,10},{10,8},{9,1... | collective-permute-start | bytes 860168 | tf_op jit(solution)/shard_map/ppermute | solution.py:35
  21.4 2.7 %collective-permute-start.12 = (bf16[560,256]{1,0:T(8,128)(2,1)S(1)}, bf16[560,256]{1,0:T(8,128)(2,1)S(1)}, u32[]{:S(2)}, u32[]{:S(2)}) collective-permute-start(bf16[560,256]{1,0:T(8,128)(2,1)S(1)} %collective-permute-done.11.refs_12_), channel_id=1, source_target_pairs={{0,1},{1,0},{2,3},{3,2},{4,5},{5,4},{6,7},{7,6},{8,9},{9,8},{10,11... | collective-permute-start | bytes 860168 | tf_op jit(solution)/shard_map/ppermute | solution.py:25
  24.3 2.4 %collective-permute-start.2 = (bf16[560,256]{1,0:T(8,128)(2,1)S(1)}, bf16[560,256]{1,0:T(8,128)(2,1)S(1)}, u32[]{:S(2)}, u32[]{:S(2)}) collective-permute-start(bf16[560,256]{1,0:T(8,128)(2,1)S(1)} %collective-permute-done.1.refs_2_), channel_id=1, source_target_pairs={{0,1},{1,0},{2,3},{3,2},{4,5},{5,4},{6,7},{7,6},{8,9},{9,8},{10,11... | collective-permute-start | bytes 860168 | tf_op jit(solution)/shard_map/ppermute | solution.py:25
  27.8 1.5 %collective-permute-start.10 = (bf16[560,256]{1,0:T(8,128)(2,1)S(1)}, bf16[560,256]{1,0:T(8,128)(2,1)}, u32[]{:S(2)}, u32[]{:S(2)}) collective-permute-start(bf16[560,256]{1,0:T(8,128)(2,1)S(1)} %collective-permute-done.9.refs_10_), channel_id=1, source_target_pairs={{0,1},{1,0},{2,3},{3,2},{4,5},{5,4},{6,7},{7,6},{8,9},{9,8},{10,11... | collective-permute-start | bytes 860168 | tf_op jit(solution)/shard_map/ppermute | solution.py:25
  29.9 2.0 %shard_map.136 = (bf16[512,256]{1,0:T(8,128)(2,1)}, bf16[512,256]{1,0:T(8,128)(2,1)}) custom-call(bf16[324,256]{1,0:T(8,128)(2,1)} %weight.1), custom_call_target="tpu_custom_call" | custom-call | tf_op jit(solution)/shard_map/pallas_call | solution.py:405
  33.4 8.8 %shard_map.138 = (bf16[4,768,256]{2,1,0:T(8,128)(2,1)}, bf16[512,256]{1,0:T(8,128)(2,1)}, bf16[512,256]{1,0:T(8,128)(2,1)}, bf16[32,256]{1,0:T(8,128)(2,1)}, bf1...) custom-call(s32[1,1,4]{2,1,0:T(1,128)} %partners.3, ...), custom_call_target="tpu_custom_call" | custom-call | flops 3000000000 | bytes 10000000 | tf_op jit(solution)/shard_map/pallas_call | solution.py:412
  42.2 4.0 %collective-permute-start.22 = (bf16[32,256]{1,0:T(8,128)(2,1)}, bf16[32,256]{1,0:T(8,128)(2,1)S(1)}, u32[]{:S(2)}, u32[]{:S(2)}) collective-permute-start(bf16[32,256]{1,0:T(8,128)(2,1)} %get-tuple-element.45), channel_id=1, source_target_pairs={{8,16},{16,8},{24,32},{32,24},{40,48},{48,40},{56,64},{64,56},{72,... | collective-permute-start | bytes 49160 | tf_op jit(solution)/shard_map/ppermute | solution.py:35
  46.5 7.6 %shard_map.139 = (f32[512,256]{1,0:T(8,128)}, bf16[3,512,256]{2,1,0:T(8,128)(2,1)}, bf16[3,512,256]{2,1,0:T(8,128)(2,1)}, bf16[3,512,256]{2,1,0:T(8,128)(2,1)}, bf16[6,512,256]{2,1,0:T(8,128)(2,1)}) custom-call(s32[1,1,4]{2,1,0:T(1,128)} %partners.3, s32[1,1]{1,0:T(1,128)S(6)} %copy.15.counts, s32[1,1]{1,0:T(1,128)S(6)} %copy.16.radius, ...), custom_call_target="tpu_custom_call" | custom-call | flops 3000000000 | bytes 10000000 | tf_op jit(solution)/shard_map/pallas_call | solution.py:449
  55.0 3.7 %collective-permute-start.24 = (bf16[18,256]{1,0:T(8,128)(2,1)S(1)}, bf16[18,256]{1,0:T(8,128)(2,1)S(1)}, u32[]{:S(2)}, u32[]{:S(2)}) collective-permute-start(bf16[18,256]{1,0:T(8,128)(2,1)S(1)} %get-tuple-element.78), channel_id=1, source_target_pairs={{1,2},{2,1},{3,4},{4,3},{5,6},{6,5},{9,10},{10,9},{11,12},{12,11},... | collective-permute-start | bytes 27656 | tf_op jit(solution)/shard_map/ppermute | solution.py:35
  60.0 1.7 %collective-permute-start.19 = (bf16[384,128]{1,0:T(8,128)(2,1)S(1)}, bf16[384,128]{1,0:T(8,128)(2,1)S(1)}, u32[]{:S(2)}, u32[]{:S(2)}) collective-permute-start(bf16[384,128]{1,0:T(8,128)(2,1)S(1)} %get-tuple-element.72), channel_id=1, source_target_pairs={{0,4},{1,5},{2,6},{3,7},{4,0},{5,1},{6,2},{7,3},{8,12},{9,13},{10,... | collective-permute-start | bytes 294920 | tf_op jit(solution)/shard_map/ppermute | solution.py:25
  61.6 1.3 %collective-permute-start.20 = (bf16[384,128]{1,0:T(8,128)(2,1)S(1)}, bf16[384,128]{1,0:T(8,128)(2,1)S(1)}, u32[]{:S(2)}, u32[]{:S(2)}) collective-permute-start(bf16[384,128]{1,0:T(8,128)(2,1)S(1)} %get-tuple-element.71), channel_id=1, source_target_pairs={{0,6},{1,7},{2,4},{3,5},{4,2},{5,3},{6,0},{7,1},{8,14},{9,15},{10,... | collective-permute-start | bytes 294920 | tf_op jit(solution)/shard_map/ppermute | solution.py:25
  63.5 3.1 %collective-permute-done.19 = bf16[384,128]{1,0:T(8,128)(2,1)S(1)} collective-permute-done((bf16[384,128]{1,0:T(8,128)(2,1)S(1)}, bf16[384,128]{1,0:T(8,128)(2,1)S(1)}, u32[]{:S(2)}, u32[]{:S(2)}) %collective-permute-start.19) | collective-permute-done | bytes 98336 | tf_op jit(solution)/shard_map/ppermute | solution.py:25
  66.7 2.4 %collective-permute-done.20 = bf16[384,128]{1,0:T(8,128)(2,1)S(1)} collective-permute-done((bf16[384,128]{1,0:T(8,128)(2,1)S(1)}, bf16[384,128]{1,0:T(8,128)(2,1)S(1)}, u32[]{:S(2)}, u32[]{:S(2)}) %collective-permute-start.20) | collective-permute-done | bytes 98336 | tf_op jit(solution)/shard_map/ppermute | solution.py:25
  70.5 1.8 %collective-permute-start.26 = (bf16[384,128]{1,0:T(8,128)(2,1)S(1)}, bf16[384,128]{1,0:T(8,128)(2,1)S(1)}, u32[]{:S(2)}, u32[]{:S(2)}) collective-permute-start(bf16[384,128]{1,0:T(8,128)(2,1)S(1)} %add_add_fusion), channel_id=1, source_target_pairs={{0,8},{8,0},{16,24},{24,16},{32,40},{40,32},{48,56},{56,48},{64,72... | collective-permute-start | bytes 294920 | tf_op jit(solution)/shard_map/ppermute | solution.py:25
  72.3 1.7 %collective-permute-start.27 = (bf16[384,128]{1,0:T(8,128)(2,1)S(1)}, bf16[384,128]{1,0:T(8,128)(2,1)S(1)}, u32[]{:S(2)}, u32[]{:S(2)}) collective-permute-start(bf16[384,128]{1,0:T(8,128)(2,1)S(1)} %add_add_fusion), channel_id=1, source_target_pairs={{0,16},{8,24},{16,0},{24,8},{32,48},{40,56},{48,32},{56,40},{64,80... | collective-permute-start | bytes 294920 | tf_op jit(solution)/shard_map/ppermute | solution.py:25
  74.9 3.7 %collective-permute-done.27 = bf16[384,128]{1,0:T(8,128)(2,1)S(1)} collective-permute-done((bf16[384,128]{1,0:T(8,128)(2,1)S(1)}, bf16[384,128]{1,0:T(8,128)(2,1)S(1)}, u32[]{:S(2)}, u32[]{:S(2)}) %collective-permute-start.27) | collective-permute-done | bytes 98336 | tf_op jit(solution)/shard_map/ppermute | solution.py:25
  78.6 2.7 %collective-permute-done.28 = bf16[384,128]{1,0:T(8,128)(2,1)S(1)} collective-permute-done((bf16[384,128]{1,0:T(8,128)(2,1)S(1)}, bf16[384,128]{1,0:T(8,128)(2,1)S(1)}, u32[]{:S(2)}, u32[]{:S(2)}) %collective-permute-start.28) | collective-permute-done | bytes 98336 | tf_op jit(solution)/shard_map/ppermute | solution.py:25
  81.5 2.9 %collective-permute-start.30 = (bf16[384,128]{1,0:T(8,128)(2,1)S(1)}, bf16[384,128]{1,0:T(8,128)(2,1)S(1)}, u32[]{:S(2)}, u32[]{:S(2)}) collective-permute-start(bf16[384,128]{1,0:T(8,128)(2,1)S(1)} %add_convert_fusion.1), channel_id=1, source_target_pairs={{0,64},{8,72},{16,80},{24,88},{32,96},{40,104},{48,112},{56,120},{... | collective-permute-start | bytes 294920 | tf_op jit(solution)/shard_map/ppermute | solution.py:25
  85.3 3.6 %collective-permute-done.30 = bf16[384,128]{1,0:T(8,128)(2,1)S(1)} collective-permute-done((bf16[384,128]{1,0:T(8,128)(2,1)S(1)}, bf16[384,128]{1,0:T(8,128)(2,1)S(1)}, u32[]{:S(2)}, u32[]{:S(2)}) %collective-permute-start.30) | collective-permute-done | bytes 98336 | tf_op jit(solution)/shard_map/ppermute | solution.py:25
  88.9 1.4 %collective-permute-done.31 = bf16[384,128]{1,0:T(8,128)(2,1)S(1)} collective-permute-done((bf16[384,128]{1,0:T(8,128)(2,1)S(1)}, bf16[384,128]{1,0:T(8,128)(2,1)S(1)}, u32[]{:S(2)}, u32[]{:S(2)}) %collective-permute-start.31) | collective-permute-done | bytes 98336 | tf_op jit(solution)/shard_map/ppermute | solution.py:25
  91.5 1.4 %collective-permute-start.33 = (bf16[384,128]{1,0:T(8,128)(2,1)S(1)}, bf16[384,128]{1,0:T(8,128)(2,1)S(1)}, u32[]{:S(2)}, u32[]{:S(2)}) collective-permute-start(bf16[384,128]{1,0:T(8,128)(2,1)S(1)} %add_convert_fusion.refs_0_), channel_id=1, source_target_pairs={{0,4},{1,5},{2,6},{3,7},{4,0},{5,1},{6,2},{7,3},{8,12},{9,13},{10,... | collective-permute-start | bytes 294920 | tf_op jit(solution)/shard_map/ppermute | solution.py:25
  92.9 1.4 %collective-permute-start.34 = (bf16[384,128]{1,0:T(8,128)(2,1)S(1)}, bf16[384,128]{1,0:T(8,128)(2,1)S(1)}, u32[]{:S(2)}, u32[]{:S(2)}) collective-permute-start(bf16[384,128]{1,0:T(8,128)(2,1)S(1)} %add_convert_fusion.refs_0_), channel_id=1, source_target_pairs={{0,6},{1,7},{2,4},{3,5},{4,2},{5,3},{6,0},{7,1},{8,14},{9,15},{10,... | collective-permute-start | bytes 294920 | tf_op jit(solution)/shard_map/ppermute | solution.py:25
  94.9 5.7 %collective-permute-start.38 = (bf16[512,256]{1,0:T(8,128)(2,1)S(1)}, bf16[512,256]{1,0:T(8,128)(2,1)S(1)}, u32[]{:S(2)}, u32[]{:S(2)}) collective-permute-start(bf16[512,256]{1,0:T(8,128)(2,1)S(1)} %get-tuple-element.69), channel_id=1, source_target_pairs={{8,16},{16,8},{24,32},{32,24},{40,48},{48,40},{56,64},{64,56},{72,... | collective-permute-start | bytes 786440 | tf_op jit(solution)/shard_map/ppermute | solution.py:35
  100.6 2.7 %shard_map.140 = bf16[512,128]{1,0:T(8,128)(2,1)} custom-call(bf16[512,256]{1,0:T(8,128)(2,1)} %get-tuple-element.36.motion, bf16[32,256]{1,0:T(8,128)(2,1)} %copy-done.13, bf16[32,256]{1,0:T(8,128)(2,1)} %copy-done.12, bf16[18,256]{1,0:T(8,128)(2,1)} %get-tuple-element.50.west, bf16[18,256]{1,0:T(8,128)(2,1)} %get-tuple-element.51.east, ...), custom_call_target="tpu_custom_call" | custom-call | flops 1000000000 | bytes 3333333 | tf_op jit(solution)/shard_map/pallas_call | solution.py:475
  103.4 2.4 %collective-permute-start.39 = (bf16[384,128]{1,0:T(8,128)(2,1)S(1)}, bf16[384,128]{1,0:T(8,128)(2,1)S(1)}, u32[]{:S(2)}, u32[]{:S(2)}) collective-permute-start(bf16[384,128]{1,0:T(8,128)(2,1)S(1)} %add_convert_fusion.refs_0_), channel_id=1, source_target_pairs={{0,1},{1,0},{2,3},{3,2},{4,5},{5,4},{6,7},{7,6},{8,9},{9,8},{10,11... | collective-permute-start | bytes 294920 | tf_op jit(solution)/shard_map/ppermute | solution.py:25
  108.7 2.5 %shard_map.141 = (f32[2304,128]{1,0:T(8,128)}, f32[324,256]{1,0:T(8,128)}) custom-call(bf16[384,128]{1,0:T(8,128)(2,1)} %copy-done.4, bf16[384,128]{1,0:T(8,128)(2,1)} %copy-done.5, bf16[384,128]{1,0:T(8,128)(2,1)} %copy-done.6, bf16[384,128]{1,0:T(8,128)(2,1)} %copy-done.7, bf16[384,128]{1,0:T(8,128)(2,1)} %copy-done.8, bf16[384,128]{1,0:T(8,128)(2,1)} %copy-done.9, ...), custom_call_target="tpu_custom_call" | custom-call | tf_op jit(solution)/shard_map/pallas_call | solution.py:491
  (130 shorter events, 16.1 us)
Async XLA Ops:
  2.5 10.8 %collective-permute-start.3 = (bf16[560,256]{1,0:T(8,128)(2,1)}, bf16[560,256]{1,0:T(8,128)(2,1)S(1)}, u32[]{:S(2)}, u32[]{:S(2)}) collective-permute-start(bf16[560,256]{1,0:T(8,128)(2,1)} %shard_map.137.refs_0_), channel_id=1, source_target_pairs={{2,4},{4,2},{3,5},{5,3},{10,12},{12,10},{11,13},{13,11},{18,20},{2... | collective-permute-start | bytes 860168 | tf_op jit(solution)/shard_map/ppermute | solution.py:35
  3.1 11.3 %collective-permute-start.1 = (bf16[560,256]{1,0:T(8,128)(2,1)}, bf16[560,256]{1,0:T(8,128)(2,1)S(1)}, u32[]{:S(2)}, u32[]{:S(2)}) collective-permute-start(bf16[560,256]{1,0:T(8,128)(2,1)} %shard_map.137.refs_0_), channel_id=1, source_target_pairs={{0,2},{2,0},{1,3},{3,1},{4,6},{6,4},{5,7},{7,5},{8,10},{10,8},{9,1... | collective-permute-start | bytes 860168 | tf_op jit(solution)/shard_map/ppermute | solution.py:35
  6.9 11.3 %collective-permute-start.11 = (bf16[560,256]{1,0:T(8,128)(2,1)}, bf16[560,256]{1,0:T(8,128)(2,1)S(1)}, u32[]{:S(2)}, u32[]{:S(2)}) collective-permute-start(bf16[560,256]{1,0:T(8,128)(2,1)} %shard_map.137.refs_0_), channel_id=1, source_target_pairs={{8,16},{16,8},{24,32},{32,24},{40,48},{48,40},{56,64},{64,56},{72,... | collective-permute-start | bytes 860168 | tf_op jit(solution)/shard_map/ppermute | solution.py:35
  11.1 7.8 %collective-permute-start.5 = (bf16[560,256]{1,0:T(8,128)(2,1)}, bf16[560,256]{1,0:T(8,128)(2,1)S(1)}, u32[]{:S(2)}, u32[]{:S(2)}) collective-permute-start(bf16[560,256]{1,0:T(8,128)(2,1)} %shard_map.137.refs_0_), channel_id=1, source_target_pairs={{0,8},{8,0},{16,24},{24,16},{32,40},{40,32},{48,56},{56,48},{64,72... | collective-permute-start | bytes 860168 | tf_op jit(solution)/shard_map/ppermute | solution.py:35
  11.4 9.9 %collective-permute-start = (bf16[560,256]{1,0:T(8,128)(2,1)}, bf16[560,256]{1,0:T(8,128)(2,1)S(1)}, u32[]{:S(2)}, u32[]{:S(2)}) collective-permute-start(bf16[560,256]{1,0:T(8,128)(2,1)} %shard_map.137.refs_0_), channel_id=1, source_target_pairs={{0,1},{1,0},{2,3},{3,2},{4,5},{5,4},{6,7},{7,6},{8,9},{9,8},{10,11... | collective-permute-start | bytes 860168 | tf_op jit(solution)/shard_map/ppermute | solution.py:25
  13.3 11.0 %collective-permute-start.9 = (bf16[560,256]{1,0:T(8,128)(2,1)S(1)}, bf16[560,256]{1,0:T(8,128)(2,1)S(1)}, u32[]{:S(2)}, u32[]{:S(2)}) collective-permute-start(bf16[560,256]{1,0:T(8,128)(2,1)S(1)} %collective-permute-done.3.refs_4_), channel_id=1, source_target_pairs={{0,8},{8,0},{16,24},{24,16},{32,40},{40,32},{48,56},{56,48},{64,72... | collective-permute-start | bytes 860168 | tf_op jit(solution)/shard_map/ppermute | solution.py:35
  14.4 12.3 %collective-permute-start.13 = (bf16[560,256]{1,0:T(8,128)(2,1)S(1)}, bf16[560,256]{1,0:T(8,128)(2,1)S(1)}, u32[]{:S(2)}, u32[]{:S(2)}) collective-permute-start(bf16[560,256]{1,0:T(8,128)(2,1)S(1)} %collective-permute-done.1.refs_2_), channel_id=1, source_target_pairs={{8,16},{16,8},{24,32},{32,24},{40,48},{48,40},{56,64},{64,56},{72,... | collective-permute-start | bytes 860168 | tf_op jit(solution)/shard_map/ppermute | solution.py:35
  18.2 9.5 %collective-permute-start.15 = (bf16[560,256]{1,0:T(8,128)(2,1)S(1)}, bf16[560,256]{1,0:T(8,128)(2,1)S(1)}, u32[]{:S(2)}, u32[]{:S(2)}) collective-permute-start(bf16[560,256]{1,0:T(8,128)(2,1)S(1)} %collective-permute-done.11.refs_12_), channel_id=1, source_target_pairs={{2,4},{4,2},{3,5},{5,3},{10,12},{12,10},{11,13},{13,11},{18,20},{2... | collective-permute-start | bytes 860168 | tf_op jit(solution)/shard_map/ppermute | solution.py:35
  18.9 8.9 %collective-permute-start.7 = (bf16[560,256]{1,0:T(8,128)(2,1)S(1)}, bf16[560,256]{1,0:T(8,128)(2,1)S(1)}, u32[]{:S(2)}, u32[]{:S(2)}) collective-permute-start(bf16[560,256]{1,0:T(8,128)(2,1)S(1)} %collective-permute-done.5.refs_6_), channel_id=1, source_target_pairs={{0,2},{2,0},{1,3},{3,1},{4,6},{6,4},{5,7},{7,5},{8,10},{10,8},{9,1... | collective-permute-start | bytes 860168 | tf_op jit(solution)/shard_map/ppermute | solution.py:35
  21.4 7.9 %collective-permute-start.12 = (bf16[560,256]{1,0:T(8,128)(2,1)S(1)}, bf16[560,256]{1,0:T(8,128)(2,1)S(1)}, u32[]{:S(2)}, u32[]{:S(2)}) collective-permute-start(bf16[560,256]{1,0:T(8,128)(2,1)S(1)} %collective-permute-done.11.refs_12_), channel_id=1, source_target_pairs={{0,1},{1,0},{2,3},{3,2},{4,5},{5,4},{6,7},{7,6},{8,9},{9,8},{10,11... | collective-permute-start | bytes 860168 | tf_op jit(solution)/shard_map/ppermute | solution.py:25
  24.3 5.1 %collective-permute-start.2 = (bf16[560,256]{1,0:T(8,128)(2,1)S(1)}, bf16[560,256]{1,0:T(8,128)(2,1)S(1)}, u32[]{:S(2)}, u32[]{:S(2)}) collective-permute-start(bf16[560,256]{1,0:T(8,128)(2,1)S(1)} %collective-permute-done.1.refs_2_), channel_id=1, source_target_pairs={{0,1},{1,0},{2,3},{3,2},{4,5},{5,4},{6,7},{7,6},{8,9},{9,8},{10,11... | collective-permute-start | bytes 860168 | tf_op jit(solution)/shard_map/ppermute | solution.py:25
  27.7 5.5 %collective-permute-start.6 = (bf16[560,256]{1,0:T(8,128)(2,1)S(1)}, bf16[560,256]{1,0:T(8,128)(2,1)}, u32[]{:S(2)}, u32[]{:S(2)}) collective-permute-start(bf16[560,256]{1,0:T(8,128)(2,1)S(1)} %collective-permute-done.5.refs_6_), channel_id=1, source_target_pairs={{0,1},{1,0},{2,3},{3,2},{4,5},{5,4},{6,7},{7,6},{8,9},{9,8},{10,11... | collective-permute-start | bytes 860168 | tf_op jit(solution)/shard_map/ppermute | solution.py:25
  27.8 5.5 %collective-permute-start.10 = (bf16[560,256]{1,0:T(8,128)(2,1)S(1)}, bf16[560,256]{1,0:T(8,128)(2,1)}, u32[]{:S(2)}, u32[]{:S(2)}) collective-permute-start(bf16[560,256]{1,0:T(8,128)(2,1)S(1)} %collective-permute-done.9.refs_10_), channel_id=1, source_target_pairs={{0,1},{1,0},{2,3},{3,2},{4,5},{5,4},{6,7},{7,6},{8,9},{9,8},{10,11... | collective-permute-start | bytes 860168 | tf_op jit(solution)/shard_map/ppermute | solution.py:25
  42.2 12.7 %collective-permute-start.22 = (bf16[32,256]{1,0:T(8,128)(2,1)}, bf16[32,256]{1,0:T(8,128)(2,1)S(1)}, u32[]{:S(2)}, u32[]{:S(2)}) collective-permute-start(bf16[32,256]{1,0:T(8,128)(2,1)} %get-tuple-element.45), channel_id=1, source_target_pairs={{8,16},{16,8},{24,32},{32,24},{40,48},{48,40},{56,64},{64,56},{72,... | collective-permute-start | bytes 49160 | tf_op jit(solution)/shard_map/ppermute | solution.py:35
  46.2 8.7 %collective-permute-start.23 = (bf16[32,256]{1,0:T(8,128)(2,1)}, bf16[32,256]{1,0:T(8,128)(2,1)S(1)}, u32[]{:S(2)}, u32[]{:S(2)}) collective-permute-start(bf16[32,256]{1,0:T(8,128)(2,1)} %get-tuple-element.46), channel_id=1, source_target_pairs={{0,8},{8,0},{16,24},{24,16},{32,40},{40,32},{48,56},{56,48},{64,72... | collective-permute-start | bytes 49160 | tf_op jit(solution)/shard_map/ppermute | solution.py:35
  54.1 15.1 %collective-permute-start.21 = (bf16[6,512,256]{2,1,0:T(8,128)(2,1)}, bf16[6,512,256]{2,1,0:T(8,128)(2,1)S(1)}, u32[]{:S(2)}, u32[]{:S(2)}) collective-permute-start(bf16[6,512,256]{2,1,0:T(8,128)(2,1)} %get-tuple-element.43), channel_id=1, source_target_pairs={{0,1},{1,0},{2,3},{3,2},{4,5},{5,4},{6,7},{7,6},{8,9},{9,8},{10,11... | collective-permute-start | bytes 4718600 | tf_op jit(solution)/shard_map/ppermute | solution.py:25
  55.0 6.6 %collective-permute-start.24 = (bf16[18,256]{1,0:T(8,128)(2,1)S(1)}, bf16[18,256]{1,0:T(8,128)(2,1)S(1)}, u32[]{:S(2)}, u32[]{:S(2)}) collective-permute-start(bf16[18,256]{1,0:T(8,128)(2,1)S(1)} %get-tuple-element.78), channel_id=1, source_target_pairs={{1,2},{2,1},{3,4},{4,3},{5,6},{6,5},{9,10},{10,9},{11,12},{12,11},... | collective-permute-start | bytes 27656 | tf_op jit(solution)/shard_map/ppermute | solution.py:35
  59.0 4.6 %collective-permute-start.18 = (bf16[384,128]{1,0:T(8,128)(2,1)S(1)}, bf16[384,128]{1,0:T(8,128)(2,1)S(1)}, u32[]{:S(2)}, u32[]{:S(2)}) collective-permute-start(bf16[384,128]{1,0:T(8,128)(2,1)S(1)} %get-tuple-element.70), channel_id=1, source_target_pairs={{0,2},{1,3},{2,0},{3,1},{4,6},{5,7},{6,4},{7,5},{8,10},{9,11},{10,... | collective-permute-start | bytes 294920 | tf_op jit(solution)/shard_map/ppermute | solution.py:25
  60.0 6.7 %collective-permute-start.19 = (bf16[384,128]{1,0:T(8,128)(2,1)S(1)}, bf16[384,128]{1,0:T(8,128)(2,1)S(1)}, u32[]{:S(2)}, u32[]{:S(2)}) collective-permute-start(bf16[384,128]{1,0:T(8,128)(2,1)S(1)} %get-tuple-element.72), channel_id=1, source_target_pairs={{0,4},{1,5},{2,6},{3,7},{4,0},{5,1},{6,2},{7,3},{8,12},{9,13},{10,... | collective-permute-start | bytes 294920 | tf_op jit(solution)/shard_map/ppermute | solution.py:25
  61.6 7.5 %collective-permute-start.20 = (bf16[384,128]{1,0:T(8,128)(2,1)S(1)}, bf16[384,128]{1,0:T(8,128)(2,1)S(1)}, u32[]{:S(2)}, u32[]{:S(2)}) collective-permute-start(bf16[384,128]{1,0:T(8,128)(2,1)S(1)} %get-tuple-element.71), channel_id=1, source_target_pairs={{0,6},{1,7},{2,4},{3,5},{4,2},{5,3},{6,0},{7,1},{8,14},{9,15},{10,... | collective-permute-start | bytes 294920 | tf_op jit(solution)/shard_map/ppermute | solution.py:25
  69.7 24.6 %collective-permute-start.35 = (bf16[3,512,256]{2,1,0:T(8,128)(2,1)S(1)}, bf16[3,512,256]{2,1,0:T(8,128)(2,1)S(1)}, u32[]{:S(2)}, u32[]{:S(2)}) collective-permute-start(bf16[3,512,256]{2,1,0:T(8,128)(2,1)S(1)} %get-tuple-element.56), channel_id=1, source_target_pairs={{0,2},{2,0},{1,3},{3,1},{4,6},{6,4},{5,7},{7,5},{8,10},{10,8},{9,1... | collective-permute-start | bytes 2359304 | tf_op jit(solution)/shard_map/ppermute | solution.py:35
  69.8 24.5 %collective-permute-start.36 = (bf16[3,512,256]{2,1,0:T(8,128)(2,1)S(1)}, bf16[3,512,256]{2,1,0:T(8,128)(2,1)S(1)}, u32[]{:S(2)}, u32[]{:S(2)}) collective-permute-start(bf16[3,512,256]{2,1,0:T(8,128)(2,1)S(1)} %get-tuple-element.57), channel_id=1, source_target_pairs={{2,4},{4,2},{3,5},{5,3},{10,12},{12,10},{11,13},{13,11},{18,20},{2... | collective-permute-start | bytes 2359304 | tf_op jit(solution)/shard_map/ppermute | solution.py:35
  70.5 4.4 %collective-permute-start.26 = (bf16[384,128]{1,0:T(8,128)(2,1)S(1)}, bf16[384,128]{1,0:T(8,128)(2,1)S(1)}, u32[]{:S(2)}, u32[]{:S(2)}) collective-permute-start(bf16[384,128]{1,0:T(8,128)(2,1)S(1)} %add_add_fusion), channel_id=1, source_target_pairs={{0,8},{8,0},{16,24},{24,16},{32,40},{40,32},{48,56},{56,48},{64,72... | collective-permute-start | bytes 294920 | tf_op jit(solution)/shard_map/ppermute | solution.py:25
  72.3 6.4 %collective-permute-start.27 = (bf16[384,128]{1,0:T(8,128)(2,1)S(1)}, bf16[384,128]{1,0:T(8,128)(2,1)S(1)}, u32[]{:S(2)}, u32[]{:S(2)}) collective-permute-start(bf16[384,128]{1,0:T(8,128)(2,1)S(1)} %add_add_fusion), channel_id=1, source_target_pairs={{0,16},{8,24},{16,0},{24,8},{32,48},{40,56},{48,32},{56,40},{64,80... | collective-permute-start | bytes 294920 | tf_op jit(solution)/shard_map/ppermute | solution.py:25
  73.9 7.4 %collective-permute-start.28 = (bf16[384,128]{1,0:T(8,128)(2,1)S(1)}, bf16[384,128]{1,0:T(8,128)(2,1)S(1)}, u32[]{:S(2)}, u32[]{:S(2)}) collective-permute-start(bf16[384,128]{1,0:T(8,128)(2,1)S(1)} %add_add_fusion), channel_id=1, source_target_pairs={{0,24},{8,16},{16,8},{24,0},{32,56},{40,48},{48,40},{56,32},{64,88... | collective-permute-start | bytes 294920 | tf_op jit(solution)/shard_map/ppermute | solution.py:25
  81.5 7.4 %collective-permute-start.30 = (bf16[384,128]{1,0:T(8,128)(2,1)S(1)}, bf16[384,128]{1,0:T(8,128)(2,1)S(1)}, u32[]{:S(2)}, u32[]{:S(2)}) collective-permute-start(bf16[384,128]{1,0:T(8,128)(2,1)S(1)} %add_convert_fusion.1), channel_id=1, source_target_pairs={{0,64},{8,72},{16,80},{24,88},{32,96},{40,104},{48,112},{56,120},{... | collective-permute-start | bytes 294920 | tf_op jit(solution)/shard_map/ppermute | solution.py:25
  84.4 5.9 %collective-permute-start.31 = (bf16[384,128]{1,0:T(8,128)(2,1)S(1)}, bf16[384,128]{1,0:T(8,128)(2,1)S(1)}, u32[]{:S(2)}, u32[]{:S(2)}) collective-permute-start(bf16[384,128]{1,0:T(8,128)(2,1)S(1)} %add_convert_fusion.1), channel_id=1, source_target_pairs={{0,96},{8,104},{16,112},{24,120},{32,64},{40,72},{48,80},{56,88},{... | collective-permute-start | bytes 294920 | tf_op jit(solution)/shard_map/ppermute | solution.py:25
  90.4 12.9 %collective-permute-start.32 = (bf16[384,128]{1,0:T(8,128)(2,1)S(1)}, bf16[384,128]{1,0:T(8,128)(2,1)S(1)}, u32[]{:S(2)}, u32[]{:S(2)}) collective-permute-start(bf16[384,128]{1,0:T(8,128)(2,1)S(1)} %add_convert_fusion.refs_0_), channel_id=1, source_target_pairs={{0,2},{1,3},{2,0},{3,1},{4,6},{5,7},{6,4},{7,5},{8,10},{9,11},{10,... | collective-permute-start | bytes 294920 | tf_op jit(solution)/shard_map/ppermute | solution.py:25
  91.5 11.8 %collective-permute-start.33 = (bf16[384,128]{1,0:T(8,128)(2,1)S(1)}, bf16[384,128]{1,0:T(8,128)(2,1)S(1)}, u32[]{:S(2)}, u32[]{:S(2)}) collective-permute-start(bf16[384,128]{1,0:T(8,128)(2,1)S(1)} %add_convert_fusion.refs_0_), channel_id=1, source_target_pairs={{0,4},{1,5},{2,6},{3,7},{4,0},{5,1},{6,2},{7,3},{8,12},{9,13},{10,... | collective-permute-start | bytes 294920 | tf_op jit(solution)/shard_map/ppermute | solution.py:25
  92.9 10.5 %collective-permute-start.34 = (bf16[384,128]{1,0:T(8,128)(2,1)S(1)}, bf16[384,128]{1,0:T(8,128)(2,1)S(1)}, u32[]{:S(2)}, u32[]{:S(2)}) collective-permute-start(bf16[384,128]{1,0:T(8,128)(2,1)S(1)} %add_convert_fusion.refs_0_), channel_id=1, source_target_pairs={{0,6},{1,7},{2,4},{3,5},{4,2},{5,3},{6,0},{7,1},{8,14},{9,15},{10,... | collective-permute-start | bytes 294920 | tf_op jit(solution)/shard_map/ppermute | solution.py:25
  94.8 16.4 %collective-permute-start.37 = (bf16[512,256]{1,0:T(8,128)(2,1)S(1)}, bf16[512,256]{1,0:T(8,128)(2,1)S(1)}, u32[]{:S(2)}, u32[]{:S(2)}) collective-permute-start(bf16[512,256]{1,0:T(8,128)(2,1)S(1)} %get-tuple-element.68), channel_id=1, source_target_pairs={{0,8},{8,0},{16,24},{24,16},{32,40},{40,32},{48,56},{56,48},{64,72... | collective-permute-start | bytes 786440 | tf_op jit(solution)/shard_map/ppermute | solution.py:35
  94.9 16.3 %collective-permute-start.38 = (bf16[512,256]{1,0:T(8,128)(2,1)S(1)}, bf16[512,256]{1,0:T(8,128)(2,1)S(1)}, u32[]{:S(2)}, u32[]{:S(2)}) collective-permute-start(bf16[512,256]{1,0:T(8,128)(2,1)S(1)} %get-tuple-element.69), channel_id=1, source_target_pairs={{8,16},{16,8},{24,32},{32,24},{40,48},{48,40},{56,64},{64,56},{72,... | collective-permute-start | bytes 786440 | tf_op jit(solution)/shard_map/ppermute | solution.py:35
  (39 other events, 285.9 us)

commit v10 on v9

--- a/solution.py
+++ b/solution.py
@@ -465,7 +465,7 @@
     ]
     total = (pieces[0] + got[0].astype(F32)) + (got[1].astype(F32) + got[2].astype(F32))
     around_motion = rim(facing, away, ends, row_even, col_even)
-    total, *ready = lax.optimization_barrier((total, *sent, *around_motion))
+    ready = lax.optimization_barrier((*sent, *around_motion))
     sent, around_motion = ready[:2], ready[2:]
     middle = kept[0].astype(F32) + lent[:3].astype(F32)
     for x in (1, 2):

time: 113 us -> 114 us (level)
  other arithmetic: 2.64 us -> 3.92 us
    ppermute x16, waiting for transfers between devices: 0.82 us -> 2.64 us  [swap_pairs(): return lax.ppermute(array, axis, pairs)]
  transfers between devices with their start and end apart: 43 -> 43, of which waited for: 13 -> 14; matrix products, arithmetic and copies ran while one was open for 1% -> 3% of each run, Pallas kernels for 13% -> 13%
where the time goes in v10:
time: 114 us
  starting transfers between devices  59.7 us (52%)
  Pallas kernels  25.4 us (22%)
  waiting for transfers between devices  21.2 us (19%)
  other arithmetic  3.92 us (3%)
  between operations  2.54 us (2%)
    ppermute x16, starting transfers between devices, swap_pairs(): return lax.ppermute(array, axis, pairs)  30.9 us
    ppermute x27, starting transfers between devices, swap(): lax.ppermute(array, axis, [(i, i ^ bits) for i in range(lax.axis_size(axi...  28.8 us
    ppermute x27, waiting for transfers between devices, swap(): lax.ppermute(array, axis, [(i, i ^ bits) for i in range(lax.axis_size(axi...  18.6 us
    pallas_call x1, Pallas kernels, body(): call(forward_kernel, (shape((slots, cells + 2 * GROUP, channels), BF16),...  8.84 us
    pallas_call x1, Pallas kernels, body(): call(backward_kernel, (shape((cells, channels), F32), *[shape((3, cells,...  7.55 us
    pallas_call x1, Pallas kernels, body(): call(features_kernel, shape((cells, out_width), BF16), [VMEM] * 6, [pltpu...  2.66 us
    ppermute x16, waiting for transfers between devices, swap_pairs(): return lax.ppermute(array, axis, pairs)  2.64 us
    pallas_call x1, Pallas kernels, body(): call(finish_kernel, (shape((9 * hidden, out_width), F32), shape(corr_weig...  2.52 us
  transfers between devices with their start and end apart: 43, of which 14 were waited for; matrix products, arithmetic and copies ran while one was open for 3% of the time, Pallas kernels for 13%

profile of v10, /device:TPU:33, one launch (start us, length us, event | category | flops | bytes accessed | tf_op | source)
XLA Modules:
  0.0 113.6 jit_solution(5876888331839392566)
XLA Ops:
  0.6 1.8 %shard_map.137.refs_0_ = bf16[560,256]{1,0:T(8,128)(2,1)} custom-call(bf16[512,256]{1,0:T(8,128)(2,1)} %bitcast.25, bf16[512,128]{1,0:T(8,128)(2,1)} %bitcast.26), custom_call_target="tpu_custom_call" | custom-call | tf_op jit(solution)/shard_map/pallas_call | solution.py:391
  3.1 3.7 %collective-permute-start.1 = (bf16[560,256]{1,0:T(8,128)(2,1)}, bf16[560,256]{1,0:T(8,128)(2,1)S(1)}, u32[]{:S(2)}, u32[]{:S(2)}) collective-permute-start(bf16[560,256]{1,0:T(8,128)(2,1)} %shard_map.137.refs_0_), channel_id=1, source_target_pairs={{0,2},{2,0},{1,3},{3,1},{4,6},{6,4},{5,7},{7,5},{8,10},{10,8},{9,1... | collective-permute-start | bytes 860168 | tf_op jit(solution)/shard_map/ppermute | solution.py:35
  6.9 4.2 %collective-permute-start.11 = (bf16[560,256]{1,0:T(8,128)(2,1)}, bf16[560,256]{1,0:T(8,128)(2,1)S(1)}, u32[]{:S(2)}, u32[]{:S(2)}) collective-permute-start(bf16[560,256]{1,0:T(8,128)(2,1)} %shard_map.137.refs_0_), channel_id=1, source_target_pairs={{8,16},{16,8},{24,32},{32,24},{40,48},{48,40},{56,64},{64,56},{72,... | collective-permute-start | bytes 860168 | tf_op jit(solution)/shard_map/ppermute | solution.py:35
  11.4 1.8 %collective-permute-start = (bf16[560,256]{1,0:T(8,128)(2,1)}, bf16[560,256]{1,0:T(8,128)(2,1)S(1)}, u32[]{:S(2)}, u32[]{:S(2)}) collective-permute-start(bf16[560,256]{1,0:T(8,128)(2,1)} %shard_map.137.refs_0_), channel_id=1, source_target_pairs={{0,1},{1,0},{2,3},{3,2},{4,5},{5,4},{6,7},{7,6},{8,9},{9,8},{10,11... | collective-permute-start | bytes 860168 | tf_op jit(solution)/shard_map/ppermute | solution.py:25
  14.4 3.2 %collective-permute-start.13 = (bf16[560,256]{1,0:T(8,128)(2,1)S(1)}, bf16[560,256]{1,0:T(8,128)(2,1)S(1)}, u32[]{:S(2)}, u32[]{:S(2)}) collective-permute-start(bf16[560,256]{1,0:T(8,128)(2,1)S(1)} %collective-permute-done.1.refs_2_), channel_id=1, source_target_pairs={{8,16},{16,8},{24,32},{32,24},{40,48},{48,40},{56,64},{64,56},{72,... | collective-permute-start | bytes 860168 | tf_op jit(solution)/shard_map/ppermute | solution.py:35
  18.9 2.5 %collective-permute-start.7 = (bf16[560,256]{1,0:T(8,128)(2,1)S(1)}, bf16[560,256]{1,0:T(8,128)(2,1)S(1)}, u32[]{:S(2)}, u32[]{:S(2)}) collective-permute-start(bf16[560,256]{1,0:T(8,128)(2,1)S(1)} %collective-permute-done.5.refs_6_), channel_id=1, source_target_pairs={{0,2},{2,0},{1,3},{3,1},{4,6},{6,4},{5,7},{7,5},{8,10},{10,8},{9,1... | collective-permute-start | bytes 860168 | tf_op jit(solution)/shard_map/ppermute | solution.py:35
  21.4 2.7 %collective-permute-start.12 = (bf16[560,256]{1,0:T(8,128)(2,1)S(1)}, bf16[560,256]{1,0:T(8,128)(2,1)S(1)}, u32[]{:S(2)}, u32[]{:S(2)}) collective-permute-start(bf16[560,256]{1,0:T(8,128)(2,1)S(1)} %collective-permute-done.11.refs_12_), channel_id=1, source_target_pairs={{0,1},{1,0},{2,3},{3,2},{4,5},{5,4},{6,7},{7,6},{8,9},{9,8},{10,11... | collective-permute-start | bytes 860168 | tf_op jit(solution)/shard_map/ppermute | solution.py:25
  24.3 2.4 %collective-permute-start.2 = (bf16[560,256]{1,0:T(8,128)(2,1)S(1)}, bf16[560,256]{1,0:T(8,128)(2,1)S(1)}, u32[]{:S(2)}, u32[]{:S(2)}) collective-permute-start(bf16[560,256]{1,0:T(8,128)(2,1)S(1)} %collective-permute-done.1.refs_2_), channel_id=1, source_target_pairs={{0,1},{1,0},{2,3},{3,2},{4,5},{5,4},{6,7},{7,6},{8,9},{9,8},{10,11... | collective-permute-start | bytes 860168 | tf_op jit(solution)/shard_map/ppermute | solution.py:25
  27.8 1.5 %collective-permute-start.10 = (bf16[560,256]{1,0:T(8,128)(2,1)S(1)}, bf16[560,256]{1,0:T(8,128)(2,1)}, u32[]{:S(2)}, u32[]{:S(2)}) collective-permute-start(bf16[560,256]{1,0:T(8,128)(2,1)S(1)} %collective-permute-done.9.refs_10_), channel_id=1, source_target_pairs={{0,1},{1,0},{2,3},{3,2},{4,5},{5,4},{6,7},{7,6},{8,9},{9,8},{10,11... | collective-permute-start | bytes 860168 | tf_op jit(solution)/shard_map/ppermute | solution.py:25
  29.9 2.0 %shard_map.136 = (bf16[512,256]{1,0:T(8,128)(2,1)}, bf16[512,256]{1,0:T(8,128)(2,1)}) custom-call(bf16[324,256]{1,0:T(8,128)(2,1)} %weight.1), custom_call_target="tpu_custom_call" | custom-call | tf_op jit(solution)/shard_map/pallas_call | solution.py:405
  33.4 8.8 %shard_map.138 = (bf16[4,768,256]{2,1,0:T(8,128)(2,1)}, bf16[512,256]{1,0:T(8,128)(2,1)}, bf16[512,256]{1,0:T(8,128)(2,1)}, bf16[32,256]{1,0:T(8,128)(2,1)}, bf1...) custom-call(s32[1,1,4]{2,1,0:T(1,128)} %partners.3, ...), custom_call_target="tpu_custom_call" | custom-call | flops 3000000000 | bytes 10000000 | tf_op jit(solution)/shard_map/pallas_call | solution.py:412
  42.7 3.9 %collective-permute-start.18 = (bf16[32,256]{1,0:T(8,128)(2,1)}, bf16[32,256]{1,0:T(8,128)(2,1)S(1)}, u32[]{:S(2)}, u32[]{:S(2)}) collective-permute-start(bf16[32,256]{1,0:T(8,128)(2,1)} %get-tuple-element.42), channel_id=1, source_target_pairs={{8,16},{16,8},{24,32},{32,24},{40,48},{48,40},{56,64},{64,56},{72,... | collective-permute-start | bytes 49160 | tf_op jit(solution)/shard_map/ppermute | solution.py:35
  46.9 7.6 %shard_map.139 = (f32[512,256]{1,0:T(8,128)}, bf16[3,512,256]{2,1,0:T(8,128)(2,1)}, bf16[3,512,256]{2,1,0:T(8,128)(2,1)}, bf16[3,512,256]{2,1,0:T(8,128)(2,1)}, bf16[6,512,256]{2,1,0:T(8,128)(2,1)}) custom-call(s32[1,1,4]{2,1,0:T(1,128)} %partners.3, s32[1,1]{1,0:T(1,128)S(6)} %copy.15.counts, s32[1,1]{1,0:T(1,128)S(6)} %copy.16.radius, ...), custom_call_target="tpu_custom_call" | custom-call | flops 3000000000 | bytes 10000000 | tf_op jit(solution)/shard_map/pallas_call | solution.py:449
  55.6 3.3 %collective-permute-start.20 = (bf16[18,256]{1,0:T(8,128)(2,1)}, bf16[18,256]{1,0:T(8,128)(2,1)}, u32[]{:S(2)}, u32[]{:S(2)}) collective-permute-start(bf16[18,256]{1,0:T(8,128)(2,1)} %get-tuple-element.76), channel_id=1, source_target_pairs={{1,2},{2,1},{3,4},{4,3},{5,6},{6,5},{9,10},{10,9},{11,12},{12,11},... | collective-permute-start | bytes 27656 | tf_op jit(solution)/shard_map/ppermute | solution.py:35
  59.1 1.8 %collective-permute-done.20 = bf16[18,256]{1,0:T(8,128)(2,1)} collective-permute-done((bf16[18,256]{1,0:T(8,128)(2,1)}, bf16[18,256]{1,0:T(8,128)(2,1)}, u32[]{:S(2)}, u32[]{:S(2)}) %collective-permute-start.20) | collective-permute-done | bytes 9248 | tf_op jit(solution)/shard_map/ppermute | solution.py:35
  61.0 1.3 %broadcast_select_fusion.2 = (bf16[18,256]{1,0:T(8,128)(2,1)}, bf16[18,256]{1,0:T(8,128)(2,1)}) fusion(bf16[18,256]{1,0:T(8,128)(2,1)} %collective-permute-done.21, bf16[18,256]{1,0:T(8,128)(2,1)} %collective-permute-done.20, pred[]{:T(512)S(6)} %eq.23), kind=kLoop, calls=%fused_computation.23 | loop fusion | flops 9216 | bytes 36865 | tf_op jit(solution)/shard_map/jit(_where)/select_n | solution.py:46
  62.4 1.5 %collective-permute-start.23 = (bf16[384,128]{1,0:T(8,128)(2,1)S(1)}, bf16[384,128]{1,0:T(8,128)(2,1)S(1)}, u32[]{:S(2)}, u32[]{:S(2)}) collective-permute-start(bf16[384,128]{1,0:T(8,128)(2,1)S(1)} %get-tuple-element.68), channel_id=1, source_target_pairs={{0,2},{1,3},{2,0},{3,1},{4,6},{5,7},{6,4},{7,5},{8,10},{9,11},{10,... | collective-permute-start | bytes 294920 | tf_op jit(solution)/shard_map/ppermute | solution.py:25
  65.1 1.3 %collective-permute-start.25 = (bf16[384,128]{1,0:T(8,128)(2,1)S(1)}, bf16[384,128]{1,0:T(8,128)(2,1)S(1)}, u32[]{:S(2)}, u32[]{:S(2)}) collective-permute-start(bf16[384,128]{1,0:T(8,128)(2,1)S(1)} %get-tuple-element.69), channel_id=1, source_target_pairs={{0,6},{1,7},{2,4},{3,5},{4,2},{5,3},{6,0},{7,1},{8,14},{9,15},{10,... | collective-permute-start | bytes 294920 | tf_op jit(solution)/shard_map/ppermute | solution.py:25
  67.9 2.0 %collective-permute-done.24 = bf16[384,128]{1,0:T(8,128)(2,1)S(1)} collective-permute-done((bf16[384,128]{1,0:T(8,128)(2,1)S(1)}, bf16[384,128]{1,0:T(8,128)(2,1)S(1)}, u32[]{:S(2)}, u32[]{:S(2)}) %collective-permute-start.24) | collective-permute-done | bytes 98336 | tf_op jit(solution)/shard_map/ppermute | solution.py:25
  69.9 2.6 %collective-permute-done.25 = bf16[384,128]{1,0:T(8,128)(2,1)S(1)} collective-permute-done((bf16[384,128]{1,0:T(8,128)(2,1)S(1)}, bf16[384,128]{1,0:T(8,128)(2,1)S(1)}, u32[]{:S(2)}, u32[]{:S(2)}) %collective-permute-start.25) | collective-permute-done | bytes 98336 | tf_op jit(solution)/shard_map/ppermute | solution.py:25
  72.6 1.8 %collective-permute-start.26 = (bf16[384,128]{1,0:T(8,128)(2,1)S(1)}, bf16[384,128]{1,0:T(8,128)(2,1)S(1)}, u32[]{:S(2)}, u32[]{:S(2)}) collective-permute-start(bf16[384,128]{1,0:T(8,128)(2,1)S(1)} %add_convert_fusion.2), channel_id=1, source_target_pairs={{0,8},{8,0},{16,24},{24,16},{32,40},{40,32},{48,56},{56,48},{64,72... | collective-permute-start | bytes 294920 | tf_op jit(solution)/shard_map/ppermute | solution.py:25
  74.3 1.7 %collective-permute-start.27 = (bf16[384,128]{1,0:T(8,128)(2,1)S(1)}, bf16[384,128]{1,0:T(8,128)(2,1)S(1)}, u32[]{:S(2)}, u32[]{:S(2)}) collective-permute-start(bf16[384,128]{1,0:T(8,128)(2,1)S(1)} %add_convert_fusion.2), channel_id=1, source_target_pairs={{0,16},{8,24},{16,0},{24,8},{32,48},{40,56},{48,32},{56,40},{64,80... | collective-permute-start | bytes 294920 | tf_op jit(solution)/shard_map/ppermute | solution.py:25
  77.0 3.7 %collective-permute-done.27 = bf16[384,128]{1,0:T(8,128)(2,1)S(1)} collective-permute-done((bf16[384,128]{1,0:T(8,128)(2,1)S(1)}, bf16[384,128]{1,0:T(8,128)(2,1)S(1)}, u32[]{:S(2)}, u32[]{:S(2)}) %collective-permute-start.27) | collective-permute-done | bytes 98336 | tf_op jit(solution)/shard_map/ppermute | solution.py:25
  80.8 2.7 %collective-permute-done.28 = bf16[384,128]{1,0:T(8,128)(2,1)S(1)} collective-permute-done((bf16[384,128]{1,0:T(8,128)(2,1)S(1)}, bf16[384,128]{1,0:T(8,128)(2,1)S(1)}, u32[]{:S(2)}, u32[]{:S(2)}) %collective-permute-start.28) | collective-permute-done | bytes 98336 | tf_op jit(solution)/shard_map/ppermute | solution.py:25
  83.6 2.7 %collective-permute-start.30 = (bf16[384,128]{1,0:T(8,128)(2,1)S(1)}, bf16[384,128]{1,0:T(8,128)(2,1)S(1)}, u32[]{:S(2)}, u32[]{:S(2)}) collective-permute-start(bf16[384,128]{1,0:T(8,128)(2,1)S(1)} %add_convert_fusion.1), channel_id=1, source_target_pairs={{0,64},{8,72},{16,80},{24,88},{32,96},{40,104},{48,112},{56,120},{... | collective-permute-start | bytes 294920 | tf_op jit(solution)/shard_map/ppermute | solution.py:25
  87.4 3.4 %collective-permute-done.30 = bf16[384,128]{1,0:T(8,128)(2,1)S(1)} collective-permute-done((bf16[384,128]{1,0:T(8,128)(2,1)S(1)}, bf16[384,128]{1,0:T(8,128)(2,1)S(1)}, u32[]{:S(2)}, u32[]{:S(2)}) %collective-permute-start.30) | collective-permute-done | bytes 98336 | tf_op jit(solution)/shard_map/ppermute | solution.py:25
  90.9 1.4 %collective-permute-done.31 = bf16[384,128]{1,0:T(8,128)(2,1)S(1)} collective-permute-done((bf16[384,128]{1,0:T(8,128)(2,1)S(1)}, bf16[384,128]{1,0:T(8,128)(2,1)S(1)}, u32[]{:S(2)}, u32[]{:S(2)}) %collective-permute-start.31) | collective-permute-done | bytes 98336 | tf_op jit(solution)/shard_map/ppermute | solution.py:25
  92.5 2.7 %collective-permute-start.33 = (bf16[384,128]{1,0:T(8,128)(2,1)S(1)}, bf16[384,128]{1,0:T(8,128)(2,1)S(1)}, u32[]{:S(2)}, u32[]{:S(2)}) collective-permute-start(bf16[384,128]{1,0:T(8,128)(2,1)S(1)} %add_convert_fusion.refs_0_), channel_id=1, source_target_pairs={{0,4},{1,5},{2,6},{3,7},{4,0},{5,1},{6,2},{7,3},{8,12},{9,13},{10,... | collective-permute-start | bytes 294920 | tf_op jit(solution)/shard_map/ppermute | solution.py:25
  96.9 5.8 %collective-permute-start.38 = (bf16[512,256]{1,0:T(8,128)(2,1)S(1)}, bf16[512,256]{1,0:T(8,128)(2,1)S(1)}, u32[]{:S(2)}, u32[]{:S(2)}) collective-permute-start(bf16[512,256]{1,0:T(8,128)(2,1)S(1)} %get-tuple-element.67), channel_id=1, source_target_pairs={{8,16},{16,8},{24,32},{32,24},{40,48},{48,40},{56,64},{64,56},{72,... | collective-permute-start | bytes 786440 | tf_op jit(solution)/shard_map/ppermute | solution.py:35
  102.7 2.7 %shard_map.140 = bf16[512,128]{1,0:T(8,128)(2,1)} custom-call(bf16[512,256]{1,0:T(8,128)(2,1)} %get-tuple-element.35.motion, bf16[32,256]{1,0:T(8,128)(2,1)} %copy-done.13, bf16[32,256]{1,0:T(8,128)(2,1)} %copy-done.12, bf16[18,256]{1,0:T(8,128)(2,1)} %get-tuple-element.47.west, bf16[18,256]{1,0:T(8,128)(2,1)} %get-tuple-element.48.east, ...), custom_call_target="tpu_custom_call" | custom-call | flops 1000000000 | bytes 3333333 | tf_op jit(solution)/shard_map/pallas_call | solution.py:475
  105.4 1.9 %collective-permute-start.39 = (bf16[384,128]{1,0:T(8,128)(2,1)S(1)}, bf16[384,128]{1,0:T(8,128)(2,1)S(1)}, u32[]{:S(2)}, u32[]{:S(2)}) collective-permute-start(bf16[384,128]{1,0:T(8,128)(2,1)S(1)} %add_convert_fusion.refs_0_), channel_id=1, source_target_pairs={{0,1},{1,0},{2,3},{3,2},{4,5},{5,4},{6,7},{7,6},{8,9},{9,8},{10,11... | collective-permute-start | bytes 294920 | tf_op jit(solution)/shard_map/ppermute | solution.py:25
  110.2 2.5 %shard_map.141 = (f32[2304,128]{1,0:T(8,128)}, f32[324,256]{1,0:T(8,128)}) custom-call(bf16[384,128]{1,0:T(8,128)(2,1)} %copy-done.4, bf16[384,128]{1,0:T(8,128)(2,1)} %copy-done.5, bf16[384,128]{1,0:T(8,128)(2,1)} %copy-done.6, bf16[384,128]{1,0:T(8,128)(2,1)} %copy-done.7, bf16[384,128]{1,0:T(8,128)(2,1)} %copy-done.8, bf16[384,128]{1,0:T(8,128)(2,1)} %copy-done.9, ...), custom_call_target="tpu_custom_call" | custom-call | tf_op jit(solution)/shard_map/pallas_call | solution.py:491
  (128 shorter events, 17.9 us)
Async XLA Ops:
  2.5 10.8 %collective-permute-start.3 = (bf16[560,256]{1,0:T(8,128)(2,1)}, bf16[560,256]{1,0:T(8,128)(2,1)S(1)}, u32[]{:S(2)}, u32[]{:S(2)}) collective-permute-start(bf16[560,256]{1,0:T(8,128)(2,1)} %shard_map.137.refs_0_), channel_id=1, source_target_pairs={{2,4},{4,2},{3,5},{5,3},{10,12},{12,10},{11,13},{13,11},{18,20},{2... | collective-permute-start | bytes 860168 | tf_op jit(solution)/shard_map/ppermute | solution.py:35
  3.1 11.3 %collective-permute-start.1 = (bf16[560,256]{1,0:T(8,128)(2,1)}, bf16[560,256]{1,0:T(8,128)(2,1)S(1)}, u32[]{:S(2)}, u32[]{:S(2)}) collective-permute-start(bf16[560,256]{1,0:T(8,128)(2,1)} %shard_map.137.refs_0_), channel_id=1, source_target_pairs={{0,2},{2,0},{1,3},{3,1},{4,6},{6,4},{5,7},{7,5},{8,10},{10,8},{9,1... | collective-permute-start | bytes 860168 | tf_op jit(solution)/shard_map/ppermute | solution.py:35
  6.9 11.3 %collective-permute-start.11 = (bf16[560,256]{1,0:T(8,128)(2,1)}, bf16[560,256]{1,0:T(8,128)(2,1)S(1)}, u32[]{:S(2)}, u32[]{:S(2)}) collective-permute-start(bf16[560,256]{1,0:T(8,128)(2,1)} %shard_map.137.refs_0_), channel_id=1, source_target_pairs={{8,16},{16,8},{24,32},{32,24},{40,48},{48,40},{56,64},{64,56},{72,... | collective-permute-start | bytes 860168 | tf_op jit(solution)/shard_map/ppermute | solution.py:35
  11.1 7.8 %collective-permute-start.5 = (bf16[560,256]{1,0:T(8,128)(2,1)}, bf16[560,256]{1,0:T(8,128)(2,1)S(1)}, u32[]{:S(2)}, u32[]{:S(2)}) collective-permute-start(bf16[560,256]{1,0:T(8,128)(2,1)} %shard_map.137.refs_0_), channel_id=1, source_target_pairs={{0,8},{8,0},{16,24},{24,16},{32,40},{40,32},{48,56},{56,48},{64,72... | collective-permute-start | bytes 860168 | tf_op jit(solution)/shard_map/ppermute | solution.py:35
  11.4 9.9 %collective-permute-start = (bf16[560,256]{1,0:T(8,128)(2,1)}, bf16[560,256]{1,0:T(8,128)(2,1)S(1)}, u32[]{:S(2)}, u32[]{:S(2)}) collective-permute-start(bf16[560,256]{1,0:T(8,128)(2,1)} %shard_map.137.refs_0_), channel_id=1, source_target_pairs={{0,1},{1,0},{2,3},{3,2},{4,5},{5,4},{6,7},{7,6},{8,9},{9,8},{10,11... | collective-permute-start | bytes 860168 | tf_op jit(solution)/shard_map/ppermute | solution.py:25
  13.3 11.0 %collective-permute-start.9 = (bf16[560,256]{1,0:T(8,128)(2,1)S(1)}, bf16[560,256]{1,0:T(8,128)(2,1)S(1)}, u32[]{:S(2)}, u32[]{:S(2)}) collective-permute-start(bf16[560,256]{1,0:T(8,128)(2,1)S(1)} %collective-permute-done.3.refs_4_), channel_id=1, source_target_pairs={{0,8},{8,0},{16,24},{24,16},{32,40},{40,32},{48,56},{56,48},{64,72... | collective-permute-start | bytes 860168 | tf_op jit(solution)/shard_map/ppermute | solution.py:35
  14.4 12.3 %collective-permute-start.13 = (bf16[560,256]{1,0:T(8,128)(2,1)S(1)}, bf16[560,256]{1,0:T(8,128)(2,1)S(1)}, u32[]{:S(2)}, u32[]{:S(2)}) collective-permute-start(bf16[560,256]{1,0:T(8,128)(2,1)S(1)} %collective-permute-done.1.refs_2_), channel_id=1, source_target_pairs={{8,16},{16,8},{24,32},{32,24},{40,48},{48,40},{56,64},{64,56},{72,... | collective-permute-start | bytes 860168 | tf_op jit(solution)/shard_map/ppermute | solution.py:35
  18.2 9.5 %collective-permute-start.15 = (bf16[560,256]{1,0:T(8,128)(2,1)S(1)}, bf16[560,256]{1,0:T(8,128)(2,1)S(1)}, u32[]{:S(2)}, u32[]{:S(2)}) collective-permute-start(bf16[560,256]{1,0:T(8,128)(2,1)S(1)} %collective-permute-done.11.refs_12_), channel_id=1, source_target_pairs={{2,4},{4,2},{3,5},{5,3},{10,12},{12,10},{11,13},{13,11},{18,20},{2... | collective-permute-start | bytes 860168 | tf_op jit(solution)/shard_map/ppermute | solution.py:35
  18.9 8.9 %collective-permute-start.7 = (bf16[560,256]{1,0:T(8,128)(2,1)S(1)}, bf16[560,256]{1,0:T(8,128)(2,1)S(1)}, u32[]{:S(2)}, u32[]{:S(2)}) collective-permute-start(bf16[560,256]{1,0:T(8,128)(2,1)S(1)} %collective-permute-done.5.refs_6_), channel_id=1, source_target_pairs={{0,2},{2,0},{1,3},{3,1},{4,6},{6,4},{5,7},{7,5},{8,10},{10,8},{9,1... | collective-permute-start | bytes 860168 | tf_op jit(solution)/shard_map/ppermute | solution.py:35
  21.4 7.9 %collective-permute-start.12 = (bf16[560,256]{1,0:T(8,128)(2,1)S(1)}, bf16[560,256]{1,0:T(8,128)(2,1)S(1)}, u32[]{:S(2)}, u32[]{:S(2)}) collective-permute-start(bf16[560,256]{1,0:T(8,128)(2,1)S(1)} %collective-permute-done.11.refs_12_), channel_id=1, source_target_pairs={{0,1},{1,0},{2,3},{3,2},{4,5},{5,4},{6,7},{7,6},{8,9},{9,8},{10,11... | collective-permute-start | bytes 860168 | tf_op jit(solution)/shard_map/ppermute | solution.py:25
  24.3 5.1 %collective-permute-start.2 = (bf16[560,256]{1,0:T(8,128)(2,1)S(1)}, bf16[560,256]{1,0:T(8,128)(2,1)S(1)}, u32[]{:S(2)}, u32[]{:S(2)}) collective-permute-start(bf16[560,256]{1,0:T(8,128)(2,1)S(1)} %collective-permute-done.1.refs_2_), channel_id=1, source_target_pairs={{0,1},{1,0},{2,3},{3,2},{4,5},{5,4},{6,7},{7,6},{8,9},{9,8},{10,11... | collective-permute-start | bytes 860168 | tf_op jit(solution)/shard_map/ppermute | solution.py:25
  27.7 5.5 %collective-permute-start.6 = (bf16[560,256]{1,0:T(8,128)(2,1)S(1)}, bf16[560,256]{1,0:T(8,128)(2,1)}, u32[]{:S(2)}, u32[]{:S(2)}) collective-permute-start(bf16[560,256]{1,0:T(8,128)(2,1)S(1)} %collective-permute-done.5.refs_6_), channel_id=1, source_target_pairs={{0,1},{1,0},{2,3},{3,2},{4,5},{5,4},{6,7},{7,6},{8,9},{9,8},{10,11... | collective-permute-start | bytes 860168 | tf_op jit(solution)/shard_map/ppermute | solution.py:25
  27.8 5.4 %collective-permute-start.10 = (bf16[560,256]{1,0:T(8,128)(2,1)S(1)}, bf16[560,256]{1,0:T(8,128)(2,1)}, u32[]{:S(2)}, u32[]{:S(2)}) collective-permute-start(bf16[560,256]{1,0:T(8,128)(2,1)S(1)} %collective-permute-done.9.refs_10_), channel_id=1, source_target_pairs={{0,1},{1,0},{2,3},{3,2},{4,5},{5,4},{6,7},{7,6},{8,9},{9,8},{10,11... | collective-permute-start | bytes 860168 | tf_op jit(solution)/shard_map/ppermute | solution.py:25
  42.2 20.1 %collective-permute-start.22 = (bf16[1536,128]{1,0:T(8,128)(2,1)}, bf16[1536,128]{1,0:T(8,128)(2,1)S(1)}, u32[]{:S(2)}, u32[]{:S(2)}) collective-permute-start(bf16[1536,128]{1,0:T(8,128)(2,1)} %get-tuple-element.50), channel_id=1, source_target_pairs={{0,1},{1,0},{2,3},{3,2},{4,5},{5,4},{6,7},{7,6},{8,9},{9,8},{10,11... | collective-permute-start | bytes 1179656 | tf_op jit(solution)/shard_map/ppermute | solution.py:25
  42.7 12.2 %collective-permute-start.18 = (bf16[32,256]{1,0:T(8,128)(2,1)}, bf16[32,256]{1,0:T(8,128)(2,1)S(1)}, u32[]{:S(2)}, u32[]{:S(2)}) collective-permute-start(bf16[32,256]{1,0:T(8,128)(2,1)} %get-tuple-element.42), channel_id=1, source_target_pairs={{8,16},{16,8},{24,32},{32,24},{40,48},{48,40},{56,64},{64,56},{72,... | collective-permute-start | bytes 49160 | tf_op jit(solution)/shard_map/ppermute | solution.py:35
  46.6 8.3 %collective-permute-start.19 = (bf16[32,256]{1,0:T(8,128)(2,1)}, bf16[32,256]{1,0:T(8,128)(2,1)S(1)}, u32[]{:S(2)}, u32[]{:S(2)}) collective-permute-start(bf16[32,256]{1,0:T(8,128)(2,1)} %get-tuple-element.43), channel_id=1, source_target_pairs={{0,8},{8,0},{16,24},{24,16},{32,40},{40,32},{48,56},{56,48},{64,72... | collective-permute-start | bytes 49160 | tf_op jit(solution)/shard_map/ppermute | solution.py:35
  54.5 12.0 %collective-permute-start.17 = (bf16[6,512,256]{2,1,0:T(8,128)(2,1)}, bf16[6,512,256]{2,1,0:T(8,128)(2,1)S(1)}, u32[]{:S(2)}, u32[]{:S(2)}) collective-permute-start(bf16[6,512,256]{2,1,0:T(8,128)(2,1)} %get-tuple-element.40), channel_id=1, source_target_pairs={{0,1},{1,0},{2,3},{3,2},{4,5},{5,4},{6,7},{7,6},{8,9},{9,8},{10,11... | collective-permute-start | bytes 4718600 | tf_op jit(solution)/shard_map/ppermute | solution.py:25
  55.6 5.3 %collective-permute-start.20 = (bf16[18,256]{1,0:T(8,128)(2,1)}, bf16[18,256]{1,0:T(8,128)(2,1)}, u32[]{:S(2)}, u32[]{:S(2)}) collective-permute-start(bf16[18,256]{1,0:T(8,128)(2,1)} %get-tuple-element.76), channel_id=1, source_target_pairs={{1,2},{2,1},{3,4},{4,3},{5,6},{6,5},{9,10},{10,9},{11,12},{12,11},... | collective-permute-start | bytes 27656 | tf_op jit(solution)/shard_map/ppermute | solution.py:35
  62.4 5.4 %collective-permute-start.23 = (bf16[384,128]{1,0:T(8,128)(2,1)S(1)}, bf16[384,128]{1,0:T(8,128)(2,1)S(1)}, u32[]{:S(2)}, u32[]{:S(2)}) collective-permute-start(bf16[384,128]{1,0:T(8,128)(2,1)S(1)} %get-tuple-element.68), channel_id=1, source_target_pairs={{0,2},{1,3},{2,0},{3,1},{4,6},{5,7},{6,4},{7,5},{8,10},{9,11},{10,... | collective-permute-start | bytes 294920 | tf_op jit(solution)/shard_map/ppermute | solution.py:25
  64.0 5.9 %collective-permute-start.24 = (bf16[384,128]{1,0:T(8,128)(2,1)S(1)}, bf16[384,128]{1,0:T(8,128)(2,1)S(1)}, u32[]{:S(2)}, u32[]{:S(2)}) collective-permute-start(bf16[384,128]{1,0:T(8,128)(2,1)S(1)} %get-tuple-element.70), channel_id=1, source_target_pairs={{0,4},{1,5},{2,6},{3,7},{4,0},{5,1},{6,2},{7,3},{8,12},{9,13},{10,... | collective-permute-start | bytes 294920 | tf_op jit(solution)/shard_map/ppermute | solution.py:25
  65.1 7.4 %collective-permute-start.25 = (bf16[384,128]{1,0:T(8,128)(2,1)S(1)}, bf16[384,128]{1,0:T(8,128)(2,1)S(1)}, u32[]{:S(2)}, u32[]{:S(2)}) collective-permute-start(bf16[384,128]{1,0:T(8,128)(2,1)S(1)} %get-tuple-element.69), channel_id=1, source_target_pairs={{0,6},{1,7},{2,4},{3,5},{4,2},{5,3},{6,0},{7,1},{8,14},{9,15},{10,... | collective-permute-start | bytes 294920 | tf_op jit(solution)/shard_map/ppermute | solution.py:25
  66.9 29.4 %collective-permute-start.35 = (bf16[3,512,256]{2,1,0:T(8,128)(2,1)S(1)}, bf16[3,512,256]{2,1,0:T(8,128)(2,1)S(1)}, u32[]{:S(2)}, u32[]{:S(2)}) collective-permute-start(bf16[3,512,256]{2,1,0:T(8,128)(2,1)S(1)} %get-tuple-element.54), channel_id=1, source_target_pairs={{0,2},{2,0},{1,3},{3,1},{4,6},{6,4},{5,7},{7,5},{8,10},{10,8},{9,1... | collective-permute-start | bytes 2359304 | tf_op jit(solution)/shard_map/ppermute | solution.py:35
  67.2 29.2 %collective-permute-start.36 = (bf16[3,512,256]{2,1,0:T(8,128)(2,1)S(1)}, bf16[3,512,256]{2,1,0:T(8,128)(2,1)S(1)}, u32[]{:S(2)}, u32[]{:S(2)}) collective-permute-start(bf16[3,512,256]{2,1,0:T(8,128)(2,1)S(1)} %get-tuple-element.55), channel_id=1, source_target_pairs={{2,4},{4,2},{3,5},{5,3},{10,12},{12,10},{11,13},{13,11},{18,20},{2... | collective-permute-start | bytes 2359304 | tf_op jit(solution)/shard_map/ppermute | solution.py:35
  74.3 6.4 %collective-permute-start.27 = (bf16[384,128]{1,0:T(8,128)(2,1)S(1)}, bf16[384,128]{1,0:T(8,128)(2,1)S(1)}, u32[]{:S(2)}, u32[]{:S(2)}) collective-permute-start(bf16[384,128]{1,0:T(8,128)(2,1)S(1)} %add_convert_fusion.2), channel_id=1, source_target_pairs={{0,16},{8,24},{16,0},{24,8},{32,48},{40,56},{48,32},{56,40},{64,80... | collective-permute-start | bytes 294920 | tf_op jit(solution)/shard_map/ppermute | solution.py:25
  76.1 7.4 %collective-permute-start.28 = (bf16[384,128]{1,0:T(8,128)(2,1)S(1)}, bf16[384,128]{1,0:T(8,128)(2,1)S(1)}, u32[]{:S(2)}, u32[]{:S(2)}) collective-permute-start(bf16[384,128]{1,0:T(8,128)(2,1)S(1)} %add_convert_fusion.2), channel_id=1, source_target_pairs={{0,24},{8,16},{16,8},{24,0},{32,56},{40,48},{48,40},{56,32},{64,88... | collective-permute-start | bytes 294920 | tf_op jit(solution)/shard_map/ppermute | solution.py:25
  83.6 7.3 %collective-permute-start.30 = (bf16[384,128]{1,0:T(8,128)(2,1)S(1)}, bf16[384,128]{1,0:T(8,128)(2,1)S(1)}, u32[]{:S(2)}, u32[]{:S(2)}) collective-permute-start(bf16[384,128]{1,0:T(8,128)(2,1)S(1)} %add_convert_fusion.1), channel_id=1, source_target_pairs={{0,64},{8,72},{16,80},{24,88},{32,96},{40,104},{48,112},{56,120},{... | collective-permute-start | bytes 294920 | tf_op jit(solution)/shard_map/ppermute | solution.py:25
  86.3 5.9 %collective-permute-start.31 = (bf16[384,128]{1,0:T(8,128)(2,1)S(1)}, bf16[384,128]{1,0:T(8,128)(2,1)S(1)}, u32[]{:S(2)}, u32[]{:S(2)}) collective-permute-start(bf16[384,128]{1,0:T(8,128)(2,1)S(1)} %add_convert_fusion.1), channel_id=1, source_target_pairs={{0,96},{8,104},{16,112},{24,120},{32,64},{40,72},{48,80},{56,88},{... | collective-permute-start | bytes 294920 | tf_op jit(solution)/shard_map/ppermute | solution.py:25
  92.4 13.0 %collective-permute-start.32 = (bf16[384,128]{1,0:T(8,128)(2,1)S(1)}, bf16[384,128]{1,0:T(8,128)(2,1)S(1)}, u32[]{:S(2)}, u32[]{:S(2)}) collective-permute-start(bf16[384,128]{1,0:T(8,128)(2,1)S(1)} %add_convert_fusion.refs_0_), channel_id=1, source_target_pairs={{0,2},{1,3},{2,0},{3,1},{4,6},{5,7},{6,4},{7,5},{8,10},{9,11},{10,... | collective-permute-start | bytes 294920 | tf_op jit(solution)/shard_map/ppermute | solution.py:25
  92.5 12.9 %collective-permute-start.33 = (bf16[384,128]{1,0:T(8,128)(2,1)S(1)}, bf16[384,128]{1,0:T(8,128)(2,1)S(1)}, u32[]{:S(2)}, u32[]{:S(2)}) collective-permute-start(bf16[384,128]{1,0:T(8,128)(2,1)S(1)} %add_convert_fusion.refs_0_), channel_id=1, source_target_pairs={{0,4},{1,5},{2,6},{3,7},{4,0},{5,1},{6,2},{7,3},{8,12},{9,13},{10,... | collective-permute-start | bytes 294920 | tf_op jit(solution)/shard_map/ppermute | solution.py:25
  95.1 10.2 %collective-permute-start.34 = (bf16[384,128]{1,0:T(8,128)(2,1)S(1)}, bf16[384,128]{1,0:T(8,128)(2,1)S(1)}, u32[]{:S(2)}, u32[]{:S(2)}) collective-permute-start(bf16[384,128]{1,0:T(8,128)(2,1)S(1)} %add_convert_fusion.refs_0_), channel_id=1, source_target_pairs={{0,6},{1,7},{2,4},{3,5},{4,2},{5,3},{6,0},{7,1},{8,14},{9,15},{10,... | collective-permute-start | bytes 294920 | tf_op jit(solution)/shard_map/ppermute | solution.py:25
  96.8 15.9 %collective-permute-start.37 = (bf16[512,256]{1,0:T(8,128)(2,1)S(1)}, bf16[512,256]{1,0:T(8,128)(2,1)S(1)}, u32[]{:S(2)}, u32[]{:S(2)}) collective-permute-start(bf16[512,256]{1,0:T(8,128)(2,1)S(1)} %get-tuple-element.66), channel_id=1, source_target_pairs={{0,8},{8,0},{16,24},{24,16},{32,40},{40,32},{48,56},{56,48},{64,72... | collective-permute-start | bytes 786440 | tf_op jit(solution)/shard_map/ppermute | solution.py:35
  96.9 15.9 %collective-permute-start.38 = (bf16[512,256]{1,0:T(8,128)(2,1)S(1)}, bf16[512,256]{1,0:T(8,128)(2,1)S(1)}, u32[]{:S(2)}, u32[]{:S(2)}) collective-permute-start(bf16[512,256]{1,0:T(8,128)(2,1)S(1)} %get-tuple-element.67), channel_id=1, source_target_pairs={{8,16},{16,8},{24,32},{32,24},{40,48},{48,40},{56,64},{64,56},{72,... | collective-permute-start | bytes 786440 | tf_op jit(solution)/shard_map/ppermute | solution.py:35
  (38 other events, 264.0 us)
